TPU v7x, 32 devices: a whole 2x2x4 slice. The times are simulated.
32 devices in a mesh: lat: 4 (over y, x), lon: 8 (over z, core).
Axes of the slice: x: 2, y: 2, z: 4, core: 2. Of those that a mesh axis runs over, the one named last changes fastest.
Arguments:
- tracer: float32 [100, 32, 1024], P(None, 'lat', 'lon'), may hold values from -100 to 100
- cotangent: float32 [100, 32, 1024], P(None, 'lat', 'lon'), may hold values from -6 to 6
- land_mask: int32 [32, 1024], P('lat', 'lon'), may hold values 0 or 1
- bottom: int32 [32, 1024], P('lat', 'lon'), may hold values from 25 to 100
- kappa: float32 [100], replicated, may hold values from 0.05 to 8
- w_in: bfloat16 [100, 512], replicated, may hold values from -0.625 to 0.625
- b_in: float32 [512], replicated, may hold values from -4 to 4
- w_out: bfloat16 [512, 100], replicated, may hold values from -0.25 to 0.25
- b_out: float32 [100], replicated, may hold values from 6 to 24
Outputs:
- tracer_adjoint: float32 [100, 32, 1024], P(None, 'lat', 'lon')
- grad_w_in: float32 [100, 512], replicated
- grad_b_in: float32 [512], replicated
- grad_w_out: float32 [512, 100], replicated
- grad_b_out: float32 [100], replicated
All inputs are finite; a program needn't handle non-finite values. No bound on the sum of `land_mask` on one device may be relied on, other than what follows from the above.
Results may differ from a plain program's by a relative error of at most 0.0069.
Values sent between devices are 32-bit elements; how exact they have to be, the bound alone decides.
No kernel may reach another device: no remote copies, remote signals or barrier semaphores. Data moves between devices by JAX's collectives and lax.ppermute only.
A program may use at most 64 MiB of HBM per device.

v0:
```python
import math

import jax
import jax.numpy as jnp
from jax import lax
from jax.sharding import PartitionSpec as P

spread_coef = 0.15
level_eps = 1e-05


def with_halo(block, sides, width):
    for axis, dim in sides:
        count = lax.axis_size(axis)
        forward = [(i, i + 1) for i in range(count - 1)]
        forward.append((count - 1, 0))
        backward = [(target, source) for source, target in forward]
        low = lax.ppermute(
            lax.slice_in_dim(block, block.shape[dim] - width, None, axis=dim), axis, forward
        )
        high = lax.ppermute(lax.slice_in_dim(block, 0, width, axis=dim), axis, backward)
        block = jnp.concatenate([low, block, high], axis=dim)
    return block


def spread_local(field_pad, wet_pad):
    center = field_pad[:, 1:-1, 1:-1]
    wet_cells = wet_pad[:, 1:-1, 1:-1]
    neighbours = (
        (field_pad[:, 2:, 1:-1], wet_pad[:, 2:, 1:-1]),
        (field_pad[:, :-2, 1:-1], wet_pad[:, :-2, 1:-1]),
        (field_pad[:, 1:-1, :-2], wet_pad[:, 1:-1, :-2]),
        (field_pad[:, 1:-1, 2:], wet_pad[:, 1:-1, 2:]),
    )
    flux_total = jnp.zeros_like(center)
    for near_field, near_wet in neighbours:
        flux_total = flux_total + wet_cells * near_wet * (near_field - center)
    return center + spread_coef * flux_total


def column_solve(below, diagonal, above, right_side):

    def sweep_down(state_pair, row_items):
        ratio_prev, value_prev = state_pair
        below_row, diag_row, above_row, right_row = row_items
        pivot = diag_row - below_row * ratio_prev
        ratio_next = above_row / pivot
        value_next = (right_row - below_row * value_prev) / pivot
        return ((ratio_next, value_next), (ratio_next, value_next))

    zeros_row = jnp.zeros_like(right_side[0])
    _, (ratios, values) = lax.scan(
        sweep_down, (zeros_row, zeros_row), (below, diagonal, above, right_side), unroll=True
    )

    def sweep_up(later, row_items):
        ratio_row, value_row = row_items
        result_row = value_row - ratio_row * later
        return (result_row, result_row)

    _, solved = lax.scan(sweep_up, zeros_row, (ratios, values), reverse=True, unroll=True)
    return solved


def network(wet_tracer, radius, w_in, b_in, w_out, b_out):
    inputs = (wet_tracer / radius[:, None]).astype(jnp.bfloat16)
    pre_act = (
        lax.dot_general(w_in, inputs, (((0,), (0,)), ((), ())), preferred_element_type=jnp.float32)
        + b_in[:, None]
    )
    hidden = jax.nn.silu(pre_act).astype(jnp.bfloat16)
    logits = (
        lax.dot_general(w_out, hidden, (((0,), (0,)), ((), ())), preferred_element_type=jnp.float32)
        + b_out[:, None]
    )
    sinking = jax.nn.softplus(logits)
    return (inputs, pre_act, hidden, logits, sinking)


def coefficients(wet_cells, kappa_col, sinking):
    open_face = wet_cells * jnp.concatenate([wet_cells[1:], jnp.zeros_like(wet_cells[:1])], 0)
    down_coef = open_face * (kappa_col + sinking)
    up_coef = open_face * kappa_col
    prev_down = jnp.concatenate([jnp.zeros_like(down_coef[:1]), down_coef[:-1]], 0)
    prev_up = jnp.concatenate([jnp.zeros_like(up_coef[:1]), up_coef[:-1]], 0)
    diagonal = 1.0 + down_coef + prev_up
    return (open_face, down_coef, up_coef, prev_down, prev_up, diagonal)


def shards(tracer, cotangent, land_mask, bottom, kappa, w_in, b_in, w_out, b_out):
    level_count, lat_rows, lon_cols = tracer.shape
    column_count = lat_rows * lax.axis_size("lat") * lon_cols * lax.axis_size("lon")
    column_depth = (land_mask * bottom).astype(jnp.float32)
    stacked = jnp.concatenate([tracer, column_depth[None]], 0)
    padded = with_halo(stacked, (("lat", 1), ("lon", 2)), 1)
    lat_place = lax.axis_index("lat")
    upper_edge = jnp.where(lat_place == 0, 0.0, 1.0).astype(jnp.float32)
    lower_edge = jnp.where(lat_place == lax.axis_size("lat") - 1, 0.0, 1.0).astype(jnp.float32)
    lat_edge = jnp.concatenate(
        [upper_edge[None], jnp.ones((lat_rows,), jnp.float32), lower_edge[None]]
    )
    depth_pad = padded[-1] * lat_edge[:, None]
    level_ids = jnp.arange(level_count, dtype=jnp.float32)[:, None, None]
    wet_pad = (level_ids < depth_pad[None]).astype(jnp.float32)
    wet_cells = wet_pad[:, 1:-1, 1:-1]
    tracer_pad = padded[:level_count]
    mixed = spread_local(tracer_pad, wet_pad)
    wet_tracer = (wet_cells * tracer).reshape(level_count, -1)
    energy = lax.psum(jnp.sum(wet_tracer * wet_tracer, axis=1), ("lat", "lon"))
    radius = jnp.sqrt(energy / column_count + level_eps)
    inputs, pre_act, hidden, logits, sinking_flat = network(
        wet_tracer, radius, w_in, b_in, w_out, b_out
    )
    sinking = sinking_flat.reshape(tracer.shape)
    kappa_col = kappa[:, None, None]
    open_face, down_coef, up_coef, prev_down, prev_up, diagonal = coefficients(
        wet_cells, kappa_col, sinking
    )
    new_tracer = column_solve(-prev_down, diagonal, -up_coef, mixed)
    adjoint = column_solve(-prev_up, diagonal, -down_coef, cotangent)
    adjoint_pad = with_halo(adjoint, (("lat", 1), ("lon", 2)), 1)
    spread_back = spread_local(adjoint_pad, wet_pad)
    adjoint_next = jnp.concatenate([adjoint[1:], jnp.zeros_like(adjoint[:1])], 0)
    d_sinking = open_face * new_tracer * (adjoint_next - adjoint)
    d_logits = (d_sinking.reshape(level_count, -1) * jax.nn.sigmoid(logits)).astype(jnp.bfloat16)
    grad_out_t = lax.dot_general(
        d_logits, hidden, (((1,), (1,)), ((), ())), preferred_element_type=jnp.float32
    )
    grad_bout = jnp.sum(d_logits.astype(jnp.float32), axis=1)
    d_hidden = jnp.dot(w_out, d_logits, preferred_element_type=jnp.float32)
    gate_sig = jax.nn.sigmoid(pre_act)
    d_pre = (d_hidden * gate_sig * (1.0 + pre_act * (1.0 - gate_sig))).astype(jnp.bfloat16)
    grad_in = lax.dot_general(
        inputs, d_pre, (((1,), (1,)), ((), ())), preferred_element_type=jnp.float32
    )
    grad_bin = jnp.sum(d_pre.astype(jnp.float32), axis=1)[None]
    d_inputs = jnp.dot(w_in, d_pre, preferred_element_type=jnp.float32)
    level_part = jnp.sum(d_inputs * wet_tracer, axis=1)
    shares = (
        lax.psum_scatter(grad_in, "lon", scatter_dimension=1, tiled=True),
        lax.psum_scatter(grad_out_t, "lon", scatter_dimension=1, tiled=True),
        lax.psum_scatter(grad_bin, "lon", scatter_dimension=1, tiled=True),
    )
    share_sums = lax.psum((shares[0], shares[1], shares[2]), "lat")
    sum_in, sum_out_t, sum_bin = (
        lax.all_gather(share_sums[0], "lon", axis=1, tiled=True),
        lax.all_gather(share_sums[1], "lon", axis=1, tiled=True),
        lax.all_gather(share_sums[2], "lon", axis=1, tiled=True),
    )
    sum_bout, level_sum = lax.psum((grad_bout, level_part), ("lat", "lon"))
    column_scale = 1.0 / math.sqrt(column_count)
    d_wet = (
        d_inputs / radius[:, None] - wet_tracer * (level_sum / (column_count * radius**3))[:, None]
    )
    tracer_adjoint = spread_back + wet_cells * d_wet.reshape(tracer.shape)
    grad_w_in = sum_in * column_scale
    grad_b_in = sum_bin[0] * column_scale
    grad_w_out = sum_out_t.T * column_scale
    grad_b_out = sum_bout * column_scale
    return (tracer_adjoint, grad_w_in, grad_b_in, grad_w_out, grad_b_out)


def solution(mesh):
    placed = (
        P(None, "lat", "lon"),
        P(None, "lat", "lon"),
        P("lat", "lon"),
        P("lat", "lon"),
        P(),
        P(),
        P(),
        P(),
        P(),
    )
    return jax.shard_map(
        shards,
        mesh=mesh,
        in_specs=placed,
        out_specs=(P(None, "lat", "lon"), P(), P(), P(), P()),
        check_vma=False,
    )
```

profile of v0, /device:TPU:0, one launch (start us, length us, event | category | flops | bytes accessed | tf_op | source)
XLA Modules:
  0.0 247.9 jit_solution(248294372197258767)
XLA Ops:
  7.9 1.2 pad_maximum_fusion.23
  9.1 3.0 %collective-permute-start = (f32[101,1,128]{2,1,0:T(1,128)S(1)}, f32[101,1,128]{2,1,0:T(1,128)S(1)}, u32[]{:S(2)}, u32[]{:S(2)}) collective-permute-start(f32[101,1,128]{2,1,0:T(1,128)S(1)} %get-tuple-element.639), channel_id=1, source_target_pairs={{0,8},{8,16},{16,24},{24,0},{1,9},{9,17},{17,25},{25,1},{2,10},{10... | collective-permute-start | bytes 155144 | tf_op jit(solution)/shard_map/ppermute | solution.py:18
  13.1 2.0 collective-permute-done
  16.3 1.2 pad_maximum_fusion
  18.5 3.5 %collective-permute-start.3 = (f32[101,10,1]{0,1,2:T(8,128)S(1)}, f32[101,10,1]{0,1,2:T(8,128)S(1)}, u32[]{:S(2)}, u32[]{:S(2)}) collective-permute-start(f32[101,10,1]{0,1,2:T(8,128)S(1)} %copy.1027), channel_id=1, source_target_pairs={{1,0},{2,1},{3,2},{4,3},{5,4},{6,5},{7,6},{0,7},{9,8},{10,9},{11,1... | collective-permute-start | bytes 12128 | tf_op jit(solution)/shard_map/ppermute | solution.py:21
  26.5 2.3 fusion.735
  29.7 39.4 %psum.42 = f32[100]{0:T(128)S(1)} all-reduce(f32[100]{0:T(128)S(1)} %get-tuple-element.633), channel_id=1, replica_groups=mesh['lat'=4,'lon'=8] {'lat','lon'}, use_global_device_ids=true, to_apply=%region_1.2 | all-reduce | flops 100 | bytes 800 | tf_op jit(solution)/shard_map/psum | solution.py:109
  69.1 1.9 fusion.5
  83.3 2.0 convert_reduce_fusion
  86.3 2.6 %collective-permute-start.4 = (f32[100,1,128]{2,1,0:T(1,128)}, f32[100,1,128]{2,1,0:T(1,128)S(1)}, u32[]{:S(2)}, u32[]{:S(2)}) collective-permute-start(f32[100,1,128]{2,1,0:T(1,128)} %get-tuple-element.642), channel_id=1, source_target_pairs={{8,0},{16,8},{24,16},{0,24},{9,1},{17,9},{25,17},{1,25},{10,2},{18... | collective-permute-start | bytes 153608 | tf_op jit(solution)/shard_map/ppermute | solution.py:21
  89.0 1.8 multiply_reduce_fusion
  90.8 1.3 fusion.834
  92.1 41.4 %all-reduce.5 = (f32[100]{0:T(128)S(1)}, f32[100]{0:T(128)S(1)}) all-reduce(f32[100]{0:T(128)S(1)} %get-tuple-element.841, f32[100]{0:T(128)S(1)} %get-tuple-element.30), channel_id=1, replica_groups=mesh['lat'=4,'lon'=8] {'lat','lon'}, use_global_device_ids=true, to_apply=%region_3.4 | all-reduce | flops 200 | bytes 1600 | tf_op jit(solution)/shard_map/psum | solution.py:150
  133.6 2.5 %fusion.543 = f32[100,512]{0,1:T(8,128)} fusion(bf16[512,1024]{0,1:T(8,128)(2,1)} %get-tuple-element.844, f32[100,1024]{1,0:T(8,128)S(1)} %bitcast.5564, f32[100]{0:T(128)S(1)} %add_sqrt_fusion), kind=kOutput, calls=%fused_computation.2098 | convolution fusion | flops 105062400 | bytes 1663376 | tf_op jit(solution)/shard_map/dot_general | solution.py:133
  136.4 1.2 fusion.832
  137.6 1.5 copy.1030
  139.5 3.5 %collective-permute-start.7 = (f32[100,10,1]{0,1,2:T(8,128)S(1)}, f32[100,10,1]{0,1,2:T(8,128)S(1)}, u32[]{:S(2)}, u32[]{:S(2)}) collective-permute-start(f32[100,10,1]{0,1,2:T(8,128)S(1)} %copy.1032), channel_id=1, source_target_pairs={{1,0},{2,1},{3,2},{4,3},{5,4},{6,5},{7,6},{0,7},{9,8},{10,9},{11,1... | collective-permute-start | bytes 12008 | tf_op jit(solution)/shard_map/ppermute | solution.py:21
  145.7 1.3 copy.1033
  147.0 3.1 %fusion.9 = f32[100,8,128]{2,1,0:T(8,128)} fusion(f32[104,8,128]{2,1,0:T(8,128)} %bitcast.5570, f32[100,8,128]{2,1,0:T(8,128)S(1)} %get-tuple-element.644, f32[100,10,1]{2,1,0:T(8,128)} %copy.1033, f32[100,1,128]{2,1,0:T(1,128)S(1)} %collective-permute-done.4, f32[100,1,128]{2,1,0:T(1,128)S(1)} %collective-permute-done.5, f32[100,10,1]{2,1,0:T(8,128)S(1)} %copy.1031, ...), kind=kLoop, calls=%fused_computation.325 | loop fusion | flops 2764800 | bytes 3387200 | tf_op jit(solution)/shard_map/add | solution.py:155
  150.1 28.8 %reduce-scatter.6.cloned.1.call-done = f32[100,64]{0,1:T(8,128)} async-done(((f32[100,512]{0,1:T(8,128)}), f32[100,64]{0,1:T(8,128)}) %reduce-scatter.6.cloned.1.call-update) | async-done | bytes 25616 | tf_op jit(solution)/shard_map/reduce_scatter | solution.py:140
  178.9 17.7 %all-reduce.6 = (f32[100,64]{0,1:T(8,128)S(1)}, f32[1,64]{1,0:T(1,128)S(1)}, f32[100,64]{0,1:T(8,128)S(1)}) all-reduce(f32[100,64]{0,1:T(8,128)} %reduce-scatter.6.cloned.1.call-done, f32[1,64]{1,0:T(1,128)S(1)} %copy.1039, f32[100,64]{0,1:T(8,128)} %reduce-scatter.8.cloned.1.call-done), channel_id=1, replica_groups=mesh['lat'=4,'lon'=8] {'lat'}, use_global_device_ids=true, to_apply=%region_5.6 | all-reduce | flops 12864 | bytes 102912 | tf_op jit(solution)/shard_map/psum | solution.py:144
  196.6 14.2 %all_gather.9 = f32[100,512]{0,1:T(8,128)S(1)} all-gather(f32[100,64]{0,1:T(8,128)S(1)} %get-tuple-element.27), channel_id=1, replica_groups=mesh['lat'=4,'lon'=8] {'lon'}, dimensions={1}, use_global_device_ids=true | all-gather | bytes 230400 | tf_op jit(solution)/shard_map/all_gather | solution.py:146
  211.7 14.2 %all_gather.11 = f32[100,512]{0,1:T(8,128)S(1)} all-gather(f32[100,64]{0,1:T(8,128)S(1)} %get-tuple-element.29), channel_id=1, replica_groups=mesh['lat'=4,'lon'=8] {'lon'}, dimensions={1}, use_global_device_ids=true | all-gather | bytes 230400 | tf_op jit(solution)/shard_map/all_gather | solution.py:147
  226.8 13.9 %all-reduce.4 = f32[512]{0:T(512)S(1)} all-reduce(f32[512]{0:T(512)S(1)} %bitcast_dynamic-update-slice_fusion), channel_id=1, replica_groups=mesh['lat'=4,'lon'=8] {'lon'}, use_global_device_ids=true, to_apply=%add.4 | all-reduce | flops 512 | bytes 4096
  (307 shorter events, 25.9 us)
Async XLA Ops:
  7.2 61.9 %copy-start = (bf16[100,512]{1,0:T(8,128)(2,1)S(1)}, bf16[100,512]{1,0:T(8,128)(2,1)}, u32[]{:S(2)}) copy-start(bf16[100,512]{1,0:T(8,128)(2,1)} %param.14) | copy-start | bytes 307204
  7.2 137.2 %reduce-scatter.10.cloned.1.call-start = ((), (), s32[]{:S(2)}) async-start(), calls=%async_computation.5 | async-start | bytes 294912
  9.1 6.0 %collective-permute-start = (f32[101,1,128]{2,1,0:T(1,128)S(1)}, f32[101,1,128]{2,1,0:T(1,128)S(1)}, u32[]{:S(2)}, u32[]{:S(2)}) collective-permute-start(f32[101,1,128]{2,1,0:T(1,128)S(1)} %get-tuple-element.639), channel_id=1, source_target_pairs={{0,8},{8,16},{16,24},{24,0},{1,9},{9,17},{17,25},{25,1},{2,10},{10... | collective-permute-start | bytes 155144 | tf_op jit(solution)/shard_map/ppermute | solution.py:18
  12.1 4.1 %collective-permute-start.1 = (f32[101,1,128]{2,1,0:T(1,128)S(1)}, f32[101,1,128]{2,1,0:T(1,128)S(1)}, u32[]{:S(2)}, u32[]{:S(2)}) collective-permute-start(f32[101,1,128]{2,1,0:T(1,128)S(1)} %get-tuple-element.640), channel_id=1, source_target_pairs={{8,0},{16,8},{24,16},{0,24},{9,1},{17,9},{25,17},{1,25},{10,2},{18... | collective-permute-start | bytes 155144 | tf_op jit(solution)/shard_map/ppermute | solution.py:21
  17.4 4.7 %copy-start.15 = (u32[32]{0:T(128)S(1)}, u32[32]{0:T(128)}, u32[]{:S(2)}) copy-start(u32[32]{0:T(128)} %constant.46) | copy-start | bytes 388
  17.7 7.5 %copy-start.1 = (f32[100,8,128]{2,1,0:T(8,128)S(1)}, f32[100,8,128]{2,1,0:T(8,128)}, u32[]{:S(2)}) copy-start(f32[100,8,128]{2,1,0:T(8,128)} %param.9) | copy-start | bytes 1228804
  18.1 5.3 %collective-permute-start.2 = (f32[101,10,1]{0,1,2:T(8,128)S(1)}, f32[101,10,1]{0,1,2:T(8,128)S(1)}, u32[]{:S(2)}, u32[]{:S(2)}) collective-permute-start(f32[101,10,1]{0,1,2:T(8,128)S(1)} %copy.1026), channel_id=1, source_target_pairs={{0,1},{1,2},{2,3},{3,4},{4,5},{5,6},{6,7},{7,0},{8,9},{9,10},{10,1... | collective-permute-start | bytes 12128 | tf_op jit(solution)/shard_map/ppermute | solution.py:18
  18.5 5.3 %collective-permute-start.3 = (f32[101,10,1]{0,1,2:T(8,128)S(1)}, f32[101,10,1]{0,1,2:T(8,128)S(1)}, u32[]{:S(2)}, u32[]{:S(2)}) collective-permute-start(f32[101,10,1]{0,1,2:T(8,128)S(1)} %copy.1027), channel_id=1, source_target_pairs={{1,0},{2,1},{3,2},{4,3},{5,4},{6,5},{7,6},{0,7},{9,8},{10,9},{11,1... | collective-permute-start | bytes 12128 | tf_op jit(solution)/shard_map/ppermute | solution.py:21
  25.3 1.2 copy-start.11
  26.5 42.6 %copy-start.13 = (f32[512]{0:T(512)S(1)}, f32[512]{0:T(512)}, u32[]{:S(2)}) copy-start(f32[512]{0:T(512)} %param.15) | copy-start | bytes 6148
  69.1 2.0 copy-start.12
  69.1 2.0 copy-start.14
  71.0 1.3 copy-start.9
  71.0 1.3 copy-start.8
  71.0 1.5 copy-start.5
  76.7 2.4 copy-start.7
  83.3 5.6 %copy-start.6 = (f32[13,8,8,128]{3,1,2,0:T(8,128)S(1)}, f32[13,8,8,128]{3,1,2,0:T(8,128)}, u32[]{:S(2)}) copy-start(f32[13,8,8,128]{3,1,2,0:T(8,128)} %copy.1040) | copy-start | bytes 1277956
  86.3 63.9 %reduce-scatter.8.cloned.1.call-start = ((), (), s32[]{:S(2)}) async-start(), calls=%async_computation.4 | async-start | bytes 294912 | tf_op jit(solution)/shard_map/reduce_scatter | solution.py:141
  86.3 4.4 %copy-start.10 = (bf16[512,1024]{0,1:T(8,128)(2,1)S(1)}, bf16[512,1024]{0,1:T(8,128)(2,1)}, u32[]{:S(2)}) copy-start(bf16[512,1024]{0,1:T(8,128)(2,1)} %copy-done.9) | copy-start | bytes 3145732
  86.3 49.9 %collective-permute-start.4 = (f32[100,1,128]{2,1,0:T(1,128)}, f32[100,1,128]{2,1,0:T(1,128)S(1)}, u32[]{:S(2)}, u32[]{:S(2)}) collective-permute-start(f32[100,1,128]{2,1,0:T(1,128)} %get-tuple-element.642), channel_id=1, source_target_pairs={{8,0},{16,8},{24,16},{0,24},{9,1},{17,9},{25,17},{1,25},{10,2},{18... | collective-permute-start | bytes 153608 | tf_op jit(solution)/shard_map/ppermute | solution.py:21
  89.0 47.3 %collective-permute-start.5 = (f32[100,1,128]{2,1,0:T(1,128)}, f32[100,1,128]{2,1,0:T(1,128)S(1)}, u32[]{:S(2)}, u32[]{:S(2)}) collective-permute-start(f32[100,1,128]{2,1,0:T(1,128)} %get-tuple-element.641), channel_id=1, source_target_pairs={{0,8},{8,16},{16,24},{24,0},{1,9},{9,17},{17,25},{25,1},{2,10},{10... | collective-permute-start | bytes 153608 | tf_op jit(solution)/shard_map/ppermute | solution.py:18
  92.1 86.9 %reduce-scatter.6.cloned.1.call-start = ((), (), s32[]{:S(2)}) async-start(), calls=%async_computation.3 | async-start | bytes 294912 | tf_op jit(solution)/shard_map/reduce_scatter | solution.py:140
  139.1 6.1 %collective-permute-start.6 = (f32[100,10,1]{0,1,2:T(8,128)S(1)}, f32[100,10,1]{0,1,2:T(8,128)S(1)}, u32[]{:S(2)}, u32[]{:S(2)}) collective-permute-start(f32[100,10,1]{0,1,2:T(8,128)S(1)} %copy.1030), channel_id=1, source_target_pairs={{0,1},{1,2},{2,3},{3,4},{4,5},{5,6},{6,7},{7,0},{8,9},{9,10},{10,1... | collective-permute-start | bytes 12008 | tf_op jit(solution)/shard_map/ppermute | solution.py:18
  139.5 6.2 %collective-permute-start.7 = (f32[100,10,1]{0,1,2:T(8,128)S(1)}, f32[100,10,1]{0,1,2:T(8,128)S(1)}, u32[]{:S(2)}, u32[]{:S(2)}) collective-permute-start(f32[100,10,1]{0,1,2:T(8,128)S(1)} %copy.1032), channel_id=1, source_target_pairs={{1,0},{2,1},{3,2},{4,3},{5,4},{6,5},{7,6},{0,7},{9,8},{10,9},{11,1... | collective-permute-start | bytes 12008 | tf_op jit(solution)/shard_map/ppermute | solution.py:21
  (3 other events, 2.8 us)
Sparse Core Ops, SparseCore 0:
  86.4 30.6 reduce-scatter.9
  119.4 28.6 reduce-scatter.7
  150.4 28.5 reduce-scatter.5
where the time goes:
time: 249 us; the launch traced here: 248 us
  blocking collectives  141 us (57%)
  waiting for transfers between devices  32 us (13%)
  other arithmetic  18 us (7%)
  local copies, waits for them, and re-layouts  16.8 us (7%)
  between operations  16.3 us (7%)
  starting transfers between devices  13.9 us (6%)
  matrix products  10.1 us (4%)
    psum x1, blocking collectives, shards(): sum_bout, level_sum = lax.psum((grad_bout, level_part), ('lat', 'lon'))  41.4 us
    psum x1, blocking collectives, shards(): energy = lax.psum(jnp.sum(wet_tracer * wet_tracer, axis=1), ('lat', 'lon'))  39.4 us
    reduce_scatter x1, waiting for transfers between devices, shards(): lax.psum_scatter(grad_in, 'lon', scatter_dimension=1, tiled=True)  28.8 us
    psum x1, blocking collectives, shards(): share_sums = lax.psum((shares[0], shares[1], shares[2]), 'lat')  17.7 us
    all_gather x1, blocking collectives, shards(): lax.all_gather(share_sums[1], 'lon', axis=1, tiled=True)  14.2 us
    all_gather x1, blocking collectives, shards(): lax.all_gather(share_sums[0], 'lon', axis=1, tiled=True)  14.2 us
    unnamed x1, blocking collectives  13.9 us
    ppermute x4, starting transfers between devices, with_halo(): lax.ppermute(lax.slice_in_dim(block, 0, width, axis=dim), axis, backward)  10.7 us
  transfers between devices with their start and end apart: 11, of which 3 were waited for; matrix products, arithmetic and copies ran while one was open for 7% of the time, Pallas kernels for 0%

commit v1 on v0

v1 whole, which is shorter than its diff:
```python
import math

import jax
import jax.numpy as jnp
from jax import lax
from jax.experimental import pallas as pl
from jax.experimental.pallas import tpu as pltpu
from jax.sharding import Mesh
from jax.sharding import PartitionSpec as P

spread_coef = 0.15
level_eps = 1e-05
f32 = jnp.float32
bf16 = jnp.bfloat16
vmem = pl.BlockSpec(memory_space=pltpu.VMEM)
smem = pl.BlockSpec(memory_space=pltpu.SMEM)
params = pltpu.CompilerParams(vmem_limit_bytes=48 * 1024 * 1024)


def round_up(value, step):
    return -(-value // step) * step


def lane_ids(shape):
    return lax.broadcasted_iota(jnp.int32, shape, 1)


def level_ids(shape):
    return lax.broadcasted_iota(jnp.int32, shape, 0).astype(f32)


def row_of(ref, row, levels, rows):
    return ref[pl.ds(row, levels, stride=rows), :]


def depth_of(mask_ref, bottom_ref):
    return (mask_ref[...] * bottom_ref[...]).astype(f32)


def lane_sums(pad_ref, block):
    pad_ref[...] = jnp.zeros(pad_ref.shape, f32)
    pad_ref[0 : block.shape[0], :] = block
    return jnp.sum(pad_ref[...].T, axis=0, keepdims=True)


def write_edges(field_ref, levels, rows, pad_ref, north, south, west, east, depth=None):
    cols = field_ref.shape[1]
    lanes = lane_ids((levels, cols))
    first = row_of(field_ref, 0, levels, rows)
    last = row_of(field_ref, rows - 1, levels, rows)
    north[0:levels, :] = first
    south[0:levels, :] = last
    tail = north.shape[0] - levels
    if depth is None:
        north[levels:, :] = jnp.zeros((tail, cols), f32)
        south[levels:, :] = jnp.zeros((tail, cols), f32)
    else:
        north[levels:, :] = jnp.broadcast_to(depth[0:1, :], (tail, cols))
        south[levels:, :] = jnp.broadcast_to(depth[rows - 1 : rows, :], (tail, cols))
    low = jnp.zeros((levels, cols), f32)
    high = jnp.zeros((levels, cols), f32)
    for row in range(rows):
        chunk = row_of(field_ref, row, levels, rows)
        low = jnp.where(lanes == row, pltpu.roll(chunk, row, 1) if row else chunk, low)
        high = jnp.where(lanes == row, pltpu.roll(chunk, (row + 1) % cols, 1), high)
    for out, packed, edge in ((west, low, 0), (east, high, cols - 1)):
        pad_ref[...] = jnp.zeros(pad_ref.shape, f32)
        pad_ref[0:levels, :] = packed
        turned = pad_ref[...].T[0:rows, :]
        if depth is not None:
            at = lane_ids(turned.shape) == levels
            turned = jnp.where(at, jnp.broadcast_to(depth[:, edge : edge + 1], turned.shape), turned)
        out[...] = turned


def spread_rows(field_ref, depth, levels, rows, halos, depth_halos):
    north, south, west, east = halos
    cols = depth.shape[1]
    lanes = lane_ids((levels, cols))
    lev = level_ids((levels, cols))
    depth_lanes = lane_ids(depth.shape)
    depth_north, depth_south, depth_west, depth_east = depth_halos
    west_depth = jnp.where(depth_lanes == 0, depth_west, pltpu.roll(depth, 1, 1))
    east_depth = jnp.where(depth_lanes == cols - 1, depth_east, pltpu.roll(depth, cols - 1, 1))
    chunks = [row_of(field_ref, row, levels, rows) for row in range(rows)]
    wets = [(lev < depth[row : row + 1, :]).astype(f32) for row in range(rows)]
    north_wet = (lev < depth_north).astype(f32)
    south_wet = (lev < depth_south).astype(f32)
    for row in range(rows):
        center = chunks[row]
        wet = wets[row]
        below, below_wet = (chunks[row + 1], wets[row + 1]) if row + 1 < rows else (south, south_wet)
        above, above_wet = (chunks[row - 1], wets[row - 1]) if row else (north, north_wet)
        left = jnp.where(
            lanes == 0, pltpu.roll(west, (cols - row) % cols, 1) if row else west, pltpu.roll(center, 1, 1)
        )
        right = jnp.where(
            lanes == cols - 1, pltpu.roll(east, cols - 1 - row, 1), pltpu.roll(center, cols - 1, 1)
        )
        left_wet = (lev < west_depth[row : row + 1, :]).astype(f32)
        right_wet = (lev < east_depth[row : row + 1, :]).astype(f32)
        flux = below_wet * (below - center) + above_wet * (above - center)
        flux = flux + left_wet * (left - center) + right_wet * (right - center)
        yield row, center, wet, center + spread_coef * (wet * flux)


def halo_values(levels, north, south, west, east):
    return (
        north[0:levels, :],
        south[0:levels, :],
        pl_turn(west[...], levels),
        pl_turn(east[...], levels),
    )


def pl_turn(packed, levels):
    rows, lanes = packed.shape
    square = jnp.concatenate([packed] + [jnp.zeros((rows, lanes), f32)] * (lanes // rows - 1), 0)
    return square.T[0:levels, :]


def halo_depths(levels, north, south, west, east, shape):
    return (
        north[levels : levels + 1, :],
        south[levels : levels + 1, :],
        jnp.broadcast_to(west[...][:, levels : levels + 1], shape),
        jnp.broadcast_to(east[...][:, levels : levels + 1], shape),
    )


def energy_kernel(levels, tracer, mask, bottom, energy, north, south, west, east, pad):
    rows, cols = mask.shape
    depth = depth_of(mask, bottom)
    lev = level_ids((levels, cols))
    total = jnp.zeros((levels, cols), f32)
    for row in range(rows):
        wet_tracer = jnp.where(lev < depth[row : row + 1, :], row_of(tracer, row, levels, rows), 0.0)
        total = total + wet_tracer * wet_tracer
    sums = lane_sums(pad, total)
    energy[...] = jnp.broadcast_to(sums[None], energy.shape)
    write_edges(tracer, levels, rows, pad, north, south, west, east, depth)


def mix_kernel(levels, tracer, mask, bottom, north, south, west, east, mixed):
    rows, cols = mask.shape
    depth = depth_of(mask, bottom)
    halos = halo_values(levels, north, south, west, east)
    depth_halos = halo_depths(levels, north, south, west, east, depth.shape)
    for row, _, _, value in spread_rows(tracer, depth, levels, rows, halos, depth_halos):
        mixed[pl.ds(row, levels, stride=rows), :] = value


def radius_columns(energy, column_count, lanes):
    total = jnp.sum(energy[...], axis=0)
    radius = jnp.sqrt(total / column_count + level_eps)
    return jnp.broadcast_to(radius, (lanes, radius.shape[1])).T


def main_kernel(
    levels,
    column_count,
    scale,
    place,
    kappa,
    energy,
    tracer,
    cotangent,
    mixed,
    mask,
    bottom,
    w_in,
    b_in,
    w_out,
    b_out,
    keep,
    send,
    adjoint,
    north,
    south,
    west,
    east,
    d_inputs,
    pad,
    x_f,
    x_b,
    wi_f,
    wo_f,
    wi_b,
    wo_b,
    hidden,
    slope,
    gate,
    dl_f,
    dl_b,
    dp_b,
    sink,
    rate_a,
    rate_b,
    inv_p,
    fwd_z,
    fwd_u,
    flow,
):
    rows, cols = mask.shape
    hid = w_in.shape[1]
    span = rows * cols
    pad_levels = x_f.shape[0]
    depth = depth_of(mask, bottom)
    lev = level_ids((levels, cols))
    radius = radius_columns(energy, column_count, cols)[0:levels, :]

    x_f[levels:, :] = jnp.where(
        lax.broadcasted_iota(jnp.int32, (pad_levels - levels, span), 0) < 3, 1.0, 0.0
    )
    for row in range(rows):
        wet_tracer = jnp.where(lev < depth[row : row + 1, :], row_of(tracer, row, levels, rows), 0.0)
        x_f[0:levels, row * cols : (row + 1) * cols] = wet_tracer / radius
    x_b[...] = x_f[...].astype(bf16)

    wi_f[...] = jnp.zeros(wi_f.shape, f32)
    wi_f[0:levels, :] = w_in[...].astype(f32)
    bias = b_in[...]
    for part in range(3):
        piece = bias.astype(bf16).astype(f32)
        wi_f[levels + part : levels + part + 1, :] = piece
        bias = bias - piece
    wi_b[...] = wi_f[...].astype(bf16)
    wi_t = wi_f[...].T.astype(bf16)
    wo_f[...] = jnp.zeros(wo_f.shape, f32)
    wo_f[:, 0:levels] = w_out[...].astype(f32)
    wo_b[...] = wo_f[...].astype(bf16)
    wo_t = wo_f[...].T.astype(bf16)

    block = hid // 4
    for part in range(4):
        at = slice(part * block, (part + 1) * block)
        pre = jnp.dot(wi_t[at, :], x_b[...], preferred_element_type=f32)
        sig = 1.0 / (1.0 + jnp.exp(-pre))
        hidden[at, :] = (pre * sig).astype(bf16)
        slope[at, :] = sig * (1.0 + pre * (1.0 - sig))

    pad[...] = jnp.zeros(pad.shape, f32)
    pad[0:1, 0:levels] = b_out[...]
    out_bias = jnp.broadcast_to(pad[0:1, :], pad.shape).T[:, 0:1]
    logits = jnp.dot(wo_t, hidden[...], preferred_element_type=f32)
    logits = logits + out_bias
    tiny = jnp.exp(-jnp.abs(logits))
    share = 1.0 / (1.0 + tiny)
    gate[...] = jnp.where(logits >= 0.0, share, tiny * share)
    soft = jnp.maximum(logits, 0.0) + jnp.log1p(tiny)
    for row in range(rows):
        sink[pl.ds(row, levels, stride=rows), :] = soft[0:levels, row * cols : (row + 1) * cols]

    def at_level(k):
        return slice(k * rows, (k + 1) * rows)

    ones = jnp.ones((rows, cols), f32)
    rest = ones
    z = mixed[at_level(0), :]
    u = cotangent[at_level(0), :]
    for k in range(levels):
        if k + 1 < levels:
            face = (depth > float(k + 1)).astype(f32)
            up = face * kappa[k]
            down = up + face * sink[at_level(k), :]
            inv = 1.0 / (rest + down)
            a = down * inv
            b = up * inv
            inv_p[at_level(k), :] = inv
            rate_a[at_level(k), :] = a
            rate_b[at_level(k), :] = b
            fwd_z[at_level(k), :] = z
            fwd_u[at_level(k), :] = u
            rest = 1.0 + b * rest
            z = mixed[at_level(k + 1), :] + a * z
            u = cotangent[at_level(k + 1), :] + b * u
    inv = 1.0 / rest
    x = z * inv
    y = u * inv
    adjoint[at_level(levels - 1), :] = y
    flow[at_level(levels - 1), :] = jnp.zeros((rows, cols), f32)
    for k in range(levels - 2, -1, -1):
        inv = inv_p[at_level(k), :]
        x = fwd_z[at_level(k), :] * inv + rate_b[at_level(k), :] * x
        y_new = fwd_u[at_level(k), :] * inv + rate_a[at_level(k), :] * y
        adjoint[at_level(k), :] = y_new
        flow[at_level(k), :] = jnp.where(depth > float(k + 1), x * (y - y_new), 0.0)
        y = y_new

    dl_f[levels:, :] = jnp.zeros((pad_levels - levels, span), f32)
    for row in range(rows):
        part = slice(row * cols, (row + 1) * cols)
        dl_f[0:levels, part] = row_of(flow, row, levels, rows) * gate[0:levels, part]
    dl_b[...] = dl_f[...].astype(bf16)
    bout = jnp.zeros((pad_levels, cols), f32)
    for row in range(rows):
        bout = bout + dl_b[:, row * cols : (row + 1) * cols].astype(f32)
    bout_row = lane_sums(pad, bout)

    for part in range(4):
        at = slice(part * block, (part + 1) * block)
        d_hidden = jnp.dot(wo_b[at, :], dl_b[...], preferred_element_type=f32)
        dp_b[at, :] = (d_hidden * slope[at, :]).astype(bf16)
    d_in = jnp.dot(wi_b[...], dp_b[...], preferred_element_type=f32)
    level = jnp.zeros((levels, cols), f32)
    for row in range(rows):
        part = d_in[0:levels, row * cols : (row + 1) * cols]
        d_inputs[row, 0:levels, :] = part
        wet_tracer = jnp.where(lev < depth[row : row + 1, :], row_of(tracer, row, levels, rows), 0.0)
        level = level + part * wet_tracer
    level_row = lane_sums(pad, level)

    contract = (((1,), (1,)), ((), ()))
    core = place[0]
    quarter = place[1]
    height = keep.shape[1]
    for part in range(4):
        at = slice(part * block, (part + 1) * block)
        slot = part ^ quarter
        g_in = lax.dot_general(x_b[...], dp_b[at, :], contract, preferred_element_type=f32)
        g_out = lax.dot_general(dl_b[...], hidden[at, :], contract, preferred_element_type=f32)
        for which, grad in ((0, g_in), (1, g_out)):

            def put(target, grad=grad, slot=slot):
                target[slot, :, :] = grad[0:height, :] * scale
                target[slot, levels + 1 : levels + 2, :] = level_row
                target[slot, levels + 2 : levels + 3, :] = bout_row * scale

            pl.when(core == which)(lambda put=put: put(keep))
            pl.when(core != which)(lambda put=put: put(send))
    write_edges(adjoint, levels, rows, pad, north, south, west, east)


def final_kernel(
    levels,
    column_count,
    energy,
    level_total,
    adjoint,
    tracer,
    d_inputs,
    mask,
    bottom,
    north,
    south,
    west,
    east,
    t_north,
    t_south,
    t_west,
    t_east,
    out,
):
    rows, cols = mask.shape
    depth = depth_of(mask, bottom)
    total = jnp.sum(energy[...], axis=0)
    radius = jnp.sqrt(total / column_count + level_eps)
    level_sum = level_total[levels + 1 : levels + 2, :]
    pull = level_sum / (column_count * (radius * radius * radius))
    shape = (cols, radius.shape[1])
    radius = jnp.broadcast_to(radius, shape).T[0:levels, :]
    pull = jnp.broadcast_to(pull, shape).T[0:levels, :]
    halos = halo_values(levels, north, south, west, east)
    depth_halos = halo_depths(levels, t_north, t_south, t_west, t_east, depth.shape)
    for row, _, wet, value in spread_rows(adjoint, depth, levels, rows, halos, depth_halos):
        wet_tracer = jnp.where(wet > 0.0, row_of(tracer, row, levels, rows), 0.0)
        d_wet = d_inputs[row, 0:levels, :] / radius - wet_tracer * pull
        out[pl.ds(row, levels, stride=rows), :] = value + wet * d_wet


def gather_kernel(levels, place, *refs):
    own, grad_in, grad_bin, grad_out, grad_bout = refs[:8], *refs[8:]
    core = place[0]
    quarter = place[1]
    block = own[0].shape[1]
    for half in range(2):
        for step in range(4):
            ref = own[half * 4 + step]
            at = pl.multiple_of((step ^ quarter) * block, block)

            def put_in(ref=ref, at=at):
                grad_in[:, pl.ds(at, block)] = ref[0:levels, :]
                grad_bin[:, pl.ds(at, block)] = ref[levels : levels + 1, :]

            def put_out(ref=ref, at=at):
                tall = jnp.concatenate([ref[...], jnp.zeros((block - ref.shape[0], block), f32)], 0)
                grad_out[pl.ds(at, block), :] = tall.T[:, 0:levels]

            which = core if half == 0 else 1 - core
            pl.when(which == 0)(put_in)
            pl.when(which == 1)(put_out)
    grad_bout[...] = own[0][levels + 2 : levels + 3, 0:levels]


def shift(axis, count, by, wrap):
    return [
        (i, (i + by) % count) for i in range(count) if wrap or 0 <= i + by < count
    ]


def flip(count, by):
    return [(i, i ^ by) for i in range(count)]


def swap_halos(north, south, west, east):
    lats = lax.axis_size("lat")
    lons = lax.axis_size("z") * lax.axis_size("core")
    from_north = lax.ppermute(south, "lat", shift("lat", lats, 1, False))
    from_south = lax.ppermute(north, "lat", shift("lat", lats, -1, False))
    from_west = lax.ppermute(east, ("z", "core"), shift("lon", lons, 1, True))
    from_east = lax.ppermute(west, ("z", "core"), shift("lon", lons, -1, True))
    return (from_north, from_south, from_west, from_east)


def shards(tracer, cotangent, land_mask, bottom, kappa, w_in, b_in, w_out, b_out):
    levels, rows, cols = tracer.shape
    hid = w_in.shape[1]
    lats, chips = lax.axis_size("lat"), lax.axis_size("z")
    devices = lats * chips * lax.axis_size("core")
    column_count = rows * cols * devices
    pad_levels = round_up(levels + 3, 128)
    height = round_up(levels + 3, 8)
    flat = (levels * rows, cols)
    span = rows * cols
    tracer = tracer.reshape(flat)
    cotangent = cotangent.reshape(flat)
    sds = jax.ShapeDtypeStruct
    edge_shapes = [sds((height, cols), f32)] * 2 + [sds((rows, pad_levels), f32)] * 2
    pad = pltpu.VMEM((pad_levels, cols), f32)

    energy, *edges = pl.pallas_call(
        lambda *refs: energy_kernel(levels, *refs),
        out_shape=[sds((devices, 1, pad_levels), f32), *edge_shapes],
        in_specs=[vmem] * 3,
        out_specs=[vmem] * 5,
        scratch_shapes=[pad],
        compiler_params=params,
    )(tracer, land_mask, bottom)
    energy = lax.all_to_all(energy, ("lat", "z", "core"), 0, 0, tiled=True)
    halos = swap_halos(*edges)
    mixed = pl.pallas_call(
        lambda *refs: mix_kernel(levels, *refs),
        out_shape=sds(flat, f32),
        in_specs=[vmem] * 7,
        out_specs=vmem,
        compiler_params=params,
    )(tracer, land_mask, bottom, *halos)

    core = lax.axis_index("core")
    quarter = lax.axis_index("lat") % 4
    place = jnp.stack([core, quarter]).astype(jnp.int32)
    flat_scratch = pltpu.VMEM(flat, f32)
    keep, send, adjoint, *rest = pl.pallas_call(
        lambda *refs: main_kernel(levels, column_count, 1.0 / math.sqrt(column_count), *refs),
        out_shape=[
            sds((4, height, hid // 4), f32),
            sds((4, height, hid // 4), f32),
            sds(flat, f32),
            *edge_shapes,
            sds((rows, height, cols), f32),
        ],
        in_specs=[smem] * 2 + [vmem] * 10,
        out_specs=[vmem] * 8,
        scratch_shapes=[
            pad,
            pltpu.VMEM((pad_levels, span), f32),
            pltpu.VMEM((pad_levels, span), bf16),
            pltpu.VMEM((pad_levels, hid), f32),
            pltpu.VMEM((hid, pad_levels), f32),
            pltpu.VMEM((pad_levels, hid), bf16),
            pltpu.VMEM((hid, pad_levels), bf16),
            pltpu.VMEM((hid, span), bf16),
            pltpu.VMEM((hid, span), f32),
            pltpu.VMEM((pad_levels, span), f32),
            pltpu.VMEM((pad_levels, span), f32),
            pltpu.VMEM((pad_levels, span), bf16),
            pltpu.VMEM((hid, span), bf16),
            *[flat_scratch] * 7,
        ],
        compiler_params=params,
    )(
        place, kappa, energy, tracer, cotangent, mixed, land_mask, bottom,
        w_in, b_in.reshape(1, hid), w_out, b_out.reshape(1, levels),
    )
    adjoint_edges, d_inputs = rest[:4], rest[4]

    chip = keep + lax.ppermute(send, "core", flip(2, 1))
    adjoint_halos = swap_halos(*adjoint_edges)
    part = chip[0]
    for step in range(1, 4):
        part = part + lax.ppermute(chip[step], "lat", flip(lats, step))
    step = 4
    while step < lats:
        part = part + lax.ppermute(part, "lat", flip(lats, step))
        step *= 2
    if chips == 4:
        part = part + sum(lax.ppermute(part, "z", flip(chips, step)) for step in range(1, 4))
    else:
        step = 1
        while step < chips:
            part = part + lax.ppermute(part, "z", flip(chips, step))
            step *= 2

    tracer_adjoint = pl.pallas_call(
        lambda *refs: final_kernel(levels, column_count, *refs),
        out_shape=sds(flat, f32),
        in_specs=[vmem] * 15,
        out_specs=vmem,
        compiler_params=params,
    )(energy, part, adjoint, tracer, d_inputs, land_mask, bottom, *adjoint_halos, *halos)

    mine = [part] + [lax.ppermute(part, "lat", flip(lats, step)) for step in range(1, 4)]
    other = [lax.ppermute(piece, "core", flip(2, 1)) for piece in mine]
    grad_w_in, grad_b_in, grad_w_out, grad_b_out = pl.pallas_call(
        lambda *refs: gather_kernel(levels, *refs),
        out_shape=[
            sds((levels, hid), f32),
            sds((1, hid), f32),
            sds((hid, levels), f32),
            sds((1, levels), f32),
        ],
        in_specs=[smem] + [vmem] * 8,
        out_specs=[vmem] * 4,
        compiler_params=params,
    )(place, *mine, *other)
    return (
        tracer_adjoint.reshape(levels, rows, cols),
        grad_w_in,
        grad_b_in.reshape(hid),
        grad_w_out,
        grad_b_out.reshape(levels),
    )


def solution(mesh):
    lats, lons = mesh.shape["lat"], mesh.shape["lon"]
    split = Mesh(mesh.devices.reshape(lats, lons // 2, 2), ("lat", "z", "core"))
    field = P(None, "lat", ("z", "core"))
    plane = P("lat", ("z", "core"))
    return jax.shard_map(
        shards,
        mesh=split,
        in_specs=(field, field, plane, plane, P(), P(), P(), P(), P()),
        out_specs=(field, P(), P(), P(), P()),
        check_vma=False,
    )
```

time: 249 us -> 67.6 us (0.27)
  blocking collectives: 141 us -> 0 us
  starting transfers between devices: 13.9 us -> 32.8 us
  other arithmetic: 18 us -> 0.14 us
  between operations: 16.3 us -> 0.87 us
  waiting for transfers between devices: 32 us -> 18.6 us
  local copies, waits for them, and re-layouts: 16.8 us -> 4.93 us
  matrix products: 10.1 us -> 0 us
  Pallas kernels: 0 us -> 9.93 us
    psum x3 -> x0, blocking collectives: 98.5 us -> none  [the longest x1 41.4 us: shards(): sum_bout, level_sum = lax.psum((grad_bout, level_part), ('lat', 'lon'))]
    reduce_scatter x2 -> x0, waiting for transfers between devices: 28.8 us -> none  [the longest x1 28.8 us: shards(): lax.psum_scatter(grad_in, 'lon', scatter_dimension=1, tiled=True)]
    all_gather x2 -> x0, blocking collectives: 28.4 us -> none  [the longest x1 14.2 us: shards(): lax.all_gather(share_sums[1], 'lon', axis=1, tiled=True)]
    ppermute x8 -> x22, waiting for transfers between devices: 3.13 us -> 18.6 us  [the longest x2 7.15 us: swap_halos(): from_south = lax.ppermute(north, 'lat', shift('lat', lats, -1, False))]
    unnamed x1 -> x0, blocking collectives: 13.9 us -> none
    ppermute x8 -> x22, starting transfers between devices: 13.8 us -> 25.5 us  [the longest x2 6.28 us: swap_halos(): from_north = lax.ppermute(south, 'lat', shift('lat', lats, 1, False))]
    dot_general x6 -> x0, matrix products: 10.1 us -> none  [the longest x1 2.51 us: shards(): lax.dot_general(inputs, d_pre, (((1,), (1,)), ((), ())), preferred_elemen...]
    pallas_call x0 -> x5, Pallas kernels: none -> 9.93 us  [the longest x1 5.17 us: shards(): pl.pallas_call(lambda *refs: main_kernel(levels, column_count, 1.0 / math...]
  transfers between devices with their start and end apart: 11 -> 23, of which waited for: 3 -> 9; matrix products, arithmetic and copies ran while one was open for 7% -> 2% of each run, Pallas kernels for 0% -> 3%
where the time goes in v1:
time: 67.6 us; the launch traced here: 67.3 us
  starting transfers between devices  32.8 us (49%)
  waiting for transfers between devices  18.6 us (28%)
  Pallas kernels  9.93 us (15%)
  local copies, waits for them, and re-layouts  4.93 us (7%)
  between operations  0.87 us (1%)
    all_to_all x1, starting transfers between devices, shards(): energy = lax.all_to_all(energy, ('lat', 'z', 'core'), 0, 0, tiled=True)  7.3 us
    ppermute x2, waiting for transfers between devices, swap_halos(): from_south = lax.ppermute(north, 'lat', shift('lat', lats, -1, False))  7.15 us
    ppermute x2, starting transfers between devices, swap_halos(): from_north = lax.ppermute(south, 'lat', shift('lat', lats, 1, False))  6.28 us
    pallas_call x1, Pallas kernels, shards(): pl.pallas_call(lambda *refs: main_kernel(levels, column_count, 1.0 / math...  5.17 us
    unnamed x24, local copies, waits for them, and re-layouts  4.92 us
    ppermute x2, waiting for transfers between devices, swap_halos(): from_west = lax.ppermute(east, ('z', 'core'), shift('lon', lons, 1, True))  4.83 us
    ppermute x3, starting transfers between devices, shards(): lax.ppermute(part, 'z', flip(chips, step))  4.45 us
    ppermute x3, starting transfers between devices, shards(): part = part + lax.ppermute(chip[step], 'lat', flip(lats, step))  3.97 us
  transfers between devices with their start and end apart: 23, of which 9 were waited for; matrix products, arithmetic and copies ran while one was open for 2% of the time, Pallas kernels for 3%

profile of v1, /device:TPU:0, one launch (start us, length us, event | category | flops | bytes accessed | tf_op | source)
XLA Modules:
  0.0 67.3 jit_solution(5478701555975156207)
XLA Ops:
  0.6 1.0 %copy-done = f32[100,8,128]{2,1,0:T(8,128)S(1)} copy-done((f32[100,8,128]{2,1,0:T(8,128)S(1)}, f32[100,8,128]{2,1,0:T(8,128)}, u32[]{:S(2)}) %copy-start) | copy-done | bytes 409624
  3.0 0.9 %shard_map.128 = (f32[32,1,128]{2,1,0:T(1,128)}, f32[104,128]{1,0:T(8,128)S(1)}, f32[104,128]{1,0:T(8,128)S(1)}, f32[8,128]{1,0:T(8,128)S(1)}, f32[8,128]{1,0:T(8,128)S(1)}) custom-call(f32[800,128]{1,0:T(8,128)S(1)} %bitcast.23, s32[8,128]{1,0:T(8,128)S(1)} %copy-done.4, s32[8,128]{1,0:T(8,128)S(1)} %copy-done.6), custom_call_target="tpu_custom_call" | custom-call | tf_op jit(solution)/shard_map/pallas_call | solution.py:431
  4.0 7.3 %all-to-all-start = ((f32[32,1,128]{2,1,0:T(1,128)}), f32[32,1,128]{2,1,0:T(1,128)S(1)}, u32[]{:S(2)}, u32[]{:S(2)}) async-start(f32[32,1,128]{2,1,0:T(1,128)} %get-tuple-element.22), calls=%async_computation | async-start | bytes 32768 | tf_op jit(solution)/shard_map/all_to_all | solution.py:439
  11.6 3.3 %collective-permute-start.3 = (f32[8,128]{1,0:T(8,128)S(1)}, f32[8,128]{1,0:T(8,128)S(1)}, u32[]{:S(2)}, u32[]{:S(2)}) collective-permute-start(f32[8,128]{1,0:T(8,128)S(1)} %get-tuple-element.26), channel_id=1, source_target_pairs={{0,7},{1,0},{2,1},{3,2},{4,3},{5,4},{6,5},{7,6},{8,15},{9,8},{10,9... | collective-permute-start | bytes 12296 | tf_op jit(solution)/shard_map/ppermute | solution.py:411
  14.9 3.7 %collective-permute-start = (f32[104,128]{1,0:T(8,128)S(1)}, f32[104,128]{1,0:T(8,128)S(1)}, u32[]{:S(2)}, u32[]{:S(2)}) collective-permute-start(f32[104,128]{1,0:T(8,128)S(1)} %get-tuple-element.23), channel_id=1, source_target_pairs={{0,8},{8,16},{16,24},{1,9},{9,17},{17,25},{2,10},{10,18},{18,26},{... | collective-permute-start | bytes 159752 | tf_op jit(solution)/shard_map/ppermute | solution.py:408
  18.5 1.3 %collective-permute-start.1 = (f32[104,128]{1,0:T(8,128)S(1)}, f32[104,128]{1,0:T(8,128)S(1)}, u32[]{:S(2)}, u32[]{:S(2)}) collective-permute-start(f32[104,128]{1,0:T(8,128)S(1)} %get-tuple-element.24), channel_id=1, source_target_pairs={{8,0},{16,8},{24,16},{9,1},{17,9},{25,17},{10,2},{18,10},{26,18},{... | collective-permute-start | bytes 159752 | tf_op jit(solution)/shard_map/ppermute | solution.py:409
  19.9 1.1 %copy.14.refs_10_ = bf16[512,100]{1,0:T(8,128)(2,1)S(1)} copy(bf16[512,100]{0,1:T(8,128)(2,1)} %param.16) | data formatting | bytes 204800 | tf_op args[7]
  21.0 3.5 %collective-permute-done.1.refs_4_.refs_12_ = f32[104,128]{1,0:T(8,128)S(1)} collective-permute-done((f32[104,128]{1,0:T(8,128)S(1)}, f32[104,128]{1,0:T(8,128)S(1)}, u32[]{:S(2)}, u32[]{:S(2)}) %collective-permute-start.1) | collective-permute-done | bytes 53280 | tf_op jit(solution)/shard_map/ppermute | solution.py:409
  25.9 5.2 %shard_map.130 = (f32[4,104,128]{2,1,0:T(8,128)S(1)}, f32[4,104,128]{2,1,0:T(8,128)S(1)}, f32[800,128]{1,0:T(8,128)S(1)}, f32[104,128]{1,0:T(8,128)S(1)}, f32[10...) custom-call(s32[2]{0:T(128)S(1)} %pad_add_fusion.refs_0_, ...), custom_call_target="tpu_custom_call" | custom-call | tf_op jit(solution)/shard_map/pallas_call | solution.py:453
  31.1 1.5 %collective-permute-done.4 = f32[4,104,128]{2,1,0:T(8,128)S(1)} collective-permute-done((f32[4,104,128]{2,1,0:T(8,128)S(1)}, f32[4,104,128]{2,1,0:T(8,128)S(1)}, u32[]{:S(2)}, u32[]{:S(2)}) %collective-permute-start.4) | collective-permute-done | bytes 213024 | tf_op jit(solution)/shard_map/ppermute | solution.py:487
  32.6 2.4 %collective-permute-start.5 = (f32[104,128]{1,0:T(8,128)S(1)}, f32[104,128]{1,0:T(8,128)S(1)}, u32[]{:S(2)}, u32[]{:S(2)}) collective-permute-start(f32[104,128]{1,0:T(8,128)S(1)} %get-tuple-element.44), channel_id=1, source_target_pairs={{0,8},{8,0},{16,24},{24,16},{1,9},{9,1},{17,25},{25,17},{2,10},{10... | collective-permute-start | bytes 159752 | tf_op jit(solution)/shard_map/ppermute | solution.py:491
  35.6 1.0 %collective-permute-start.6 = (f32[104,128]{1,0:T(8,128)S(1)}, f32[104,128]{1,0:T(8,128)S(1)}, u32[]{:S(2)}, u32[]{:S(2)}) collective-permute-start(f32[104,128]{1,0:T(8,128)S(1)} %get-tuple-element.46), channel_id=1, source_target_pairs={{0,16},{8,24},{16,0},{24,8},{1,17},{9,25},{17,1},{25,9},{2,18},{10... | collective-permute-start | bytes 159752 | tf_op jit(solution)/shard_map/ppermute | solution.py:491
  36.6 1.1 %collective-permute-done.5 = f32[104,128]{1,0:T(8,128)S(1)} collective-permute-done((f32[104,128]{1,0:T(8,128)S(1)}, f32[104,128]{1,0:T(8,128)S(1)}, u32[]{:S(2)}, u32[]{:S(2)}) %collective-permute-start.5) | collective-permute-done | bytes 53280 | tf_op jit(solution)/shard_map/ppermute | solution.py:491
  37.7 2.5 %collective-permute-done.7 = f32[104,128]{1,0:T(8,128)S(1)} collective-permute-done((f32[104,128]{1,0:T(8,128)S(1)}, f32[104,128]{1,0:T(8,128)S(1)}, u32[]{:S(2)}, u32[]{:S(2)}) %collective-permute-start.7) | collective-permute-done | bytes 53280 | tf_op jit(solution)/shard_map/ppermute | solution.py:491
  40.3 1.6 %collective-permute-start.10 = (f32[104,128]{1,0:T(8,128)S(1)}, f32[104,128]{1,0:T(8,128)S(1)}, u32[]{:S(2)}, u32[]{:S(2)}) collective-permute-start(f32[104,128]{1,0:T(8,128)S(1)} %fusion.2), channel_id=1, source_target_pairs={{0,6},{2,4},{4,2},{6,0},{1,7},{3,5},{5,3},{7,1},{8,14},{10,12},{12... | collective-permute-start | bytes 159752 | tf_op jit(solution)/shard_map/ppermute | solution.py:497
  42.0 2.8 %collective-permute-start.8 = (f32[104,128]{1,0:T(8,128)S(1)}, f32[104,128]{1,0:T(8,128)S(1)}, u32[]{:S(2)}, u32[]{:S(2)}) collective-permute-start(f32[104,128]{1,0:T(8,128)S(1)} %fusion.2), channel_id=1, source_target_pairs={{0,2},{2,0},{4,6},{6,4},{1,3},{3,1},{5,7},{7,5},{8,10},{10,8},{12,... | collective-permute-start | bytes 159752 | tf_op jit(solution)/shard_map/ppermute | solution.py:497
  44.8 2.6 %collective-permute-start.11 = (f32[104,128]{1,0:T(8,128)S(1)}, f32[104,128]{1,0:T(8,128)S(1)}, u32[]{:S(2)}, u32[]{:S(2)}) collective-permute-start(f32[104,128]{1,0:T(8,128)S(1)} %get-tuple-element.31), channel_id=1, source_target_pairs={{0,8},{8,16},{16,24},{1,9},{9,17},{17,25},{2,10},{10,18},{18,26},{... | collective-permute-start | bytes 159752 | tf_op jit(solution)/shard_map/ppermute | solution.py:408
  47.5 2.0 %collective-permute-start.17 = (f32[104,128]{1,0:T(8,128)S(1)}, f32[104,128]{1,0:T(8,128)S(1)}, u32[]{:S(2)}, u32[]{:S(2)}) collective-permute-start(f32[104,128]{1,0:T(8,128)S(1)} %add_add_fusion.refs_1_), channel_id=1, source_target_pairs={{0,24},{8,16},{16,8},{24,0},{1,25},{9,17},{17,9},{25,1},{2,26},{10... | collective-permute-start | bytes 159752 | tf_op jit(solution)/shard_map/ppermute | solution.py:512
  51.1 4.8 %collective-permute-done.13.refs_9_ = f32[8,128]{1,0:T(8,128)S(1)} collective-permute-done((f32[8,128]{1,0:T(8,128)S(1)}, f32[8,128]{1,0:T(8,128)S(1)}, u32[]{:S(2)}, u32[]{:S(2)}) %collective-permute-start.13) | collective-permute-done | bytes 4128 | tf_op jit(solution)/shard_map/ppermute | solution.py:410
  55.9 1.3 %collective-permute-done.14.refs_10_ = f32[8,128]{1,0:T(8,128)S(1)} collective-permute-done((f32[8,128]{1,0:T(8,128)S(1)}, f32[8,128]{1,0:T(8,128)S(1)}, u32[]{:S(2)}, u32[]{:S(2)}) %collective-permute-start.14) | collective-permute-done | bytes 4128 | tf_op jit(solution)/shard_map/ppermute | solution.py:411
  57.2 1.3 %collective-permute-start.12 = (f32[104,128]{1,0:T(8,128)S(1)}, f32[104,128]{1,0:T(8,128)S(1)}, u32[]{:S(2)}, u32[]{:S(2)}) collective-permute-start(f32[104,128]{1,0:T(8,128)S(1)} %get-tuple-element.32), channel_id=1, source_target_pairs={{8,0},{16,8},{24,16},{9,1},{17,9},{25,17},{10,2},{18,10},{26,18},{... | collective-permute-start | bytes 159752 | tf_op jit(solution)/shard_map/ppermute | solution.py:409
  59.6 3.6 %collective-permute-done.12.refs_8_ = f32[104,128]{1,0:T(8,128)S(1)} collective-permute-done((f32[104,128]{1,0:T(8,128)S(1)}, f32[104,128]{1,0:T(8,128)S(1)}, u32[]{:S(2)}, u32[]{:S(2)}) %collective-permute-start.12) | collective-permute-done | bytes 53280 | tf_op jit(solution)/shard_map/ppermute | solution.py:409
  63.2 1.5 %shard_map.131 = f32[800,128]{1,0:T(8,128)} custom-call(f32[32,1,128]{2,1,0:T(1,128)S(1)} %all-to-all-done.refs_2_.refs_0_, f32[104,128]{1,0:T(8,128)S(1)} %add_add_fusion.refs_1_, f32[800,128]{1,0:T(8,128)S(1)} %get-tuple-element.29.refs_2_, f32[800,128]{1,0:T(8,128)S(1)} %bitcast.26, f32[8,104,128]{2,1,0:T(8,128)S(1)} %get-tuple-element.30.refs_4_, ...), custom_call_target="tpu_custom_call" | custom-call | tf_op jit(solution)/shard_map/pallas_call | solution.py:504
  64.8 1.7 %shard_map.132 = (f32[100,512]{1,0:T(8,128)}, f32[1,512]{1,0:T(1,128)}, f32[512,100]{1,0:T(8,128)S(1)}, f32[1,100]{1,0:T(1,128)}) custom-call(s32[2]{0:T(128)S(1)} %pad_add_fusion.refs_0_, f32[104,128]{1,0:T(8,128)S(1)} %add_add_fusion.refs_1_, f32[104,128]{1,0:T(8,128)S(1)} %collective-permute-done.15.refs_2_, ...), custom_call_target="tpu_custom_call" | custom-call | tf_op jit(solution)/shard_map/pallas_call | solution.py:514
  (56 shorter events, 7.4 us)
Async XLA Ops:
  3.0 21.5 %copy-start.1 = (f32[100,8,128]{2,1,0:T(8,128)S(1)}, f32[100,8,128]{2,1,0:T(8,128)}, u32[]{:S(2)}) copy-start(f32[100,8,128]{2,1,0:T(8,128)} %param.9) | copy-start | bytes 1228804
  4.0 21.2 %all-to-all-start = ((f32[32,1,128]{2,1,0:T(1,128)}), f32[32,1,128]{2,1,0:T(1,128)S(1)}, u32[]{:S(2)}, u32[]{:S(2)}) async-start(f32[32,1,128]{2,1,0:T(1,128)} %get-tuple-element.22), calls=%async_computation | async-start | bytes 32768 | tf_op jit(solution)/shard_map/all_to_all | solution.py:439
  11.3 9.7 %collective-permute-start.2 = (f32[8,128]{1,0:T(8,128)S(1)}, f32[8,128]{1,0:T(8,128)S(1)}, u32[]{:S(2)}, u32[]{:S(2)}) collective-permute-start(f32[8,128]{1,0:T(8,128)S(1)} %get-tuple-element.25), channel_id=1, source_target_pairs={{0,1},{1,2},{2,3},{3,4},{4,5},{5,6},{6,7},{7,0},{8,9},{9,10},{10,1... | collective-permute-start | bytes 12296 | tf_op jit(solution)/shard_map/ppermute | solution.py:410
  11.6 9.4 %collective-permute-start.3 = (f32[8,128]{1,0:T(8,128)S(1)}, f32[8,128]{1,0:T(8,128)S(1)}, u32[]{:S(2)}, u32[]{:S(2)}) collective-permute-start(f32[8,128]{1,0:T(8,128)S(1)} %get-tuple-element.26), channel_id=1, source_target_pairs={{0,7},{1,0},{2,1},{3,2},{4,3},{5,4},{6,5},{7,6},{8,15},{9,8},{10,9... | collective-permute-start | bytes 12296 | tf_op jit(solution)/shard_map/ppermute | solution.py:411
  14.9 6.2 %collective-permute-start = (f32[104,128]{1,0:T(8,128)S(1)}, f32[104,128]{1,0:T(8,128)S(1)}, u32[]{:S(2)}, u32[]{:S(2)}) collective-permute-start(f32[104,128]{1,0:T(8,128)S(1)} %get-tuple-element.23), channel_id=1, source_target_pairs={{0,8},{8,16},{16,24},{1,9},{9,17},{17,25},{2,10},{10,18},{18,26},{... | collective-permute-start | bytes 159752 | tf_op jit(solution)/shard_map/ppermute | solution.py:408
  18.5 6.0 %collective-permute-start.1 = (f32[104,128]{1,0:T(8,128)S(1)}, f32[104,128]{1,0:T(8,128)S(1)}, u32[]{:S(2)}, u32[]{:S(2)}) collective-permute-start(f32[104,128]{1,0:T(8,128)S(1)} %get-tuple-element.24), channel_id=1, source_target_pairs={{8,0},{16,8},{24,16},{9,1},{17,9},{25,17},{10,2},{18,10},{26,18},{... | collective-permute-start | bytes 159752 | tf_op jit(solution)/shard_map/ppermute | solution.py:409
  31.1 1.5 %collective-permute-start.4 = (f32[4,104,128]{2,1,0:T(8,128)S(1)}, f32[4,104,128]{2,1,0:T(8,128)S(1)}, u32[]{:S(2)}, u32[]{:S(2)}) collective-permute-start(f32[4,104,128]{2,1,0:T(8,128)S(1)} %get-tuple-element.28), channel_id=1, source_target_pairs={{0,1},{1,0},{2,3},{3,2},{4,5},{5,4},{6,7},{7,6},{8,9},{9,8},{10,11... | collective-permute-start | bytes 638984 | tf_op jit(solution)/shard_map/ppermute | solution.py:487
  32.6 5.0 %collective-permute-start.5 = (f32[104,128]{1,0:T(8,128)S(1)}, f32[104,128]{1,0:T(8,128)S(1)}, u32[]{:S(2)}, u32[]{:S(2)}) collective-permute-start(f32[104,128]{1,0:T(8,128)S(1)} %get-tuple-element.44), channel_id=1, source_target_pairs={{0,8},{8,0},{16,24},{24,16},{1,9},{9,1},{17,25},{25,17},{2,10},{10... | collective-permute-start | bytes 159752 | tf_op jit(solution)/shard_map/ppermute | solution.py:491
  35.0 5.1 %collective-permute-start.7 = (f32[104,128]{1,0:T(8,128)S(1)}, f32[104,128]{1,0:T(8,128)S(1)}, u32[]{:S(2)}, u32[]{:S(2)}) collective-permute-start(f32[104,128]{1,0:T(8,128)S(1)} %get-tuple-element.45), channel_id=1, source_target_pairs={{0,24},{8,16},{16,8},{24,0},{1,25},{9,17},{17,9},{25,1},{2,26},{10... | collective-permute-start | bytes 159752 | tf_op jit(solution)/shard_map/ppermute | solution.py:491
  35.6 4.7 %collective-permute-start.6 = (f32[104,128]{1,0:T(8,128)S(1)}, f32[104,128]{1,0:T(8,128)S(1)}, u32[]{:S(2)}, u32[]{:S(2)}) collective-permute-start(f32[104,128]{1,0:T(8,128)S(1)} %get-tuple-element.46), channel_id=1, source_target_pairs={{0,16},{8,24},{16,0},{24,8},{1,17},{9,25},{17,1},{25,9},{2,18},{10... | collective-permute-start | bytes 159752 | tf_op jit(solution)/shard_map/ppermute | solution.py:491
  40.3 7.1 %collective-permute-start.10 = (f32[104,128]{1,0:T(8,128)S(1)}, f32[104,128]{1,0:T(8,128)S(1)}, u32[]{:S(2)}, u32[]{:S(2)}) collective-permute-start(f32[104,128]{1,0:T(8,128)S(1)} %fusion.2), channel_id=1, source_target_pairs={{0,6},{2,4},{4,2},{6,0},{1,7},{3,5},{5,3},{7,1},{8,14},{10,12},{12... | collective-permute-start | bytes 159752 | tf_op jit(solution)/shard_map/ppermute | solution.py:497
  42.0 5.5 %collective-permute-start.9 = (f32[104,128]{1,0:T(8,128)S(1)}, f32[104,128]{1,0:T(8,128)S(1)}, u32[]{:S(2)}, u32[]{:S(2)}) collective-permute-start(f32[104,128]{1,0:T(8,128)S(1)} %fusion.2), channel_id=1, source_target_pairs={{0,4},{2,6},{4,0},{6,2},{1,5},{3,7},{5,1},{7,3},{8,12},{10,14},{12... | collective-permute-start | bytes 159752 | tf_op jit(solution)/shard_map/ppermute | solution.py:497
  42.0 5.5 %collective-permute-start.8 = (f32[104,128]{1,0:T(8,128)S(1)}, f32[104,128]{1,0:T(8,128)S(1)}, u32[]{:S(2)}, u32[]{:S(2)}) collective-permute-start(f32[104,128]{1,0:T(8,128)S(1)} %fusion.2), channel_id=1, source_target_pairs={{0,2},{2,0},{4,6},{6,4},{1,3},{3,1},{5,7},{7,5},{8,10},{10,8},{12,... | collective-permute-start | bytes 159752 | tf_op jit(solution)/shard_map/ppermute | solution.py:497
  44.8 13.7 %collective-permute-start.11 = (f32[104,128]{1,0:T(8,128)S(1)}, f32[104,128]{1,0:T(8,128)S(1)}, u32[]{:S(2)}, u32[]{:S(2)}) collective-permute-start(f32[104,128]{1,0:T(8,128)S(1)} %get-tuple-element.31), channel_id=1, source_target_pairs={{0,8},{8,16},{16,24},{1,9},{9,17},{17,25},{2,10},{10,18},{18,26},{... | collective-permute-start | bytes 159752 | tf_op jit(solution)/shard_map/ppermute | solution.py:408
  47.5 11.1 %collective-permute-start.17 = (f32[104,128]{1,0:T(8,128)S(1)}, f32[104,128]{1,0:T(8,128)S(1)}, u32[]{:S(2)}, u32[]{:S(2)}) collective-permute-start(f32[104,128]{1,0:T(8,128)S(1)} %add_add_fusion.refs_1_), channel_id=1, source_target_pairs={{0,24},{8,16},{16,8},{24,0},{1,25},{9,17},{17,9},{25,1},{2,26},{10... | collective-permute-start | bytes 159752 | tf_op jit(solution)/shard_map/ppermute | solution.py:512
  49.5 9.6 %collective-permute-start.16 = (f32[104,128]{1,0:T(8,128)S(1)}, f32[104,128]{1,0:T(8,128)S(1)}, u32[]{:S(2)}, u32[]{:S(2)}) collective-permute-start(f32[104,128]{1,0:T(8,128)S(1)} %add_add_fusion.refs_1_), channel_id=1, source_target_pairs={{0,16},{8,24},{16,0},{24,8},{1,17},{9,25},{17,1},{25,9},{2,18},{10... | collective-permute-start | bytes 159752 | tf_op jit(solution)/shard_map/ppermute | solution.py:512
  50.3 8.9 %collective-permute-start.15 = (f32[104,128]{1,0:T(8,128)S(1)}, f32[104,128]{1,0:T(8,128)S(1)}, u32[]{:S(2)}, u32[]{:S(2)}) collective-permute-start(f32[104,128]{1,0:T(8,128)S(1)} %add_add_fusion.refs_1_), channel_id=1, source_target_pairs={{0,8},{8,0},{16,24},{24,16},{1,9},{9,1},{17,25},{25,17},{2,10},{10... | collective-permute-start | bytes 159752 | tf_op jit(solution)/shard_map/ppermute | solution.py:512
  51.1 4.8 %collective-permute-start.13 = (f32[8,128]{1,0:T(8,128)S(1)}, f32[8,128]{1,0:T(8,128)S(1)}, u32[]{:S(2)}, u32[]{:S(2)}) collective-permute-start(f32[8,128]{1,0:T(8,128)S(1)} %get-tuple-element.33), channel_id=1, source_target_pairs={{0,1},{1,2},{2,3},{3,4},{4,5},{5,6},{6,7},{7,0},{8,9},{9,10},{10,1... | collective-permute-start | bytes 12296 | tf_op jit(solution)/shard_map/ppermute | solution.py:410
  55.9 1.3 %collective-permute-start.14 = (f32[8,128]{1,0:T(8,128)S(1)}, f32[8,128]{1,0:T(8,128)S(1)}, u32[]{:S(2)}, u32[]{:S(2)}) collective-permute-start(f32[8,128]{1,0:T(8,128)S(1)} %get-tuple-element.34), channel_id=1, source_target_pairs={{0,7},{1,0},{2,1},{3,2},{4,3},{5,4},{6,5},{7,6},{8,15},{9,8},{10,9... | collective-permute-start | bytes 12296 | tf_op jit(solution)/shard_map/ppermute | solution.py:411
  57.2 6.0 %collective-permute-start.12 = (f32[104,128]{1,0:T(8,128)S(1)}, f32[104,128]{1,0:T(8,128)S(1)}, u32[]{:S(2)}, u32[]{:S(2)}) collective-permute-start(f32[104,128]{1,0:T(8,128)S(1)} %get-tuple-element.32), channel_id=1, source_target_pairs={{8,0},{16,8},{24,16},{9,1},{17,9},{25,17},{10,2},{18,10},{26,18},{... | collective-permute-start | bytes 159752 | tf_op jit(solution)/shard_map/ppermute | solution.py:409
  58.5 6.2 %collective-permute-start.18 = (f32[104,128]{1,0:T(8,128)S(1)}, f32[104,128]{1,0:T(8,128)S(1)}, u32[]{:S(2)}, u32[]{:S(2)}) collective-permute-start(f32[104,128]{1,0:T(8,128)S(1)} %add_add_fusion.refs_1_), channel_id=1, source_target_pairs={{0,1},{1,0},{2,3},{3,2},{4,5},{5,4},{6,7},{7,6},{8,9},{9,8},{10,11... | collective-permute-start | bytes 159752 | tf_op jit(solution)/shard_map/ppermute | solution.py:513
  58.6 6.1 %collective-permute-start.21 = (f32[104,128]{1,0:T(8,128)S(1)}, f32[104,128]{1,0:T(8,128)S(1)}, u32[]{:S(2)}, u32[]{:S(2)}) collective-permute-start(f32[104,128]{1,0:T(8,128)S(1)} %collective-permute-done.17.refs_4_), channel_id=1, source_target_pairs={{0,1},{1,0},{2,3},{3,2},{4,5},{5,4},{6,7},{7,6},{8,9},{9,8},{10,11... | collective-permute-start | bytes 159752 | tf_op jit(solution)/shard_map/ppermute | solution.py:513
  59.1 5.7 %collective-permute-start.20 = (f32[104,128]{1,0:T(8,128)S(1)}, f32[104,128]{1,0:T(8,128)S(1)}, u32[]{:S(2)}, u32[]{:S(2)}) collective-permute-start(f32[104,128]{1,0:T(8,128)S(1)} %collective-permute-done.16.refs_3_), channel_id=1, source_target_pairs={{0,1},{1,0},{2,3},{3,2},{4,5},{5,4},{6,7},{7,6},{8,9},{9,8},{10,11... | collective-permute-start | bytes 159752 | tf_op jit(solution)/shard_map/ppermute | solution.py:513
  59.2 5.6 %collective-permute-start.19 = (f32[104,128]{1,0:T(8,128)S(1)}, f32[104,128]{1,0:T(8,128)S(1)}, u32[]{:S(2)}, u32[]{:S(2)}) collective-permute-start(f32[104,128]{1,0:T(8,128)S(1)} %collective-permute-done.15.refs_2_), channel_id=1, source_target_pairs={{0,1},{1,0},{2,3},{3,2},{4,5},{5,4},{6,7},{7,6},{8,9},{9,8},{10,11... | collective-permute-start | bytes 159752 | tf_op jit(solution)/shard_map/ppermute | solution.py:513
  (10 other events, 22.2 us)

commit v2 on v1

v2 whole, which is shorter than its diff:
```python
import math

import jax
import jax.numpy as jnp
from jax import lax
from jax.experimental import pallas as pl
from jax.experimental.pallas import tpu as pltpu
from jax.sharding import Mesh
from jax.sharding import PartitionSpec as P

spread_coef = 0.15
level_eps = 1e-05
f32 = jnp.float32
bf16 = jnp.bfloat16
vmem = pl.BlockSpec(memory_space=pltpu.VMEM)
hbm = pl.BlockSpec(memory_space=pltpu.HBM)
params = pltpu.CompilerParams(vmem_limit_bytes=24 * 1024 * 1024)


def round_up(value, step):
    return -(-value // step) * step


def lane_ids(shape):
    return lax.broadcasted_iota(jnp.int32, shape, 1)


def level_ids(shape):
    return lax.broadcasted_iota(jnp.int32, shape, 0).astype(f32)


def row_of(ref, row, levels, rows):
    return ref[pl.ds(row, levels, stride=rows), :]


def lane_sums(pad_ref, block):
    pad_ref[...] = jnp.zeros(pad_ref.shape, f32)
    pad_ref[0 : block.shape[0], :] = block
    return jnp.sum(pad_ref[...].T, axis=0, keepdims=True)


def write_edges(field_ref, levels, rows, pad_ref, outs, odd, depth=None):
    lat_a, lat_b, lon_a, lon_b = outs
    lat_odd, lon_odd = odd
    cols = field_ref.shape[1]
    lanes = lane_ids((levels, cols))
    first = row_of(field_ref, 0, levels, rows)
    last = row_of(field_ref, rows - 1, levels, rows)
    tail = (lat_a.shape[0] - levels, cols)
    first_tail = last_tail = jnp.zeros(tail, f32)
    if depth is not None:
        first_tail = jnp.broadcast_to(depth[0:1, :], tail)
        last_tail = jnp.broadcast_to(depth[rows - 1 : rows, :], tail)
    lat_a[0:levels, :] = jnp.where(lat_odd, first, last)
    lat_b[0:levels, :] = jnp.where(lat_odd, last, first)
    lat_a[levels:, :] = jnp.where(lat_odd, first_tail, last_tail)
    lat_b[levels:, :] = jnp.where(lat_odd, last_tail, first_tail)
    low = jnp.zeros((levels, cols), f32)
    high = jnp.zeros((levels, cols), f32)
    for row in range(rows):
        chunk = row_of(field_ref, row, levels, rows)
        low = jnp.where(lanes == row, pltpu.roll(chunk, row, 1) if row else chunk, low)
        high = jnp.where(lanes == row, pltpu.roll(chunk, (row + 1) % cols, 1), high)
    turned = []
    for packed, edge in ((low, 0), (high, cols - 1)):
        pad_ref[...] = jnp.zeros(pad_ref.shape, f32)
        pad_ref[0:levels, :] = packed
        flat = pad_ref[...].T[0:rows, :]
        if depth is not None:
            at = lane_ids(flat.shape) == levels
            flat = jnp.where(at, jnp.broadcast_to(depth[:, edge : edge + 1], flat.shape), flat)
        turned.append(flat)
    lon_a[...] = jnp.where(lon_odd, turned[0], turned[1])
    lon_b[...] = jnp.where(lon_odd, turned[1], turned[0])


def spread_rows(field_ref, depth, levels, rows, halos, depth_halos):
    north, south, west, east = halos
    cols = depth.shape[1]
    lanes = lane_ids((levels, cols))
    lev = level_ids((levels, cols))
    depth_lanes = lane_ids(depth.shape)
    depth_north, depth_south, depth_west, depth_east = depth_halos
    west_depth = jnp.where(depth_lanes == 0, depth_west, pltpu.roll(depth, 1, 1))
    east_depth = jnp.where(depth_lanes == cols - 1, depth_east, pltpu.roll(depth, cols - 1, 1))
    chunks = [row_of(field_ref, row, levels, rows) for row in range(rows)]
    wets = [(lev < depth[row : row + 1, :]).astype(f32) for row in range(rows)]
    north_wet = (lev < depth_north).astype(f32)
    south_wet = (lev < depth_south).astype(f32)
    for row in range(rows):
        center = chunks[row]
        wet = wets[row]
        below, below_wet = (chunks[row + 1], wets[row + 1]) if row + 1 < rows else (south, south_wet)
        above, above_wet = (chunks[row - 1], wets[row - 1]) if row else (north, north_wet)
        left = jnp.where(
            lanes == 0, pltpu.roll(west, (cols - row) % cols, 1) if row else west, pltpu.roll(center, 1, 1)
        )
        right = jnp.where(
            lanes == cols - 1, pltpu.roll(east, cols - 1 - row, 1), pltpu.roll(center, cols - 1, 1)
        )
        left_wet = (lev < west_depth[row : row + 1, :]).astype(f32)
        right_wet = (lev < east_depth[row : row + 1, :]).astype(f32)
        flux = below_wet * (below - center) + above_wet * (above - center)
        flux = flux + left_wet * (left - center) + right_wet * (right - center)
        yield row, center, wet, center + spread_coef * (wet * flux)


def turn(packed, levels):
    rows, lanes = packed.shape
    square = jnp.concatenate([packed] + [jnp.zeros((rows, lanes), f32)] * (lanes // rows - 1), 0)
    return square.T[0:levels, :]


def halo_values(levels, north, south, west, east):
    return (north[0:levels, :], south[0:levels, :], turn(west[...], levels), turn(east[...], levels))


def halo_depths(levels, north, south, west, east, shape):
    return (
        north[levels : levels + 1, :],
        south[levels : levels + 1, :],
        jnp.broadcast_to(west[...][:, levels : levels + 1], shape),
        jnp.broadcast_to(east[...][:, levels : levels + 1], shape),
    )


def odd_places():
    return (lax.axis_index("lat") % 2 == 1, lax.axis_index("core") == 1)


def lon_neighbours():
    lons = lax.axis_size("z") * lax.axis_size("core")
    lon = lax.axis_index("z") * lax.axis_size("core") + lax.axis_index("core")
    base = lax.axis_index("lat") * lons
    return base + (lon + lons - 1) % lons, base + (lon + 1) % lons


def energy_slots(levels, rows, lanes):
    per = -(-levels // rows)
    assert levels + 1 + per <= lanes
    return [(row, row * per, levels + 1, per) for row in range(rows)]


def energy_kernel(
    levels, tracer_hbm, mask_hbm, bottom_hbm, b_in_hbm, b_out_hbm, kappa_hbm,
    rows_out, lat_a, lat_b, tracer, depth_out, b_in, b_out, kappa,
    mask, bottom, lon_a, lon_b, pad, sems,
):
    rows, cols = mask.shape
    pairs = (
        (mask_hbm, mask), (bottom_hbm, bottom), (tracer_hbm, tracer),
        (b_in_hbm, b_in), (b_out_hbm, b_out), (kappa_hbm, kappa),
    )
    copies = [pltpu.make_async_copy(src, dst, sems.at[i]) for i, (src, dst) in enumerate(pairs)]
    for copy in copies:
        copy.start()
    for copy in copies[:3]:
        copy.wait()
    depth = (mask[...] * bottom[...]).astype(f32)
    depth_out[...] = depth
    lev = level_ids((levels, cols))
    total = jnp.zeros((levels, cols), f32)
    for row in range(rows):
        wet_tracer = jnp.where(lev < depth[row : row + 1, :], row_of(tracer, row, levels, rows), 0.0)
        total = total + wet_tracer * wet_tracer
    sums = jnp.broadcast_to(lane_sums(pad, total), lon_a.shape)
    odd = odd_places()
    write_edges(tracer, levels, rows, pad, (lat_a, lat_b, lon_a, lon_b), odd, depth)
    shape = lon_a.shape
    sub = lax.broadcasted_iota(jnp.int32, shape, 0)
    lanes = lane_ids(shape)
    packed = jnp.zeros(shape, f32)
    for row, source, target, count in energy_slots(levels, rows, shape[1]):
        here = (sub == row) & (lanes >= target) & (lanes < target + count)
        packed = jnp.where(here, pltpu.roll(sums, (target - source) % shape[1], 1), packed)
    rows_out[...] = jnp.broadcast_to(packed[None], rows_out.shape)
    facing = jnp.where(lanes <= levels, lon_a[...], packed)
    outer = jnp.where(lanes <= levels, lon_b[...], packed)
    west, east = lon_neighbours()
    rows_out[west] = jnp.where(odd[1], facing, outer)
    rows_out[east] = jnp.where(odd[1], outer, facing)
    for copy in copies[3:]:
        copy.wait()


def energy_total(gathered, levels):
    total = jnp.sum(gathered[...], axis=0)
    rows, width = total.shape
    sub = lax.broadcasted_iota(jnp.int32, total.shape, 0)
    lanes = lane_ids(total.shape)
    out = jnp.zeros(total.shape, f32)
    for row, source, target, count in energy_slots(levels, rows, width):
        here = (sub == row) & (lanes >= source) & (lanes < min(source + count, levels))
        out = jnp.where(here, pltpu.roll(total, (source - target) % width, 1), out)
    return jnp.sum(out, axis=0, keepdims=True)


def columns_of(row, lanes):
    return jnp.broadcast_to(row, (lanes, row.shape[1])).T


def network_kernel(
    levels, column_count, gathered, tracer, depth_ref, w_in, b_in, w_out_t, b_out, kappa,
    radius_row, x_b, wi_b, hidden, slope, gate, up_out, down_out,
    pad, x_f, wi_f, wo_f,
):
    rows, cols = depth_ref.shape
    hid = w_in.shape[1]
    span = rows * cols
    pad_levels = x_f.shape[0]
    depth = depth_ref[...]
    lev = level_ids((levels, cols))
    radius_line = jnp.sqrt(energy_total(gathered, levels) / column_count + level_eps)
    radius_row[...] = radius_line
    radius = columns_of(radius_line, cols)[0:levels, :]
    scale = 1.0 / radius

    x_f[levels:, :] = jnp.where(
        lax.broadcasted_iota(jnp.int32, (pad_levels - levels, span), 0) < 3, 1.0, 0.0
    )
    for row in range(rows):
        wet_tracer = jnp.where(lev < depth[row : row + 1, :], row_of(tracer, row, levels, rows), 0.0)
        x_f[0:levels, row * cols : (row + 1) * cols] = wet_tracer * scale
    x_b[...] = x_f[...].astype(bf16)

    wi_f[...] = jnp.zeros(wi_f.shape, f32)
    wi_f[0:levels, :] = w_in[...].astype(f32)
    bias = b_in[...]
    for part in range(3):
        piece = bias.astype(bf16).astype(f32)
        wi_f[levels + part : levels + part + 1, :] = piece
        bias = bias - piece
    wi_b[...] = wi_f[...].astype(bf16)
    wi_t = wi_f[...].T.astype(bf16)
    wo_f[...] = jnp.zeros(wo_f.shape, f32)
    wo_f[0:levels, :] = w_out_t[...].astype(f32)

    block = hid // 4
    for part in range(4):
        at = slice(part * block, (part + 1) * block)
        pre = jnp.dot(wi_t[at, :], x_b[...], preferred_element_type=f32)
        sig = 1.0 / (1.0 + jnp.exp(-pre))
        hidden[at, :] = (pre * sig).astype(bf16)
        slope[at, :] = sig * (1.0 + pre * (1.0 - sig))

    pad[...] = jnp.zeros(pad.shape, f32)
    pad[0:1, 0:levels] = b_out[...]
    pad[1:2, 0:levels] = kappa[...]
    turned = pad[...].T
    logits = jnp.dot(wo_f[...].astype(bf16), hidden[...], preferred_element_type=f32) + turned[:, 0:1]
    tiny = jnp.exp(-jnp.abs(logits))
    share = 1.0 / (1.0 + tiny)
    gate[...] = jnp.where(logits >= 0.0, share, tiny * share)
    soft = jnp.maximum(logits, 0.0) + jnp.log1p(tiny)
    kappa_col = jnp.broadcast_to(turned[0:levels, 1:2], (levels, cols))
    for row in range(rows):
        open_face = (lev + 1.0 < depth[row : row + 1, :]) & (lev + 1.0 < float(levels))
        at = pl.ds(row, levels, stride=rows)
        sinking = soft[0:levels, row * cols : (row + 1) * cols]
        up_out[at, :] = jnp.where(open_face, kappa_col, 0.0)
        down_out[at, :] = jnp.where(open_face, kappa_col + sinking, 0.0)


def solve_kernel(
    levels, scale,
    gathered, tracer, cotangent, depth_ref, up_ref, down_ref, north, south, w_out_t, wi_b, x_b, hidden, slope, gate,
    keep, send, adjoint, lat_a, lat_b, d_inputs,
    pad, wo_f, dl_f, dl_b, dp_b, mixed, rate_a, rate_b, inv_p, fwd_z, fwd_u, flow,
):
    rows, cols = depth_ref.shape
    hid = w_out_t.shape[1]
    span = rows * cols
    pad_levels = dl_f.shape[0]
    depth = depth_ref[...]
    lev = level_ids((levels, cols))
    west_at, east_at = lon_neighbours()
    west, east = gathered.at[west_at], gathered.at[east_at]
    halos = halo_values(levels, north, south, west, east)
    depth_halos = halo_depths(levels, north, south, west, east, depth.shape)
    for row, _, _, value in spread_rows(tracer, depth, levels, rows, halos, depth_halos):
        mixed[pl.ds(row, levels, stride=rows), :] = value

    def at_level(k):
        return slice(k * rows, (k + 1) * rows)

    rest = jnp.ones((rows, cols), f32)
    z = mixed[at_level(0), :]
    u = cotangent[at_level(0), :]
    for k in range(levels - 1):
        down = down_ref[at_level(k), :]
        inv = 1.0 / (rest + down)
        a = down * inv
        b = up_ref[at_level(k), :] * inv
        inv_p[at_level(k), :] = inv
        rate_a[at_level(k), :] = a
        rate_b[at_level(k), :] = b
        fwd_z[at_level(k), :] = z
        fwd_u[at_level(k), :] = u
        rest = 1.0 + b * rest
        z = mixed[at_level(k + 1), :] + a * z
        u = cotangent[at_level(k + 1), :] + b * u
    inv = 1.0 / rest
    x = z * inv
    y = u * inv
    adjoint[at_level(levels - 1), :] = y
    flow[at_level(levels - 1), :] = jnp.zeros((rows, cols), f32)
    for k in range(levels - 2, -1, -1):
        inv = inv_p[at_level(k), :]
        x = fwd_z[at_level(k), :] * inv + rate_b[at_level(k), :] * x
        y_new = fwd_u[at_level(k), :] * inv + rate_a[at_level(k), :] * y
        adjoint[at_level(k), :] = y_new
        flow[at_level(k), :] = jnp.where(depth > float(k + 1), x * (y - y_new), 0.0)
        y = y_new

    dl_f[levels:, :] = jnp.zeros((pad_levels - levels, span), f32)
    for row in range(rows):
        part = slice(row * cols, (row + 1) * cols)
        dl_f[0:levels, part] = row_of(flow, row, levels, rows) * gate[0:levels, part]
    dl_b[...] = dl_f[...].astype(bf16)
    bout = jnp.zeros((pad_levels, cols), f32)
    for row in range(rows):
        bout = bout + dl_b[:, row * cols : (row + 1) * cols].astype(f32)
    bout_row = lane_sums(pad, bout) * scale

    wo_f[...] = jnp.zeros(wo_f.shape, f32)
    wo_f[0:levels, :] = w_out_t[...].astype(f32)
    wo_b = wo_f[...].T.astype(bf16)
    block = hid // 4
    for part in range(4):
        at = slice(part * block, (part + 1) * block)
        d_hidden = jnp.dot(wo_b[at, :], dl_b[...], preferred_element_type=f32)
        dp_b[at, :] = (d_hidden * slope[at, :]).astype(bf16)
    d_in = jnp.dot(wi_b[...], dp_b[...], preferred_element_type=f32)
    level = jnp.zeros((levels, cols), f32)
    for row in range(rows):
        part = d_in[0:levels, row * cols : (row + 1) * cols]
        d_inputs[row, 0:levels, :] = part
        wet_tracer = jnp.where(lev < depth[row : row + 1, :], row_of(tracer, row, levels, rows), 0.0)
        level = level + part * wet_tracer
    level_row = lane_sums(pad, level)

    contract = (((1,), (1,)), ((), ()))
    lat_odd, lon_odd = odd_places()
    quarter = lax.axis_index("lat") % 4
    height = keep.shape[1]
    for part in range(4):
        at = slice(part * block, (part + 1) * block)
        slot = part ^ quarter
        g_in = lax.dot_general(x_b[...], dp_b[at, :], contract, preferred_element_type=f32)
        g_out = lax.dot_general(dl_b[...], hidden[at, :], contract, preferred_element_type=f32)
        g_in = g_in[0:height, :] * scale
        g_out = g_out[0:height, :] * scale
        keep[slot] = jnp.where(lon_odd, g_out, g_in)
        send[pl.ds(pl.multiple_of(slot * height, 8), height), :] = jnp.where(lon_odd, g_in, g_out)
        keep[slot, levels + 1 : levels + 2, :] = level_row
        keep[slot, levels + 2 : levels + 3, :] = bout_row
        lower = send.at[pl.ds(pl.multiple_of(slot * height, 8), height), :]
        lower[levels + 1 : levels + 2, :] = level_row
        lower[levels + 2 : levels + 3, :] = bout_row
    lon_a = send.at[4 * height : 4 * height + rows, :]
    lon_b = send.at[4 * height + rows : 4 * height + 2 * rows, :]
    write_edges(adjoint, levels, rows, pad, (lat_a, lat_b, lon_a, lon_b), (lat_odd, lon_odd))


def final_kernel(
    levels, column_count, gathered, radius_row, level_total, adjoint, tracer, d_inputs, depth_ref,
    north, south, west, east, t_north, t_south, out,
):
    rows, cols = depth_ref.shape
    depth = depth_ref[...]
    radius_line = radius_row[...]
    level_sum = level_total[levels + 1 : levels + 2, :]
    pull = level_sum / (column_count * (radius_line * radius_line * radius_line))
    radius = columns_of(radius_line, cols)[0:levels, :]
    pull = columns_of(pull, cols)[0:levels, :]
    west_at, east_at = lon_neighbours()
    halos = halo_values(levels, north, south, west, east)
    depth_halos = halo_depths(
        levels, t_north, t_south, gathered.at[west_at], gathered.at[east_at], depth.shape
    )
    scale = 1.0 / radius
    for row, _, wet, value in spread_rows(adjoint, depth, levels, rows, halos, depth_halos):
        wet_tracer = wet * row_of(tracer, row, levels, rows)
        d_wet = d_inputs[row, 0:levels, :] * scale - wet_tracer * pull
        out[pl.ds(row, levels, stride=rows), :] = value + wet * d_wet


def gather_kernel(levels, *refs):
    mine, other = refs[0:4], refs[4:8]
    grad_in, grad_bin, grad_out, grad_bout = refs[8:]
    lon_odd = lax.axis_index("core") == 1
    quarter = lax.axis_index("lat") % 4
    block = mine[0].shape[1]
    for step in range(4):
        at = pl.ds(pl.multiple_of((step ^ quarter) * block, block), block)
        inner = jnp.where(lon_odd, other[step][...], mine[step][...])
        outer = jnp.where(lon_odd, mine[step][...], other[step][...])
        grad_in[:, at] = inner[0:levels, :]
        grad_bin[:, at] = inner[levels : levels + 1, :]
        grad_out[:, at] = outer[0:levels, :]
    grad_bout[...] = mine[0][levels + 2 : levels + 3, 0:levels]


def flip(count, by):
    return [(i, i ^ by) for i in range(count)]


def far_pairs(count, ring):
    pairs = [(i, i + 1) for i in range(1, count - 1, 2)]
    if ring:
        pairs.append((count - 1, 0))
    return pairs + [(j, i) for i, j in pairs]


def in_order(odd, near, far):
    return jnp.where(odd, near, far), jnp.where(odd, far, near)


def shards(tracer, cotangent, land_mask, bottom, kappa, w_in, b_in, w_out, b_out):
    levels, rows, cols = tracer.shape
    hid = w_in.shape[1]
    lats, chips = lax.axis_size("lat"), lax.axis_size("z")
    lons = 2 * chips
    devices = lats * lons
    column_count = rows * cols * devices
    pad_levels = round_up(levels + 3, 128)
    height = round_up(levels + 3, 8)
    flat = (levels * rows, cols)
    span = rows * cols
    tracer = tracer.reshape(flat)
    cotangent = cotangent.reshape(flat)
    w_out_t = w_out.T
    sds = jax.ShapeDtypeStruct
    lat_edge = sds((height, cols), f32)
    pad = pltpu.VMEM((pad_levels, cols), f32)
    lon_edge = pltpu.VMEM((rows, pad_levels), f32)
    lat_odd, lon_odd = odd_places()

    gathered, lat_a, lat_b, tracer, depth, b_in, b_out, kappa = pl.pallas_call(
        lambda *refs: energy_kernel(levels, *refs),
        out_shape=[
            sds((devices, rows, pad_levels), f32),
            lat_edge,
            lat_edge,
            sds(flat, f32),
            sds((rows, cols), f32),
            sds((1, hid), f32),
            sds((1, levels), f32),
            sds((1, levels), f32),
        ],
        in_specs=[hbm] * 6,
        out_specs=[vmem] * 8,
        scratch_shapes=[
            pltpu.VMEM((rows, cols), jnp.int32),
            pltpu.VMEM((rows, cols), jnp.int32),
            lon_edge,
            lon_edge,
            pad,
            pltpu.SemaphoreType.DMA((6,)),
        ],
        compiler_params=params,
    )(tracer, land_mask, bottom, b_in.reshape(1, hid), b_out.reshape(1, levels), kappa.reshape(1, levels))
    gathered = lax.all_to_all(gathered, ("lat", "z", "core"), 0, 0, tiled=True)
    t_north, t_south = in_order(
        lat_odd,
        lax.ppermute(lat_a, "lat", flip(lats, 1)),
        lax.ppermute(lat_b, "lat", far_pairs(lats, False)),
    )

    radius_row, x_b, wi_b, hidden, slope, gate, up, down = pl.pallas_call(
        lambda *refs: network_kernel(levels, column_count, *refs),
        out_shape=[
            sds((1, pad_levels), f32),
            sds((pad_levels, span), bf16),
            sds((pad_levels, hid), bf16),
            sds((hid, span), bf16),
            sds((hid, span), f32),
            sds((pad_levels, span), f32),
            sds(flat, f32),
            sds(flat, f32),
        ],
        in_specs=[vmem] * 8,
        out_specs=[vmem] * 8,
        scratch_shapes=[
            pad,
            pltpu.VMEM((pad_levels, span), f32),
            pltpu.VMEM((pad_levels, hid), f32),
            pltpu.VMEM((pad_levels, hid), f32),
        ],
        compiler_params=params,
    )(gathered, tracer, depth, w_in, b_in, w_out_t, b_out, kappa)

    keep, send, adjoint, lat_a, lat_b, d_inputs = pl.pallas_call(
        lambda *refs: solve_kernel(levels, 1.0 / math.sqrt(column_count), *refs),
        out_shape=[
            sds((4, height, hid // 4), f32),
            sds((4 * height + 2 * rows, hid // 4), f32),
            sds(flat, f32),
            lat_edge,
            lat_edge,
            sds((rows, height, cols), f32),
        ],
        in_specs=[vmem] * 14,
        out_specs=[vmem] * 6,
        scratch_shapes=[
            pad,
            pltpu.VMEM((pad_levels, hid), f32),
            pltpu.VMEM((pad_levels, span), f32),
            pltpu.VMEM((pad_levels, span), bf16),
            pltpu.VMEM((hid, span), bf16),
            *[pltpu.VMEM(flat, f32)] * 7,
        ],
        compiler_params=params,
    )(
        gathered, tracer, cotangent, depth, up, down, t_north, t_south,
        w_out_t, wi_b, x_b, hidden, slope, gate,
    )

    got = lax.ppermute(send, "core", flip(2, 1))
    chip = keep + got[: 4 * height].reshape(keep.shape)
    lon_near = got[4 * height : 4 * height + rows]
    lon_pass = got[4 * height + rows :]
    part = chip[0]
    if lats == 4:
        near = lax.ppermute(jnp.concatenate([chip[1], lat_a], 0), "lat", flip(lats, 1))
        far = lax.ppermute(jnp.concatenate([chip[3], lat_b], 0), "lat", flip(lats, 3))
        cross = lax.ppermute(chip[2], "lat", flip(lats, 2))
        part = part + near[:height] + far[:height] + cross
        north, south = in_order(lat_odd, near[height:], far[height:])
    else:
        for step in range(1, 4):
            part = part + lax.ppermute(chip[step], "lat", flip(lats, step))
        step = 4
        while step < lats:
            part = part + lax.ppermute(part, "lat", flip(lats, step))
            step *= 2
        north, south = in_order(
            lat_odd,
            lax.ppermute(lat_a, "lat", flip(lats, 1)),
            lax.ppermute(lat_b, "lat", far_pairs(lats, False)),
        )
    if chips == 4:
        packed = jnp.concatenate([part, lon_pass], 0)
        near = lax.ppermute(packed, "z", flip(chips, 1))
        far = lax.ppermute(packed, "z", flip(chips, 3))
        cross = lax.ppermute(part, "z", flip(chips, 2))
        part = part + near[:height] + far[:height] + cross
        from_near = (lax.axis_index("z") + lax.axis_index("core")) % 2 == 1
        lon_far = jnp.where(from_near, near[height:], far[height:])
    else:
        step = 1
        while step < chips:
            part = part + lax.ppermute(part, "z", flip(chips, step))
            step *= 2
        lon_b = send[4 * height + rows :]
        lon_far = lax.ppermute(lon_b, ("z", "core"), far_pairs(lons, True))
    west, east = in_order(lon_odd, lon_near, lon_far)

    tracer_adjoint = pl.pallas_call(
        lambda *refs: final_kernel(levels, column_count, *refs),
        out_shape=sds(flat, f32),
        in_specs=[vmem] * 13,
        out_specs=vmem,
        compiler_params=params,
    )(
        gathered, radius_row, part, adjoint, tracer, d_inputs, depth,
        north, south, west, east, t_north, t_south,
    )

    mine = [part] + [lax.ppermute(part, "lat", flip(lats, step)) for step in range(1, 4)]
    other = [lax.ppermute(piece, "core", flip(2, 1)) for piece in mine]
    grad_w_in, grad_b_in, grad_w_out_t, grad_b_out = pl.pallas_call(
        lambda *refs: gather_kernel(levels, *refs),
        out_shape=[
            sds((levels, hid), f32),
            sds((1, hid), f32),
            sds((levels, hid), f32),
            sds((1, levels), f32),
        ],
        in_specs=[vmem] * 8,
        out_specs=[vmem] * 4,
        compiler_params=params,
    )(*mine, *other)
    return (
        tracer_adjoint.reshape(levels, rows, cols),
        grad_w_in,
        grad_b_in.reshape(hid),
        grad_w_out_t.T,
        grad_b_out.reshape(levels),
    )


def solution(mesh):
    lats, lons = mesh.shape["lat"], mesh.shape["lon"]
    split = Mesh(mesh.devices.reshape(lats, lons // 2, 2), ("lat", "z", "core"))
    field = P(None, "lat", ("z", "core"))
    plane = P("lat", ("z", "core"))
    return jax.shard_map(
        shards,
        mesh=split,
        in_specs=(field, field, plane, plane, P(), P(), P(), P(), P()),
        out_specs=(field, P(), P(), P(), P()),
        check_vma=False,
    )
```

time: 67.6 us -> 60.5 us (0.89)
  starting transfers between devices: 32.8 us -> 23.6 us
  local copies, waits for them, and re-layouts: 4.93 us -> 8.07 us
  Pallas kernels: 9.93 us -> 8.31 us
    ppermute x15 -> x9, waiting for transfers between devices: 18.5 us -> 7.81 us  [the longest x1 3.66 us: shards(): cross = lax.ppermute(chip[2], 'lat', flip(lats, 2))]
    all_to_all x1, waiting for transfers between devices: 0.01 us -> 8.12 us  [shards(): gathered = lax.all_to_all(gathered, ('lat', 'z', 'core'), 0, 0, tiled=True)]
    ppermute x15 -> x9, starting transfers between devices: 20.9 us -> 14.9 us  [the longest x1 5.74 us: shards(): lax.ppermute(lat_a, 'lat', flip(lats, 1))]
    ppermute x3, waiting for transfers between devices: 0.01 us -> 3.15 us  [shards(): lax.ppermute(part, 'lat', flip(lats, step))]
    unnamed x24 -> x20, local copies, waits for them, and re-layouts: 4.92 us -> 8.04 us
    all_to_all x1, starting transfers between devices: 7.3 us -> 4.84 us  [shards(): gathered = lax.all_to_all(gathered, ('lat', 'z', 'core'), 0, 0, tiled=True)]
    pallas_call x2, Pallas kernels: 5.79 us -> 4.59 us  [the longest x1 2.73 us: shards(): pl.pallas_call(lambda *refs: solve_kernel(levels, 1.0 / math.sqrt(column_...]
    pallas_call x1, Pallas kernels: 1.68 us -> 0.83 us  [shards(): pl.pallas_call(lambda *refs: gather_kernel(levels, *refs), out_shape=[sds...]
  transfers between devices with their start and end apart: 23 -> 17, of which waited for: 9 -> 8; matrix products, arithmetic and copies ran while one was open for 2% -> 0% of each run, Pallas kernels for 3% -> 3%
where the time goes in v2:
time: 60.5 us; the launch traced here: 60 us
  starting transfers between devices  23.6 us (39%)
  waiting for transfers between devices  19.1 us (32%)
  Pallas kernels  8.31 us (14%)
  local copies, waits for them, and re-layouts  8.07 us (13%)
  between operations  0.79 us (1%)
    all_to_all x1, waiting for transfers between devices, shards(): gathered = lax.all_to_all(gathered, ('lat', 'z', 'core'), 0, 0, tiled=True)  8.12 us
    unnamed x20, local copies, waits for them, and re-layouts  8.04 us
    ppermute x1, starting transfers between devices, shards(): lax.ppermute(lat_a, 'lat', flip(lats, 1))  5.74 us
    all_to_all x1, starting transfers between devices, shards(): gathered = lax.all_to_all(gathered, ('lat', 'z', 'core'), 0, 0, tiled=True)  4.84 us
    ppermute x1, waiting for transfers between devices, shards(): cross = lax.ppermute(chip[2], 'lat', flip(lats, 2))  3.66 us
    ppermute x3, starting transfers between devices, shards(): lax.ppermute(part, 'lat', flip(lats, step))  3.55 us
    ppermute x1, starting transfers between devices, shards(): cross = lax.ppermute(part, 'z', flip(chips, 2))  3.43 us
    ppermute x3, waiting for transfers between devices, shards(): lax.ppermute(part, 'lat', flip(lats, step))  3.15 us
  transfers between devices with their start and end apart: 17, of which 8 were waited for; matrix products, arithmetic and copies ran while one was open for 0% of the time, Pallas kernels for 3%

profile of v2, /device:TPU:0, one launch (start us, length us, event | category | flops | bytes accessed | tf_op | source)
XLA Modules:
  0.0 60.0 jit_solution(15504211617982086242)
XLA Ops:
  0.6 1.0 %copy-done.3 = f32[100,8,128]{2,1,0:T(8,128)S(1)} copy-done((f32[100,8,128]{2,1,0:T(8,128)S(1)}, f32[100,8,128]{2,1,0:T(8,128)}, u32[]{:S(2)}) %copy-start.3) | copy-done | bytes 409624
  5.0 1.4 %shard_map.128 = (f32[32,8,128]{2,1,0:T(8,128)}, f32[104,128]{1,0:T(8,128)S(1)}, f32[104,128]{1,0:T(8,128)S(1)}, f32[800,128]{1,0:T(8,128)S(1)}, f32[8,128]{1,0:...) custom-call(f32[800,128]{1,0:T(8,128)S(1)} %bitcast.24, s32[8,128]{1,0:T(8,128)S(1)} %copy-done.5, ...), custom_call_target="tpu_custom_call" | custom-call | tf_op jit(solution)/shard_map/pallas_call | solution.py:439
  7.0 5.7 %collective-permute-start = (f32[104,128]{1,0:T(8,128)S(1)}, f32[104,128]{1,0:T(8,128)S(1)}, u32[]{:S(2)}, u32[]{:S(2)}) collective-permute-start(f32[104,128]{1,0:T(8,128)S(1)} %get-tuple-element.40), channel_id=1, source_target_pairs={{0,8},{8,0},{16,24},{24,16},{1,9},{9,1},{17,25},{25,17},{2,10},{10... | collective-permute-start | bytes 159752 | tf_op jit(solution)/shard_map/ppermute | solution.py:466
  12.8 4.8 %all-to-all-start = ((f32[32,8,128]{2,1,0:T(8,128)}), f32[32,8,128]{2,1,0:T(8,128)S(1)}, u32[]{:S(2)}, u32[]{:S(2)}) async-start(f32[32,8,128]{2,1,0:T(8,128)} %get-tuple-element.31), calls=%async_computation | async-start | bytes 262144 | tf_op jit(solution)/shard_map/all_to_all | solution.py:463
  17.7 8.1 %all-to-all-done.refs_0_ = f32[32,8,128]{2,1,0:T(8,128)S(1)} async-done(((f32[32,8,128]{2,1,0:T(8,128)}), f32[32,8,128]{2,1,0:T(8,128)S(1)}, u32[]{:S(2)}, u32[]{:S(2)}) %all-to-all-start) | async-done | bytes 131104 | tf_op jit(solution)/shard_map/all_to_all | solution.py:463
  25.8 0.9 %copy-done = bf16[512,100]{0,1:T(8,128)(2,1)S(1)} copy-done((bf16[512,100]{0,1:T(8,128)(2,1)S(1)}, bf16[512,100]{0,1:T(8,128)(2,1)}, u32[]{:S(2)}) %copy-start) | copy-done | bytes 102424
  26.7 0.9 %copy-done.4 = bf16[100,512]{1,0:T(8,128)(2,1)S(1)} copy-done((bf16[100,512]{1,0:T(8,128)(2,1)S(1)}, bf16[100,512]{1,0:T(8,128)(2,1)}, u32[]{:S(2)}) %copy-start.4) | copy-done | bytes 102424
  27.6 1.9 %shard_map.129 = (f32[1,128]{1,0:T(1,128)S(1)}, bf16[128,1024]{1,0:T(8,128)(2,1)S(1)}, bf16[128,512]{1,0:T(8,128)(2,1)S(1)}, bf16[512,1024]{1,0:T(8,128)(2,1)S(1...) custom-call(f32[32,8,128]{2,1,0:T(8,128)S(1)} %all-to-all-done.refs_0_, ...), custom_call_target="tpu_custom_call" | custom-call | tf_op jit(solution)/shard_map/pallas_call | solution.py:470
  29.5 0.9 %copy-done.1 = bf16[512,100]{0,1:T(8,128)(2,1)S(1)} copy-done((bf16[512,100]{0,1:T(8,128)(2,1)S(1)}, bf16[512,100]{0,1:T(8,128)(2,1)}, u32[]{:S(2)}) %copy-start.1) | copy-done | bytes 102424
  30.4 1.0 %copy-done.2 = f32[100,8,128]{2,1,0:T(8,128)S(1)} copy-done((f32[100,8,128]{2,1,0:T(8,128)S(1)}, f32[100,8,128]{2,1,0:T(8,128)}, u32[]{:S(2)}) %copy-start.2) | copy-done | bytes 409624
  31.4 2.7 %shard_map.130 = (f32[4,104,128]{2,1,0:T(8,128)S(1)}, f32[432,128]{1,0:T(8,128)S(1)}, f32[800,128]{1,0:T(8,128)S(1)}, f32[104,128]{1,0:T(8,128)S(1)}, f32[104,12...) custom-call(f32[32,8,128]{2,1,0:T(8,128)S(1)} %all-to-all-done.refs_0_, f32[800,128]{1,0:T(8,128)S(1)} %get-tuple-element.32.refs_1_.refs_4_, ...), custom_call_target="tpu_custom_call" | custom-call | tf_op jit(solution)/shard_map/pallas_call | solution.py:493
  34.5 1.2 %collective-permute-done.2 = f32[432,128]{1,0:T(8,128)S(1)} collective-permute-done((f32[432,128]{1,0:T(8,128)S(1)}, f32[432,128]{1,0:T(8,128)S(1)}, u32[]{:S(2)}, u32[]{:S(2)}) %collective-permute-start.2) | collective-permute-done | bytes 221216 | tf_op jit(solution)/shard_map/ppermute | solution.py:519
  35.7 1.0 %collective-permute-start.4 = (f32[208,128]{1,0:T(8,128)S(1)}, f32[208,128]{1,0:T(8,128)S(1)}, u32[]{:S(2)}, u32[]{:S(2)}) collective-permute-start(f32[208,128]{1,0:T(8,128)S(1)} %pad_maximum_fusion.1), channel_id=1, source_target_pairs={{0,24},{8,16},{16,8},{24,0},{1,25},{9,17},{17,9},{25,1},{2,26},{10... | collective-permute-start | bytes 319496 | tf_op jit(solution)/shard_map/ppermute | solution.py:526
  36.8 1.4 %collective-permute-start.3 = (f32[208,128]{1,0:T(8,128)S(1)}, f32[208,128]{1,0:T(8,128)S(1)}, u32[]{:S(2)}, u32[]{:S(2)}) collective-permute-start(f32[208,128]{1,0:T(8,128)S(1)} %pad_maximum_fusion), channel_id=1, source_target_pairs={{0,8},{8,0},{16,24},{24,16},{1,9},{9,1},{17,25},{25,17},{2,10},{10... | collective-permute-start | bytes 319496 | tf_op jit(solution)/shard_map/ppermute | solution.py:525
  38.2 1.2 %collective-permute-start.5 = (f32[104,128]{1,0:T(8,128)S(1)}, f32[104,128]{1,0:T(8,128)S(1)}, u32[]{:S(2)}, u32[]{:S(2)}) collective-permute-start(f32[104,128]{1,0:T(8,128)S(1)} %get-tuple-element.63), channel_id=1, source_target_pairs={{0,16},{8,24},{16,0},{24,8},{1,17},{9,25},{17,1},{25,9},{2,18},{10... | collective-permute-start | bytes 159752 | tf_op jit(solution)/shard_map/ppermute | solution.py:527
  39.4 3.7 %collective-permute-done.5 = f32[104,128]{1,0:T(8,128)S(1)} collective-permute-done((f32[104,128]{1,0:T(8,128)S(1)}, f32[104,128]{1,0:T(8,128)S(1)}, u32[]{:S(2)}, u32[]{:S(2)}) %collective-permute-start.5) | collective-permute-done | bytes 53280 | tf_op jit(solution)/shard_map/ppermute | solution.py:527
  43.4 1.0 %collective-permute-start.7 = (f32[112,128]{1,0:T(8,128)S(1)}, f32[112,128]{1,0:T(8,128)S(1)}, u32[]{:S(2)}, u32[]{:S(2)}) collective-permute-start(f32[112,128]{1,0:T(8,128)S(1)} %pad_maximum_fusion.2), channel_id=1, source_target_pairs={{0,6},{2,4},{4,2},{6,0},{1,7},{3,5},{5,3},{7,1},{8,14},{10,12},{12... | collective-permute-start | bytes 172040 | tf_op jit(solution)/shard_map/ppermute | solution.py:545
  44.4 3.4 %collective-permute-start.8 = (f32[104,128]{1,0:T(8,128)S(1)}, f32[104,128]{1,0:T(8,128)S(1)}, u32[]{:S(2)}, u32[]{:S(2)}) collective-permute-start(f32[104,128]{1,0:T(8,128)S(1)} %get-tuple-element.61), channel_id=1, source_target_pairs={{0,4},{2,6},{4,0},{6,2},{1,5},{3,7},{5,1},{7,3},{8,12},{10,14},{12... | collective-permute-start | bytes 159752 | tf_op jit(solution)/shard_map/ppermute | solution.py:546
  47.9 2.6 %collective-permute-done.8 = f32[104,128]{1,0:T(8,128)S(1)} collective-permute-done((f32[104,128]{1,0:T(8,128)S(1)}, f32[104,128]{1,0:T(8,128)S(1)}, u32[]{:S(2)}, u32[]{:S(2)}) %collective-permute-start.8) | collective-permute-done | bytes 53280 | tf_op jit(solution)/shard_map/ppermute | solution.py:546
  51.1 1.4 %collective-permute-start.10 = (f32[104,128]{1,0:T(8,128)S(1)}, f32[104,128]{1,0:T(8,128)S(1)}, u32[]{:S(2)}, u32[]{:S(2)}) collective-permute-start(f32[104,128]{1,0:T(8,128)S(1)} %fusion.refs_2_.refs_0_), channel_id=1, source_target_pairs={{0,16},{8,24},{16,0},{24,8},{1,17},{9,25},{17,1},{25,9},{2,18},{10... | collective-permute-start | bytes 159752 | tf_op jit(solution)/shard_map/ppermute | solution.py:570
  52.6 1.5 %collective-permute-start.11 = (f32[104,128]{1,0:T(8,128)S(1)}, f32[104,128]{1,0:T(8,128)S(1)}, u32[]{:S(2)}, u32[]{:S(2)}) collective-permute-start(f32[104,128]{1,0:T(8,128)S(1)} %fusion.refs_2_.refs_0_), channel_id=1, source_target_pairs={{0,24},{8,16},{16,8},{24,0},{1,25},{9,17},{17,9},{25,1},{2,26},{10... | collective-permute-start | bytes 159752 | tf_op jit(solution)/shard_map/ppermute | solution.py:570
  54.1 1.1 %collective-permute-done.9.refs_1_ = f32[104,128]{1,0:T(8,128)S(1)} collective-permute-done((f32[104,128]{1,0:T(8,128)S(1)}, f32[104,128]{1,0:T(8,128)S(1)}, u32[]{:S(2)}, u32[]{:S(2)}) %collective-permute-start.9) | collective-permute-done | bytes 53280 | tf_op jit(solution)/shard_map/ppermute | solution.py:570
  55.7 1.9 %collective-permute-done.11.refs_3_ = f32[104,128]{1,0:T(8,128)S(1)} collective-permute-done((f32[104,128]{1,0:T(8,128)S(1)}, f32[104,128]{1,0:T(8,128)S(1)}, u32[]{:S(2)}, u32[]{:S(2)}) %collective-permute-start.11) | collective-permute-done | bytes 53280 | tf_op jit(solution)/shard_map/ppermute | solution.py:570
  57.6 1.5 %shard_map.131 = f32[800,128]{1,0:T(8,128)} custom-call(f32[32,8,128]{2,1,0:T(8,128)S(1)} %all-to-all-done.refs_0_, f32[1,128]{1,0:T(1,128)S(1)} %get-tuple-element.37.refs_1_, f32[104,128]{1,0:T(8,128)S(1)} %fusion.refs_2_.refs_0_, f32[800,128]{1,0:T(8,128)S(1)} %get-tuple-element.51.refs_3_, f32[800,128]{1,0:T(8,128)S(1)} %get-tuple-element.32.refs_1_.refs_4_, ...), custom_call_target="tpu_custom_call" | custom-call | tf_op jit(solution)/shard_map/pallas_call | solution.py:559
  (46 shorter events, 6.9 us)
Async XLA Ops:
  0.6 1.0 %copy-start.3 = (f32[100,8,128]{2,1,0:T(8,128)S(1)}, f32[100,8,128]{2,1,0:T(8,128)}, u32[]{:S(2)}) copy-start(f32[100,8,128]{2,1,0:T(8,128)} %param.9) | copy-start | bytes 1228804
  1.6 0.7 %copy-start.5 = (s32[8,128]{1,0:T(8,128)S(1)}, s32[8,128]{1,0:T(8,128)}, u32[]{:S(2)}) copy-start(s32[8,128]{1,0:T(8,128)} %refs_1_.1) | copy-start | bytes 12292
  2.3 0.7 %copy-start.6 = (s32[8,128]{1,0:T(8,128)S(1)}, s32[8,128]{1,0:T(8,128)}, u32[]{:S(2)}) copy-start(s32[8,128]{1,0:T(8,128)} %refs_2_.1) | copy-start | bytes 12292
  6.4 11.3 %collective-permute-start.1 = (f32[104,128]{1,0:T(8,128)S(1)}, f32[104,128]{1,0:T(8,128)S(1)}, u32[]{:S(2)}, u32[]{:S(2)}) collective-permute-start(f32[104,128]{1,0:T(8,128)S(1)} %get-tuple-element.41), channel_id=1, source_target_pairs={{8,16},{16,8},{9,17},{17,9},{10,18},{18,10},{11,19},{19,11},{12,20... | collective-permute-start | bytes 159752 | tf_op jit(solution)/shard_map/ppermute | solution.py:467
  7.0 10.6 %collective-permute-start = (f32[104,128]{1,0:T(8,128)S(1)}, f32[104,128]{1,0:T(8,128)S(1)}, u32[]{:S(2)}, u32[]{:S(2)}) collective-permute-start(f32[104,128]{1,0:T(8,128)S(1)} %get-tuple-element.40), channel_id=1, source_target_pairs={{0,8},{8,0},{16,24},{24,16},{1,9},{9,1},{17,25},{25,17},{2,10},{10... | collective-permute-start | bytes 159752 | tf_op jit(solution)/shard_map/ppermute | solution.py:466
  12.8 13.0 %all-to-all-start = ((f32[32,8,128]{2,1,0:T(8,128)}), f32[32,8,128]{2,1,0:T(8,128)S(1)}, u32[]{:S(2)}, u32[]{:S(2)}) async-start(f32[32,8,128]{2,1,0:T(8,128)} %get-tuple-element.31), calls=%async_computation | async-start | bytes 262144 | tf_op jit(solution)/shard_map/all_to_all | solution.py:463
  25.8 0.9 %copy-start = (bf16[512,100]{0,1:T(8,128)(2,1)S(1)}, bf16[512,100]{0,1:T(8,128)(2,1)}, u32[]{:S(2)}) copy-start(bf16[512,100]{0,1:T(8,128)(2,1)} %param.16) | copy-start | bytes 307204
  26.7 0.9 %copy-start.4 = (bf16[100,512]{1,0:T(8,128)(2,1)S(1)}, bf16[100,512]{1,0:T(8,128)(2,1)}, u32[]{:S(2)}) copy-start(bf16[100,512]{1,0:T(8,128)(2,1)} %refs_3_.1) | copy-start | bytes 307204
  29.5 0.9 %copy-start.1 = (bf16[512,100]{0,1:T(8,128)(2,1)S(1)}, bf16[512,100]{0,1:T(8,128)(2,1)}, u32[]{:S(2)}) copy-start(bf16[512,100]{0,1:T(8,128)(2,1)} %param.16) | copy-start | bytes 307204
  30.4 1.0 %copy-start.2 = (f32[100,8,128]{2,1,0:T(8,128)S(1)}, f32[100,8,128]{2,1,0:T(8,128)}, u32[]{:S(2)}) copy-start(f32[100,8,128]{2,1,0:T(8,128)} %param.10) | copy-start | bytes 1228804
  34.1 1.5 %collective-permute-start.2 = (f32[432,128]{1,0:T(8,128)S(1)}, f32[432,128]{1,0:T(8,128)S(1)}, u32[]{:S(2)}, u32[]{:S(2)}) collective-permute-start(f32[432,128]{1,0:T(8,128)S(1)} %get-tuple-element.48), channel_id=1, source_target_pairs={{0,1},{1,0},{2,3},{3,2},{4,5},{5,4},{6,7},{7,6},{8,9},{9,8},{10,11... | collective-permute-start | bytes 663560 | tf_op jit(solution)/shard_map/ppermute | solution.py:519
  35.7 7.3 %collective-permute-start.4 = (f32[208,128]{1,0:T(8,128)S(1)}, f32[208,128]{1,0:T(8,128)S(1)}, u32[]{:S(2)}, u32[]{:S(2)}) collective-permute-start(f32[208,128]{1,0:T(8,128)S(1)} %pad_maximum_fusion.1), channel_id=1, source_target_pairs={{0,24},{8,16},{16,8},{24,0},{1,25},{9,17},{17,9},{25,1},{2,26},{10... | collective-permute-start | bytes 319496 | tf_op jit(solution)/shard_map/ppermute | solution.py:526
  36.8 6.6 %collective-permute-start.3 = (f32[208,128]{1,0:T(8,128)S(1)}, f32[208,128]{1,0:T(8,128)S(1)}, u32[]{:S(2)}, u32[]{:S(2)}) collective-permute-start(f32[208,128]{1,0:T(8,128)S(1)} %pad_maximum_fusion), channel_id=1, source_target_pairs={{0,8},{8,0},{16,24},{24,16},{1,9},{9,1},{17,25},{25,17},{2,10},{10... | collective-permute-start | bytes 319496 | tf_op jit(solution)/shard_map/ppermute | solution.py:525
  38.2 4.9 %collective-permute-start.5 = (f32[104,128]{1,0:T(8,128)S(1)}, f32[104,128]{1,0:T(8,128)S(1)}, u32[]{:S(2)}, u32[]{:S(2)}) collective-permute-start(f32[104,128]{1,0:T(8,128)S(1)} %get-tuple-element.63), channel_id=1, source_target_pairs={{0,16},{8,24},{16,0},{24,8},{1,17},{9,25},{17,1},{25,9},{2,18},{10... | collective-permute-start | bytes 159752 | tf_op jit(solution)/shard_map/ppermute | solution.py:527
  43.4 7.1 %collective-permute-start.7 = (f32[112,128]{1,0:T(8,128)S(1)}, f32[112,128]{1,0:T(8,128)S(1)}, u32[]{:S(2)}, u32[]{:S(2)}) collective-permute-start(f32[112,128]{1,0:T(8,128)S(1)} %pad_maximum_fusion.2), channel_id=1, source_target_pairs={{0,6},{2,4},{4,2},{6,0},{1,7},{3,5},{5,3},{7,1},{8,14},{10,12},{12... | collective-permute-start | bytes 172040 | tf_op jit(solution)/shard_map/ppermute | solution.py:545
  44.4 6.1 %collective-permute-start.6 = (f32[112,128]{1,0:T(8,128)S(1)}, f32[112,128]{1,0:T(8,128)S(1)}, u32[]{:S(2)}, u32[]{:S(2)}) collective-permute-start(f32[112,128]{1,0:T(8,128)S(1)} %pad_maximum_fusion.2), channel_id=1, source_target_pairs={{0,2},{2,0},{4,6},{6,4},{1,3},{3,1},{5,7},{7,5},{8,10},{10,8},{12,... | collective-permute-start | bytes 172040 | tf_op jit(solution)/shard_map/ppermute | solution.py:544
  44.4 6.1 %collective-permute-start.8 = (f32[104,128]{1,0:T(8,128)S(1)}, f32[104,128]{1,0:T(8,128)S(1)}, u32[]{:S(2)}, u32[]{:S(2)}) collective-permute-start(f32[104,128]{1,0:T(8,128)S(1)} %get-tuple-element.61), channel_id=1, source_target_pairs={{0,4},{2,6},{4,0},{6,2},{1,5},{3,7},{5,1},{7,3},{8,12},{10,14},{12... | collective-permute-start | bytes 159752 | tf_op jit(solution)/shard_map/ppermute | solution.py:546
  50.5 4.7 %collective-permute-start.9 = (f32[104,128]{1,0:T(8,128)S(1)}, f32[104,128]{1,0:T(8,128)S(1)}, u32[]{:S(2)}, u32[]{:S(2)}) collective-permute-start(f32[104,128]{1,0:T(8,128)S(1)} %fusion.refs_2_.refs_0_), channel_id=1, source_target_pairs={{0,8},{8,0},{16,24},{24,16},{1,9},{9,1},{17,25},{25,17},{2,10},{10... | collective-permute-start | bytes 159752 | tf_op jit(solution)/shard_map/ppermute | solution.py:570
  51.1 4.2 %collective-permute-start.10 = (f32[104,128]{1,0:T(8,128)S(1)}, f32[104,128]{1,0:T(8,128)S(1)}, u32[]{:S(2)}, u32[]{:S(2)}) collective-permute-start(f32[104,128]{1,0:T(8,128)S(1)} %fusion.refs_2_.refs_0_), channel_id=1, source_target_pairs={{0,16},{8,24},{16,0},{24,8},{1,17},{9,25},{17,1},{25,9},{2,18},{10... | collective-permute-start | bytes 159752 | tf_op jit(solution)/shard_map/ppermute | solution.py:570
  52.6 5.0 %collective-permute-start.11 = (f32[104,128]{1,0:T(8,128)S(1)}, f32[104,128]{1,0:T(8,128)S(1)}, u32[]{:S(2)}, u32[]{:S(2)}) collective-permute-start(f32[104,128]{1,0:T(8,128)S(1)} %fusion.refs_2_.refs_0_), channel_id=1, source_target_pairs={{0,24},{8,16},{16,8},{24,0},{1,25},{9,17},{17,9},{25,1},{2,26},{10... | collective-permute-start | bytes 159752 | tf_op jit(solution)/shard_map/ppermute | solution.py:570
  54.1 5.1 %collective-permute-start.12 = (f32[104,128]{1,0:T(8,128)S(1)}, f32[104,128]{1,0:T(8,128)S(1)}, u32[]{:S(2)}, u32[]{:S(2)}) collective-permute-start(f32[104,128]{1,0:T(8,128)S(1)} %fusion.refs_2_.refs_0_), channel_id=1, source_target_pairs={{0,1},{1,0},{2,3},{3,2},{4,5},{5,4},{6,7},{7,6},{8,9},{9,8},{10,11... | collective-permute-start | bytes 159752 | tf_op jit(solution)/shard_map/ppermute | solution.py:571
  55.2 4.0 %collective-permute-start.13 = (f32[104,128]{1,0:T(8,128)S(1)}, f32[104,128]{1,0:T(8,128)S(1)}, u32[]{:S(2)}, u32[]{:S(2)}) collective-permute-start(f32[104,128]{1,0:T(8,128)S(1)} %collective-permute-done.9.refs_1_), channel_id=1, source_target_pairs={{0,1},{1,0},{2,3},{3,2},{4,5},{5,4},{6,7},{7,6},{8,9},{9,8},{10,11... | collective-permute-start | bytes 159752 | tf_op jit(solution)/shard_map/ppermute | solution.py:571
  55.3 3.8 %collective-permute-start.14 = (f32[104,128]{1,0:T(8,128)S(1)}, f32[104,128]{1,0:T(8,128)S(1)}, u32[]{:S(2)}, u32[]{:S(2)}) collective-permute-start(f32[104,128]{1,0:T(8,128)S(1)} %collective-permute-done.10.refs_2_), channel_id=1, source_target_pairs={{0,1},{1,0},{2,3},{3,2},{4,5},{5,4},{6,7},{7,6},{8,9},{9,8},{10,11... | collective-permute-start | bytes 159752 | tf_op jit(solution)/shard_map/ppermute | solution.py:571
  57.6 1.6 %collective-permute-start.15 = (f32[104,128]{1,0:T(8,128)S(1)}, f32[104,128]{1,0:T(8,128)S(1)}, u32[]{:S(2)}, u32[]{:S(2)}) collective-permute-start(f32[104,128]{1,0:T(8,128)S(1)} %collective-permute-done.11.refs_3_), channel_id=1, source_target_pairs={{0,1},{1,0},{2,3},{3,2},{4,5},{5,4},{6,7},{7,6},{8,9},{9,8},{10,11... | collective-permute-start | bytes 159752 | tf_op jit(solution)/shard_map/ppermute | solution.py:571
  (3 other events, 2.0 us)

commit v3 on v2

--- a/solution.py
+++ b/solution.py
@@ -39,11 +39,11 @@
     return jnp.sum(pad_ref[...].T, axis=0, keepdims=True)
 
 
-def write_edges(field_ref, levels, rows, pad_ref, outs, odd, depth=None):
-    lat_a, lat_b, lon_a, lon_b = outs
-    lat_odd, lon_odd = odd
+ahead = pl.CostEstimate(flops=10**9, bytes_accessed=10**8, transcendentals=0)
+
+
+def write_lat_edges(field_ref, levels, rows, lat_a, lat_b, lat_odd, depth=None):
     cols = field_ref.shape[1]
-    lanes = lane_ids((levels, cols))
     first = row_of(field_ref, 0, levels, rows)
     last = row_of(field_ref, rows - 1, levels, rows)
     tail = (lat_a.shape[0] - levels, cols)
@@ -55,6 +55,11 @@
     lat_b[0:levels, :] = jnp.where(lat_odd, last, first)
     lat_a[levels:, :] = jnp.where(lat_odd, first_tail, last_tail)
     lat_b[levels:, :] = jnp.where(lat_odd, last_tail, first_tail)
+
+
+def write_lon_edges(field_ref, levels, rows, pad_ref, lon_a, lon_b, lon_odd, depth=None):
+    cols = field_ref.shape[1]
+    lanes = lane_ids((levels, cols))
     low = jnp.zeros((levels, cols), f32)
     high = jnp.zeros((levels, cols), f32)
     for row in range(rows):
@@ -116,9 +121,11 @@
 
 
 def halo_depths(levels, north, south, west, east, shape):
+    place = lax.axis_index("lat")
+    last = lax.axis_size("lat") - 1
     return (
-        north[levels : levels + 1, :],
-        south[levels : levels + 1, :],
+        jnp.where(place == 0, 0.0, north[levels : levels + 1, :]),
+        jnp.where(place == last, 0.0, south[levels : levels + 1, :]),
         jnp.broadcast_to(west[...][:, levels : levels + 1], shape),
         jnp.broadcast_to(east[...][:, levels : levels + 1], shape),
     )
@@ -128,34 +135,12 @@
     return (lax.axis_index("lat") % 2 == 1, lax.axis_index("core") == 1)
 
 
-def lon_neighbours():
-    lons = lax.axis_size("z") * lax.axis_size("core")
-    lon = lax.axis_index("z") * lax.axis_size("core") + lax.axis_index("core")
-    base = lax.axis_index("lat") * lons
-    return base + (lon + lons - 1) % lons, base + (lon + 1) % lons
-
-
-def energy_slots(levels, rows, lanes):
-    per = -(-levels // rows)
-    assert levels + 1 + per <= lanes
-    return [(row, row * per, levels + 1, per) for row in range(rows)]
-
-
-def energy_kernel(
-    levels, tracer_hbm, mask_hbm, bottom_hbm, b_in_hbm, b_out_hbm, kappa_hbm,
-    rows_out, lat_a, lat_b, tracer, depth_out, b_in, b_out, kappa,
-    mask, bottom, lon_a, lon_b, pad, sems,
-):
+def zero_kernel(out):
+    out[...] = jnp.zeros(out.shape, f32)
+
+
+def energy_kernel(levels, zero, tracer, mask, bottom, small, lat_a, lat_b, depth_out, pad):
     rows, cols = mask.shape
-    pairs = (
-        (mask_hbm, mask), (bottom_hbm, bottom), (tracer_hbm, tracer),
-        (b_in_hbm, b_in), (b_out_hbm, b_out), (kappa_hbm, kappa),
-    )
-    copies = [pltpu.make_async_copy(src, dst, sems.at[i]) for i, (src, dst) in enumerate(pairs)]
-    for copy in copies:
-        copy.start()
-    for copy in copies[:3]:
-        copy.wait()
     depth = (mask[...] * bottom[...]).astype(f32)
     depth_out[...] = depth
     lev = level_ids((levels, cols))
@@ -163,36 +148,22 @@
     for row in range(rows):
         wet_tracer = jnp.where(lev < depth[row : row + 1, :], row_of(tracer, row, levels, rows), 0.0)
         total = total + wet_tracer * wet_tracer
-    sums = jnp.broadcast_to(lane_sums(pad, total), lon_a.shape)
-    odd = odd_places()
-    write_edges(tracer, levels, rows, pad, (lat_a, lat_b, lon_a, lon_b), odd, depth)
-    shape = lon_a.shape
-    sub = lax.broadcasted_iota(jnp.int32, shape, 0)
-    lanes = lane_ids(shape)
-    packed = jnp.zeros(shape, f32)
-    for row, source, target, count in energy_slots(levels, rows, shape[1]):
-        here = (sub == row) & (lanes >= target) & (lanes < target + count)
-        packed = jnp.where(here, pltpu.roll(sums, (target - source) % shape[1], 1), packed)
-    rows_out[...] = jnp.broadcast_to(packed[None], rows_out.shape)
-    facing = jnp.where(lanes <= levels, lon_a[...], packed)
-    outer = jnp.where(lanes <= levels, lon_b[...], packed)
-    west, east = lon_neighbours()
-    rows_out[west] = jnp.where(odd[1], facing, outer)
-    rows_out[east] = jnp.where(odd[1], outer, facing)
-    for copy in copies[3:]:
-        copy.wait()
-
-
-def energy_total(gathered, levels):
-    total = jnp.sum(gathered[...], axis=0)
-    rows, width = total.shape
-    sub = lax.broadcasted_iota(jnp.int32, total.shape, 0)
-    lanes = lane_ids(total.shape)
-    out = jnp.zeros(total.shape, f32)
-    for row, source, target, count in energy_slots(levels, rows, width):
-        here = (sub == row) & (lanes >= source) & (lanes < min(source + count, levels))
-        out = jnp.where(here, pltpu.roll(total, (source - target) % width, 1), out)
-    return jnp.sum(out, axis=0, keepdims=True)
+    small[2 * rows :, :] = zero[...] + lane_sums(pad, total)
+    lat_odd, lon_odd = odd_places()
+    lon_a, lon_b = small.at[0:rows, :], small.at[rows : 2 * rows, :]
+    write_lon_edges(tracer, levels, rows, pad, lon_a, lon_b, lon_odd, depth)
+    write_lat_edges(tracer, levels, rows, lat_a, lat_b, lat_odd, depth)
+
+
+def mix_kernel(levels, tracer, depth_ref, north, south, mixed):
+    rows, cols = depth_ref.shape
+    depth = depth_ref[...]
+    blank = jnp.zeros((levels, cols), f32)
+    dry = jnp.zeros((rows, cols), f32)
+    halos = (north[0:levels, :], south[0:levels, :], blank, blank)
+    depths = halo_depths(levels, north, south, dry, dry, dry.shape)[0:2] + (dry, dry)
+    for row, _, _, value in spread_rows(tracer, depth, levels, rows, halos, depths):
+        mixed[pl.ds(row, levels, stride=rows), :] = value
 
 
 def columns_of(row, lanes):
@@ -200,8 +171,8 @@
 
 
 def network_kernel(
-    levels, column_count, gathered, tracer, depth_ref, w_in, b_in, w_out_t, b_out, kappa,
-    radius_row, x_b, wi_b, hidden, slope, gate, up_out, down_out,
+    levels, column_count, energy, tracer, depth_ref, w_in, b_in, w_out_t, b_out, kappa, inner, west_ref, east_ref,
+    radius_row, x_b, wi_b, hidden, slope, gate, up_out, down_out, mixed,
     pad, x_f, wi_f, wo_f,
 ):
     rows, cols = depth_ref.shape
@@ -210,7 +181,7 @@
     pad_levels = x_f.shape[0]
     depth = depth_ref[...]
     lev = level_ids((levels, cols))
-    radius_line = jnp.sqrt(energy_total(gathered, levels) / column_count + level_eps)
+    radius_line = jnp.sqrt(energy[0:1, :] / column_count + level_eps)
     radius_row[...] = radius_line
     radius = columns_of(radius_line, cols)[0:levels, :]
     scale = 1.0 / radius
@@ -260,12 +231,33 @@
         up_out[at, :] = jnp.where(open_face, kappa_col, 0.0)
         down_out[at, :] = jnp.where(open_face, kappa_col + sinking, 0.0)
 
+    lanes = lane_ids((levels, cols))
+    west, east = west_ref[...], east_ref[...]
+    west_cols, east_cols = turn(west, levels), turn(east, levels)
+    for row in range(rows):
+        near = jnp.where(
+            lanes == 0,
+            pltpu.roll(west_cols, (cols - row) % cols, 1) if row else west_cols,
+            pltpu.roll(east_cols, cols - 1 - row, 1),
+        )
+        level_depth = depth[row : row + 1, :]
+        level_depth = jnp.minimum(
+            level_depth,
+            jnp.where(
+                lanes[0:1, :] == 0, jnp.broadcast_to(west[row : row + 1, levels : levels + 1], (1, cols)),
+                jnp.broadcast_to(east[row : row + 1, levels : levels + 1], (1, cols)),
+            ),
+        )
+        both = (lev < level_depth) & ((lanes == 0) | (lanes == cols - 1))
+        flux = jnp.where(both, near - row_of(tracer, row, levels, rows), 0.0)
+        mixed[pl.ds(row, levels, stride=rows), :] = row_of(inner, row, levels, rows) + spread_coef * flux
+
 
 def solve_kernel(
     levels, scale,
-    gathered, tracer, cotangent, depth_ref, up_ref, down_ref, north, south, w_out_t, wi_b, x_b, hidden, slope, gate,
+    tracer, cotangent, depth_ref, up_ref, down_ref, mixed, w_out_t, wi_b, x_b, hidden, slope, gate,
     keep, send, adjoint, lat_a, lat_b, d_inputs,
-    pad, wo_f, dl_f, dl_b, dp_b, mixed, rate_a, rate_b, inv_p, fwd_z, fwd_u, flow,
+    pad, wo_f, dl_f, dl_b, dp_b, rate_a, rate_b, inv_p, fwd_z, fwd_u, flow,
 ):
     rows, cols = depth_ref.shape
     hid = w_out_t.shape[1]
@@ -273,13 +265,6 @@
     pad_levels = dl_f.shape[0]
     depth = depth_ref[...]
     lev = level_ids((levels, cols))
-    west_at, east_at = lon_neighbours()
-    west, east = gathered.at[west_at], gathered.at[east_at]
-    halos = halo_values(levels, north, south, west, east)
-    depth_halos = halo_depths(levels, north, south, west, east, depth.shape)
-    for row, _, _, value in spread_rows(tracer, depth, levels, rows, halos, depth_halos):
-        mixed[pl.ds(row, levels, stride=rows), :] = value
-
     def at_level(k):
         return slice(k * rows, (k + 1) * rows)
 
@@ -359,12 +344,13 @@
         lower[levels + 2 : levels + 3, :] = bout_row
     lon_a = send.at[4 * height : 4 * height + rows, :]
     lon_b = send.at[4 * height + rows : 4 * height + 2 * rows, :]
-    write_edges(adjoint, levels, rows, pad, (lat_a, lat_b, lon_a, lon_b), (lat_odd, lon_odd))
+    write_lat_edges(adjoint, levels, rows, lat_a, lat_b, lat_odd)
+    write_lon_edges(adjoint, levels, rows, pad, lon_a, lon_b, lon_odd)
 
 
 def final_kernel(
-    levels, column_count, gathered, radius_row, level_total, adjoint, tracer, d_inputs, depth_ref,
-    north, south, west, east, t_north, t_south, out,
+    levels, column_count, radius_row, level_total, adjoint, tracer, d_inputs, depth_ref,
+    north, south, west, east, t_north, t_south, t_west, t_east, out,
 ):
     rows, cols = depth_ref.shape
     depth = depth_ref[...]
@@ -373,11 +359,8 @@
     pull = level_sum / (column_count * (radius_line * radius_line * radius_line))
     radius = columns_of(radius_line, cols)[0:levels, :]
     pull = columns_of(pull, cols)[0:levels, :]
-    west_at, east_at = lon_neighbours()
     halos = halo_values(levels, north, south, west, east)
-    depth_halos = halo_depths(
-        levels, t_north, t_south, gathered.at[west_at], gathered.at[east_at], depth.shape
-    )
+    depth_halos = halo_depths(levels, t_north, t_south, t_west, t_east, depth.shape)
     scale = 1.0 / radius
     for row, _, wet, value in spread_rows(adjoint, depth, levels, rows, halos, depth_halos):
         wet_tracer = wet * row_of(tracer, row, levels, rows)
@@ -386,19 +369,16 @@
 
 
 def gather_kernel(levels, *refs):
-    mine, other = refs[0:4], refs[4:8]
-    grad_in, grad_bin, grad_out, grad_bout = refs[8:]
-    lon_odd = lax.axis_index("core") == 1
+    pairs = refs[0:4]
+    grad_in, grad_bin, grad_out, grad_bout = refs[4:]
     quarter = lax.axis_index("lat") % 4
-    block = mine[0].shape[1]
+    height, block = pairs[0].shape[0] // 2, pairs[0].shape[1]
     for step in range(4):
         at = pl.ds(pl.multiple_of((step ^ quarter) * block, block), block)
-        inner = jnp.where(lon_odd, other[step][...], mine[step][...])
-        outer = jnp.where(lon_odd, mine[step][...], other[step][...])
-        grad_in[:, at] = inner[0:levels, :]
-        grad_bin[:, at] = inner[levels : levels + 1, :]
-        grad_out[:, at] = outer[0:levels, :]
-    grad_bout[...] = mine[0][levels + 2 : levels + 3, 0:levels]
+        grad_in[:, at] = pairs[step][0:levels, :]
+        grad_bin[:, at] = pairs[step][levels : levels + 1, :]
+        grad_out[:, at] = pairs[step][height : height + levels, :]
+    grad_bout[...] = pairs[0][levels + 2 : levels + 3, 0:levels]
 
 
 def flip(count, by):
@@ -416,13 +396,20 @@
     return jnp.where(odd, near, far), jnp.where(odd, far, near)
 
 
+def swap_lat(lat_odd, lats, lat_a, lat_b):
+    return in_order(
+        lat_odd,
+        lax.ppermute(lat_a, "lat", flip(lats, 1)),
+        lax.ppermute(lat_b, "lat", far_pairs(lats, False)),
+    )
+
+
 def shards(tracer, cotangent, land_mask, bottom, kappa, w_in, b_in, w_out, b_out):
     levels, rows, cols = tracer.shape
     hid = w_in.shape[1]
     lats, chips = lax.axis_size("lat"), lax.axis_size("z")
     lons = 2 * chips
-    devices = lats * lons
-    column_count = rows * cols * devices
+    column_count = rows * cols * lats * lons
     pad_levels = round_up(levels + 3, 128)
     height = round_up(levels + 3, 8)
     flat = (levels * rows, cols)
@@ -433,41 +420,66 @@
     sds = jax.ShapeDtypeStruct
     lat_edge = sds((height, cols), f32)
     pad = pltpu.VMEM((pad_levels, cols), f32)
-    lon_edge = pltpu.VMEM((rows, pad_levels), f32)
     lat_odd, lon_odd = odd_places()
-
-    gathered, lat_a, lat_b, tracer, depth, b_in, b_out, kappa = pl.pallas_call(
+    from_near = (lax.axis_index("z") + lax.axis_index("core")) % 2 == 1
+    b_in = b_in.reshape(1, hid)
+    b_out = b_out.reshape(1, levels)
+    kappa = kappa.reshape(1, levels)
+
+    zero = pl.pallas_call(
+        zero_kernel,
+        out_shape=sds((rows, pad_levels), f32),
+        out_specs=vmem,
+        cost_estimate=ahead,
+    )()
+    small, lat_a, lat_b, depth = pl.pallas_call(
         lambda *refs: energy_kernel(levels, *refs),
         out_shape=[
-            sds((devices, rows, pad_levels), f32),
+            sds((3 * rows, pad_levels), f32),
             lat_edge,
             lat_edge,
-            sds(flat, f32),
             sds((rows, cols), f32),
-            sds((1, hid), f32),
-            sds((1, levels), f32),
-            sds((1, levels), f32),
         ],
-        in_specs=[hbm] * 6,
-        out_specs=[vmem] * 8,
-        scratch_shapes=[
-            pltpu.VMEM((rows, cols), jnp.int32),
-            pltpu.VMEM((rows, cols), jnp.int32),
-            lon_edge,
-            lon_edge,
-            pad,
-            pltpu.SemaphoreType.DMA((6,)),
-        ],
+        in_specs=[vmem] * 4,
+        out_specs=[vmem] * 4,
+        scratch_shapes=[pad],
         compiler_params=params,
-    )(tracer, land_mask, bottom, b_in.reshape(1, hid), b_out.reshape(1, levels), kappa.reshape(1, levels))
-    gathered = lax.all_to_all(gathered, ("lat", "z", "core"), 0, 0, tiled=True)
-    t_north, t_south = in_order(
-        lat_odd,
-        lax.ppermute(lat_a, "lat", flip(lats, 1)),
-        lax.ppermute(lat_b, "lat", far_pairs(lats, False)),
-    )
-
-    radius_row, x_b, wi_b, hidden, slope, gate, up, down = pl.pallas_call(
+        cost_estimate=ahead,
+    )(zero, tracer, land_mask, bottom)
+    got = lax.ppermute(small, "core", flip(2, 1))
+    energy = small[2 * rows :] + got[2 * rows :]
+    t_near, t_pass = got[:rows], got[rows : 2 * rows]
+    if lats == 4:
+        near = lax.ppermute(jnp.concatenate([lat_a, energy], 0), "lat", flip(lats, 1))
+        far = lax.ppermute(jnp.concatenate([lat_b, energy], 0), "lat", flip(lats, 3))
+        cross = lax.ppermute(energy, "lat", flip(lats, 2))
+        t_north, t_south = in_order(lat_odd, near[:height], far[:height])
+        energy = energy + near[height:] + far[height:] + cross
+    else:
+        t_north, t_south = swap_lat(lat_odd, lats, lat_a, lat_b)
+        energy = lax.psum(energy, "lat")
+    if chips == 4:
+        packed = jnp.concatenate([energy, t_pass], 0)
+        near = lax.ppermute(packed, "z", flip(chips, 1))
+        far = lax.ppermute(packed, "z", flip(chips, 3))
+        cross = lax.ppermute(energy, "z", flip(chips, 2))
+        energy = energy + near[:rows] + far[:rows] + cross
+        t_far = jnp.where(from_near, near[rows:], far[rows:])
+    else:
+        energy = lax.psum(energy, "z")
+        t_far = lax.ppermute(small[rows : 2 * rows], ("z", "core"), far_pairs(lons, True))
+    t_west, t_east = in_order(lon_odd, t_near, t_far)
+
+    inner = pl.pallas_call(
+        lambda *refs: mix_kernel(levels, *refs),
+        out_shape=sds(flat, f32),
+        in_specs=[vmem] * 4,
+        out_specs=vmem,
+        compiler_params=params,
+        cost_estimate=ahead,
+    )(tracer, depth, t_north, t_south)
+
+    radius_row, x_b, wi_b, hidden, slope, gate, up, down, mixed = pl.pallas_call(
         lambda *refs: network_kernel(levels, column_count, *refs),
         out_shape=[
             sds((1, pad_levels), f32),
@@ -478,9 +490,10 @@
             sds((pad_levels, span), f32),
             sds(flat, f32),
             sds(flat, f32),
+            sds(flat, f32),
         ],
-        in_specs=[vmem] * 8,
-        out_specs=[vmem] * 8,
+        in_specs=[vmem] * 11,
+        out_specs=[vmem] * 9,
         scratch_shapes=[
             pad,
             pltpu.VMEM((pad_levels, span), f32),
@@ -488,7 +501,7 @@
             pltpu.VMEM((pad_levels, hid), f32),
         ],
         compiler_params=params,
-    )(gathered, tracer, depth, w_in, b_in, w_out_t, b_out, kappa)
+    )(energy, tracer, depth, w_in, b_in, w_out_t, b_out, kappa, inner, t_west, t_east)
 
     keep, send, adjoint, lat_a, lat_b, d_inputs = pl.pallas_call(
         lambda *refs: solve_kernel(levels, 1.0 / math.sqrt(column_count), *refs),
@@ -500,7 +513,7 @@
             lat_edge,
             sds((rows, height, cols), f32),
         ],
-        in_specs=[vmem] * 14,
+        in_specs=[vmem] * 12,
         out_specs=[vmem] * 6,
         scratch_shapes=[
             pad,
@@ -508,44 +521,32 @@
             pltpu.VMEM((pad_levels, span), f32),
             pltpu.VMEM((pad_levels, span), bf16),
             pltpu.VMEM((hid, span), bf16),
-            *[pltpu.VMEM(flat, f32)] * 7,
+            *[pltpu.VMEM(flat, f32)] * 6,
         ],
         compiler_params=params,
     )(
-        gathered, tracer, cotangent, depth, up, down, t_north, t_south,
-        w_out_t, wi_b, x_b, hidden, slope, gate,
+        tracer, cotangent, depth, up, down, mixed, w_out_t,
+        wi_b, x_b, hidden, slope, gate,
     )
 
     got = lax.ppermute(send, "core", flip(2, 1))
+    north, south = swap_lat(lat_odd, lats, lat_a, lat_b)
     chip = keep + got[: 4 * height].reshape(keep.shape)
     lon_near = got[4 * height : 4 * height + rows]
     lon_pass = got[4 * height + rows :]
     part = chip[0]
-    if lats == 4:
-        near = lax.ppermute(jnp.concatenate([chip[1], lat_a], 0), "lat", flip(lats, 1))
-        far = lax.ppermute(jnp.concatenate([chip[3], lat_b], 0), "lat", flip(lats, 3))
-        cross = lax.ppermute(chip[2], "lat", flip(lats, 2))
-        part = part + near[:height] + far[:height] + cross
-        north, south = in_order(lat_odd, near[height:], far[height:])
-    else:
-        for step in range(1, 4):
-            part = part + lax.ppermute(chip[step], "lat", flip(lats, step))
-        step = 4
-        while step < lats:
-            part = part + lax.ppermute(part, "lat", flip(lats, step))
-            step *= 2
-        north, south = in_order(
-            lat_odd,
-            lax.ppermute(lat_a, "lat", flip(lats, 1)),
-            lax.ppermute(lat_b, "lat", far_pairs(lats, False)),
-        )
+    for step in range(1, 4):
+        part = part + lax.ppermute(chip[step], "lat", flip(lats, step))
+    step = 4
+    while step < lats:
+        part = part + lax.ppermute(part, "lat", flip(lats, step))
+        step *= 2
     if chips == 4:
         packed = jnp.concatenate([part, lon_pass], 0)
         near = lax.ppermute(packed, "z", flip(chips, 1))
         far = lax.ppermute(packed, "z", flip(chips, 3))
         cross = lax.ppermute(part, "z", flip(chips, 2))
         part = part + near[:height] + far[:height] + cross
-        from_near = (lax.axis_index("z") + lax.axis_index("core")) % 2 == 1
         lon_far = jnp.where(from_near, near[height:], far[height:])
     else:
         step = 1
@@ -554,21 +555,22 @@
             step *= 2
         lon_b = send[4 * height + rows :]
         lon_far = lax.ppermute(lon_b, ("z", "core"), far_pairs(lons, True))
+
     west, east = in_order(lon_odd, lon_near, lon_far)
-
     tracer_adjoint = pl.pallas_call(
         lambda *refs: final_kernel(levels, column_count, *refs),
         out_shape=sds(flat, f32),
-        in_specs=[vmem] * 13,
+        in_specs=[vmem] * 14,
         out_specs=vmem,
         compiler_params=params,
     )(
-        gathered, radius_row, part, adjoint, tracer, d_inputs, depth,
-        north, south, west, east, t_north, t_south,
+        radius_row, part, adjoint, tracer, d_inputs, depth,
+        north, south, west, east, t_north, t_south, t_west, t_east,
     )
 
-    mine = [part] + [lax.ppermute(part, "lat", flip(lats, step)) for step in range(1, 4)]
-    other = [lax.ppermute(piece, "core", flip(2, 1)) for piece in mine]
+    other = lax.ppermute(part, "core", flip(2, 1))
+    pair = jnp.concatenate([jnp.where(lon_odd, other, part), jnp.where(lon_odd, part, other)], 0)
+    pairs = [pair] + [lax.ppermute(pair, "lat", flip(lats, step)) for step in (3, 2, 1)][::-1]
     grad_w_in, grad_b_in, grad_w_out_t, grad_b_out = pl.pallas_call(
         lambda *refs: gather_kernel(levels, *refs),
         out_shape=[
@@ -577,10 +579,10 @@
             sds((levels, hid), f32),
             sds((1, levels), f32),
         ],
-        in_specs=[vmem] * 8,
+        in_specs=[vmem] * 4,
         out_specs=[vmem] * 4,
         compiler_params=params,
-    )(*mine, *other)
+    )(*pairs)
     return (
         tracer_adjoint.reshape(levels, rows, cols),
         grad_w_in,

time: 60.5 us -> 54.4 us (0.90)
  local copies, waits for them, and re-layouts: 8.07 us -> 1.17 us
  starting transfers between devices: 23.6 us -> 24.8 us
    all_to_all x1 -> x0, waiting for transfers between devices: 8.12 us -> none  [shards(): gathered = lax.all_to_all(gathered, ('lat', 'z', 'core'), 0, 0, tiled=True)]
    unnamed x20, local copies, waits for them, and re-layouts: 8.04 us -> 1.14 us
    ppermute x12 -> x14, waiting for transfers between devices: 7.17 us -> 12.4 us  [the longest x3 3.67 us: shards(): part = part + lax.ppermute(chip[step], 'lat', flip(lats, step))]
    all_to_all x1 -> x0, starting transfers between devices: 4.84 us -> none  [shards(): gathered = lax.all_to_all(gathered, ('lat', 'z', 'core'), 0, 0, tiled=True)]
    ppermute x12 -> x14, starting transfers between devices: 13.9 us -> 18.7 us  [the longest x3 6.23 us: shards(): lax.ppermute(pair, 'lat', flip(lats, step))]
    ppermute x1 -> x2, waiting for transfers between devices: 0.01 us -> 3.43 us  [shards(): far = lax.ppermute(packed, 'z', flip(chips, 3))]
    ppermute x1 -> x2, starting transfers between devices: 1 us -> 3.43 us  [shards(): far = lax.ppermute(packed, 'z', flip(chips, 3))]
    ppermute x1, starting transfers between devices: 3.43 us -> 2.37 us  [shards(): cross = lax.ppermute(part, 'z', flip(chips, 2))]
  transfers between devices with their start and end apart: 17 -> 20, of which waited for: 8 -> 13; matrix products, arithmetic and copies ran while one was open for 0% -> 0% of each run, Pallas kernels for 3% -> 4%
where the time goes in v3:
time: 54.4 us; the launch traced here: 54.2 us
  starting transfers between devices  24.8 us (46%)
  waiting for transfers between devices  19 us (35%)
  Pallas kernels  8.16 us (15%)
  local copies, waits for them, and re-layouts  1.17 us (2%)
  between operations  0.88 us (2%)
    ppermute x3, starting transfers between devices, shards(): lax.ppermute(pair, 'lat', flip(lats, step))  6.23 us
    ppermute x3, waiting for transfers between devices, shards(): part = part + lax.ppermute(chip[step], 'lat', flip(lats, step))  3.67 us
    ppermute x1, waiting for transfers between devices, shards(): cross = lax.ppermute(energy, 'lat', flip(lats, 2))  3.58 us
    ppermute x3, starting transfers between devices, shards(): part = part + lax.ppermute(chip[step], 'lat', flip(lats, step))  3.55 us
    ppermute x2, starting transfers between devices, shards(): far = lax.ppermute(packed, 'z', flip(chips, 3))  3.43 us
    ppermute x2, waiting for transfers between devices, shards(): far = lax.ppermute(packed, 'z', flip(chips, 3))  3.43 us
    ppermute x3, waiting for transfers between devices, shards(): lax.ppermute(pair, 'lat', flip(lats, step))  3.12 us
    ppermute x1, starting transfers between devices, shards(): lax.ppermute(jnp.concatenate([lat_a, energy], 0), 'lat', flip(lats, 1))  2.9 us
  transfers between devices with their start and end apart: 20, of which 13 were waited for; matrix products, arithmetic and copies ran while one was open for 0% of the time, Pallas kernels for 4%

profile of v3, /device:TPU:0, one launch (start us, length us, event | category | flops | bytes accessed | tf_op | source)
XLA Modules:
  0.0 54.2 jit_solution(12750372701757631602)
XLA Ops:
  3.2 0.8 %collective-permute-done = f32[24,128]{1,0:T(8,128)S(1)} collective-permute-done((f32[24,128]{1,0:T(8,128)S(1)}, f32[24,128]{1,0:T(8,128)S(1)}, u32[]{:S(2)}, u32[]{:S(2)}) %collective-permute-start) | collective-permute-done | bytes 12320 | tf_op jit(solution)/shard_map/ppermute | solution.py:449
  4.1 2.9 %collective-permute-start.1 = (f32[112,128]{1,0:T(8,128)S(1)}, f32[112,128]{1,0:T(8,128)S(1)}, u32[]{:S(2)}, u32[]{:S(2)}) collective-permute-start(f32[112,128]{1,0:T(8,128)S(1)} %get-tuple-element.67), channel_id=1, source_target_pairs={{0,8},{8,0},{16,24},{24,16},{1,9},{9,1},{17,25},{25,17},{2,10},{10... | collective-permute-start | bytes 172040 | tf_op jit(solution)/shard_map/ppermute | solution.py:453
  7.0 1.5 %collective-permute-start.2 = (f32[112,128]{1,0:T(8,128)S(1)}, f32[112,128]{1,0:T(8,128)S(1)}, u32[]{:S(2)}, u32[]{:S(2)}) collective-permute-start(f32[112,128]{1,0:T(8,128)S(1)} %get-tuple-element.68), channel_id=1, source_target_pairs={{0,24},{8,16},{16,8},{24,0},{1,25},{9,17},{17,9},{25,1},{2,26},{10... | collective-permute-start | bytes 172040 | tf_op jit(solution)/shard_map/ppermute | solution.py:454
  8.6 3.6 %collective-permute-done.3 = f32[8,128]{1,0:T(8,128)S(1)} collective-permute-done((f32[8,128]{1,0:T(8,128)S(1)}, f32[8,128]{1,0:T(8,128)S(1)}, u32[]{:S(2)}, u32[]{:S(2)}) %collective-permute-start.3) | collective-permute-done | bytes 4128 | tf_op jit(solution)/shard_map/ppermute | solution.py:455
  12.2 2.7 %collective-permute-start.6 = (f32[8,128]{1,0:T(8,128)S(1)}, f32[8,128]{1,0:T(8,128)S(1)}, u32[]{:S(2)}, u32[]{:S(2)}) collective-permute-start(f32[8,128]{1,0:T(8,128)S(1)} %fusion.5), channel_id=1, source_target_pairs={{0,4},{2,6},{4,0},{6,2},{1,5},{3,7},{5,1},{7,3},{8,12},{10,14},{12... | collective-permute-start | bytes 12296 | tf_op jit(solution)/shard_map/ppermute | solution.py:465
  14.8 1.3 %collective-permute-start.5 = (f32[16,128]{1,0:T(8,128)S(1)}, f32[16,128]{1,0:T(8,128)S(1)}, u32[]{:S(2)}, u32[]{:S(2)}) collective-permute-start(f32[16,128]{1,0:T(8,128)S(1)} %pad_maximum_fusion.4), channel_id=1, source_target_pairs={{0,6},{2,4},{4,2},{6,0},{1,7},{3,5},{5,3},{7,1},{8,14},{10,12},{12... | collective-permute-start | bytes 24584 | tf_op jit(solution)/shard_map/ppermute | solution.py:464
  16.8 3.4 %collective-permute-done.5 = f32[16,128]{1,0:T(8,128)S(1)} collective-permute-done((f32[16,128]{1,0:T(8,128)S(1)}, f32[16,128]{1,0:T(8,128)S(1)}, u32[]{:S(2)}, u32[]{:S(2)}) %collective-permute-start.5) | collective-permute-done | bytes 8224 | tf_op jit(solution)/shard_map/ppermute | solution.py:464
  20.3 1.9 %shard_map.131 = (f32[1,128]{1,0:T(1,128)S(1)}, bf16[128,1024]{1,0:T(8,128)(2,1)S(1)}, bf16[128,512]{1,0:T(8,128)(2,1)S(1)}, bf16[512,1024]{1,0:T(8,128)(2,1)S(1...) custom-call(f32[8,128]{1,0:T(8,128)S(1)} %get-tuple-element.64.refs_, ...), custom_call_target="tpu_custom_call" | custom-call | tf_op jit(solution)/shard_map/pallas_call | solution.py:482
  22.2 2.6 %shard_map.132 = (f32[4,104,128]{2,1,0:T(8,128)S(1)}, f32[432,128]{1,0:T(8,128)S(1)}, f32[800,128]{1,0:T(8,128)S(1)}, f32[104,128]{1,0:T(8,128)S(1)}, f32[104,12...) custom-call(f32[800,128]{1,0:T(8,128)S(1)} %bitcast.28, f32[800,128]{1,0:T(8,128)S(1)} %bitcast.32, ...), custom_call_target="tpu_custom_call" | custom-call | tf_op jit(solution)/shard_map/pallas_call | solution.py:506
  24.9 1.5 %collective-permute-done.7 = f32[432,128]{1,0:T(8,128)S(1)} collective-permute-done((f32[432,128]{1,0:T(8,128)S(1)}, f32[432,128]{1,0:T(8,128)S(1)}, u32[]{:S(2)}, u32[]{:S(2)}) %collective-permute-start.7) | collective-permute-done | bytes 221216 | tf_op jit(solution)/shard_map/ppermute | solution.py:532
  26.4 1.5 %collective-permute-start.8 = (f32[104,128]{1,0:T(8,128)S(1)}, f32[104,128]{1,0:T(8,128)S(1)}, u32[]{:S(2)}, u32[]{:S(2)}) collective-permute-start(f32[104,128]{1,0:T(8,128)S(1)} %get-tuple-element.53), channel_id=1, source_target_pairs={{0,8},{8,0},{16,24},{24,16},{1,9},{9,1},{17,25},{25,17},{2,10},{10... | collective-permute-start | bytes 159752 | tf_op jit(solution)/shard_map/ppermute | solution.py:539
  28.0 1.4 %collective-permute-start.10 = (f32[104,128]{1,0:T(8,128)S(1)}, f32[104,128]{1,0:T(8,128)S(1)}, u32[]{:S(2)}, u32[]{:S(2)}) collective-permute-start(f32[104,128]{1,0:T(8,128)S(1)} %get-tuple-element.54), channel_id=1, source_target_pairs={{0,24},{8,16},{16,8},{24,0},{1,25},{9,17},{17,9},{25,1},{2,26},{10... | collective-permute-start | bytes 159752 | tf_op jit(solution)/shard_map/ppermute | solution.py:539
  30.0 0.9 %collective-permute-done.8 = f32[104,128]{1,0:T(8,128)S(1)} collective-permute-done((f32[104,128]{1,0:T(8,128)S(1)}, f32[104,128]{1,0:T(8,128)S(1)}, u32[]{:S(2)}, u32[]{:S(2)}) %collective-permute-start.8) | collective-permute-done | bytes 53280 | tf_op jit(solution)/shard_map/ppermute | solution.py:539
  30.9 2.2 %collective-permute-done.10 = f32[104,128]{1,0:T(8,128)S(1)} collective-permute-done((f32[104,128]{1,0:T(8,128)S(1)}, f32[104,128]{1,0:T(8,128)S(1)}, u32[]{:S(2)}, u32[]{:S(2)}) %collective-permute-start.10) | collective-permute-done | bytes 53280 | tf_op jit(solution)/shard_map/ppermute | solution.py:539
  33.7 2.1 %collective-permute-start.12 = (f32[112,128]{1,0:T(8,128)S(1)}, f32[112,128]{1,0:T(8,128)S(1)}, u32[]{:S(2)}, u32[]{:S(2)}) collective-permute-start(f32[112,128]{1,0:T(8,128)S(1)} %pad_maximum_fusion.3), channel_id=1, source_target_pairs={{0,6},{2,4},{4,2},{6,0},{1,7},{3,5},{5,3},{7,1},{8,14},{10,12},{12... | collective-permute-start | bytes 172040 | tf_op jit(solution)/shard_map/ppermute | solution.py:547
  35.8 2.4 %collective-permute-start.13 = (f32[104,128]{1,0:T(8,128)S(1)}, f32[104,128]{1,0:T(8,128)S(1)}, u32[]{:S(2)}, u32[]{:S(2)}) collective-permute-start(f32[104,128]{1,0:T(8,128)S(1)} %fusion.3), channel_id=1, source_target_pairs={{0,4},{2,6},{4,0},{6,2},{1,5},{3,7},{5,1},{7,3},{8,12},{10,14},{12... | collective-permute-start | bytes 159752 | tf_op jit(solution)/shard_map/ppermute | solution.py:548
  39.4 1.6 %collective-permute-done.13 = f32[104,128]{1,0:T(8,128)S(1)} collective-permute-done((f32[104,128]{1,0:T(8,128)S(1)}, f32[104,128]{1,0:T(8,128)S(1)}, u32[]{:S(2)}, u32[]{:S(2)}) %collective-permute-start.13) | collective-permute-done | bytes 53280 | tf_op jit(solution)/shard_map/ppermute | solution.py:548
  41.2 1.0 %collective-permute-done.14 = f32[104,128]{1,0:T(8,128)S(1)} collective-permute-done((f32[104,128]{1,0:T(8,128)S(1)}, f32[104,128]{1,0:T(8,128)S(1)}, u32[]{:S(2)}, u32[]{:S(2)}) %collective-permute-start.14) | collective-permute-done | bytes 53280 | tf_op jit(solution)/shard_map/ppermute | solution.py:402
  42.5 1.8 %collective-permute-start.19 = (f32[208,128]{1,0:T(8,128)S(1)}, f32[208,128]{1,0:T(8,128)S(1)}, u32[]{:S(2)}, u32[]{:S(2)}) collective-permute-start(f32[208,128]{1,0:T(8,128)S(1)} %pad_maximum_fusion.refs_0_), channel_id=1, source_target_pairs={{0,24},{8,16},{16,8},{24,0},{1,25},{9,17},{17,9},{25,1},{2,26},{10... | collective-permute-start | bytes 319496 | tf_op jit(solution)/shard_map/ppermute | solution.py:573
  44.2 4.4 %collective-permute-start.18 = (f32[208,128]{1,0:T(8,128)S(1)}, f32[208,128]{1,0:T(8,128)S(1)}, u32[]{:S(2)}, u32[]{:S(2)}) collective-permute-start(f32[208,128]{1,0:T(8,128)S(1)} %pad_maximum_fusion.refs_0_), channel_id=1, source_target_pairs={{0,16},{8,24},{16,0},{24,8},{1,17},{9,25},{17,1},{25,9},{2,18},{10... | collective-permute-start | bytes 319496 | tf_op jit(solution)/shard_map/ppermute | solution.py:573
  48.7 1.5 %shard_map.133 = f32[800,128]{1,0:T(8,128)} custom-call(f32[1,128]{1,0:T(1,128)S(1)} %get-tuple-element.32.refs_0_, f32[104,128]{1,0:T(8,128)S(1)} %fusion.refs_1_, f32[800,128]{1,0:T(8,128)S(1)} %get-tuple-element.43.refs_2_, f32[800,128]{1,0:T(8,128)S(1)} %bitcast.29, f32[8,104,128]{2,1,0:T(8,128)S(1)} %get-tuple-element.44.refs_4_, ...), custom_call_target="tpu_custom_call" | custom-call | tf_op jit(solution)/shard_map/pallas_call | solution.py:560
  50.3 1.3 %collective-permute-done.18.refs_2_ = f32[208,128]{1,0:T(8,128)S(1)} collective-permute-done((f32[208,128]{1,0:T(8,128)S(1)}, f32[208,128]{1,0:T(8,128)S(1)}, u32[]{:S(2)}, u32[]{:S(2)}) %collective-permute-start.18) | collective-permute-done | bytes 106528 | tf_op jit(solution)/shard_map/ppermute | solution.py:573
  51.5 1.9 %collective-permute-done.17.refs_1_ = f32[208,128]{1,0:T(8,128)S(1)} collective-permute-done((f32[208,128]{1,0:T(8,128)S(1)}, f32[208,128]{1,0:T(8,128)S(1)}, u32[]{:S(2)}, u32[]{:S(2)}) %collective-permute-start.17) | collective-permute-done | bytes 106528 | tf_op jit(solution)/shard_map/ppermute | solution.py:573
  53.4 0.8 %shard_map.134 = (f32[100,512]{1,0:T(8,128)}, f32[1,512]{1,0:T(1,128)}, f32[100,512]{1,0:T(8,128)}, f32[1,100]{1,0:T(1,128)}) custom-call(f32[208,128]{1,0:T(8,128)S(1)} %pad_maximum_fusion.refs_0_, f32[208,128]{1,0:T(8,128)S(1)} %collective-permute-done.17.refs_1_, f32[208,128]{1,0:T(8,128)S(1)} %collective-permute-done.18.refs_2_, ...), custom_call_target="tpu_custom_call" | custom-call | tf_op jit(solution)/shard_map/pallas_call | solution.py:574
  (60 shorter events, 6.4 us)
Async XLA Ops:
  2.7 1.3 %collective-permute-start = (f32[24,128]{1,0:T(8,128)S(1)}, f32[24,128]{1,0:T(8,128)S(1)}, u32[]{:S(2)}, u32[]{:S(2)}) collective-permute-start(f32[24,128]{1,0:T(8,128)S(1)} %get-tuple-element.28), channel_id=1, source_target_pairs={{0,1},{1,0},{2,3},{3,2},{4,5},{5,4},{6,7},{7,6},{8,9},{9,8},{10,11... | collective-permute-start | bytes 36872 | tf_op jit(solution)/shard_map/ppermute | solution.py:449
  4.1 16.2 %copy-start.1 = (bf16[512,100]{0,1:T(8,128)(2,1)S(1)}, bf16[512,100]{0,1:T(8,128)(2,1)}, u32[]{:S(2)}) copy-start(bf16[512,100]{0,1:T(8,128)(2,1)} %param.16) | copy-start | bytes 307204
  4.1 16.2 %copy-start.3 = (bf16[100,512]{1,0:T(8,128)(2,1)S(1)}, bf16[100,512]{1,0:T(8,128)(2,1)}, u32[]{:S(2)}) copy-start(bf16[100,512]{1,0:T(8,128)(2,1)} %refs_3_.3) | copy-start | bytes 307204
  4.1 16.2 %copy-start.4 = (f32[512]{0:T(512)S(1)}, f32[512]{0:T(512)}, u32[]{:S(2)}) copy-start(f32[512]{0:T(512)} %param.15) | copy-start | bytes 6148
  4.1 16.2 %copy-start.5 = (f32[100]{0:T(128)S(1)}, f32[100]{0:T(128)}, u32[]{:S(2)}) copy-start(f32[100]{0:T(128)} %param.17) | copy-start | bytes 1204
  4.1 8.0 %collective-permute-start.1 = (f32[112,128]{1,0:T(8,128)S(1)}, f32[112,128]{1,0:T(8,128)S(1)}, u32[]{:S(2)}, u32[]{:S(2)}) collective-permute-start(f32[112,128]{1,0:T(8,128)S(1)} %get-tuple-element.67), channel_id=1, source_target_pairs={{0,8},{8,0},{16,24},{24,16},{1,9},{9,1},{17,25},{25,17},{2,10},{10... | collective-permute-start | bytes 172040 | tf_op jit(solution)/shard_map/ppermute | solution.py:453
  7.0 5.1 %collective-permute-start.2 = (f32[112,128]{1,0:T(8,128)S(1)}, f32[112,128]{1,0:T(8,128)S(1)}, u32[]{:S(2)}, u32[]{:S(2)}) collective-permute-start(f32[112,128]{1,0:T(8,128)S(1)} %get-tuple-element.68), channel_id=1, source_target_pairs={{0,24},{8,16},{16,8},{24,0},{1,25},{9,17},{17,9},{25,1},{2,26},{10... | collective-permute-start | bytes 172040 | tf_op jit(solution)/shard_map/ppermute | solution.py:454
  8.5 3.6 %collective-permute-start.3 = (f32[8,128]{1,0:T(8,128)S(1)}, f32[8,128]{1,0:T(8,128)S(1)}, u32[]{:S(2)}, u32[]{:S(2)}) collective-permute-start(f32[8,128]{1,0:T(8,128)S(1)} %get-tuple-element.66), channel_id=1, source_target_pairs={{0,16},{8,24},{16,0},{24,8},{1,17},{9,25},{17,1},{25,9},{2,18},{10... | collective-permute-start | bytes 12296 | tf_op jit(solution)/shard_map/ppermute | solution.py:455
  12.2 4.7 %collective-permute-start.6 = (f32[8,128]{1,0:T(8,128)S(1)}, f32[8,128]{1,0:T(8,128)S(1)}, u32[]{:S(2)}, u32[]{:S(2)}) collective-permute-start(f32[8,128]{1,0:T(8,128)S(1)} %fusion.5), channel_id=1, source_target_pairs={{0,4},{2,6},{4,0},{6,2},{1,5},{3,7},{5,1},{7,3},{8,12},{10,14},{12... | collective-permute-start | bytes 12296 | tf_op jit(solution)/shard_map/ppermute | solution.py:465
  14.8 5.4 %collective-permute-start.5 = (f32[16,128]{1,0:T(8,128)S(1)}, f32[16,128]{1,0:T(8,128)S(1)}, u32[]{:S(2)}, u32[]{:S(2)}) collective-permute-start(f32[16,128]{1,0:T(8,128)S(1)} %pad_maximum_fusion.4), channel_id=1, source_target_pairs={{0,6},{2,4},{4,2},{6,0},{1,7},{3,5},{5,3},{7,1},{8,14},{10,12},{12... | collective-permute-start | bytes 24584 | tf_op jit(solution)/shard_map/ppermute | solution.py:464
  16.2 4.1 %collective-permute-start.4 = (f32[16,128]{1,0:T(8,128)S(1)}, f32[16,128]{1,0:T(8,128)S(1)}, u32[]{:S(2)}, u32[]{:S(2)}) collective-permute-start(f32[16,128]{1,0:T(8,128)S(1)} %pad_maximum_fusion.4), channel_id=1, source_target_pairs={{0,2},{2,0},{4,6},{6,4},{1,3},{3,1},{5,7},{7,5},{8,10},{10,8},{12,... | collective-permute-start | bytes 24584 | tf_op jit(solution)/shard_map/ppermute | solution.py:463
  24.8 1.5 %collective-permute-start.7 = (f32[432,128]{1,0:T(8,128)S(1)}, f32[432,128]{1,0:T(8,128)S(1)}, u32[]{:S(2)}, u32[]{:S(2)}) collective-permute-start(f32[432,128]{1,0:T(8,128)S(1)} %get-tuple-element.42), channel_id=1, source_target_pairs={{0,1},{1,0},{2,3},{3,2},{4,5},{5,4},{6,7},{7,6},{8,9},{9,8},{10,11... | collective-permute-start | bytes 663560 | tf_op jit(solution)/shard_map/ppermute | solution.py:532
  26.4 4.5 %collective-permute-start.8 = (f32[104,128]{1,0:T(8,128)S(1)}, f32[104,128]{1,0:T(8,128)S(1)}, u32[]{:S(2)}, u32[]{:S(2)}) collective-permute-start(f32[104,128]{1,0:T(8,128)S(1)} %get-tuple-element.53), channel_id=1, source_target_pairs={{0,8},{8,0},{16,24},{24,16},{1,9},{9,1},{17,25},{25,17},{2,10},{10... | collective-permute-start | bytes 159752 | tf_op jit(solution)/shard_map/ppermute | solution.py:539
  28.0 5.1 %collective-permute-start.10 = (f32[104,128]{1,0:T(8,128)S(1)}, f32[104,128]{1,0:T(8,128)S(1)}, u32[]{:S(2)}, u32[]{:S(2)}) collective-permute-start(f32[104,128]{1,0:T(8,128)S(1)} %get-tuple-element.54), channel_id=1, source_target_pairs={{0,24},{8,16},{16,8},{24,0},{1,25},{9,17},{17,9},{25,1},{2,26},{10... | collective-permute-start | bytes 159752 | tf_op jit(solution)/shard_map/ppermute | solution.py:539
  29.3 4.3 %collective-permute-start.9 = (f32[104,128]{1,0:T(8,128)S(1)}, f32[104,128]{1,0:T(8,128)S(1)}, u32[]{:S(2)}, u32[]{:S(2)}) collective-permute-start(f32[104,128]{1,0:T(8,128)S(1)} %get-tuple-element.55), channel_id=1, source_target_pairs={{0,16},{8,24},{16,0},{24,8},{1,17},{9,25},{17,1},{25,9},{2,18},{10... | collective-permute-start | bytes 159752 | tf_op jit(solution)/shard_map/ppermute | solution.py:539
  33.7 7.4 %collective-permute-start.12 = (f32[112,128]{1,0:T(8,128)S(1)}, f32[112,128]{1,0:T(8,128)S(1)}, u32[]{:S(2)}, u32[]{:S(2)}) collective-permute-start(f32[112,128]{1,0:T(8,128)S(1)} %pad_maximum_fusion.3), channel_id=1, source_target_pairs={{0,6},{2,4},{4,2},{6,0},{1,7},{3,5},{5,3},{7,1},{8,14},{10,12},{12... | collective-permute-start | bytes 172040 | tf_op jit(solution)/shard_map/ppermute | solution.py:547
  35.8 5.4 %collective-permute-start.11 = (f32[112,128]{1,0:T(8,128)S(1)}, f32[112,128]{1,0:T(8,128)S(1)}, u32[]{:S(2)}, u32[]{:S(2)}) collective-permute-start(f32[112,128]{1,0:T(8,128)S(1)} %pad_maximum_fusion.3), channel_id=1, source_target_pairs={{0,2},{2,0},{4,6},{6,4},{1,3},{3,1},{5,7},{7,5},{8,10},{10,8},{12,... | collective-permute-start | bytes 172040 | tf_op jit(solution)/shard_map/ppermute | solution.py:546
  35.8 5.3 %collective-permute-start.13 = (f32[104,128]{1,0:T(8,128)S(1)}, f32[104,128]{1,0:T(8,128)S(1)}, u32[]{:S(2)}, u32[]{:S(2)}) collective-permute-start(f32[104,128]{1,0:T(8,128)S(1)} %fusion.3), channel_id=1, source_target_pairs={{0,4},{2,6},{4,0},{6,2},{1,5},{3,7},{5,1},{7,3},{8,12},{10,14},{12... | collective-permute-start | bytes 159752 | tf_op jit(solution)/shard_map/ppermute | solution.py:548
  38.1 4.1 %collective-permute-start.14 = (f32[104,128]{1,0:T(8,128)S(1)}, f32[104,128]{1,0:T(8,128)S(1)}, u32[]{:S(2)}, u32[]{:S(2)}) collective-permute-start(f32[104,128]{1,0:T(8,128)S(1)} %get-tuple-element.45), channel_id=1, source_target_pairs={{0,8},{8,0},{16,24},{24,16},{1,9},{9,1},{17,25},{25,17},{2,10},{10... | collective-permute-start | bytes 159752 | tf_op jit(solution)/shard_map/ppermute | solution.py:402
  38.8 3.5 %collective-permute-start.15 = (f32[104,128]{1,0:T(8,128)S(1)}, f32[104,128]{1,0:T(8,128)S(1)}, u32[]{:S(2)}, u32[]{:S(2)}) collective-permute-start(f32[104,128]{1,0:T(8,128)S(1)} %get-tuple-element.46), channel_id=1, source_target_pairs={{8,16},{16,8},{9,17},{17,9},{10,18},{18,10},{11,19},{19,11},{12,20... | collective-permute-start | bytes 159752 | tf_op jit(solution)/shard_map/ppermute | solution.py:403
  41.1 1.3 %collective-permute-start.16 = (f32[104,128]{1,0:T(8,128)S(1)}, f32[104,128]{1,0:T(8,128)S(1)}, u32[]{:S(2)}, u32[]{:S(2)}) collective-permute-start(f32[104,128]{1,0:T(8,128)S(1)} %fusion.refs_1_), channel_id=1, source_target_pairs={{0,1},{1,0},{2,3},{3,2},{4,5},{5,4},{6,7},{7,6},{8,9},{9,8},{10,11... | collective-permute-start | bytes 159752 | tf_op jit(solution)/shard_map/ppermute | solution.py:571
  42.5 7.8 %collective-permute-start.19 = (f32[208,128]{1,0:T(8,128)S(1)}, f32[208,128]{1,0:T(8,128)S(1)}, u32[]{:S(2)}, u32[]{:S(2)}) collective-permute-start(f32[208,128]{1,0:T(8,128)S(1)} %pad_maximum_fusion.refs_0_), channel_id=1, source_target_pairs={{0,24},{8,16},{16,8},{24,0},{1,25},{9,17},{17,9},{25,1},{2,26},{10... | collective-permute-start | bytes 319496 | tf_op jit(solution)/shard_map/ppermute | solution.py:573
  44.2 7.3 %collective-permute-start.18 = (f32[208,128]{1,0:T(8,128)S(1)}, f32[208,128]{1,0:T(8,128)S(1)}, u32[]{:S(2)}, u32[]{:S(2)}) collective-permute-start(f32[208,128]{1,0:T(8,128)S(1)} %pad_maximum_fusion.refs_0_), channel_id=1, source_target_pairs={{0,16},{8,24},{16,0},{24,8},{1,17},{9,25},{17,1},{25,9},{2,18},{10... | collective-permute-start | bytes 319496 | tf_op jit(solution)/shard_map/ppermute | solution.py:573
  48.7 4.7 %collective-permute-start.17 = (f32[208,128]{1,0:T(8,128)S(1)}, f32[208,128]{1,0:T(8,128)S(1)}, u32[]{:S(2)}, u32[]{:S(2)}) collective-permute-start(f32[208,128]{1,0:T(8,128)S(1)} %pad_maximum_fusion.refs_0_), channel_id=1, source_target_pairs={{0,8},{8,0},{16,24},{24,16},{1,9},{9,1},{17,25},{25,17},{2,10},{10... | collective-permute-start | bytes 319496 | tf_op jit(solution)/shard_map/ppermute | solution.py:573
  (6 other events, 25.1 us)

commit v4 on v3

--- a/solution.py
+++ b/solution.py
@@ -155,15 +155,48 @@
     write_lat_edges(tracer, levels, rows, lat_a, lat_b, lat_odd, depth)
 
 
-def mix_kernel(levels, tracer, depth_ref, north, south, mixed):
+def prepare_kernel(
+    levels, tracer, depth_ref, north, south, w_in, b_in, w_out_t, b_out, kappa,
+    inner, wet_tracer, wi_t, wi_b, wo_t, wo_b, bias, up_out,
+    pad, wi_f, wo_f,
+):
     rows, cols = depth_ref.shape
+    pad_levels, span = wet_tracer.shape
     depth = depth_ref[...]
     blank = jnp.zeros((levels, cols), f32)
     dry = jnp.zeros((rows, cols), f32)
     halos = (north[0:levels, :], south[0:levels, :], blank, blank)
     depths = halo_depths(levels, north, south, dry, dry, dry.shape)[0:2] + (dry, dry)
-    for row, _, _, value in spread_rows(tracer, depth, levels, rows, halos, depths):
-        mixed[pl.ds(row, levels, stride=rows), :] = value
+    wet_tracer[levels:, :] = jnp.where(
+        lax.broadcasted_iota(jnp.int32, (pad_levels - levels, span), 0) < 3, 1.0, 0.0
+    )
+    pad[...] = jnp.zeros(pad.shape, f32)
+    pad[0:1, 0:levels] = b_out[...]
+    pad[1:2, 0:levels] = kappa[...]
+    turned = pad[...].T
+    bias[...] = jnp.broadcast_to(turned[:, 0:1], bias.shape)
+    kappa_col = jnp.broadcast_to(turned[0:levels, 1:2], (levels, cols))
+    lev = level_ids((levels, cols))
+    for row, center, wet, value in spread_rows(tracer, depth, levels, rows, halos, depths):
+        at = pl.ds(row, levels, stride=rows)
+        inner[at, :] = value
+        wet_tracer[0:levels, row * cols : (row + 1) * cols] = wet * center
+        open_face = (lev + 1.0 < depth[row : row + 1, :]) & (lev + 1.0 < float(levels))
+        up_out[at, :] = jnp.where(open_face, kappa_col, 0.0)
+
+    wi_f[...] = jnp.zeros(wi_f.shape, f32)
+    wi_f[0:levels, :] = w_in[...].astype(f32)
+    rest = b_in[...]
+    for part in range(3):
+        piece = rest.astype(bf16).astype(f32)
+        wi_f[levels + part : levels + part + 1, :] = piece
+        rest = rest - piece
+    wi_b[...] = wi_f[...].astype(bf16)
+    wi_t[...] = wi_f[...].T.astype(bf16)
+    wo_f[...] = jnp.zeros(wo_f.shape, f32)
+    wo_f[0:levels, :] = w_out_t[...].astype(f32)
+    wo_t[...] = wo_f[...].astype(bf16)
+    wo_b[...] = wo_f[...].T.astype(bf16)
 
 
 def columns_of(row, lanes):
@@ -171,65 +204,37 @@
 
 
 def network_kernel(
-    levels, column_count, energy, tracer, depth_ref, w_in, b_in, w_out_t, b_out, kappa, inner, west_ref, east_ref,
-    radius_row, x_b, wi_b, hidden, slope, gate, up_out, down_out, mixed,
-    pad, x_f, wi_f, wo_f,
+    levels, column_count, energy, tracer, depth_ref, inner, wet_tracer, wi_t, wo_t, bias, up, west_ref, east_ref,
+    radius_row, x_b, hidden, slope, gate, down_out, mixed,
 ):
     rows, cols = depth_ref.shape
-    hid = w_in.shape[1]
-    span = rows * cols
-    pad_levels = x_f.shape[0]
+    hid = wi_t.shape[0]
     depth = depth_ref[...]
     lev = level_ids((levels, cols))
     radius_line = jnp.sqrt(energy[0:1, :] / column_count + level_eps)
     radius_row[...] = radius_line
-    radius = columns_of(radius_line, cols)[0:levels, :]
-    scale = 1.0 / radius
-
-    x_f[levels:, :] = jnp.where(
-        lax.broadcasted_iota(jnp.int32, (pad_levels - levels, span), 0) < 3, 1.0, 0.0
-    )
-    for row in range(rows):
-        wet_tracer = jnp.where(lev < depth[row : row + 1, :], row_of(tracer, row, levels, rows), 0.0)
-        x_f[0:levels, row * cols : (row + 1) * cols] = wet_tracer * scale
-    x_b[...] = x_f[...].astype(bf16)
-
-    wi_f[...] = jnp.zeros(wi_f.shape, f32)
-    wi_f[0:levels, :] = w_in[...].astype(f32)
-    bias = b_in[...]
-    for part in range(3):
-        piece = bias.astype(bf16).astype(f32)
-        wi_f[levels + part : levels + part + 1, :] = piece
-        bias = bias - piece
-    wi_b[...] = wi_f[...].astype(bf16)
-    wi_t = wi_f[...].T.astype(bf16)
-    wo_f[...] = jnp.zeros(wo_f.shape, f32)
-    wo_f[0:levels, :] = w_out_t[...].astype(f32)
+    scale = columns_of(jnp.where(lane_ids(radius_line.shape) < levels, 1.0 / radius_line, 1.0), cols)
+    for row in range(rows):
+        part = slice(row * cols, (row + 1) * cols)
+        x_b[:, part] = (wet_tracer[:, part] * scale).astype(bf16)
 
     block = hid // 4
     for part in range(4):
         at = slice(part * block, (part + 1) * block)
         pre = jnp.dot(wi_t[at, :], x_b[...], preferred_element_type=f32)
-        sig = 1.0 / (1.0 + jnp.exp(-pre))
-        hidden[at, :] = (pre * sig).astype(bf16)
-        slope[at, :] = sig * (1.0 + pre * (1.0 - sig))
-
-    pad[...] = jnp.zeros(pad.shape, f32)
-    pad[0:1, 0:levels] = b_out[...]
-    pad[1:2, 0:levels] = kappa[...]
-    turned = pad[...].T
-    logits = jnp.dot(wo_f[...].astype(bf16), hidden[...], preferred_element_type=f32) + turned[:, 0:1]
-    tiny = jnp.exp(-jnp.abs(logits))
-    share = 1.0 / (1.0 + tiny)
-    gate[...] = jnp.where(logits >= 0.0, share, tiny * share)
-    soft = jnp.maximum(logits, 0.0) + jnp.log1p(tiny)
-    kappa_col = jnp.broadcast_to(turned[0:levels, 1:2], (levels, cols))
-    for row in range(rows):
-        open_face = (lev + 1.0 < depth[row : row + 1, :]) & (lev + 1.0 < float(levels))
+        sig = 0.5 + 0.5 * jnp.tanh(0.5 * pre)
+        product = pre * sig
+        hidden[at, :] = product.astype(bf16)
+        slope[at, :] = sig + product * (1.0 - sig)
+
+    for row in range(rows):
+        part = slice(row * cols, (row + 1) * cols)
         at = pl.ds(row, levels, stride=rows)
-        sinking = soft[0:levels, row * cols : (row + 1) * cols]
-        up_out[at, :] = jnp.where(open_face, kappa_col, 0.0)
-        down_out[at, :] = jnp.where(open_face, kappa_col + sinking, 0.0)
+        logits = jnp.dot(wo_t[...], hidden[:, part], preferred_element_type=f32) + bias[...]
+        gate[:, part] = 0.5 + 0.5 * jnp.tanh(0.5 * logits)
+        soft = jnp.maximum(logits, 0.0) + jnp.log(1.0 + jnp.exp(-jnp.abs(logits)))
+        face_up = row_of(up, row, levels, rows)
+        down_out[at, :] = jnp.where(face_up > 0.0, face_up + soft[0:levels, :], 0.0)
 
     lanes = lane_ids((levels, cols))
     west, east = west_ref[...], east_ref[...]
@@ -255,47 +260,83 @@
 
 def solve_kernel(
     levels, scale,
-    tracer, cotangent, depth_ref, up_ref, down_ref, mixed, w_out_t, wi_b, x_b, hidden, slope, gate,
+    wet_tracer, cotangent, depth_ref, up_ref, down_ref, mixed, wo_b, wi_b, x_b, hidden, slope, gate,
     keep, send, adjoint, lat_a, lat_b, d_inputs,
-    pad, wo_f, dl_f, dl_b, dp_b, rate_a, rate_b, inv_p, fwd_z, fwd_u, flow,
+    pad, dl_f, dl_b, dp_b, rate_a, rate_b, inv_p, fwd_z, fwd_u, flow,
 ):
     rows, cols = depth_ref.shape
-    hid = w_out_t.shape[1]
+    hid = wo_b.shape[0]
     span = rows * cols
     pad_levels = dl_f.shape[0]
     depth = depth_ref[...]
-    lev = level_ids((levels, cols))
     def at_level(k):
         return slice(k * rows, (k + 1) * rows)
 
-    rest = jnp.ones((rows, cols), f32)
+    mid = levels // 2
+    top = jnp.ones((rows, cols), f32)
     z = mixed[at_level(0), :]
     u = cotangent[at_level(0), :]
-    for k in range(levels - 1):
-        down = down_ref[at_level(k), :]
-        inv = 1.0 / (rest + down)
-        a = down * inv
-        b = up_ref[at_level(k), :] * inv
+    end = jnp.ones((rows, cols), f32)
+    z_end = mixed[at_level(levels - 1), :]
+    u_end = cotangent[at_level(levels - 1), :]
+    for step in range(mid):
+        k = step
+        down, up = down_ref[at_level(k), :], up_ref[at_level(k), :]
+        inv = 1.0 / (top + down)
+        a, b = down * inv, up * inv
         inv_p[at_level(k), :] = inv
         rate_a[at_level(k), :] = a
         rate_b[at_level(k), :] = b
         fwd_z[at_level(k), :] = z
         fwd_u[at_level(k), :] = u
-        rest = 1.0 + b * rest
+        top = 1.0 + b * top
         z = mixed[at_level(k + 1), :] + a * z
         u = cotangent[at_level(k + 1), :] + b * u
-    inv = 1.0 / rest
-    x = z * inv
-    y = u * inv
-    adjoint[at_level(levels - 1), :] = y
+        k = levels - 1 - step
+        if k > mid:
+            down, up = down_ref[at_level(k - 1), :], up_ref[at_level(k - 1), :]
+            inv = 1.0 / (end + up)
+            a, b = down * inv, up * inv
+            inv_p[at_level(k), :] = inv
+            rate_a[at_level(k), :] = a
+            rate_b[at_level(k), :] = b
+            fwd_z[at_level(k), :] = z_end
+            fwd_u[at_level(k), :] = u_end
+            end = a * end
+            z_end = b * z_end
+            u_end = a * u_end
+            if k - 1 > mid:
+                end = 1.0 + end
+                z_end = mixed[at_level(k - 1), :] + z_end
+                u_end = cotangent[at_level(k - 1), :] + u_end
+    inv = 1.0 / (top + end)
+    x_up = x_down = (z + z_end) * inv
+    y_up = y_down = (u + u_end) * inv
+    adjoint[at_level(mid), :] = y_up
+    for step in range(1, levels - mid):
+        k = mid + step
+        inv = inv_p[at_level(k), :]
+        x_new = fwd_z[at_level(k), :] * inv + rate_a[at_level(k), :] * x_down
+        y_new = fwd_u[at_level(k), :] * inv + rate_b[at_level(k), :] * y_down
+        adjoint[at_level(k), :] = y_new
+        flow[at_level(k - 1), :] = jnp.where(depth > float(k), x_down * (y_new - y_down), 0.0)
+        x_down, y_down = x_new, y_new
+        k = mid - step
+        if k >= 0:
+            inv = inv_p[at_level(k), :]
+            x_up = fwd_z[at_level(k), :] * inv + rate_b[at_level(k), :] * x_up
+            y_new = fwd_u[at_level(k), :] * inv + rate_a[at_level(k), :] * y_up
+            adjoint[at_level(k), :] = y_new
+            flow[at_level(k), :] = jnp.where(depth > float(k + 1), x_up * (y_up - y_new), 0.0)
+            y_up = y_new
+    for k in range(mid - (levels - mid), -1, -1):
+        inv = inv_p[at_level(k), :]
+        x_up = fwd_z[at_level(k), :] * inv + rate_b[at_level(k), :] * x_up
+        y_new = fwd_u[at_level(k), :] * inv + rate_a[at_level(k), :] * y_up
+        adjoint[at_level(k), :] = y_new
+        flow[at_level(k), :] = jnp.where(depth > float(k + 1), x_up * (y_up - y_new), 0.0)
+        y_up = y_new
     flow[at_level(levels - 1), :] = jnp.zeros((rows, cols), f32)
-    for k in range(levels - 2, -1, -1):
-        inv = inv_p[at_level(k), :]
-        x = fwd_z[at_level(k), :] * inv + rate_b[at_level(k), :] * x
-        y_new = fwd_u[at_level(k), :] * inv + rate_a[at_level(k), :] * y
-        adjoint[at_level(k), :] = y_new
-        flow[at_level(k), :] = jnp.where(depth > float(k + 1), x * (y - y_new), 0.0)
-        y = y_new
 
     dl_f[levels:, :] = jnp.zeros((pad_levels - levels, span), f32)
     for row in range(rows):
@@ -307,9 +348,6 @@
         bout = bout + dl_b[:, row * cols : (row + 1) * cols].astype(f32)
     bout_row = lane_sums(pad, bout) * scale
 
-    wo_f[...] = jnp.zeros(wo_f.shape, f32)
-    wo_f[0:levels, :] = w_out_t[...].astype(f32)
-    wo_b = wo_f[...].T.astype(bf16)
     block = hid // 4
     for part in range(4):
         at = slice(part * block, (part + 1) * block)
@@ -318,30 +356,32 @@
     d_in = jnp.dot(wi_b[...], dp_b[...], preferred_element_type=f32)
     level = jnp.zeros((levels, cols), f32)
     for row in range(rows):
-        part = d_in[0:levels, row * cols : (row + 1) * cols]
+        at = slice(row * cols, (row + 1) * cols)
+        part = d_in[0:levels, at]
         d_inputs[row, 0:levels, :] = part
-        wet_tracer = jnp.where(lev < depth[row : row + 1, :], row_of(tracer, row, levels, rows), 0.0)
-        level = level + part * wet_tracer
+        level = level + part * wet_tracer[0:levels, at]
     level_row = lane_sums(pad, level)
 
     contract = (((1,), (1,)), ((), ()))
     lat_odd, lon_odd = odd_places()
     quarter = lax.axis_index("lat") % 4
     height = keep.shape[1]
-    for part in range(4):
-        at = slice(part * block, (part + 1) * block)
-        slot = part ^ quarter
-        g_in = lax.dot_general(x_b[...], dp_b[at, :], contract, preferred_element_type=f32)
-        g_out = lax.dot_general(dl_b[...], hidden[at, :], contract, preferred_element_type=f32)
-        g_in = g_in[0:height, :] * scale
-        g_out = g_out[0:height, :] * scale
-        keep[slot] = jnp.where(lon_odd, g_out, g_in)
-        send[pl.ds(pl.multiple_of(slot * height, 8), height), :] = jnp.where(lon_odd, g_in, g_out)
-        keep[slot, levels + 1 : levels + 2, :] = level_row
-        keep[slot, levels + 2 : levels + 3, :] = bout_row
-        lower = send.at[pl.ds(pl.multiple_of(slot * height, 8), height), :]
-        lower[levels + 1 : levels + 2, :] = level_row
-        lower[levels + 2 : levels + 3, :] = bout_row
+    for half in range(2):
+        wide = slice(2 * half * block, (2 * half + 2) * block)
+        both_in = lax.dot_general(x_b[...], dp_b[wide, :], contract, preferred_element_type=f32)
+        both_out = lax.dot_general(dl_b[...], hidden[wide, :], contract, preferred_element_type=f32)
+        for part in range(2):
+            at = slice(part * block, (part + 1) * block)
+            slot = (2 * half + part) ^ quarter
+            g_in = both_in[0:height, at] * scale
+            g_out = both_out[0:height, at] * scale
+            lower = send.at[pl.ds(pl.multiple_of(slot * height, 8), height), :]
+            keep[slot] = jnp.where(lon_odd, g_out, g_in)
+            lower[...] = jnp.where(lon_odd, g_in, g_out)
+            keep[slot, levels + 1 : levels + 2, :] = level_row
+            keep[slot, levels + 2 : levels + 3, :] = bout_row
+            lower[levels + 1 : levels + 2, :] = level_row
+            lower[levels + 2 : levels + 3, :] = bout_row
     lon_a = send.at[4 * height : 4 * height + rows, :]
     lon_b = send.at[4 * height + rows : 4 * height + 2 * rows, :]
     write_lat_edges(adjoint, levels, rows, lat_a, lat_b, lat_odd)
@@ -349,7 +389,7 @@
 
 
 def final_kernel(
-    levels, column_count, radius_row, level_total, adjoint, tracer, d_inputs, depth_ref,
+    levels, column_count, radius_row, level_total, adjoint, wet_tracer, d_inputs, depth_ref,
     north, south, west, east, t_north, t_south, t_west, t_east, out,
 ):
     rows, cols = depth_ref.shape
@@ -363,22 +403,24 @@
     depth_halos = halo_depths(levels, t_north, t_south, t_west, t_east, depth.shape)
     scale = 1.0 / radius
     for row, _, wet, value in spread_rows(adjoint, depth, levels, rows, halos, depth_halos):
-        wet_tracer = wet * row_of(tracer, row, levels, rows)
-        d_wet = d_inputs[row, 0:levels, :] * scale - wet_tracer * pull
+        pulled = wet_tracer[0:levels, row * cols : (row + 1) * cols] * pull
+        d_wet = d_inputs[row, 0:levels, :] * scale - pulled
         out[pl.ds(row, levels, stride=rows), :] = value + wet * d_wet
 
 
-def gather_kernel(levels, *refs):
-    pairs = refs[0:4]
-    grad_in, grad_bin, grad_out, grad_bout = refs[4:]
+def gather_kernel(levels, height, mine, other, grad_in, grad_bin, grad_out, grad_bout):
+    lon_odd = lax.axis_index("core") == 1
     quarter = lax.axis_index("lat") % 4
-    height, block = pairs[0].shape[0] // 2, pairs[0].shape[1]
+    block = mine.shape[1]
     for step in range(4):
         at = pl.ds(pl.multiple_of((step ^ quarter) * block, block), block)
-        grad_in[:, at] = pairs[step][0:levels, :]
-        grad_bin[:, at] = pairs[step][levels : levels + 1, :]
-        grad_out[:, at] = pairs[step][height : height + levels, :]
-    grad_bout[...] = pairs[0][levels + 2 : levels + 3, 0:levels]
+        rows = slice(step * height, (step + 1) * height)
+        inner = jnp.where(lon_odd, other[rows, :], mine[rows, :])
+        outer = jnp.where(lon_odd, mine[rows, :], other[rows, :])
+        grad_in[:, at] = inner[0:levels, :]
+        grad_bin[:, at] = inner[levels : levels + 1, :]
+        grad_out[:, at] = outer[0:levels, :]
+    grad_bout[...] = mine[levels + 2 : levels + 3, 0:levels]
 
 
 def flip(count, by):
@@ -430,6 +472,7 @@
         zero_kernel,
         out_shape=sds((rows, pad_levels), f32),
         out_specs=vmem,
+        compiler_params=pltpu.CompilerParams(vmem_limit_bytes=1024 * 1024),
         cost_estimate=ahead,
     )()
     small, lat_a, lat_b, depth = pl.pallas_call(
@@ -470,38 +513,41 @@
         t_far = lax.ppermute(small[rows : 2 * rows], ("z", "core"), far_pairs(lons, True))
     t_west, t_east = in_order(lon_odd, t_near, t_far)
 
-    inner = pl.pallas_call(
-        lambda *refs: mix_kernel(levels, *refs),
-        out_shape=sds(flat, f32),
-        in_specs=[vmem] * 4,
-        out_specs=vmem,
+    wide = sds((pad_levels, span), f32)
+    inner, wet_tracer, wi_t, wi_b, wo_t, wo_b, bias, up = pl.pallas_call(
+        lambda *refs: prepare_kernel(levels, *refs),
+        out_shape=[
+            sds(flat, f32),
+            wide,
+            sds((hid, pad_levels), bf16),
+            sds((pad_levels, hid), bf16),
+            sds((pad_levels, hid), bf16),
+            sds((hid, pad_levels), bf16),
+            sds((pad_levels, cols), f32),
+            sds(flat, f32),
+        ],
+        in_specs=[vmem] * 9,
+        out_specs=[vmem] * 8,
+        scratch_shapes=[pad] + [pltpu.VMEM((pad_levels, hid), f32)] * 2,
         compiler_params=params,
         cost_estimate=ahead,
-    )(tracer, depth, t_north, t_south)
-
-    radius_row, x_b, wi_b, hidden, slope, gate, up, down, mixed = pl.pallas_call(
+    )(tracer, depth, t_north, t_south, w_in, b_in, w_out_t, b_out, kappa)
+
+    radius_row, x_b, hidden, slope, gate, down, mixed = pl.pallas_call(
         lambda *refs: network_kernel(levels, column_count, *refs),
         out_shape=[
             sds((1, pad_levels), f32),
             sds((pad_levels, span), bf16),
-            sds((pad_levels, hid), bf16),
             sds((hid, span), bf16),
             sds((hid, span), f32),
-            sds((pad_levels, span), f32),
-            sds(flat, f32),
+            wide,
             sds(flat, f32),
             sds(flat, f32),
         ],
         in_specs=[vmem] * 11,
-        out_specs=[vmem] * 9,
-        scratch_shapes=[
-            pad,
-            pltpu.VMEM((pad_levels, span), f32),
-            pltpu.VMEM((pad_levels, hid), f32),
-            pltpu.VMEM((pad_levels, hid), f32),
-        ],
+        out_specs=[vmem] * 7,
         compiler_params=params,
-    )(energy, tracer, depth, w_in, b_in, w_out_t, b_out, kappa, inner, t_west, t_east)
+    )(energy, tracer, depth, inner, wet_tracer, wi_t, wo_t, bias, up, t_west, t_east)
 
     keep, send, adjoint, lat_a, lat_b, d_inputs = pl.pallas_call(
         lambda *refs: solve_kernel(levels, 1.0 / math.sqrt(column_count), *refs),
@@ -517,30 +563,33 @@
         out_specs=[vmem] * 6,
         scratch_shapes=[
             pad,
-            pltpu.VMEM((pad_levels, hid), f32),
             pltpu.VMEM((pad_levels, span), f32),
             pltpu.VMEM((pad_levels, span), bf16),
             pltpu.VMEM((hid, span), bf16),
             *[pltpu.VMEM(flat, f32)] * 6,
         ],
         compiler_params=params,
-    )(
-        tracer, cotangent, depth, up, down, mixed, w_out_t,
-        wi_b, x_b, hidden, slope, gate,
-    )
+    )(wet_tracer, cotangent, depth, up, down, mixed, wo_b, wi_b, x_b, hidden, slope, gate)
 
     got = lax.ppermute(send, "core", flip(2, 1))
-    north, south = swap_lat(lat_odd, lats, lat_a, lat_b)
     chip = keep + got[: 4 * height].reshape(keep.shape)
     lon_near = got[4 * height : 4 * height + rows]
     lon_pass = got[4 * height + rows :]
     part = chip[0]
-    for step in range(1, 4):
-        part = part + lax.ppermute(chip[step], "lat", flip(lats, step))
-    step = 4
-    while step < lats:
-        part = part + lax.ppermute(part, "lat", flip(lats, step))
-        step *= 2
+    if lats == 4:
+        near = lax.ppermute(jnp.concatenate([chip[1], lat_a], 0), "lat", flip(lats, 1))
+        far = lax.ppermute(jnp.concatenate([chip[3], lat_b], 0), "lat", flip(lats, 3))
+        cross = lax.ppermute(chip[2], "lat", flip(lats, 2))
+        part = part + near[:height] + far[:height] + cross
+        north, south = in_order(lat_odd, near[height:], far[height:])
+    else:
+        for step in range(1, 4):
+            part = part + lax.ppermute(chip[step], "lat", flip(lats, step))
+        step = 4
+        while step < lats:
+            part = part + lax.ppermute(part, "lat", flip(lats, step))
+            step *= 2
+        north, south = swap_lat(lat_odd, lats, lat_a, lat_b)
     if chips == 4:
         packed = jnp.concatenate([part, lon_pass], 0)
         near = lax.ppermute(packed, "z", flip(chips, 1))
@@ -564,25 +613,26 @@
         out_specs=vmem,
         compiler_params=params,
     )(
-        radius_row, part, adjoint, tracer, d_inputs, depth,
+        radius_row, part, adjoint, wet_tracer, d_inputs, depth,
         north, south, west, east, t_north, t_south, t_west, t_east,
     )
 
-    other = lax.ppermute(part, "core", flip(2, 1))
-    pair = jnp.concatenate([jnp.where(lon_odd, other, part), jnp.where(lon_odd, part, other)], 0)
-    pairs = [pair] + [lax.ppermute(pair, "lat", flip(lats, step)) for step in (3, 2, 1)][::-1]
+    mine = [part] + [lax.ppermute(part, "lat", flip(lats, step)) for step in range(1, 4)]
+    mine, tracer_adjoint = lax.optimization_barrier((mine, tracer_adjoint))
+    mine = jnp.concatenate(mine, 0)
+    other = lax.ppermute(mine, "core", flip(2, 1))
     grad_w_in, grad_b_in, grad_w_out_t, grad_b_out = pl.pallas_call(
-        lambda *refs: gather_kernel(levels, *refs),
+        lambda *refs: gather_kernel(levels, height, *refs),
         out_shape=[
             sds((levels, hid), f32),
             sds((1, hid), f32),
             sds((levels, hid), f32),
             sds((1, levels), f32),
         ],
-        in_specs=[vmem] * 4,
+        in_specs=[vmem] * 2,
         out_specs=[vmem] * 4,
         compiler_params=params,
-    )(*pairs)
+    )(mine, other)
     return (
         tracer_adjoint.reshape(levels, rows, cols),
         grad_w_in,

time: 54.4 us -> 49.8 us (0.915)
  starting transfers between devices: 24.8 us -> 20.9 us
  Pallas kernels: 8.16 us -> 7.29 us
    ppermute x9 -> x7, starting transfers between devices: 11.2 us -> 7.24 us  [the longest x3 3.55 us: shards(): lax.ppermute(part, 'lat', flip(lats, step))]
    ppermute x1, waiting for transfers between devices: 1.62 us -> 2.85 us  [shards(): cross = lax.ppermute(part, 'z', flip(chips, 2))]
    pallas_call x1, Pallas kernels: 0.6 us -> 0.01 us  [shards(): pl.pallas_call(zero_kernel, out_shape=sds((rows, pad_levels), f32), out_s...]
    ppermute x9 -> x7, waiting for transfers between devices: 8 us -> 7.52 us  [the longest x1 3.61 us: shards(): cross = lax.ppermute(chip[2], 'lat', flip(lats, 2))]
    unnamed x20 -> x21, local copies, waits for them, and re-layouts: 1.14 us -> 1.04 us
  transfers between devices with their start and end apart: 20 -> 18, of which waited for: 13 -> 10; matrix products, arithmetic and copies ran while one was open for 0% -> 0% of each run, Pallas kernels for 4% -> 4%
where the time goes in v4:
time: 49.8 us; the launch traced here: 49.6 us
  starting transfers between devices  20.9 us (42%)
  waiting for transfers between devices  19.3 us (39%)
  Pallas kernels  7.29 us (15%)
  local copies, waits for them, and re-layouts  1.08 us (2%)
  between operations  0.87 us (2%)
    ppermute x1, waiting for transfers between devices, shards(): cross = lax.ppermute(chip[2], 'lat', flip(lats, 2))  3.61 us
    ppermute x1, waiting for transfers between devices, shards(): cross = lax.ppermute(energy, 'lat', flip(lats, 2))  3.58 us
    ppermute x3, starting transfers between devices, shards(): lax.ppermute(part, 'lat', flip(lats, step))  3.55 us
    ppermute x2, starting transfers between devices, shards(): far = lax.ppermute(packed, 'z', flip(chips, 3))  3.43 us
    ppermute x2, waiting for transfers between devices, shards(): far = lax.ppermute(packed, 'z', flip(chips, 3))  3.07 us
    ppermute x1, starting transfers between devices, shards(): lax.ppermute(jnp.concatenate([lat_a, energy], 0), 'lat', flip(lats, 1))  2.89 us
    ppermute x1, waiting for transfers between devices, shards(): cross = lax.ppermute(part, 'z', flip(chips, 2))  2.85 us
    ppermute x1, starting transfers between devices, shards(): cross = lax.ppermute(energy, 'z', flip(chips, 2))  2.65 us
  transfers between devices with their start and end apart: 18, of which 10 were waited for; matrix products, arithmetic and copies ran while one was open for 0% of the time, Pallas kernels for 4%

profile of v4, /device:TPU:0, one launch (start us, length us, event | category | flops | bytes accessed | tf_op | source)
XLA Modules:
  0.0 49.6 jit_solution(5852765626124769605)
XLA Ops:
  2.5 0.8 %collective-permute-done = f32[24,128]{1,0:T(8,128)S(1)} collective-permute-done((f32[24,128]{1,0:T(8,128)S(1)}, f32[24,128]{1,0:T(8,128)S(1)}, u32[]{:S(2)}, u32[]{:S(2)}) %collective-permute-start) | collective-permute-done | bytes 12320 | tf_op jit(solution)/shard_map/ppermute | solution.py:492
  3.4 2.9 %collective-permute-start.1 = (f32[112,128]{1,0:T(8,128)S(1)}, f32[112,128]{1,0:T(8,128)S(1)}, u32[]{:S(2)}, u32[]{:S(2)}) collective-permute-start(f32[112,128]{1,0:T(8,128)S(1)} %get-tuple-element.88), channel_id=1, source_target_pairs={{0,8},{8,0},{16,24},{24,16},{1,9},{9,1},{17,25},{25,17},{2,10},{10... | collective-permute-start | bytes 172040 | tf_op jit(solution)/shard_map/ppermute | solution.py:496
  6.3 1.5 %collective-permute-start.2 = (f32[112,128]{1,0:T(8,128)S(1)}, f32[112,128]{1,0:T(8,128)S(1)}, u32[]{:S(2)}, u32[]{:S(2)}) collective-permute-start(f32[112,128]{1,0:T(8,128)S(1)} %get-tuple-element.89), channel_id=1, source_target_pairs={{0,24},{8,16},{16,8},{24,0},{1,25},{9,17},{17,9},{25,1},{2,26},{10... | collective-permute-start | bytes 172040 | tf_op jit(solution)/shard_map/ppermute | solution.py:497
  7.8 3.6 %collective-permute-done.3 = f32[8,128]{1,0:T(8,128)S(1)} collective-permute-done((f32[8,128]{1,0:T(8,128)S(1)}, f32[8,128]{1,0:T(8,128)S(1)}, u32[]{:S(2)}, u32[]{:S(2)}) %collective-permute-start.3) | collective-permute-done | bytes 4128 | tf_op jit(solution)/shard_map/ppermute | solution.py:498
  11.4 2.7 %collective-permute-start.6 = (f32[8,128]{1,0:T(8,128)S(1)}, f32[8,128]{1,0:T(8,128)S(1)}, u32[]{:S(2)}, u32[]{:S(2)}) collective-permute-start(f32[8,128]{1,0:T(8,128)S(1)} %fusion.3), channel_id=1, source_target_pairs={{0,4},{2,6},{4,0},{6,2},{1,5},{3,7},{5,1},{7,3},{8,12},{10,14},{12... | collective-permute-start | bytes 12296 | tf_op jit(solution)/shard_map/ppermute | solution.py:508
  14.1 1.3 %collective-permute-start.5 = (f32[16,128]{1,0:T(8,128)S(1)}, f32[16,128]{1,0:T(8,128)S(1)}, u32[]{:S(2)}, u32[]{:S(2)}) collective-permute-start(f32[16,128]{1,0:T(8,128)S(1)} %pad_maximum_fusion.5), channel_id=1, source_target_pairs={{0,6},{2,4},{4,2},{6,0},{1,7},{3,5},{5,3},{7,1},{8,14},{10,12},{12... | collective-permute-start | bytes 24584 | tf_op jit(solution)/shard_map/ppermute | solution.py:507
  16.5 3.1 %collective-permute-done.5 = f32[16,128]{1,0:T(8,128)S(1)} collective-permute-done((f32[16,128]{1,0:T(8,128)S(1)}, f32[16,128]{1,0:T(8,128)S(1)}, u32[]{:S(2)}, u32[]{:S(2)}) %collective-permute-start.5) | collective-permute-done | bytes 8224 | tf_op jit(solution)/shard_map/ppermute | solution.py:507
  19.5 1.7 %shard_map.131 = (f32[1,128]{1,0:T(1,128)S(1)}, bf16[128,1024]{1,0:T(8,128)(2,1)S(1)}, bf16[512,1024]{1,0:T(8,128)(2,1)S(1)}, f32[512,1024]{1,0:T(8,128)S(1)}, f...) custom-call(f32[8,128]{1,0:T(8,128)S(1)} %get-tuple-element.85.refs_0_, ...), custom_call_target="tpu_custom_call" | custom-call | tf_op jit(solution)/shard_map/pallas_call | solution.py:536
  21.3 2.2 %shard_map.132 = (f32[4,104,128]{2,1,0:T(8,128)S(1)}, f32[432,128]{1,0:T(8,128)S(1)}, f32[800,128]{1,0:T(8,128)S(1)}, f32[104,128]{1,0:T(8,128)S(1)}, f32[104,12...) custom-call(f32[128,1024]{1,0:T(8,128)S(1)} %get-tuple-element.43.refs_4_.refs_0_.refs_3_, f32[800,128]{1,0:T(8,128)S(1)} %bitcast.24, ...), custom_call_target="tpu_custom_call" | custom-call | tf_op jit(solution)/shard_map/pallas_call | solution.py:552
  23.5 1.5 %collective-permute-done.7 = f32[432,128]{1,0:T(8,128)S(1)} collective-permute-done((f32[432,128]{1,0:T(8,128)S(1)}, f32[432,128]{1,0:T(8,128)S(1)}, u32[]{:S(2)}, u32[]{:S(2)}) %collective-permute-start.7) | collective-permute-done | bytes 221216 | tf_op jit(solution)/shard_map/ppermute | solution.py:574
  25.1 1.6 %collective-permute-start.9 = (f32[208,128]{1,0:T(8,128)S(1)}, f32[208,128]{1,0:T(8,128)S(1)}, u32[]{:S(2)}, u32[]{:S(2)}) collective-permute-start(f32[208,128]{1,0:T(8,128)S(1)} %pad_maximum_fusion.1), channel_id=1, source_target_pairs={{0,24},{8,16},{16,8},{24,0},{1,25},{9,17},{17,9},{25,1},{2,26},{10... | collective-permute-start | bytes 319496 | tf_op jit(solution)/shard_map/ppermute | solution.py:581
  26.7 1.4 %collective-permute-start.8 = (f32[208,128]{1,0:T(8,128)S(1)}, f32[208,128]{1,0:T(8,128)S(1)}, u32[]{:S(2)}, u32[]{:S(2)}) collective-permute-start(f32[208,128]{1,0:T(8,128)S(1)} %pad_maximum_fusion), channel_id=1, source_target_pairs={{0,8},{8,0},{16,24},{24,16},{1,9},{9,1},{17,25},{25,17},{2,10},{10... | collective-permute-start | bytes 319496 | tf_op jit(solution)/shard_map/ppermute | solution.py:580
  28.7 3.6 %collective-permute-done.10 = f32[104,128]{1,0:T(8,128)S(1)} collective-permute-done((f32[104,128]{1,0:T(8,128)S(1)}, f32[104,128]{1,0:T(8,128)S(1)}, u32[]{:S(2)}, u32[]{:S(2)}) %collective-permute-start.10) | collective-permute-done | bytes 53280 | tf_op jit(solution)/shard_map/ppermute | solution.py:582
  32.3 0.9 %collective-permute-done.8 = f32[208,128]{1,0:T(8,128)S(1)} collective-permute-done((f32[208,128]{1,0:T(8,128)S(1)}, f32[208,128]{1,0:T(8,128)S(1)}, u32[]{:S(2)}, u32[]{:S(2)}) %collective-permute-start.8) | collective-permute-done | bytes 106528 | tf_op jit(solution)/shard_map/ppermute | solution.py:580
  33.3 2.1 %collective-permute-start.12 = (f32[112,128]{1,0:T(8,128)S(1)}, f32[112,128]{1,0:T(8,128)S(1)}, u32[]{:S(2)}, u32[]{:S(2)}) collective-permute-start(f32[112,128]{1,0:T(8,128)S(1)} %pad_maximum_fusion.4), channel_id=1, source_target_pairs={{0,6},{2,4},{4,2},{6,0},{1,7},{3,5},{5,3},{7,1},{8,14},{10,12},{12... | collective-permute-start | bytes 172040 | tf_op jit(solution)/shard_map/ppermute | solution.py:596
  35.4 2.4 %collective-permute-start.13 = (f32[104,128]{1,0:T(8,128)S(1)}, f32[104,128]{1,0:T(8,128)S(1)}, u32[]{:S(2)}, u32[]{:S(2)}) collective-permute-start(f32[104,128]{1,0:T(8,128)S(1)} %get-tuple-element.77), channel_id=1, source_target_pairs={{0,4},{2,6},{4,0},{6,2},{1,5},{3,7},{5,1},{7,3},{8,12},{10,14},{12... | collective-permute-start | bytes 159752 | tf_op jit(solution)/shard_map/ppermute | solution.py:597
  37.8 2.8 %collective-permute-done.13 = f32[104,128]{1,0:T(8,128)S(1)} collective-permute-done((f32[104,128]{1,0:T(8,128)S(1)}, f32[104,128]{1,0:T(8,128)S(1)}, u32[]{:S(2)}, u32[]{:S(2)}) %collective-permute-start.13) | collective-permute-done | bytes 53280 | tf_op jit(solution)/shard_map/ppermute | solution.py:597
  40.7 1.6 %collective-permute-start.16 = (f32[104,128]{1,0:T(8,128)S(1)}, f32[104,128]{1,0:T(8,128)S(1)}, u32[]{:S(2)}, u32[]{:S(2)}) collective-permute-start(f32[104,128]{1,0:T(8,128)S(1)} %fusion.refs_1_), channel_id=1, source_target_pairs={{0,24},{8,16},{16,8},{24,0},{1,25},{9,17},{17,9},{25,1},{2,26},{10... | collective-permute-start | bytes 159752 | tf_op jit(solution)/shard_map/ppermute | solution.py:620
  42.3 0.8 %collective-permute-start.15 = (f32[104,128]{1,0:T(8,128)S(1)}, f32[104,128]{1,0:T(8,128)S(1)}, u32[]{:S(2)}, u32[]{:S(2)}) collective-permute-start(f32[104,128]{1,0:T(8,128)S(1)} %fusion.refs_1_), channel_id=1, source_target_pairs={{0,16},{8,24},{16,0},{24,8},{1,17},{9,25},{17,1},{25,9},{2,18},{10... | collective-permute-start | bytes 159752 | tf_op jit(solution)/shard_map/ppermute | solution.py:620
  43.1 1.1 %collective-permute-start.14 = (f32[104,128]{1,0:T(8,128)S(1)}, f32[104,128]{1,0:T(8,128)S(1)}, u32[]{:S(2)}, u32[]{:S(2)}) collective-permute-start(f32[104,128]{1,0:T(8,128)S(1)} %fusion.refs_1_), channel_id=1, source_target_pairs={{0,8},{8,0},{16,24},{24,16},{1,9},{9,1},{17,25},{25,17},{2,10},{10... | collective-permute-start | bytes 159752 | tf_op jit(solution)/shard_map/ppermute | solution.py:620
  44.2 1.5 %shard_map.133 = f32[800,128]{1,0:T(8,128)} custom-call(f32[1,128]{1,0:T(1,128)S(1)} %get-tuple-element.61.refs_0_, f32[104,128]{1,0:T(8,128)S(1)} %fusion.refs_1_, f32[800,128]{1,0:T(8,128)S(1)} %get-tuple-element.62.refs_2_, f32[128,1024]{1,0:T(8,128)S(1)} %get-tuple-element.43.refs_4_.refs_0_.refs_3_, f32[8,104,128]{2,1,0:T(8,128)S(1)} %get-tuple-element.63.refs_4_, ...), custom_call_target="tpu_custom_call" | custom-call | tf_op jit(solution)/shard_map/pallas_call | solution.py:609
  46.4 0.8 %collective-permute-done.14 = f32[104,128]{1,0:T(8,128)S(1)} collective-permute-done((f32[104,128]{1,0:T(8,128)S(1)}, f32[104,128]{1,0:T(8,128)S(1)}, u32[]{:S(2)}, u32[]{:S(2)}) %collective-permute-start.14) | collective-permute-done | bytes 53280 | tf_op jit(solution)/shard_map/ppermute | solution.py:620
  47.3 1.5 %collective-permute-done.17.refs_1_ = f32[416,128]{1,0:T(8,128)S(1)} collective-permute-done((f32[416,128]{1,0:T(8,128)S(1)}, f32[416,128]{1,0:T(8,128)S(1)}, u32[]{:S(2)}, u32[]{:S(2)}) %collective-permute-start.17) | collective-permute-done | bytes 213024 | tf_op jit(solution)/shard_map/ppermute | solution.py:623
  48.8 0.8 %shard_map.134 = (f32[100,512]{1,0:T(8,128)}, f32[1,512]{1,0:T(1,128)}, f32[100,512]{1,0:T(8,128)}, f32[1,100]{1,0:T(1,128)}) custom-call(f32[416,128]{1,0:T(8,128)S(1)} %constant_dynamic-update-slice_fusion.refs_0_, f32[416,128]{1,0:T(8,128)S(1)} %collective-permute-done.17.refs_1_), custom_call_target="tpu_custom_call" | custom-call | tf_op jit(solution)/shard_map/pallas_call | solution.py:624
  (57 shorter events, 4.5 us)
Async XLA Ops:
  1.7 14.0 %copy-start.2 = (bf16[100,512]{1,0:T(8,128)(2,1)S(1)}, bf16[100,512]{1,0:T(8,128)(2,1)}, u32[]{:S(2)}) copy-start(bf16[100,512]{1,0:T(8,128)(2,1)} %refs_4_.1) | copy-start | bytes 307204
  1.7 14.0 %copy-start.3 = (bf16[512,100]{0,1:T(8,128)(2,1)S(1)}, bf16[512,100]{0,1:T(8,128)(2,1)}, u32[]{:S(2)}) copy-start(bf16[512,100]{0,1:T(8,128)(2,1)} %param.16) | copy-start | bytes 307204
  1.7 14.0 %copy-start.6 = (f32[512]{0:T(512)S(1)}, f32[512]{0:T(512)}, u32[]{:S(2)}) copy-start(f32[512]{0:T(512)} %param.15) | copy-start | bytes 6148
  1.7 14.0 %copy-start.7 = (f32[100]{0:T(128)S(1)}, f32[100]{0:T(128)}, u32[]{:S(2)}) copy-start(f32[100]{0:T(128)} %param.17) | copy-start | bytes 1204
  1.7 14.0 %copy-start.8 = (f32[100]{0:T(128)S(1)}, f32[100]{0:T(128)}, u32[]{:S(2)}) copy-start(f32[100]{0:T(128)} %param.13) | copy-start | bytes 1204
  2.1 1.3 %collective-permute-start = (f32[24,128]{1,0:T(8,128)S(1)}, f32[24,128]{1,0:T(8,128)S(1)}, u32[]{:S(2)}, u32[]{:S(2)}) collective-permute-start(f32[24,128]{1,0:T(8,128)S(1)} %get-tuple-element.41), channel_id=1, source_target_pairs={{0,1},{1,0},{2,3},{3,2},{4,5},{5,4},{6,7},{7,6},{8,9},{9,8},{10,11... | collective-permute-start | bytes 36872 | tf_op jit(solution)/shard_map/ppermute | solution.py:492
  3.4 8.0 %collective-permute-start.1 = (f32[112,128]{1,0:T(8,128)S(1)}, f32[112,128]{1,0:T(8,128)S(1)}, u32[]{:S(2)}, u32[]{:S(2)}) collective-permute-start(f32[112,128]{1,0:T(8,128)S(1)} %get-tuple-element.88), channel_id=1, source_target_pairs={{0,8},{8,0},{16,24},{24,16},{1,9},{9,1},{17,25},{25,17},{2,10},{10... | collective-permute-start | bytes 172040 | tf_op jit(solution)/shard_map/ppermute | solution.py:496
  6.3 5.1 %collective-permute-start.2 = (f32[112,128]{1,0:T(8,128)S(1)}, f32[112,128]{1,0:T(8,128)S(1)}, u32[]{:S(2)}, u32[]{:S(2)}) collective-permute-start(f32[112,128]{1,0:T(8,128)S(1)} %get-tuple-element.89), channel_id=1, source_target_pairs={{0,24},{8,16},{16,8},{24,0},{1,25},{9,17},{17,9},{25,1},{2,26},{10... | collective-permute-start | bytes 172040 | tf_op jit(solution)/shard_map/ppermute | solution.py:497
  7.8 3.6 %collective-permute-start.3 = (f32[8,128]{1,0:T(8,128)S(1)}, f32[8,128]{1,0:T(8,128)S(1)}, u32[]{:S(2)}, u32[]{:S(2)}) collective-permute-start(f32[8,128]{1,0:T(8,128)S(1)} %get-tuple-element.87), channel_id=1, source_target_pairs={{0,16},{8,24},{16,0},{24,8},{1,17},{9,25},{17,1},{25,9},{2,18},{10... | collective-permute-start | bytes 12296 | tf_op jit(solution)/shard_map/ppermute | solution.py:498
  11.4 5.0 %collective-permute-start.6 = (f32[8,128]{1,0:T(8,128)S(1)}, f32[8,128]{1,0:T(8,128)S(1)}, u32[]{:S(2)}, u32[]{:S(2)}) collective-permute-start(f32[8,128]{1,0:T(8,128)S(1)} %fusion.3), channel_id=1, source_target_pairs={{0,4},{2,6},{4,0},{6,2},{1,5},{3,7},{5,1},{7,3},{8,12},{10,14},{12... | collective-permute-start | bytes 12296 | tf_op jit(solution)/shard_map/ppermute | solution.py:508
  14.1 5.4 %collective-permute-start.5 = (f32[16,128]{1,0:T(8,128)S(1)}, f32[16,128]{1,0:T(8,128)S(1)}, u32[]{:S(2)}, u32[]{:S(2)}) collective-permute-start(f32[16,128]{1,0:T(8,128)S(1)} %pad_maximum_fusion.5), channel_id=1, source_target_pairs={{0,6},{2,4},{4,2},{6,0},{1,7},{3,5},{5,3},{7,1},{8,14},{10,12},{12... | collective-permute-start | bytes 24584 | tf_op jit(solution)/shard_map/ppermute | solution.py:507
  15.4 4.1 %collective-permute-start.4 = (f32[16,128]{1,0:T(8,128)S(1)}, f32[16,128]{1,0:T(8,128)S(1)}, u32[]{:S(2)}, u32[]{:S(2)}) collective-permute-start(f32[16,128]{1,0:T(8,128)S(1)} %pad_maximum_fusion.5), channel_id=1, source_target_pairs={{0,2},{2,0},{4,6},{6,4},{1,3},{3,1},{5,7},{7,5},{8,10},{10,8},{12,... | collective-permute-start | bytes 24584 | tf_op jit(solution)/shard_map/ppermute | solution.py:506
  15.7 5.5 %copy-start.1 = (f32[100,8,128]{2,1,0:T(8,128)S(1)}, f32[100,8,128]{2,1,0:T(8,128)}, u32[]{:S(2)}) copy-start(f32[100,8,128]{2,1,0:T(8,128)} %param.10) | copy-start | bytes 1228804
  23.5 1.5 %collective-permute-start.7 = (f32[432,128]{1,0:T(8,128)S(1)}, f32[432,128]{1,0:T(8,128)S(1)}, u32[]{:S(2)}, u32[]{:S(2)}) collective-permute-start(f32[432,128]{1,0:T(8,128)S(1)} %get-tuple-element.58), channel_id=1, source_target_pairs={{0,1},{1,0},{2,3},{3,2},{4,5},{5,4},{6,7},{7,6},{8,9},{9,8},{10,11... | collective-permute-start | bytes 663560 | tf_op jit(solution)/shard_map/ppermute | solution.py:574
  25.1 7.2 %collective-permute-start.9 = (f32[208,128]{1,0:T(8,128)S(1)}, f32[208,128]{1,0:T(8,128)S(1)}, u32[]{:S(2)}, u32[]{:S(2)}) collective-permute-start(f32[208,128]{1,0:T(8,128)S(1)} %pad_maximum_fusion.1), channel_id=1, source_target_pairs={{0,24},{8,16},{16,8},{24,0},{1,25},{9,17},{17,9},{25,1},{2,26},{10... | collective-permute-start | bytes 319496 | tf_op jit(solution)/shard_map/ppermute | solution.py:581
  26.7 6.6 %collective-permute-start.8 = (f32[208,128]{1,0:T(8,128)S(1)}, f32[208,128]{1,0:T(8,128)S(1)}, u32[]{:S(2)}, u32[]{:S(2)}) collective-permute-start(f32[208,128]{1,0:T(8,128)S(1)} %pad_maximum_fusion), channel_id=1, source_target_pairs={{0,8},{8,0},{16,24},{24,16},{1,9},{9,1},{17,25},{25,17},{2,10},{10... | collective-permute-start | bytes 319496 | tf_op jit(solution)/shard_map/ppermute | solution.py:580
  28.1 4.2 %collective-permute-start.10 = (f32[104,128]{1,0:T(8,128)S(1)}, f32[104,128]{1,0:T(8,128)S(1)}, u32[]{:S(2)}, u32[]{:S(2)}) collective-permute-start(f32[104,128]{1,0:T(8,128)S(1)} %get-tuple-element.79), channel_id=1, source_target_pairs={{0,16},{8,24},{16,0},{24,8},{1,17},{9,25},{17,1},{25,9},{2,18},{10... | collective-permute-start | bytes 159752 | tf_op jit(solution)/shard_map/ppermute | solution.py:582
  33.3 7.3 %collective-permute-start.12 = (f32[112,128]{1,0:T(8,128)S(1)}, f32[112,128]{1,0:T(8,128)S(1)}, u32[]{:S(2)}, u32[]{:S(2)}) collective-permute-start(f32[112,128]{1,0:T(8,128)S(1)} %pad_maximum_fusion.4), channel_id=1, source_target_pairs={{0,6},{2,4},{4,2},{6,0},{1,7},{3,5},{5,3},{7,1},{8,14},{10,12},{12... | collective-permute-start | bytes 172040 | tf_op jit(solution)/shard_map/ppermute | solution.py:596
  35.4 5.2 %collective-permute-start.11 = (f32[112,128]{1,0:T(8,128)S(1)}, f32[112,128]{1,0:T(8,128)S(1)}, u32[]{:S(2)}, u32[]{:S(2)}) collective-permute-start(f32[112,128]{1,0:T(8,128)S(1)} %pad_maximum_fusion.4), channel_id=1, source_target_pairs={{0,2},{2,0},{4,6},{6,4},{1,3},{3,1},{5,7},{7,5},{8,10},{10,8},{12,... | collective-permute-start | bytes 172040 | tf_op jit(solution)/shard_map/ppermute | solution.py:595
  35.4 5.2 %collective-permute-start.13 = (f32[104,128]{1,0:T(8,128)S(1)}, f32[104,128]{1,0:T(8,128)S(1)}, u32[]{:S(2)}, u32[]{:S(2)}) collective-permute-start(f32[104,128]{1,0:T(8,128)S(1)} %get-tuple-element.77), channel_id=1, source_target_pairs={{0,4},{2,6},{4,0},{6,2},{1,5},{3,7},{5,1},{7,3},{8,12},{10,14},{12... | collective-permute-start | bytes 159752 | tf_op jit(solution)/shard_map/ppermute | solution.py:597
  40.7 5.1 %collective-permute-start.16 = (f32[104,128]{1,0:T(8,128)S(1)}, f32[104,128]{1,0:T(8,128)S(1)}, u32[]{:S(2)}, u32[]{:S(2)}) collective-permute-start(f32[104,128]{1,0:T(8,128)S(1)} %fusion.refs_1_), channel_id=1, source_target_pairs={{0,24},{8,16},{16,8},{24,0},{1,25},{9,17},{17,9},{25,1},{2,26},{10... | collective-permute-start | bytes 159752 | tf_op jit(solution)/shard_map/ppermute | solution.py:620
  42.3 4.1 %collective-permute-start.15 = (f32[104,128]{1,0:T(8,128)S(1)}, f32[104,128]{1,0:T(8,128)S(1)}, u32[]{:S(2)}, u32[]{:S(2)}) collective-permute-start(f32[104,128]{1,0:T(8,128)S(1)} %fusion.refs_1_), channel_id=1, source_target_pairs={{0,16},{8,24},{16,0},{24,8},{1,17},{9,25},{17,1},{25,9},{2,18},{10... | collective-permute-start | bytes 159752 | tf_op jit(solution)/shard_map/ppermute | solution.py:620
  43.1 4.1 %collective-permute-start.14 = (f32[104,128]{1,0:T(8,128)S(1)}, f32[104,128]{1,0:T(8,128)S(1)}, u32[]{:S(2)}, u32[]{:S(2)}) collective-permute-start(f32[104,128]{1,0:T(8,128)S(1)} %fusion.refs_1_), channel_id=1, source_target_pairs={{0,8},{8,0},{16,24},{24,16},{1,9},{9,1},{17,25},{25,17},{2,10},{10... | collective-permute-start | bytes 159752 | tf_op jit(solution)/shard_map/ppermute | solution.py:620
  47.3 1.5 %collective-permute-start.17 = (f32[416,128]{1,0:T(8,128)S(1)}, f32[416,128]{1,0:T(8,128)S(1)}, u32[]{:S(2)}, u32[]{:S(2)}) collective-permute-start(f32[416,128]{1,0:T(8,128)S(1)} %constant_dynamic-update-slice_fusion.refs_0_), channel_id=1, source_target_pairs={{0,1},{1,0},{2,3},{3,2},{4,5},{5,4},{6,7},{7,6},{8,9},{9,8},{10,11... | collective-permute-start | bytes 638984 | tf_op jit(solution)/shard_map/ppermute | solution.py:623
  (3 other events, 2.4 us)

commit v5 on v4

--- a/solution.py
+++ b/solution.py
@@ -139,34 +139,35 @@
     out[...] = jnp.zeros(out.shape, f32)
 
 
-def energy_kernel(levels, zero, tracer, mask, bottom, small, lat_a, lat_b, depth_out, pad):
-    rows, cols = mask.shape
+def edge_kernel(levels, tracer, mask, bottom, small, lat_a, lat_b, depth_out, pad):
+    rows = mask.shape[0]
     depth = (mask[...] * bottom[...]).astype(f32)
     depth_out[...] = depth
+    lat_odd, lon_odd = odd_places()
+    lon_a, lon_b = small.at[0:rows, :], small.at[rows:, :]
+    write_lon_edges(tracer, levels, rows, pad, lon_a, lon_b, lon_odd, depth)
+    write_lat_edges(tracer, levels, rows, lat_a, lat_b, lat_odd, depth)
+
+
+def energy_kernel(levels, tracer, depth_ref, energy, pad):
+    rows, cols = depth_ref.shape
+    depth = depth_ref[...]
     lev = level_ids((levels, cols))
     total = jnp.zeros((levels, cols), f32)
     for row in range(rows):
         wet_tracer = jnp.where(lev < depth[row : row + 1, :], row_of(tracer, row, levels, rows), 0.0)
         total = total + wet_tracer * wet_tracer
-    small[2 * rows :, :] = zero[...] + lane_sums(pad, total)
-    lat_odd, lon_odd = odd_places()
-    lon_a, lon_b = small.at[0:rows, :], small.at[rows : 2 * rows, :]
-    write_lon_edges(tracer, levels, rows, pad, lon_a, lon_b, lon_odd, depth)
-    write_lat_edges(tracer, levels, rows, lat_a, lat_b, lat_odd, depth)
+    energy[...] = jnp.broadcast_to(lane_sums(pad, total)[None], energy.shape)
 
 
 def prepare_kernel(
-    levels, tracer, depth_ref, north, south, w_in, b_in, w_out_t, b_out, kappa,
-    inner, wet_tracer, wi_t, wi_b, wo_t, wo_b, bias, up_out,
+    levels, tracer, depth_ref, w_in, b_in, w_out_t, b_out, kappa,
+    wet_tracer, wi_t, wi_b, wo_t, wo_b, bias, up_out,
     pad, wi_f, wo_f,
 ):
     rows, cols = depth_ref.shape
     pad_levels, span = wet_tracer.shape
     depth = depth_ref[...]
-    blank = jnp.zeros((levels, cols), f32)
-    dry = jnp.zeros((rows, cols), f32)
-    halos = (north[0:levels, :], south[0:levels, :], blank, blank)
-    depths = halo_depths(levels, north, south, dry, dry, dry.shape)[0:2] + (dry, dry)
     wet_tracer[levels:, :] = jnp.where(
         lax.broadcasted_iota(jnp.int32, (pad_levels - levels, span), 0) < 3, 1.0, 0.0
     )
@@ -177,10 +178,10 @@
     bias[...] = jnp.broadcast_to(turned[:, 0:1], bias.shape)
     kappa_col = jnp.broadcast_to(turned[0:levels, 1:2], (levels, cols))
     lev = level_ids((levels, cols))
-    for row, center, wet, value in spread_rows(tracer, depth, levels, rows, halos, depths):
+    for row in range(rows):
         at = pl.ds(row, levels, stride=rows)
-        inner[at, :] = value
-        wet_tracer[0:levels, row * cols : (row + 1) * cols] = wet * center
+        wet = (lev < depth[row : row + 1, :]).astype(f32)
+        wet_tracer[0:levels, row * cols : (row + 1) * cols] = wet * row_of(tracer, row, levels, rows)
         open_face = (lev + 1.0 < depth[row : row + 1, :]) & (lev + 1.0 < float(levels))
         up_out[at, :] = jnp.where(open_face, kappa_col, 0.0)
 
@@ -204,14 +205,12 @@
 
 
 def network_kernel(
-    levels, column_count, energy, tracer, depth_ref, inner, wet_tracer, wi_t, wo_t, bias, up, west_ref, east_ref,
-    radius_row, x_b, hidden, slope, gate, down_out, mixed,
+    levels, rows, column_count, energy, wet_tracer, wi_t, wo_t, bias, up,
+    radius_row, x_b, hidden, slope, gate, down_out,
 ):
-    rows, cols = depth_ref.shape
+    cols = bias.shape[1]
     hid = wi_t.shape[0]
-    depth = depth_ref[...]
-    lev = level_ids((levels, cols))
-    radius_line = jnp.sqrt(energy[0:1, :] / column_count + level_eps)
+    radius_line = jnp.sqrt(jnp.sum(energy[...], axis=0) / column_count + level_eps)
     radius_row[...] = radius_line
     scale = columns_of(jnp.where(lane_ids(radius_line.shape) < levels, 1.0 / radius_line, 1.0), cols)
     for row in range(rows):
@@ -236,39 +235,24 @@
         face_up = row_of(up, row, levels, rows)
         down_out[at, :] = jnp.where(face_up > 0.0, face_up + soft[0:levels, :], 0.0)
 
-    lanes = lane_ids((levels, cols))
-    west, east = west_ref[...], east_ref[...]
-    west_cols, east_cols = turn(west, levels), turn(east, levels)
-    for row in range(rows):
-        near = jnp.where(
-            lanes == 0,
-            pltpu.roll(west_cols, (cols - row) % cols, 1) if row else west_cols,
-            pltpu.roll(east_cols, cols - 1 - row, 1),
-        )
-        level_depth = depth[row : row + 1, :]
-        level_depth = jnp.minimum(
-            level_depth,
-            jnp.where(
-                lanes[0:1, :] == 0, jnp.broadcast_to(west[row : row + 1, levels : levels + 1], (1, cols)),
-                jnp.broadcast_to(east[row : row + 1, levels : levels + 1], (1, cols)),
-            ),
-        )
-        both = (lev < level_depth) & ((lanes == 0) | (lanes == cols - 1))
-        flux = jnp.where(both, near - row_of(tracer, row, levels, rows), 0.0)
-        mixed[pl.ds(row, levels, stride=rows), :] = row_of(inner, row, levels, rows) + spread_coef * flux
-
 
 def solve_kernel(
     levels, scale,
-    wet_tracer, cotangent, depth_ref, up_ref, down_ref, mixed, wo_b, wi_b, x_b, hidden, slope, gate,
+    tracer, north, south, west, east, wet_tracer, cotangent, depth_ref, up_ref, down_ref,
+    wo_b, wi_b, x_b, hidden, slope, gate,
     keep, send, adjoint, lat_a, lat_b, d_inputs,
-    pad, dl_f, dl_b, dp_b, rate_a, rate_b, inv_p, fwd_z, fwd_u, flow,
+    pad, mixed, dl_f, dl_b, dp_b, rate_a, rate_b, inv_p, fwd_z, fwd_u, flow,
 ):
     rows, cols = depth_ref.shape
     hid = wo_b.shape[0]
     span = rows * cols
     pad_levels = dl_f.shape[0]
     depth = depth_ref[...]
+    halos = halo_values(levels, north, south, west, east)
+    depth_halos = halo_depths(levels, north, south, west, east, depth.shape)
+    for row, _, _, value in spread_rows(tracer, depth, levels, rows, halos, depth_halos):
+        mixed[pl.ds(row, levels, stride=rows), :] = value
+
     def at_level(k):
         return slice(k * rows, (k + 1) * rows)
 
@@ -442,7 +426,7 @@
     return in_order(
         lat_odd,
         lax.ppermute(lat_a, "lat", flip(lats, 1)),
-        lax.ppermute(lat_b, "lat", far_pairs(lats, False)),
+        lax.ppermute(lat_b, "lat", far_pairs(lats, True)),
     )
 
 
@@ -476,9 +460,9 @@
         cost_estimate=ahead,
     )()
     small, lat_a, lat_b, depth = pl.pallas_call(
-        lambda *refs: energy_kernel(levels, *refs),
+        lambda zero, *refs: edge_kernel(levels, *refs),
         out_shape=[
-            sds((3 * rows, pad_levels), f32),
+            sds((2 * rows, pad_levels), f32),
             lat_edge,
             lat_edge,
             sds((rows, cols), f32),
@@ -487,37 +471,29 @@
         out_specs=[vmem] * 4,
         scratch_shapes=[pad],
         compiler_params=params,
+    )(zero, tracer, land_mask, bottom)
+    energy = pl.pallas_call(
+        lambda *refs: energy_kernel(levels, *refs),
+        out_shape=sds((lats * lons, 1, pad_levels), f32),
+        in_specs=[vmem] * 2,
+        out_specs=vmem,
+        scratch_shapes=[pad],
+        compiler_params=params,
         cost_estimate=ahead,
-    )(zero, tracer, land_mask, bottom)
-    got = lax.ppermute(small, "core", flip(2, 1))
-    energy = small[2 * rows :] + got[2 * rows :]
-    t_near, t_pass = got[:rows], got[rows : 2 * rows]
-    if lats == 4:
-        near = lax.ppermute(jnp.concatenate([lat_a, energy], 0), "lat", flip(lats, 1))
-        far = lax.ppermute(jnp.concatenate([lat_b, energy], 0), "lat", flip(lats, 3))
-        cross = lax.ppermute(energy, "lat", flip(lats, 2))
-        t_north, t_south = in_order(lat_odd, near[:height], far[:height])
-        energy = energy + near[height:] + far[height:] + cross
-    else:
-        t_north, t_south = swap_lat(lat_odd, lats, lat_a, lat_b)
-        energy = lax.psum(energy, "lat")
-    if chips == 4:
-        packed = jnp.concatenate([energy, t_pass], 0)
-        near = lax.ppermute(packed, "z", flip(chips, 1))
-        far = lax.ppermute(packed, "z", flip(chips, 3))
-        cross = lax.ppermute(energy, "z", flip(chips, 2))
-        energy = energy + near[:rows] + far[:rows] + cross
-        t_far = jnp.where(from_near, near[rows:], far[rows:])
-    else:
-        energy = lax.psum(energy, "z")
-        t_far = lax.ppermute(small[rows : 2 * rows], ("z", "core"), far_pairs(lons, True))
-    t_west, t_east = in_order(lon_odd, t_near, t_far)
-
+    )(tracer, depth)
+    energy = lax.all_to_all(energy, ("lat", "z", "core"), 0, 0, tiled=True)
+    t_west, t_east = in_order(
+        lon_odd,
+        lax.ppermute(small[:rows], ("z", "core"), flip(lons, 1)),
+        lax.ppermute(small[rows:], ("z", "core"), far_pairs(lons, True)),
+    )
+    t_north, t_south = swap_lat(lat_odd, lats, lat_a, lat_b)
+
+    flat_scratch = pltpu.VMEM(flat, f32)
     wide = sds((pad_levels, span), f32)
-    inner, wet_tracer, wi_t, wi_b, wo_t, wo_b, bias, up = pl.pallas_call(
+    wet_tracer, wi_t, wi_b, wo_t, wo_b, bias, up = pl.pallas_call(
         lambda *refs: prepare_kernel(levels, *refs),
         out_shape=[
-            sds(flat, f32),
             wide,
             sds((hid, pad_levels), bf16),
             sds((pad_levels, hid), bf16),
@@ -526,15 +502,15 @@
             sds((pad_levels, cols), f32),
             sds(flat, f32),
         ],
-        in_specs=[vmem] * 9,
-        out_specs=[vmem] * 8,
+        in_specs=[vmem] * 7,
+        out_specs=[vmem] * 7,
         scratch_shapes=[pad] + [pltpu.VMEM((pad_levels, hid), f32)] * 2,
         compiler_params=params,
         cost_estimate=ahead,
-    )(tracer, depth, t_north, t_south, w_in, b_in, w_out_t, b_out, kappa)
-
-    radius_row, x_b, hidden, slope, gate, down, mixed = pl.pallas_call(
-        lambda *refs: network_kernel(levels, column_count, *refs),
+    )(tracer, depth, w_in, b_in, w_out_t, b_out, kappa)
+
+    radius_row, x_b, hidden, slope, gate, down = pl.pallas_call(
+        lambda *refs: network_kernel(levels, rows, column_count, *refs),
         out_shape=[
             sds((1, pad_levels), f32),
             sds((pad_levels, span), bf16),
@@ -542,12 +518,11 @@
             sds((hid, span), f32),
             wide,
             sds(flat, f32),
-            sds(flat, f32),
         ],
-        in_specs=[vmem] * 11,
-        out_specs=[vmem] * 7,
+        in_specs=[vmem] * 6,
+        out_specs=[vmem] * 6,
         compiler_params=params,
-    )(energy, tracer, depth, inner, wet_tracer, wi_t, wo_t, bias, up, t_west, t_east)
+    )(energy, wet_tracer, wi_t, wo_t, bias, up)
 
     keep, send, adjoint, lat_a, lat_b, d_inputs = pl.pallas_call(
         lambda *refs: solve_kernel(levels, 1.0 / math.sqrt(column_count), *refs),
@@ -559,17 +534,21 @@
             lat_edge,
             sds((rows, height, cols), f32),
         ],
-        in_specs=[vmem] * 12,
+        in_specs=[vmem] * 16,
         out_specs=[vmem] * 6,
         scratch_shapes=[
             pad,
+            flat_scratch,
             pltpu.VMEM((pad_levels, span), f32),
             pltpu.VMEM((pad_levels, span), bf16),
             pltpu.VMEM((hid, span), bf16),
-            *[pltpu.VMEM(flat, f32)] * 6,
+            *[flat_scratch] * 6,
         ],
         compiler_params=params,
-    )(wet_tracer, cotangent, depth, up, down, mixed, wo_b, wi_b, x_b, hidden, slope, gate)
+    )(
+        tracer, t_north, t_south, t_west, t_east, wet_tracer, cotangent, depth, up, down,
+        wo_b, wi_b, x_b, hidden, slope, gate,
+    )
 
     got = lax.ppermute(send, "core", flip(2, 1))
     chip = keep + got[: 4 * height].reshape(keep.shape)

time: 49.8 us -> 47.6 us (0.956)
  waiting for transfers between devices: 19.3 us -> 14.5 us
  starting transfers between devices: 20.9 us -> 23.1 us
  Pallas kernels: 7.29 us -> 7.79 us
    ppermute x5 -> x4, waiting for transfers between devices: 4.42 us -> 0.01 us  [the longest x1 0.01 us: shards(): lax.ppermute(small[:rows], ('z', 'core'), flip(lons, 1))]
    all_to_all x0 -> x1, starting transfers between devices: none -> 3.48 us  [shards(): energy = lax.all_to_all(energy, ('lat', 'z', 'core'), 0, 0, tiled=True)]
    all_to_all x0 -> x1, waiting for transfers between devices: none -> 3.34 us  [shards(): energy = lax.all_to_all(energy, ('lat', 'z', 'core'), 0, 0, tiled=True)]
    ppermute x2 -> x1, waiting for transfers between devices: 3.07 us -> 0.01 us  [shards(): far = lax.ppermute(packed, 'z', flip(chips, 3))]
    ppermute x1, starting transfers between devices: 1.55 us -> 0.66 us  [shards(): lax.ppermute(jnp.concatenate([chip[3], lat_b], 0), 'lat', flip(lats, 3))]
    ppermute x2 -> x1, starting transfers between devices: 3.43 us -> 2.56 us  [shards(): far = lax.ppermute(packed, 'z', flip(chips, 3))]
    ppermute x1, starting transfers between devices: 0.62 us -> 1.43 us  [shards(): cross = lax.ppermute(chip[2], 'lat', flip(lats, 2))]
    ppermute x1, waiting for transfers between devices: 0.95 us -> 0.27 us  [shards(): lax.ppermute(jnp.concatenate([chip[1], lat_a], 0), 'lat', flip(lats, 1))]
  transfers between devices with their start and end apart: 18 -> 16, of which waited for: 10 -> 9; matrix products, arithmetic and copies ran while one was open for 0% -> 0% of each run, Pallas kernels for 4% -> 9%
where the time goes in v5:
time: 47.6 us; the launch traced here: 47.4 us
  starting transfers between devices  23.1 us (49%)
  waiting for transfers between devices  14.5 us (30%)
  Pallas kernels  7.79 us (16%)
  local copies, waits for them, and re-layouts  1.03 us (2%)
  between operations  0.91 us (2%)
    ppermute x1, starting transfers between devices, shards(): lax.ppermute(small[rows:], ('z', 'core'), far_pairs(lons, True))  4.53 us
    ppermute x3, starting transfers between devices, shards(): lax.ppermute(part, 'lat', flip(lats, step))  3.55 us
    all_to_all x1, starting transfers between devices, shards(): energy = lax.all_to_all(energy, ('lat', 'z', 'core'), 0, 0, tiled=True)  3.48 us
    ppermute x1, waiting for transfers between devices, shards(): cross = lax.ppermute(chip[2], 'lat', flip(lats, 2))  3.48 us
    all_to_all x1, waiting for transfers between devices, shards(): energy = lax.all_to_all(energy, ('lat', 'z', 'core'), 0, 0, tiled=True)  3.34 us
    ppermute x1, waiting for transfers between devices, shards(): cross = lax.ppermute(part, 'z', flip(chips, 2))  3.32 us
    ppermute x1, starting transfers between devices, shards(): far = lax.ppermute(packed, 'z', flip(chips, 3))  2.56 us
    pallas_call x1, Pallas kernels, shards(): pl.pallas_call(lambda *refs: solve_kernel(levels, 1.0 / math.sqrt(column_...  2.53 us
  transfers between devices with their start and end apart: 16, of which 9 were waited for; matrix products, arithmetic and copies ran while one was open for 0% of the time, Pallas kernels for 9%

profile of v5, /device:TPU:0, one launch (start us, length us, event | category | flops | bytes accessed | tf_op | source)
XLA Modules:
  0.0 47.4 jit_solution(17399326483081704587)
XLA Ops:
  0.7 0.6 %copy-done.3 = s32[8,128]{1,0:T(8,128)S(1)} copy-done((s32[8,128]{1,0:T(8,128)S(1)}, s32[8,128]{1,0:T(8,128)}, u32[]{:S(2)}) %copy-start.3) | copy-done | bytes 4120
  2.0 4.5 %collective-permute-start.3 = (f32[8,128]{1,0:T(8,128)S(1)}, f32[8,128]{1,0:T(8,128)S(1)}, u32[]{:S(2)}, u32[]{:S(2)}) collective-permute-start(f32[8,128]{1,0:T(8,128)S(1)} %get-tuple-element.81), channel_id=1, source_target_pairs={{1,2},{3,4},{5,6},{7,0},{2,1},{4,3},{6,5},{0,7},{9,10},{11,12},{13... | collective-permute-start | bytes 12296 | tf_op jit(solution)/shard_map/ppermute | solution.py:488
  6.5 0.8 %shard_map.131 = f32[32,1,128]{2,1,0:T(1,128)} custom-call(f32[800,128]{1,0:T(8,128)S(1)} %bitcast.22, f32[8,128]{1,0:T(8,128)S(1)} %get-tuple-element.40.refs_1_.refs_7_.refs_5_), custom_call_target="tpu_custom_call" | custom-call | flops 1000000000 | bytes 100000000 | tf_op jit(solution)/shard_map/pallas_call | solution.py:475
  7.3 3.5 %all-to-all-start = ((f32[32,1,128]{2,1,0:T(1,128)}), f32[32,1,128]{2,1,0:T(1,128)S(1)}, u32[]{:S(2)}, u32[]{:S(2)}) async-start(f32[32,1,128]{2,1,0:T(1,128)} %shard_map.131), calls=%async_computation | async-start | bytes 32768 | tf_op jit(solution)/shard_map/all_to_all | solution.py:484
  10.8 1.8 %collective-permute-start = (f32[104,128]{1,0:T(8,128)S(1)}, f32[104,128]{1,0:T(8,128)S(1)}, u32[]{:S(2)}, u32[]{:S(2)}) collective-permute-start(f32[104,128]{1,0:T(8,128)S(1)} %get-tuple-element.37), channel_id=1, source_target_pairs={{0,8},{8,0},{16,24},{24,16},{1,9},{9,1},{17,25},{25,17},{2,10},{10... | collective-permute-start | bytes 159752 | tf_op jit(solution)/shard_map/ppermute | solution.py:428
  12.6 1.5 %collective-permute-start.1 = (f32[104,128]{1,0:T(8,128)S(1)}, f32[104,128]{1,0:T(8,128)S(1)}, u32[]{:S(2)}, u32[]{:S(2)}) collective-permute-start(f32[104,128]{1,0:T(8,128)S(1)} %get-tuple-element.38), channel_id=1, source_target_pairs={{8,16},{24,0},{16,8},{0,24},{9,17},{25,1},{17,9},{1,25},{10,18},{2... | collective-permute-start | bytes 159752 | tf_op jit(solution)/shard_map/ppermute | solution.py:429
  14.5 3.3 %all-to-all-done.refs_0_ = f32[32,1,128]{2,1,0:T(1,128)S(1)} async-done(((f32[32,1,128]{2,1,0:T(1,128)}), f32[32,1,128]{2,1,0:T(1,128)S(1)}, u32[]{:S(2)}, u32[]{:S(2)}) %all-to-all-start) | async-done | bytes 16416 | tf_op jit(solution)/shard_map/all_to_all | solution.py:484
  17.9 1.5 %shard_map.132 = (f32[1,128]{1,0:T(1,128)S(1)}, bf16[128,1024]{1,0:T(8,128)(2,1)S(1)}, bf16[512,1024]{1,0:T(8,128)(2,1)S(1)}, f32[512,1024]{1,0:T(8,128)S(1)}, f...) custom-call(f32[32,1,128]{2,1,0:T(1,128)S(1)} %all-to-all-done.refs_0_, ...), custom_call_target="tpu_custom_call" | custom-call | tf_op jit(solution)/shard_map/pallas_call | solution.py:512
  19.4 2.5 %shard_map.133 = (f32[4,104,128]{2,1,0:T(8,128)S(1)}, f32[432,128]{1,0:T(8,128)S(1)}, f32[800,128]{1,0:T(8,128)S(1)}, f32[104,128]{1,0:T(8,128)S(1)}, f32[104,12...) custom-call(f32[800,128]{1,0:T(8,128)S(1)} %bitcast.24, f32[104,128]{1,0:T(8,128)S(1)} %get-tuple-element.78.refs_1_.refs_10_, ...), custom_call_target="tpu_custom_call" | custom-call | tf_op jit(solution)/shard_map/pallas_call | solution.py:527
  22.0 1.5 %collective-permute-done.4 = f32[432,128]{1,0:T(8,128)S(1)} collective-permute-done((f32[432,128]{1,0:T(8,128)S(1)}, f32[432,128]{1,0:T(8,128)S(1)}, u32[]{:S(2)}, u32[]{:S(2)}) %collective-permute-start.4) | collective-permute-done | bytes 221216 | tf_op jit(solution)/shard_map/ppermute | solution.py:553
  23.6 0.7 %collective-permute-start.6 = (f32[208,128]{1,0:T(8,128)S(1)}, f32[208,128]{1,0:T(8,128)S(1)}, u32[]{:S(2)}, u32[]{:S(2)}) collective-permute-start(f32[208,128]{1,0:T(8,128)S(1)} %pad_maximum_fusion.1), channel_id=1, source_target_pairs={{0,24},{8,16},{16,8},{24,0},{1,25},{9,17},{17,9},{25,1},{2,26},{10... | collective-permute-start | bytes 319496 | tf_op jit(solution)/shard_map/ppermute | solution.py:560
  24.3 1.5 %collective-permute-start.5 = (f32[208,128]{1,0:T(8,128)S(1)}, f32[208,128]{1,0:T(8,128)S(1)}, u32[]{:S(2)}, u32[]{:S(2)}) collective-permute-start(f32[208,128]{1,0:T(8,128)S(1)} %pad_maximum_fusion), channel_id=1, source_target_pairs={{0,8},{8,0},{16,24},{24,16},{1,9},{9,1},{17,25},{25,17},{2,10},{10... | collective-permute-start | bytes 319496 | tf_op jit(solution)/shard_map/ppermute | solution.py:559
  25.8 1.4 %collective-permute-start.7 = (f32[104,128]{1,0:T(8,128)S(1)}, f32[104,128]{1,0:T(8,128)S(1)}, u32[]{:S(2)}, u32[]{:S(2)}) collective-permute-start(f32[104,128]{1,0:T(8,128)S(1)} %get-tuple-element.75), channel_id=1, source_target_pairs={{0,16},{8,24},{16,0},{24,8},{1,17},{9,25},{17,1},{25,9},{2,18},{10... | collective-permute-start | bytes 159752 | tf_op jit(solution)/shard_map/ppermute | solution.py:561
  27.2 3.5 %collective-permute-done.7 = f32[104,128]{1,0:T(8,128)S(1)} collective-permute-done((f32[104,128]{1,0:T(8,128)S(1)}, f32[104,128]{1,0:T(8,128)S(1)}, u32[]{:S(2)}, u32[]{:S(2)}) %collective-permute-start.7) | collective-permute-done | bytes 53280 | tf_op jit(solution)/shard_map/ppermute | solution.py:561
  31.0 2.6 %collective-permute-start.9 = (f32[112,128]{1,0:T(8,128)S(1)}, f32[112,128]{1,0:T(8,128)S(1)}, u32[]{:S(2)}, u32[]{:S(2)}) collective-permute-start(f32[112,128]{1,0:T(8,128)S(1)} %pad_maximum_fusion.2), channel_id=1, source_target_pairs={{0,6},{2,4},{4,2},{6,0},{1,7},{3,5},{5,3},{7,1},{8,14},{10,12},{12... | collective-permute-start | bytes 172040 | tf_op jit(solution)/shard_map/ppermute | solution.py:575
  33.6 1.9 %collective-permute-start.10 = (f32[104,128]{1,0:T(8,128)S(1)}, f32[104,128]{1,0:T(8,128)S(1)}, u32[]{:S(2)}, u32[]{:S(2)}) collective-permute-start(f32[104,128]{1,0:T(8,128)S(1)} %get-tuple-element.73), channel_id=1, source_target_pairs={{0,4},{2,6},{4,0},{6,2},{1,5},{3,7},{5,1},{7,3},{8,12},{10,14},{12... | collective-permute-start | bytes 159752 | tf_op jit(solution)/shard_map/ppermute | solution.py:576
  35.5 3.3 %collective-permute-done.10 = f32[104,128]{1,0:T(8,128)S(1)} collective-permute-done((f32[104,128]{1,0:T(8,128)S(1)}, f32[104,128]{1,0:T(8,128)S(1)}, u32[]{:S(2)}, u32[]{:S(2)}) %collective-permute-start.10) | collective-permute-done | bytes 53280 | tf_op jit(solution)/shard_map/ppermute | solution.py:576
  38.8 1.0 %collective-permute-start.13 = (f32[104,128]{1,0:T(8,128)S(1)}, f32[104,128]{1,0:T(8,128)S(1)}, u32[]{:S(2)}, u32[]{:S(2)}) collective-permute-start(f32[104,128]{1,0:T(8,128)S(1)} %fusion.refs_1_), channel_id=1, source_target_pairs={{0,24},{8,16},{16,8},{24,0},{1,25},{9,17},{17,9},{25,1},{2,26},{10... | collective-permute-start | bytes 159752 | tf_op jit(solution)/shard_map/ppermute | solution.py:599
  39.8 1.1 %collective-permute-start.12 = (f32[104,128]{1,0:T(8,128)S(1)}, f32[104,128]{1,0:T(8,128)S(1)}, u32[]{:S(2)}, u32[]{:S(2)}) collective-permute-start(f32[104,128]{1,0:T(8,128)S(1)} %fusion.refs_1_), channel_id=1, source_target_pairs={{0,16},{8,24},{16,0},{24,8},{1,17},{9,25},{17,1},{25,9},{2,18},{10... | collective-permute-start | bytes 159752 | tf_op jit(solution)/shard_map/ppermute | solution.py:599
  40.9 1.5 %collective-permute-start.11 = (f32[104,128]{1,0:T(8,128)S(1)}, f32[104,128]{1,0:T(8,128)S(1)}, u32[]{:S(2)}, u32[]{:S(2)}) collective-permute-start(f32[104,128]{1,0:T(8,128)S(1)} %fusion.refs_1_), channel_id=1, source_target_pairs={{0,8},{8,0},{16,24},{24,16},{1,9},{9,1},{17,25},{25,17},{2,10},{10... | collective-permute-start | bytes 159752 | tf_op jit(solution)/shard_map/ppermute | solution.py:599
  42.4 1.5 %shard_map.134 = f32[800,128]{1,0:T(8,128)} custom-call(f32[1,128]{1,0:T(1,128)S(1)} %get-tuple-element.57.refs_0_, f32[104,128]{1,0:T(8,128)S(1)} %fusion.refs_1_, f32[800,128]{1,0:T(8,128)S(1)} %get-tuple-element.58.refs_2_, f32[128,1024]{1,0:T(8,128)S(1)} %get-tuple-element.41.refs_1_.refs_5_.refs_3_, f32[8,104,128]{2,1,0:T(8,128)S(1)} %get-tuple-element.59.refs_4_, ...), custom_call_target="tpu_custom_call" | custom-call | tf_op jit(solution)/shard_map/pallas_call | solution.py:588
  44.5 0.5 %collective-permute-done.11 = f32[104,128]{1,0:T(8,128)S(1)} collective-permute-done((f32[104,128]{1,0:T(8,128)S(1)}, f32[104,128]{1,0:T(8,128)S(1)}, u32[]{:S(2)}, u32[]{:S(2)}) %collective-permute-start.11) | collective-permute-done | bytes 53280 | tf_op jit(solution)/shard_map/ppermute | solution.py:599
  45.2 1.5 %collective-permute-done.14.refs_1_ = f32[416,128]{1,0:T(8,128)S(1)} collective-permute-done((f32[416,128]{1,0:T(8,128)S(1)}, f32[416,128]{1,0:T(8,128)S(1)}, u32[]{:S(2)}, u32[]{:S(2)}) %collective-permute-start.14) | collective-permute-done | bytes 213024 | tf_op jit(solution)/shard_map/ppermute | solution.py:602
  46.6 0.8 %shard_map.135 = (f32[100,512]{1,0:T(8,128)}, f32[1,512]{1,0:T(1,128)}, f32[100,512]{1,0:T(8,128)}, f32[1,100]{1,0:T(1,128)}) custom-call(f32[416,128]{1,0:T(8,128)S(1)} %constant_dynamic-update-slice_fusion.refs_0_, f32[416,128]{1,0:T(8,128)S(1)} %collective-permute-done.14.refs_1_), custom_call_target="tpu_custom_call" | custom-call | tf_op jit(solution)/shard_map/pallas_call | solution.py:603
  (51 shorter events, 2.3 us)
Async XLA Ops:
  0.6 0.7 %copy-start.2 = (s32[8,128]{1,0:T(8,128)S(1)}, s32[8,128]{1,0:T(8,128)}, u32[]{:S(2)}) copy-start(s32[8,128]{1,0:T(8,128)} %refs_1_.1) | copy-start | bytes 12292
  0.7 1.0 %copy-start = (f32[100,8,128]{2,1,0:T(8,128)S(1)}, f32[100,8,128]{2,1,0:T(8,128)}, u32[]{:S(2)}) copy-start(f32[100,8,128]{2,1,0:T(8,128)} %param.9) | copy-start | bytes 1228804
  0.7 13.4 %copy-start.4 = (bf16[100,512]{1,0:T(8,128)(2,1)S(1)}, bf16[100,512]{1,0:T(8,128)(2,1)}, u32[]{:S(2)}) copy-start(bf16[100,512]{1,0:T(8,128)(2,1)} %refs_2_.3) | copy-start | bytes 307204
  0.7 13.4 %copy-start.5 = (bf16[512,100]{0,1:T(8,128)(2,1)S(1)}, bf16[512,100]{0,1:T(8,128)(2,1)}, u32[]{:S(2)}) copy-start(bf16[512,100]{0,1:T(8,128)(2,1)} %param.16) | copy-start | bytes 307204
  0.7 13.4 %copy-start.6 = (f32[512]{0:T(512)S(1)}, f32[512]{0:T(512)}, u32[]{:S(2)}) copy-start(f32[512]{0:T(512)} %param.15) | copy-start | bytes 6148
  0.7 13.4 %copy-start.7 = (f32[100]{0:T(128)S(1)}, f32[100]{0:T(128)}, u32[]{:S(2)}) copy-start(f32[100]{0:T(128)} %param.17) | copy-start | bytes 1204
  0.7 13.4 %copy-start.8 = (f32[100]{0:T(128)S(1)}, f32[100]{0:T(128)}, u32[]{:S(2)}) copy-start(f32[100]{0:T(128)} %param.13) | copy-start | bytes 1204
  2.0 12.5 %collective-permute-start.3 = (f32[8,128]{1,0:T(8,128)S(1)}, f32[8,128]{1,0:T(8,128)S(1)}, u32[]{:S(2)}, u32[]{:S(2)}) collective-permute-start(f32[8,128]{1,0:T(8,128)S(1)} %get-tuple-element.81), channel_id=1, source_target_pairs={{1,2},{3,4},{5,6},{7,0},{2,1},{4,3},{6,5},{0,7},{9,10},{11,12},{13... | collective-permute-start | bytes 12296 | tf_op jit(solution)/shard_map/ppermute | solution.py:488
  6.5 8.0 %collective-permute-start.2 = (f32[8,128]{1,0:T(8,128)S(1)}, f32[8,128]{1,0:T(8,128)S(1)}, u32[]{:S(2)}, u32[]{:S(2)}) collective-permute-start(f32[8,128]{1,0:T(8,128)S(1)} %get-tuple-element.82), channel_id=1, source_target_pairs={{0,1},{1,0},{2,3},{3,2},{4,5},{5,4},{6,7},{7,6},{8,9},{9,8},{10,11... | collective-permute-start | bytes 12296 | tf_op jit(solution)/shard_map/ppermute | solution.py:487
  7.3 10.6 %all-to-all-start = ((f32[32,1,128]{2,1,0:T(1,128)}), f32[32,1,128]{2,1,0:T(1,128)S(1)}, u32[]{:S(2)}, u32[]{:S(2)}) async-start(f32[32,1,128]{2,1,0:T(1,128)} %shard_map.131), calls=%async_computation | async-start | bytes 32768 | tf_op jit(solution)/shard_map/all_to_all | solution.py:484
  10.8 8.6 %collective-permute-start = (f32[104,128]{1,0:T(8,128)S(1)}, f32[104,128]{1,0:T(8,128)S(1)}, u32[]{:S(2)}, u32[]{:S(2)}) collective-permute-start(f32[104,128]{1,0:T(8,128)S(1)} %get-tuple-element.37), channel_id=1, source_target_pairs={{0,8},{8,0},{16,24},{24,16},{1,9},{9,1},{17,25},{25,17},{2,10},{10... | collective-permute-start | bytes 159752 | tf_op jit(solution)/shard_map/ppermute | solution.py:428
  12.6 6.8 %collective-permute-start.1 = (f32[104,128]{1,0:T(8,128)S(1)}, f32[104,128]{1,0:T(8,128)S(1)}, u32[]{:S(2)}, u32[]{:S(2)}) collective-permute-start(f32[104,128]{1,0:T(8,128)S(1)} %get-tuple-element.38), channel_id=1, source_target_pairs={{8,16},{24,0},{16,8},{0,24},{9,17},{25,1},{17,9},{1,25},{10,18},{2... | collective-permute-start | bytes 159752 | tf_op jit(solution)/shard_map/ppermute | solution.py:429
  14.1 5.3 %copy-start.1 = (f32[100,8,128]{2,1,0:T(8,128)S(1)}, f32[100,8,128]{2,1,0:T(8,128)}, u32[]{:S(2)}) copy-start(f32[100,8,128]{2,1,0:T(8,128)} %param.10) | copy-start | bytes 1228804
  22.0 1.5 %collective-permute-start.4 = (f32[432,128]{1,0:T(8,128)S(1)}, f32[432,128]{1,0:T(8,128)S(1)}, u32[]{:S(2)}, u32[]{:S(2)}) collective-permute-start(f32[432,128]{1,0:T(8,128)S(1)} %get-tuple-element.54), channel_id=1, source_target_pairs={{0,1},{1,0},{2,3},{3,2},{4,5},{5,4},{6,7},{7,6},{8,9},{9,8},{10,11... | collective-permute-start | bytes 663560 | tf_op jit(solution)/shard_map/ppermute | solution.py:553
  23.6 7.1 %collective-permute-start.6 = (f32[208,128]{1,0:T(8,128)S(1)}, f32[208,128]{1,0:T(8,128)S(1)}, u32[]{:S(2)}, u32[]{:S(2)}) collective-permute-start(f32[208,128]{1,0:T(8,128)S(1)} %pad_maximum_fusion.1), channel_id=1, source_target_pairs={{0,24},{8,16},{16,8},{24,0},{1,25},{9,17},{17,9},{25,1},{2,26},{10... | collective-permute-start | bytes 319496 | tf_op jit(solution)/shard_map/ppermute | solution.py:560
  24.3 6.7 %collective-permute-start.5 = (f32[208,128]{1,0:T(8,128)S(1)}, f32[208,128]{1,0:T(8,128)S(1)}, u32[]{:S(2)}, u32[]{:S(2)}) collective-permute-start(f32[208,128]{1,0:T(8,128)S(1)} %pad_maximum_fusion), channel_id=1, source_target_pairs={{0,8},{8,0},{16,24},{24,16},{1,9},{9,1},{17,25},{25,17},{2,10},{10... | collective-permute-start | bytes 319496 | tf_op jit(solution)/shard_map/ppermute | solution.py:559
  25.8 4.9 %collective-permute-start.7 = (f32[104,128]{1,0:T(8,128)S(1)}, f32[104,128]{1,0:T(8,128)S(1)}, u32[]{:S(2)}, u32[]{:S(2)}) collective-permute-start(f32[104,128]{1,0:T(8,128)S(1)} %get-tuple-element.75), channel_id=1, source_target_pairs={{0,16},{8,24},{16,0},{24,8},{1,17},{9,25},{17,1},{25,9},{2,18},{10... | collective-permute-start | bytes 159752 | tf_op jit(solution)/shard_map/ppermute | solution.py:561
  31.0 7.8 %collective-permute-start.9 = (f32[112,128]{1,0:T(8,128)S(1)}, f32[112,128]{1,0:T(8,128)S(1)}, u32[]{:S(2)}, u32[]{:S(2)}) collective-permute-start(f32[112,128]{1,0:T(8,128)S(1)} %pad_maximum_fusion.2), channel_id=1, source_target_pairs={{0,6},{2,4},{4,2},{6,0},{1,7},{3,5},{5,3},{7,1},{8,14},{10,12},{12... | collective-permute-start | bytes 172040 | tf_op jit(solution)/shard_map/ppermute | solution.py:575
  33.6 5.2 %collective-permute-start.8 = (f32[112,128]{1,0:T(8,128)S(1)}, f32[112,128]{1,0:T(8,128)S(1)}, u32[]{:S(2)}, u32[]{:S(2)}) collective-permute-start(f32[112,128]{1,0:T(8,128)S(1)} %pad_maximum_fusion.2), channel_id=1, source_target_pairs={{0,2},{2,0},{4,6},{6,4},{1,3},{3,1},{5,7},{7,5},{8,10},{10,8},{12,... | collective-permute-start | bytes 172040 | tf_op jit(solution)/shard_map/ppermute | solution.py:574
  33.6 5.2 %collective-permute-start.10 = (f32[104,128]{1,0:T(8,128)S(1)}, f32[104,128]{1,0:T(8,128)S(1)}, u32[]{:S(2)}, u32[]{:S(2)}) collective-permute-start(f32[104,128]{1,0:T(8,128)S(1)} %get-tuple-element.73), channel_id=1, source_target_pairs={{0,4},{2,6},{4,0},{6,2},{1,5},{3,7},{5,1},{7,3},{8,12},{10,14},{12... | collective-permute-start | bytes 159752 | tf_op jit(solution)/shard_map/ppermute | solution.py:576
  38.8 5.2 %collective-permute-start.13 = (f32[104,128]{1,0:T(8,128)S(1)}, f32[104,128]{1,0:T(8,128)S(1)}, u32[]{:S(2)}, u32[]{:S(2)}) collective-permute-start(f32[104,128]{1,0:T(8,128)S(1)} %fusion.refs_1_), channel_id=1, source_target_pairs={{0,24},{8,16},{16,8},{24,0},{1,25},{9,17},{17,9},{25,1},{2,26},{10... | collective-permute-start | bytes 159752 | tf_op jit(solution)/shard_map/ppermute | solution.py:599
  39.8 4.7 %collective-permute-start.12 = (f32[104,128]{1,0:T(8,128)S(1)}, f32[104,128]{1,0:T(8,128)S(1)}, u32[]{:S(2)}, u32[]{:S(2)}) collective-permute-start(f32[104,128]{1,0:T(8,128)S(1)} %fusion.refs_1_), channel_id=1, source_target_pairs={{0,16},{8,24},{16,0},{24,8},{1,17},{9,25},{17,1},{25,9},{2,18},{10... | collective-permute-start | bytes 159752 | tf_op jit(solution)/shard_map/ppermute | solution.py:599
  40.9 4.1 %collective-permute-start.11 = (f32[104,128]{1,0:T(8,128)S(1)}, f32[104,128]{1,0:T(8,128)S(1)}, u32[]{:S(2)}, u32[]{:S(2)}) collective-permute-start(f32[104,128]{1,0:T(8,128)S(1)} %fusion.refs_1_), channel_id=1, source_target_pairs={{0,8},{8,0},{16,24},{24,16},{1,9},{9,1},{17,25},{25,17},{2,10},{10... | collective-permute-start | bytes 159752 | tf_op jit(solution)/shard_map/ppermute | solution.py:599
  45.1 1.5 %collective-permute-start.14 = (f32[416,128]{1,0:T(8,128)S(1)}, f32[416,128]{1,0:T(8,128)S(1)}, u32[]{:S(2)}, u32[]{:S(2)}) collective-permute-start(f32[416,128]{1,0:T(8,128)S(1)} %constant_dynamic-update-slice_fusion.refs_0_), channel_id=1, source_target_pairs={{0,1},{1,0},{2,3},{3,2},{4,5},{5,4},{6,7},{7,6},{8,9},{9,8},{10,11... | collective-permute-start | bytes 638984 | tf_op jit(solution)/shard_map/ppermute | solution.py:602
  (1 other events, 0.7 us)

commit v6 on v5

--- a/solution.py
+++ b/solution.py
@@ -555,26 +555,19 @@
     lon_near = got[4 * height : 4 * height + rows]
     lon_pass = got[4 * height + rows :]
     part = chip[0]
-    if lats == 4:
-        near = lax.ppermute(jnp.concatenate([chip[1], lat_a], 0), "lat", flip(lats, 1))
-        far = lax.ppermute(jnp.concatenate([chip[3], lat_b], 0), "lat", flip(lats, 3))
-        cross = lax.ppermute(chip[2], "lat", flip(lats, 2))
-        part = part + near[:height] + far[:height] + cross
-        north, south = in_order(lat_odd, near[height:], far[height:])
-    else:
-        for step in range(1, 4):
-            part = part + lax.ppermute(chip[step], "lat", flip(lats, step))
-        step = 4
-        while step < lats:
-            part = part + lax.ppermute(part, "lat", flip(lats, step))
-            step *= 2
-        north, south = swap_lat(lat_odd, lats, lat_a, lat_b)
+    for step in (1, 2, 3):
+        part = part + lax.ppermute(chip[step], "lat", flip(lats, step))
+    step = 4
+    while step < lats:
+        part = part + lax.ppermute(part, "lat", flip(lats, step))
+        step *= 2
+    north, south = swap_lat(lat_odd, lats, lat_a, lat_b)
     if chips == 4:
         packed = jnp.concatenate([part, lon_pass], 0)
-        near = lax.ppermute(packed, "z", flip(chips, 1))
-        far = lax.ppermute(packed, "z", flip(chips, 3))
-        cross = lax.ppermute(part, "z", flip(chips, 2))
-        part = part + near[:height] + far[:height] + cross
+        came = {step: lax.ppermute(packed, "z", flip(chips, step)) for step in (1, 2, 3)}
+        for step in (1, 2, 3):
+            part = part + came[step][:height]
+        near, far = came[1], came[3]
         lon_far = jnp.where(from_near, near[height:], far[height:])
     else:
         step = 1
@@ -596,7 +589,8 @@
         north, south, west, east, t_north, t_south, t_west, t_east,
     )
 
-    mine = [part] + [lax.ppermute(part, "lat", flip(lats, step)) for step in range(1, 4)]
+    came = {step: lax.ppermute(part, "lat", flip(lats, step)) for step in (1, 2, 3)}
+    mine = [part] + [came[step] for step in range(1, 4)]
     mine, tracer_adjoint = lax.optimization_barrier((mine, tracer_adjoint))
     mine = jnp.concatenate(mine, 0)
     other = lax.ppermute(mine, "core", flip(2, 1))

time: 47.6 us -> 46.9 us (0.985)
  waiting for transfers between devices: 14.5 us -> 11.8 us
  starting transfers between devices: 23.1 us -> 25.1 us
    ppermute x6, waiting for transfers between devices: 7.08 us -> 4.37 us  [the longest x3 3.57 us: shards(): lax.ppermute(packed, 'z', flip(chips, step))]
    ppermute x1 -> x2, starting transfers between devices: 1.46 us -> 2.95 us  [swap_lat(): lax.ppermute(lat_b, 'lat', far_pairs(lats, True))]
    ppermute x1 -> x2, starting transfers between devices: 1.83 us -> 2.4 us  [swap_lat(): lax.ppermute(lat_a, 'lat', flip(lats, 1))]
  transfers between devices with their start and end apart: 16 -> 18, of which waited for: 9 -> 10; matrix products, arithmetic and copies ran while one was open for 0% -> 0% of each run, Pallas kernels for 9% -> 9%
where the time goes in v6:
time: 46.9 us; the launch traced here: 46.7 us
  starting transfers between devices  25.1 us (54%)
  waiting for transfers between devices  11.8 us (25%)
  Pallas kernels  7.79 us (17%)
  local copies, waits for them, and re-layouts  1.03 us (2%)
  between operations  0.9 us (2%)
    ppermute x1, starting transfers between devices, shards(): lax.ppermute(small[rows:], ('z', 'core'), far_pairs(lons, True))  4.53 us
    ppermute x3, starting transfers between devices, shards(): lax.ppermute(packed, 'z', flip(chips, step))  4.45 us
    ppermute x3, waiting for transfers between devices, shards(): lax.ppermute(packed, 'z', flip(chips, step))  3.57 us
    ppermute x3, starting transfers between devices, shards(): part = part + lax.ppermute(chip[step], 'lat', flip(lats, step))  3.55 us
    ppermute x3, starting transfers between devices, shards(): lax.ppermute(part, 'lat', flip(lats, step))  3.55 us
    all_to_all x1, starting transfers between devices, shards(): energy = lax.all_to_all(energy, ('lat', 'z', 'core'), 0, 0, tiled=True)  3.48 us
    all_to_all x1, waiting for transfers between devices, shards(): energy = lax.all_to_all(energy, ('lat', 'z', 'core'), 0, 0, tiled=True)  3.34 us
    ppermute x2, starting transfers between devices, swap_lat(): lax.ppermute(lat_b, 'lat', far_pairs(lats, True))  2.95 us
  transfers between devices with their start and end apart: 18, of which 10 were waited for; matrix products, arithmetic and copies ran while one was open for 0% of the time, Pallas kernels for 9%

profile of v6, /device:TPU:0, one launch (start us, length us, event | category | flops | bytes accessed | tf_op | source)
XLA Modules:
  0.0 46.7 jit_solution(14288332415545999835)
XLA Ops:
  2.0 4.5 %collective-permute-start.3 = (f32[8,128]{1,0:T(8,128)S(1)}, f32[8,128]{1,0:T(8,128)S(1)}, u32[]{:S(2)}, u32[]{:S(2)}) collective-permute-start(f32[8,128]{1,0:T(8,128)S(1)} %get-tuple-element.80), channel_id=1, source_target_pairs={{1,2},{3,4},{5,6},{7,0},{2,1},{4,3},{6,5},{0,7},{9,10},{11,12},{13... | collective-permute-start | bytes 12296 | tf_op jit(solution)/shard_map/ppermute | solution.py:488
  6.5 0.8 %shard_map.131 = f32[32,1,128]{2,1,0:T(1,128)} custom-call(f32[800,128]{1,0:T(8,128)S(1)} %bitcast.26, f32[8,128]{1,0:T(8,128)S(1)} %get-tuple-element.40.refs_1_.refs_7_.refs_5_), custom_call_target="tpu_custom_call" | custom-call | flops 1000000000 | bytes 100000000 | tf_op jit(solution)/shard_map/pallas_call | solution.py:475
  7.3 3.5 %all-to-all-start = ((f32[32,1,128]{2,1,0:T(1,128)}), f32[32,1,128]{2,1,0:T(1,128)S(1)}, u32[]{:S(2)}, u32[]{:S(2)}) async-start(f32[32,1,128]{2,1,0:T(1,128)} %shard_map.131), calls=%async_computation | async-start | bytes 32768 | tf_op jit(solution)/shard_map/all_to_all | solution.py:484
  10.8 1.8 %collective-permute-start = (f32[104,128]{1,0:T(8,128)S(1)}, f32[104,128]{1,0:T(8,128)S(1)}, u32[]{:S(2)}, u32[]{:S(2)}) collective-permute-start(f32[104,128]{1,0:T(8,128)S(1)} %get-tuple-element.37), channel_id=1, source_target_pairs={{0,8},{8,0},{16,24},{24,16},{1,9},{9,1},{17,25},{25,17},{2,10},{10... | collective-permute-start | bytes 159752 | tf_op jit(solution)/shard_map/ppermute | solution.py:428
  12.6 1.5 %collective-permute-start.1 = (f32[104,128]{1,0:T(8,128)S(1)}, f32[104,128]{1,0:T(8,128)S(1)}, u32[]{:S(2)}, u32[]{:S(2)}) collective-permute-start(f32[104,128]{1,0:T(8,128)S(1)} %get-tuple-element.38), channel_id=1, source_target_pairs={{8,16},{24,0},{16,8},{0,24},{9,17},{25,1},{17,9},{1,25},{10,18},{2... | collective-permute-start | bytes 159752 | tf_op jit(solution)/shard_map/ppermute | solution.py:429
  14.5 3.3 %all-to-all-done.refs_0_ = f32[32,1,128]{2,1,0:T(1,128)S(1)} async-done(((f32[32,1,128]{2,1,0:T(1,128)}), f32[32,1,128]{2,1,0:T(1,128)S(1)}, u32[]{:S(2)}, u32[]{:S(2)}) %all-to-all-start) | async-done | bytes 16416 | tf_op jit(solution)/shard_map/all_to_all | solution.py:484
  17.9 1.5 %shard_map.132 = (f32[1,128]{1,0:T(1,128)S(1)}, bf16[128,1024]{1,0:T(8,128)(2,1)S(1)}, bf16[512,1024]{1,0:T(8,128)(2,1)S(1)}, f32[512,1024]{1,0:T(8,128)S(1)}, f...) custom-call(f32[32,1,128]{2,1,0:T(1,128)S(1)} %all-to-all-done.refs_0_, ...), custom_call_target="tpu_custom_call" | custom-call | tf_op jit(solution)/shard_map/pallas_call | solution.py:512
  19.4 2.5 %shard_map.133 = (f32[4,104,128]{2,1,0:T(8,128)S(1)}, f32[432,128]{1,0:T(8,128)S(1)}, f32[800,128]{1,0:T(8,128)S(1)}, f32[104,128]{1,0:T(8,128)S(1)}, f32[104,12...) custom-call(f32[800,128]{1,0:T(8,128)S(1)} %bitcast.28, f32[104,128]{1,0:T(8,128)S(1)} %get-tuple-element.77.refs_1_.refs_10_, ...), custom_call_target="tpu_custom_call" | custom-call | tf_op jit(solution)/shard_map/pallas_call | solution.py:527
  22.0 1.5 %collective-permute-done.4 = f32[432,128]{1,0:T(8,128)S(1)} collective-permute-done((f32[432,128]{1,0:T(8,128)S(1)}, f32[432,128]{1,0:T(8,128)S(1)}, u32[]{:S(2)}, u32[]{:S(2)}) %collective-permute-start.4) | collective-permute-done | bytes 221216 | tf_op jit(solution)/shard_map/ppermute | solution.py:553
  23.6 0.6 %collective-permute-start.5 = (f32[104,128]{1,0:T(8,128)S(1)}, f32[104,128]{1,0:T(8,128)S(1)}, u32[]{:S(2)}, u32[]{:S(2)}) collective-permute-start(f32[104,128]{1,0:T(8,128)S(1)} %get-tuple-element.71), channel_id=1, source_target_pairs={{0,8},{8,0},{16,24},{24,16},{1,9},{9,1},{17,25},{25,17},{2,10},{10... | collective-permute-start | bytes 159752 | tf_op jit(solution)/shard_map/ppermute | solution.py:559
  24.2 1.5 %collective-permute-start.7 = (f32[104,128]{1,0:T(8,128)S(1)}, f32[104,128]{1,0:T(8,128)S(1)}, u32[]{:S(2)}, u32[]{:S(2)}) collective-permute-start(f32[104,128]{1,0:T(8,128)S(1)} %get-tuple-element.72), channel_id=1, source_target_pairs={{0,24},{8,16},{16,8},{24,0},{1,25},{9,17},{17,9},{25,1},{2,26},{10... | collective-permute-start | bytes 159752 | tf_op jit(solution)/shard_map/ppermute | solution.py:559
  25.7 1.4 %collective-permute-start.6 = (f32[104,128]{1,0:T(8,128)S(1)}, f32[104,128]{1,0:T(8,128)S(1)}, u32[]{:S(2)}, u32[]{:S(2)}) collective-permute-start(f32[104,128]{1,0:T(8,128)S(1)} %get-tuple-element.73), channel_id=1, source_target_pairs={{0,16},{8,24},{16,0},{24,8},{1,17},{9,25},{17,1},{25,9},{2,18},{10... | collective-permute-start | bytes 159752 | tf_op jit(solution)/shard_map/ppermute | solution.py:559
  27.7 1.5 %collective-permute-start.15 = (f32[104,128]{1,0:T(8,128)S(1)}, f32[104,128]{1,0:T(8,128)S(1)}, u32[]{:S(2)}, u32[]{:S(2)}) collective-permute-start(f32[104,128]{1,0:T(8,128)S(1)} %get-tuple-element.59), channel_id=1, source_target_pairs={{8,16},{24,0},{16,8},{0,24},{9,17},{25,1},{17,9},{1,25},{10,18},{2... | collective-permute-start | bytes 159752 | tf_op jit(solution)/shard_map/ppermute | solution.py:429
  30.0 3.0 %collective-permute-start.10 = (f32[112,128]{1,0:T(8,128)S(1)}, f32[112,128]{1,0:T(8,128)S(1)}, u32[]{:S(2)}, u32[]{:S(2)}) collective-permute-start(f32[112,128]{1,0:T(8,128)S(1)} %pad_maximum_fusion), channel_id=1, source_target_pairs={{0,6},{2,4},{4,2},{6,0},{1,7},{3,5},{5,3},{7,1},{8,14},{10,12},{12... | collective-permute-start | bytes 172040 | tf_op jit(solution)/shard_map/ppermute | solution.py:567
  33.0 1.5 %collective-permute-start.8 = (f32[112,128]{1,0:T(8,128)S(1)}, f32[112,128]{1,0:T(8,128)S(1)}, u32[]{:S(2)}, u32[]{:S(2)}) collective-permute-start(f32[112,128]{1,0:T(8,128)S(1)} %pad_maximum_fusion), channel_id=1, source_target_pairs={{0,2},{2,0},{4,6},{6,4},{1,3},{3,1},{5,7},{7,5},{8,10},{10,8},{12,... | collective-permute-start | bytes 172040 | tf_op jit(solution)/shard_map/ppermute | solution.py:567
  34.5 1.9 %collective-permute-done.10 = f32[112,128]{1,0:T(8,128)S(1)} collective-permute-done((f32[112,128]{1,0:T(8,128)S(1)}, f32[112,128]{1,0:T(8,128)S(1)}, u32[]{:S(2)}, u32[]{:S(2)}) %collective-permute-start.10) | collective-permute-done | bytes 57376 | tf_op jit(solution)/shard_map/ppermute | solution.py:567
  36.4 1.7 %collective-permute-done.9 = f32[112,128]{1,0:T(8,128)S(1)} collective-permute-done((f32[112,128]{1,0:T(8,128)S(1)}, f32[112,128]{1,0:T(8,128)S(1)}, u32[]{:S(2)}, u32[]{:S(2)}) %collective-permute-start.9) | collective-permute-done | bytes 57376 | tf_op jit(solution)/shard_map/ppermute | solution.py:567
  38.1 1.4 %collective-permute-start.13 = (f32[104,128]{1,0:T(8,128)S(1)}, f32[104,128]{1,0:T(8,128)S(1)}, u32[]{:S(2)}, u32[]{:S(2)}) collective-permute-start(f32[104,128]{1,0:T(8,128)S(1)} %slice_add_fusion.refs_1_), channel_id=1, source_target_pairs={{0,24},{8,16},{16,8},{24,0},{1,25},{9,17},{17,9},{25,1},{2,26},{10... | collective-permute-start | bytes 159752 | tf_op jit(solution)/shard_map/ppermute | solution.py:592
  39.5 0.7 %collective-permute-start.12 = (f32[104,128]{1,0:T(8,128)S(1)}, f32[104,128]{1,0:T(8,128)S(1)}, u32[]{:S(2)}, u32[]{:S(2)}) collective-permute-start(f32[104,128]{1,0:T(8,128)S(1)} %slice_add_fusion.refs_1_), channel_id=1, source_target_pairs={{0,16},{8,24},{16,0},{24,8},{1,17},{9,25},{17,1},{25,9},{2,18},{10... | collective-permute-start | bytes 159752 | tf_op jit(solution)/shard_map/ppermute | solution.py:592
  40.2 1.5 %collective-permute-start.11 = (f32[104,128]{1,0:T(8,128)S(1)}, f32[104,128]{1,0:T(8,128)S(1)}, u32[]{:S(2)}, u32[]{:S(2)}) collective-permute-start(f32[104,128]{1,0:T(8,128)S(1)} %slice_add_fusion.refs_1_), channel_id=1, source_target_pairs={{0,8},{8,0},{16,24},{24,16},{1,9},{9,1},{17,25},{25,17},{2,10},{10... | collective-permute-start | bytes 159752 | tf_op jit(solution)/shard_map/ppermute | solution.py:592
  41.7 1.5 %shard_map.134 = f32[800,128]{1,0:T(8,128)} custom-call(f32[1,128]{1,0:T(1,128)S(1)} %get-tuple-element.55.refs_0_, f32[104,128]{1,0:T(8,128)S(1)} %slice_add_fusion.refs_1_, f32[800,128]{1,0:T(8,128)S(1)} %get-tuple-element.56.refs_2_, f32[128,1024]{1,0:T(8,128)S(1)} %get-tuple-element.41.refs_1_.refs_5_.refs_3_, ...), custom_call_target="tpu_custom_call" | custom-call | tf_op jit(solution)/shard_map/pallas_call | solution.py:581
  43.2 0.6 %collective-permute-done.13 = f32[104,128]{1,0:T(8,128)S(1)} collective-permute-done((f32[104,128]{1,0:T(8,128)S(1)}, f32[104,128]{1,0:T(8,128)S(1)}, u32[]{:S(2)}, u32[]{:S(2)}) %collective-permute-start.13) | collective-permute-done | bytes 53280 | tf_op jit(solution)/shard_map/ppermute | solution.py:592
  44.5 1.5 %collective-permute-done.16.refs_1_ = f32[416,128]{1,0:T(8,128)S(1)} collective-permute-done((f32[416,128]{1,0:T(8,128)S(1)}, f32[416,128]{1,0:T(8,128)S(1)}, u32[]{:S(2)}, u32[]{:S(2)}) %collective-permute-start.16) | collective-permute-done | bytes 213024 | tf_op jit(solution)/shard_map/ppermute | solution.py:596
  45.9 0.8 %shard_map.135 = (f32[100,512]{1,0:T(8,128)}, f32[1,512]{1,0:T(1,128)}, f32[100,512]{1,0:T(8,128)}, f32[1,100]{1,0:T(1,128)}) custom-call(f32[416,128]{1,0:T(8,128)S(1)} %constant_dynamic-update-slice_fusion.refs_0_, f32[416,128]{1,0:T(8,128)S(1)} %collective-permute-done.16.refs_1_), custom_call_target="tpu_custom_call" | custom-call | tf_op jit(solution)/shard_map/pallas_call | solution.py:597
  (54 shorter events, 3.9 us)
Async XLA Ops:
  0.7 13.4 %copy-start.4 = (bf16[100,512]{1,0:T(8,128)(2,1)S(1)}, bf16[100,512]{1,0:T(8,128)(2,1)}, u32[]{:S(2)}) copy-start(bf16[100,512]{1,0:T(8,128)(2,1)} %refs_2_.3) | copy-start | bytes 307204
  0.7 13.4 %copy-start.5 = (bf16[512,100]{0,1:T(8,128)(2,1)S(1)}, bf16[512,100]{0,1:T(8,128)(2,1)}, u32[]{:S(2)}) copy-start(bf16[512,100]{0,1:T(8,128)(2,1)} %param.16) | copy-start | bytes 307204
  0.7 13.4 %copy-start.6 = (f32[512]{0:T(512)S(1)}, f32[512]{0:T(512)}, u32[]{:S(2)}) copy-start(f32[512]{0:T(512)} %param.15) | copy-start | bytes 6148
  0.7 13.4 %copy-start.7 = (f32[100]{0:T(128)S(1)}, f32[100]{0:T(128)}, u32[]{:S(2)}) copy-start(f32[100]{0:T(128)} %param.17) | copy-start | bytes 1204
  0.7 13.4 %copy-start.8 = (f32[100]{0:T(128)S(1)}, f32[100]{0:T(128)}, u32[]{:S(2)}) copy-start(f32[100]{0:T(128)} %param.13) | copy-start | bytes 1204
  2.0 12.5 %collective-permute-start.3 = (f32[8,128]{1,0:T(8,128)S(1)}, f32[8,128]{1,0:T(8,128)S(1)}, u32[]{:S(2)}, u32[]{:S(2)}) collective-permute-start(f32[8,128]{1,0:T(8,128)S(1)} %get-tuple-element.80), channel_id=1, source_target_pairs={{1,2},{3,4},{5,6},{7,0},{2,1},{4,3},{6,5},{0,7},{9,10},{11,12},{13... | collective-permute-start | bytes 12296 | tf_op jit(solution)/shard_map/ppermute | solution.py:488
  6.5 8.0 %collective-permute-start.2 = (f32[8,128]{1,0:T(8,128)S(1)}, f32[8,128]{1,0:T(8,128)S(1)}, u32[]{:S(2)}, u32[]{:S(2)}) collective-permute-start(f32[8,128]{1,0:T(8,128)S(1)} %get-tuple-element.81), channel_id=1, source_target_pairs={{0,1},{1,0},{2,3},{3,2},{4,5},{5,4},{6,7},{7,6},{8,9},{9,8},{10,11... | collective-permute-start | bytes 12296 | tf_op jit(solution)/shard_map/ppermute | solution.py:487
  7.3 10.6 %all-to-all-start = ((f32[32,1,128]{2,1,0:T(1,128)}), f32[32,1,128]{2,1,0:T(1,128)S(1)}, u32[]{:S(2)}, u32[]{:S(2)}) async-start(f32[32,1,128]{2,1,0:T(1,128)} %shard_map.131), calls=%async_computation | async-start | bytes 32768 | tf_op jit(solution)/shard_map/all_to_all | solution.py:484
  10.8 8.6 %collective-permute-start = (f32[104,128]{1,0:T(8,128)S(1)}, f32[104,128]{1,0:T(8,128)S(1)}, u32[]{:S(2)}, u32[]{:S(2)}) collective-permute-start(f32[104,128]{1,0:T(8,128)S(1)} %get-tuple-element.37), channel_id=1, source_target_pairs={{0,8},{8,0},{16,24},{24,16},{1,9},{9,1},{17,25},{25,17},{2,10},{10... | collective-permute-start | bytes 159752 | tf_op jit(solution)/shard_map/ppermute | solution.py:428
  12.6 6.8 %collective-permute-start.1 = (f32[104,128]{1,0:T(8,128)S(1)}, f32[104,128]{1,0:T(8,128)S(1)}, u32[]{:S(2)}, u32[]{:S(2)}) collective-permute-start(f32[104,128]{1,0:T(8,128)S(1)} %get-tuple-element.38), channel_id=1, source_target_pairs={{8,16},{24,0},{16,8},{0,24},{9,17},{25,1},{17,9},{1,25},{10,18},{2... | collective-permute-start | bytes 159752 | tf_op jit(solution)/shard_map/ppermute | solution.py:429
  14.1 5.3 %copy-start.1 = (f32[100,8,128]{2,1,0:T(8,128)S(1)}, f32[100,8,128]{2,1,0:T(8,128)}, u32[]{:S(2)}) copy-start(f32[100,8,128]{2,1,0:T(8,128)} %param.10) | copy-start | bytes 1228804
  22.0 1.5 %collective-permute-start.4 = (f32[432,128]{1,0:T(8,128)S(1)}, f32[432,128]{1,0:T(8,128)S(1)}, u32[]{:S(2)}, u32[]{:S(2)}) collective-permute-start(f32[432,128]{1,0:T(8,128)S(1)} %get-tuple-element.54), channel_id=1, source_target_pairs={{0,1},{1,0},{2,3},{3,2},{4,5},{5,4},{6,7},{7,6},{8,9},{9,8},{10,11... | collective-permute-start | bytes 663560 | tf_op jit(solution)/shard_map/ppermute | solution.py:553
  23.6 5.6 %collective-permute-start.5 = (f32[104,128]{1,0:T(8,128)S(1)}, f32[104,128]{1,0:T(8,128)S(1)}, u32[]{:S(2)}, u32[]{:S(2)}) collective-permute-start(f32[104,128]{1,0:T(8,128)S(1)} %get-tuple-element.71), channel_id=1, source_target_pairs={{0,8},{8,0},{16,24},{24,16},{1,9},{9,1},{17,25},{25,17},{2,10},{10... | collective-permute-start | bytes 159752 | tf_op jit(solution)/shard_map/ppermute | solution.py:559
  24.2 5.3 %collective-permute-start.7 = (f32[104,128]{1,0:T(8,128)S(1)}, f32[104,128]{1,0:T(8,128)S(1)}, u32[]{:S(2)}, u32[]{:S(2)}) collective-permute-start(f32[104,128]{1,0:T(8,128)S(1)} %get-tuple-element.72), channel_id=1, source_target_pairs={{0,24},{8,16},{16,8},{24,0},{1,25},{9,17},{17,9},{25,1},{2,26},{10... | collective-permute-start | bytes 159752 | tf_op jit(solution)/shard_map/ppermute | solution.py:559
  25.7 4.3 %collective-permute-start.6 = (f32[104,128]{1,0:T(8,128)S(1)}, f32[104,128]{1,0:T(8,128)S(1)}, u32[]{:S(2)}, u32[]{:S(2)}) collective-permute-start(f32[104,128]{1,0:T(8,128)S(1)} %get-tuple-element.73), channel_id=1, source_target_pairs={{0,16},{8,24},{16,0},{24,8},{1,17},{9,25},{17,1},{25,9},{2,18},{10... | collective-permute-start | bytes 159752 | tf_op jit(solution)/shard_map/ppermute | solution.py:559
  27.1 7.4 %collective-permute-start.14 = (f32[104,128]{1,0:T(8,128)S(1)}, f32[104,128]{1,0:T(8,128)S(1)}, u32[]{:S(2)}, u32[]{:S(2)}) collective-permute-start(f32[104,128]{1,0:T(8,128)S(1)} %get-tuple-element.58), channel_id=1, source_target_pairs={{0,8},{8,0},{16,24},{24,16},{1,9},{9,1},{17,25},{25,17},{2,10},{10... | collective-permute-start | bytes 159752 | tf_op jit(solution)/shard_map/ppermute | solution.py:428
  27.7 6.8 %collective-permute-start.15 = (f32[104,128]{1,0:T(8,128)S(1)}, f32[104,128]{1,0:T(8,128)S(1)}, u32[]{:S(2)}, u32[]{:S(2)}) collective-permute-start(f32[104,128]{1,0:T(8,128)S(1)} %get-tuple-element.59), channel_id=1, source_target_pairs={{8,16},{24,0},{16,8},{0,24},{9,17},{25,1},{17,9},{1,25},{10,18},{2... | collective-permute-start | bytes 159752 | tf_op jit(solution)/shard_map/ppermute | solution.py:429
  30.0 6.4 %collective-permute-start.10 = (f32[112,128]{1,0:T(8,128)S(1)}, f32[112,128]{1,0:T(8,128)S(1)}, u32[]{:S(2)}, u32[]{:S(2)}) collective-permute-start(f32[112,128]{1,0:T(8,128)S(1)} %pad_maximum_fusion), channel_id=1, source_target_pairs={{0,6},{2,4},{4,2},{6,0},{1,7},{3,5},{5,3},{7,1},{8,14},{10,12},{12... | collective-permute-start | bytes 172040 | tf_op jit(solution)/shard_map/ppermute | solution.py:567
  33.0 5.1 %collective-permute-start.9 = (f32[112,128]{1,0:T(8,128)S(1)}, f32[112,128]{1,0:T(8,128)S(1)}, u32[]{:S(2)}, u32[]{:S(2)}) collective-permute-start(f32[112,128]{1,0:T(8,128)S(1)} %pad_maximum_fusion), channel_id=1, source_target_pairs={{0,4},{2,6},{4,0},{6,2},{1,5},{3,7},{5,1},{7,3},{8,12},{10,14},{12... | collective-permute-start | bytes 172040 | tf_op jit(solution)/shard_map/ppermute | solution.py:567
  33.0 5.1 %collective-permute-start.8 = (f32[112,128]{1,0:T(8,128)S(1)}, f32[112,128]{1,0:T(8,128)S(1)}, u32[]{:S(2)}, u32[]{:S(2)}) collective-permute-start(f32[112,128]{1,0:T(8,128)S(1)} %pad_maximum_fusion), channel_id=1, source_target_pairs={{0,2},{2,0},{4,6},{6,4},{1,3},{3,1},{5,7},{7,5},{8,10},{10,8},{12,... | collective-permute-start | bytes 172040 | tf_op jit(solution)/shard_map/ppermute | solution.py:567
  38.1 5.6 %collective-permute-start.13 = (f32[104,128]{1,0:T(8,128)S(1)}, f32[104,128]{1,0:T(8,128)S(1)}, u32[]{:S(2)}, u32[]{:S(2)}) collective-permute-start(f32[104,128]{1,0:T(8,128)S(1)} %slice_add_fusion.refs_1_), channel_id=1, source_target_pairs={{0,24},{8,16},{16,8},{24,0},{1,25},{9,17},{17,9},{25,1},{2,26},{10... | collective-permute-start | bytes 159752 | tf_op jit(solution)/shard_map/ppermute | solution.py:592
  39.5 4.5 %collective-permute-start.12 = (f32[104,128]{1,0:T(8,128)S(1)}, f32[104,128]{1,0:T(8,128)S(1)}, u32[]{:S(2)}, u32[]{:S(2)}) collective-permute-start(f32[104,128]{1,0:T(8,128)S(1)} %slice_add_fusion.refs_1_), channel_id=1, source_target_pairs={{0,16},{8,24},{16,0},{24,8},{1,17},{9,25},{17,1},{25,9},{2,18},{10... | collective-permute-start | bytes 159752 | tf_op jit(solution)/shard_map/ppermute | solution.py:592
  40.2 4.1 %collective-permute-start.11 = (f32[104,128]{1,0:T(8,128)S(1)}, f32[104,128]{1,0:T(8,128)S(1)}, u32[]{:S(2)}, u32[]{:S(2)}) collective-permute-start(f32[104,128]{1,0:T(8,128)S(1)} %slice_add_fusion.refs_1_), channel_id=1, source_target_pairs={{0,8},{8,0},{16,24},{24,16},{1,9},{9,1},{17,25},{25,17},{2,10},{10... | collective-permute-start | bytes 159752 | tf_op jit(solution)/shard_map/ppermute | solution.py:592
  44.4 1.5 %collective-permute-start.16 = (f32[416,128]{1,0:T(8,128)S(1)}, f32[416,128]{1,0:T(8,128)S(1)}, u32[]{:S(2)}, u32[]{:S(2)}) collective-permute-start(f32[416,128]{1,0:T(8,128)S(1)} %constant_dynamic-update-slice_fusion.refs_0_), channel_id=1, source_target_pairs={{0,1},{1,0},{2,3},{3,2},{4,5},{5,4},{6,7},{7,6},{8,9},{9,8},{10,11... | collective-permute-start | bytes 638984 | tf_op jit(solution)/shard_map/ppermute | solution.py:596
  (3 other events, 2.4 us)

commit v7 on v6

--- a/solution.py
+++ b/solution.py
@@ -57,26 +57,80 @@
     lat_b[levels:, :] = jnp.where(lat_odd, last_tail, first_tail)
 
 
-def write_lon_edges(field_ref, levels, rows, pad_ref, lon_a, lon_b, lon_odd, depth=None):
-    cols = field_ref.shape[1]
-    lanes = lane_ids((levels, cols))
-    low = jnp.zeros((levels, cols), f32)
-    high = jnp.zeros((levels, cols), f32)
-    for row in range(rows):
-        chunk = row_of(field_ref, row, levels, rows)
-        low = jnp.where(lanes == row, pltpu.roll(chunk, row, 1) if row else chunk, low)
-        high = jnp.where(lanes == row, pltpu.roll(chunk, (row + 1) % cols, 1), high)
-    turned = []
-    for packed, edge in ((low, 0), (high, cols - 1)):
-        pad_ref[...] = jnp.zeros(pad_ref.shape, f32)
-        pad_ref[0:levels, :] = packed
-        flat = pad_ref[...].T[0:rows, :]
-        if depth is not None:
-            at = lane_ids(flat.shape) == levels
-            flat = jnp.where(at, jnp.broadcast_to(depth[:, edge : edge + 1], flat.shape), flat)
-        turned.append(flat)
-    lon_a[...] = jnp.where(lon_odd, turned[0], turned[1])
-    lon_b[...] = jnp.where(lon_odd, turned[1], turned[0])
+def lon_edges(values, levels):
+    low = high = None
+    for k, value in values:
+        lanes = lane_ids(value.shape)
+        cols = value.shape[1]
+        if low is None:
+            low = high = jnp.zeros(value.shape, f32)
+        low = jnp.where(lanes == k, pltpu.roll(value, k, 1) if k else value, low)
+        high = jnp.where(lanes == k, pltpu.roll(value, (k + 1) % cols, 1), high)
+    return low, high
+
+
+def exchange_sublanes(parts):
+    count = len(parts)
+    sub = lax.broadcasted_iota(jnp.int32, parts[0].shape, 0)
+    step = 1
+    while step < count:
+        low = (sub & step) == 0
+        turned = list(parts)
+        for i in range(count):
+            if i & step == 0:
+                a, b = parts[i], parts[i + step]
+                turned[i] = jnp.where(low, a, pltpu.roll(b, step, 0))
+                turned[i + step] = jnp.where(low, pltpu.roll(a, count - step, 0), b)
+        parts = turned
+        step *= 2
+    return parts
+
+
+def sum_rows(parts):
+    count = len(parts)
+    sub = lax.broadcasted_iota(jnp.int32, parts[0].shape, 0)
+    step = count // 2
+    while step:
+        low = (sub & step) == 0
+        parts = [
+            jnp.where(low, a, pltpu.roll(b, step, 0)) + jnp.where(low, pltpu.roll(a, count - step, 0), b)
+            for a, b in zip(parts[:step], parts[step:])
+        ]
+        step //= 2
+    return parts[0]
+
+
+def spread_levels(field_ref, depth, levels, halos, depth_halos):
+    north, south, west, east = halos
+    rows, cols = depth.shape
+    sub = lax.broadcasted_iota(jnp.int32, depth.shape, 0)
+    lanes = lane_ids(depth.shape)
+
+    def shifted(value, first, last, left, right):
+        return (
+            jnp.where(sub == rows - 1, last, pltpu.roll(value, rows - 1, 0)),
+            jnp.where(sub == 0, first, pltpu.roll(value, 1, 0)),
+            jnp.where(lanes == 0, left, pltpu.roll(value, 1, 1)),
+            jnp.where(lanes == cols - 1, right, pltpu.roll(value, cols - 1, 1)),
+        )
+
+    shared = [jnp.minimum(depth, near) for near in shifted(depth, *depth_halos)]
+
+    def spread(k):
+        center = field_ref[k * rows : (k + 1) * rows, :]
+        near = shifted(
+            center,
+            north[k : k + 1, :],
+            south[k : k + 1, :],
+            pltpu.roll(west, (cols - k) % cols, 1) if k else west,
+            pltpu.roll(east, cols - 1 - k, 1),
+        )
+        flux = jnp.zeros(center.shape, f32)
+        for value, limit in zip(near, shared):
+            flux = flux + jnp.where(limit > float(k), value - center, 0.0)
+        return center + spread_coef * flux
+
+    return spread
 
 
 def spread_rows(field_ref, depth, levels, rows, halos, depth_halos):
@@ -131,6 +185,14 @@
     )
 
 
+def turn_of(lat):
+    return (lat ^ (lat >> 1)) & 1
+
+
+def half_odd():
+    return (lax.axis_index("core") ^ turn_of(lax.axis_index("lat"))) == 1
+
+
 def odd_places():
     return (lax.axis_index("lat") % 2 == 1, lax.axis_index("core") == 1)
 
@@ -139,35 +201,55 @@
     out[...] = jnp.zeros(out.shape, f32)
 
 
-def edge_kernel(levels, tracer, mask, bottom, small, lat_a, lat_b, depth_out, pad):
+def edge_kernel(levels, tracer, mask, bottom, small, lat_a, lat_b, depth_out):
     rows = mask.shape[0]
     depth = (mask[...] * bottom[...]).astype(f32)
     depth_out[...] = depth
     lat_odd, lon_odd = odd_places()
-    lon_a, lon_b = small.at[0:rows, :], small.at[rows:, :]
-    write_lon_edges(tracer, levels, rows, pad, lon_a, lon_b, lon_odd, depth)
+    low, high = lon_edges([(k, tracer[k * rows : (k + 1) * rows, :]) for k in range(levels)], levels)
+    at = lane_ids(low.shape) == levels
+    cols = low.shape[1]
+    low = jnp.where(at, jnp.broadcast_to(depth[:, 0:1], low.shape), low)
+    high = jnp.where(at, jnp.broadcast_to(depth[:, cols - 1 :], high.shape), high)
+    small[0:rows, :] = jnp.where(lon_odd, low, high)
+    small[rows:, :] = jnp.where(lon_odd, high, low)
     write_lat_edges(tracer, levels, rows, lat_a, lat_b, lat_odd, depth)
 
 
 def energy_kernel(levels, tracer, depth_ref, energy, pad):
     rows, cols = depth_ref.shape
     depth = depth_ref[...]
-    lev = level_ids((levels, cols))
-    total = jnp.zeros((levels, cols), f32)
-    for row in range(rows):
-        wet_tracer = jnp.where(lev < depth[row : row + 1, :], row_of(tracer, row, levels, rows), 0.0)
-        total = total + wet_tracer * wet_tracer
-    energy[...] = jnp.broadcast_to(lane_sums(pad, total)[None], energy.shape)
+    pad[...] = jnp.zeros(pad.shape, f32)
+    for group in range(0, levels, rows):
+        squares = []
+        for k in range(group, group + rows):
+            if k < levels:
+                wet_tracer = jnp.where(depth > float(k), tracer[k * rows : (k + 1) * rows, :], 0.0)
+                squares.append(wet_tracer * wet_tracer)
+            else:
+                squares.append(jnp.zeros((rows, cols), f32))
+        pad[group : group + rows, :] = sum_rows(squares)
+    sums = jnp.sum(pad[...].T, axis=0, keepdims=True)
+    energy[...] = jnp.broadcast_to(sums[None], energy.shape)
 
 
 def prepare_kernel(
     levels, tracer, depth_ref, w_in, b_in, w_out_t, b_out, kappa,
-    wet_tracer, wi_t, wi_b, wo_t, wo_b, bias, up_out,
+    wet_tracer, wi_t, wi_b, wo_t, wo_b, bias, kappa_col,
     pad, wi_f, wo_f,
 ):
     rows, cols = depth_ref.shape
     pad_levels, span = wet_tracer.shape
     depth = depth_ref[...]
+    for group in range(0, levels, rows):
+        parts = []
+        for k in range(group, group + rows):
+            if k < levels:
+                parts.append(jnp.where(depth > float(k), tracer[k * rows : (k + 1) * rows, :], 0.0))
+            else:
+                parts.append(jnp.zeros((rows, cols), f32))
+        for row, part in enumerate(exchange_sublanes(parts)):
+            wet_tracer[group : group + rows, row * cols : (row + 1) * cols] = part
     wet_tracer[levels:, :] = jnp.where(
         lax.broadcasted_iota(jnp.int32, (pad_levels - levels, span), 0) < 3, 1.0, 0.0
     )
@@ -176,14 +258,7 @@
     pad[1:2, 0:levels] = kappa[...]
     turned = pad[...].T
     bias[...] = jnp.broadcast_to(turned[:, 0:1], bias.shape)
-    kappa_col = jnp.broadcast_to(turned[0:levels, 1:2], (levels, cols))
-    lev = level_ids((levels, cols))
-    for row in range(rows):
-        at = pl.ds(row, levels, stride=rows)
-        wet = (lev < depth[row : row + 1, :]).astype(f32)
-        wet_tracer[0:levels, row * cols : (row + 1) * cols] = wet * row_of(tracer, row, levels, rows)
-        open_face = (lev + 1.0 < depth[row : row + 1, :]) & (lev + 1.0 < float(levels))
-        up_out[at, :] = jnp.where(open_face, kappa_col, 0.0)
+    kappa_col[...] = jnp.broadcast_to(turned[:, 1:2], kappa_col.shape)
 
     wi_f[...] = jnp.zeros(wi_f.shape, f32)
     wi_f[0:levels, :] = w_in[...].astype(f32)
@@ -205,8 +280,8 @@
 
 
 def network_kernel(
-    levels, rows, column_count, energy, wet_tracer, wi_t, wo_t, bias, up,
-    radius_row, x_b, hidden, slope, gate, down_out,
+    levels, rows, column_count, energy, wet_tracer, wi_t, wo_t, bias,
+    radius_row, x_b, hidden, slope, gate, sinking, soft,
 ):
     cols = bias.shape[1]
     hid = wi_t.shape[0]
@@ -226,106 +301,133 @@
         hidden[at, :] = product.astype(bf16)
         slope[at, :] = sig + product * (1.0 - sig)
 
+    used = round_up(levels, 16)
     for row in range(rows):
         part = slice(row * cols, (row + 1) * cols)
-        at = pl.ds(row, levels, stride=rows)
-        logits = jnp.dot(wo_t[...], hidden[:, part], preferred_element_type=f32) + bias[...]
-        gate[:, part] = 0.5 + 0.5 * jnp.tanh(0.5 * logits)
-        soft = jnp.maximum(logits, 0.0) + jnp.log(1.0 + jnp.exp(-jnp.abs(logits)))
-        face_up = row_of(up, row, levels, rows)
-        down_out[at, :] = jnp.where(face_up > 0.0, face_up + soft[0:levels, :], 0.0)
+        logits = jnp.dot(wo_t[0:used, :], hidden[:, part], preferred_element_type=f32) + bias[0:used, :]
+        gate[0:used, part] = 0.5 + 0.5 * jnp.tanh(0.5 * logits)
+        soft[0:used, part] = jnp.maximum(logits, 0.0) + jnp.log(1.0 + jnp.exp(-jnp.abs(logits)))
+    for group in range(0, levels, rows):
+        parts = [soft[group : group + rows, row * cols : (row + 1) * cols] for row in range(rows)]
+        for k, part in enumerate(exchange_sublanes(parts), group):
+            if k < levels:
+                sinking[k * rows : (k + 1) * rows, :] = part
 
 
 def solve_kernel(
     levels, scale,
-    tracer, north, south, west, east, wet_tracer, cotangent, depth_ref, up_ref, down_ref,
+    tracer, north, south, west, east, wet_tracer, cotangent, depth_ref, kappa_col, sinking,
     wo_b, wi_b, x_b, hidden, slope, gate,
     keep, send, adjoint, lat_a, lat_b, d_inputs,
-    pad, mixed, dl_f, dl_b, dp_b, rate_a, rate_b, inv_p, fwd_z, fwd_u, flow,
+    pad, mixed, dl_f, dl_b, dp_b, rate_a, rate_b, inv_p, fwd_z, fwd_u,
 ):
     rows, cols = depth_ref.shape
     hid = wo_b.shape[0]
     span = rows * cols
     pad_levels = dl_f.shape[0]
     depth = depth_ref[...]
-    halos = halo_values(levels, north, south, west, east)
     depth_halos = halo_depths(levels, north, south, west, east, depth.shape)
-    for row, _, _, value in spread_rows(tracer, depth, levels, rows, halos, depth_halos):
-        mixed[pl.ds(row, levels, stride=rows), :] = value
+    spread = spread_levels(tracer, depth, levels, (north, south, west[...], east[...]), depth_halos)
+
+    def face_terms(k):
+        open_face = depth > float(k + 1)
+        kappa = jnp.broadcast_to(kappa_col[k : k + 1, :], (rows, cols))
+        up = jnp.where(open_face, kappa, 0.0)
+        return jnp.where(open_face, kappa + sinking[at_level(k), :], 0.0), up
 
     def at_level(k):
         return slice(k * rows, (k + 1) * rows)
 
     mid = levels // 2
-    top = jnp.ones((rows, cols), f32)
+    ones = jnp.ones((rows, cols), f32)
+    num, den = ones, ones
+    num_end, den_end = ones, ones
+    for step in range(mid):
+        k = step
+        down, up = face_terms(k)
+        pivot = num + down * den
+        over = 1.0 / pivot
+        inv = den * over
+        inv_p[at_level(k), :] = inv
+        rate_a[at_level(k), :] = down * inv
+        rate_b[at_level(k), :] = up * inv
+        num, den = pivot + up * num, pivot
+        if step % 4 == 3:
+            num, den = num * over, ones
+        k = levels - 1 - step
+        if k > mid:
+            down, up = face_terms(k - 1)
+            pivot = num_end + up * den_end
+            over = 1.0 / pivot
+            inv = den_end * over
+            inv_p[at_level(k), :] = inv
+            rate_a[at_level(k), :] = down * inv
+            rate_b[at_level(k), :] = up * inv
+            num_end, den_end = down * num_end, pivot
+            if k - 1 > mid:
+                num_end = pivot + num_end
+            if step % 4 == 3:
+                num_end, den_end = num_end * over, ones
+        mixed[at_level(step), :] = spread(step)
+        mixed[at_level(levels - 1 - step), :] = spread(levels - 1 - step)
+    if levels % 2:
+        mixed[at_level(mid), :] = spread(mid)
+    middle = 1.0 / (num / den + num_end / den_end)
+
     z = mixed[at_level(0), :]
     u = cotangent[at_level(0), :]
-    end = jnp.ones((rows, cols), f32)
     z_end = mixed[at_level(levels - 1), :]
     u_end = cotangent[at_level(levels - 1), :]
     for step in range(mid):
         k = step
-        down, up = down_ref[at_level(k), :], up_ref[at_level(k), :]
-        inv = 1.0 / (top + down)
-        a, b = down * inv, up * inv
-        inv_p[at_level(k), :] = inv
-        rate_a[at_level(k), :] = a
-        rate_b[at_level(k), :] = b
-        fwd_z[at_level(k), :] = z
-        fwd_u[at_level(k), :] = u
-        top = 1.0 + b * top
+        inv, a, b = inv_p[at_level(k), :], rate_a[at_level(k), :], rate_b[at_level(k), :]
+        fwd_z[at_level(k), :] = z * inv
+        fwd_u[at_level(k), :] = u * inv
         z = mixed[at_level(k + 1), :] + a * z
         u = cotangent[at_level(k + 1), :] + b * u
         k = levels - 1 - step
         if k > mid:
-            down, up = down_ref[at_level(k - 1), :], up_ref[at_level(k - 1), :]
-            inv = 1.0 / (end + up)
-            a, b = down * inv, up * inv
-            inv_p[at_level(k), :] = inv
-            rate_a[at_level(k), :] = a
-            rate_b[at_level(k), :] = b
-            fwd_z[at_level(k), :] = z_end
-            fwd_u[at_level(k), :] = u_end
-            end = a * end
+            inv, a, b = inv_p[at_level(k), :], rate_a[at_level(k), :], rate_b[at_level(k), :]
+            fwd_z[at_level(k), :] = z_end * inv
+            fwd_u[at_level(k), :] = u_end * inv
             z_end = b * z_end
             u_end = a * u_end
             if k - 1 > mid:
-                end = 1.0 + end
                 z_end = mixed[at_level(k - 1), :] + z_end
                 u_end = cotangent[at_level(k - 1), :] + u_end
-    inv = 1.0 / (top + end)
-    x_up = x_down = (z + z_end) * inv
-    y_up = y_down = (u + u_end) * inv
+    x_up = x_down = (z + z_end) * middle
+    y_up = y_down = (u + u_end) * middle
     adjoint[at_level(mid), :] = y_up
-    for step in range(1, levels - mid):
+
+    flows = {levels - 1: jnp.zeros((rows, cols), f32)}
+
+    def put(k, value):
+        flows[k] = value
+        first = k - k % rows
+        members = range(first, min(first + rows, levels))
+        if all(member in flows for member in members):
+            parts = [flows[member] for member in members]
+            parts += [jnp.zeros((rows, cols), f32)] * (rows - len(parts))
+            for row, part in enumerate(exchange_sublanes(parts)):
+                at = slice(row * cols, (row + 1) * cols)
+                dl_f[first : first + rows, at] = part * gate[first : first + rows, at]
+
+    dl_f[round_up(levels, rows) :, :] = jnp.zeros((pad_levels - round_up(levels, rows), span), f32)
+    for step in range(1, max(levels - mid, mid + 1)):
         k = mid + step
-        inv = inv_p[at_level(k), :]
-        x_new = fwd_z[at_level(k), :] * inv + rate_a[at_level(k), :] * x_down
-        y_new = fwd_u[at_level(k), :] * inv + rate_b[at_level(k), :] * y_down
-        adjoint[at_level(k), :] = y_new
-        flow[at_level(k - 1), :] = jnp.where(depth > float(k), x_down * (y_new - y_down), 0.0)
-        x_down, y_down = x_new, y_new
+        if k < levels:
+            x_new = fwd_z[at_level(k), :] + rate_a[at_level(k), :] * x_down
+            y_new = fwd_u[at_level(k), :] + rate_b[at_level(k), :] * y_down
+            adjoint[at_level(k), :] = y_new
+            put(k - 1, jnp.where(depth > float(k), x_down * (y_new - y_down), 0.0))
+            x_down, y_down = x_new, y_new
         k = mid - step
         if k >= 0:
-            inv = inv_p[at_level(k), :]
-            x_up = fwd_z[at_level(k), :] * inv + rate_b[at_level(k), :] * x_up
-            y_new = fwd_u[at_level(k), :] * inv + rate_a[at_level(k), :] * y_up
+            x_up = fwd_z[at_level(k), :] + rate_b[at_level(k), :] * x_up
+            y_new = fwd_u[at_level(k), :] + rate_a[at_level(k), :] * y_up
             adjoint[at_level(k), :] = y_new
-            flow[at_level(k), :] = jnp.where(depth > float(k + 1), x_up * (y_up - y_new), 0.0)
+            put(k, jnp.where(depth > float(k + 1), x_up * (y_up - y_new), 0.0))
             y_up = y_new
-    for k in range(mid - (levels - mid), -1, -1):
-        inv = inv_p[at_level(k), :]
-        x_up = fwd_z[at_level(k), :] * inv + rate_b[at_level(k), :] * x_up
-        y_new = fwd_u[at_level(k), :] * inv + rate_a[at_level(k), :] * y_up
-        adjoint[at_level(k), :] = y_new
-        flow[at_level(k), :] = jnp.where(depth > float(k + 1), x_up * (y_up - y_new), 0.0)
-        y_up = y_new
-    flow[at_level(levels - 1), :] = jnp.zeros((rows, cols), f32)
-
-    dl_f[levels:, :] = jnp.zeros((pad_levels - levels, span), f32)
-    for row in range(rows):
-        part = slice(row * cols, (row + 1) * cols)
-        dl_f[0:levels, part] = row_of(flow, row, levels, rows) * gate[0:levels, part]
     dl_b[...] = dl_f[...].astype(bf16)
     bout = jnp.zeros((pad_levels, cols), f32)
     for row in range(rows):
@@ -337,7 +439,7 @@
         at = slice(part * block, (part + 1) * block)
         d_hidden = jnp.dot(wo_b[at, :], dl_b[...], preferred_element_type=f32)
         dp_b[at, :] = (d_hidden * slope[at, :]).astype(bf16)
-    d_in = jnp.dot(wi_b[...], dp_b[...], preferred_element_type=f32)
+    d_in = jnp.dot(wi_b[0 : round_up(levels, 16), :], dp_b[...], preferred_element_type=f32)
     level = jnp.zeros((levels, cols), f32)
     for row in range(rows):
         at = slice(row * cols, (row + 1) * cols)
@@ -347,21 +449,23 @@
     level_row = lane_sums(pad, level)
 
     contract = (((1,), (1,)), ((), ()))
+    used = round_up(levels + 3, 16)
     lat_odd, lon_odd = odd_places()
+    keeps_out = half_odd()
     quarter = lax.axis_index("lat") % 4
     height = keep.shape[1]
     for half in range(2):
         wide = slice(2 * half * block, (2 * half + 2) * block)
-        both_in = lax.dot_general(x_b[...], dp_b[wide, :], contract, preferred_element_type=f32)
-        both_out = lax.dot_general(dl_b[...], hidden[wide, :], contract, preferred_element_type=f32)
+        both_in = lax.dot_general(x_b[0:used, :], dp_b[wide, :], contract, preferred_element_type=f32)
+        both_out = lax.dot_general(dl_b[0:used, :], hidden[wide, :], contract, preferred_element_type=f32)
         for part in range(2):
             at = slice(part * block, (part + 1) * block)
             slot = (2 * half + part) ^ quarter
             g_in = both_in[0:height, at] * scale
             g_out = both_out[0:height, at] * scale
             lower = send.at[pl.ds(pl.multiple_of(slot * height, 8), height), :]
-            keep[slot] = jnp.where(lon_odd, g_out, g_in)
-            lower[...] = jnp.where(lon_odd, g_in, g_out)
+            keep[slot] = jnp.where(keeps_out, g_out, g_in)
+            lower[...] = jnp.where(keeps_out, g_in, g_out)
             keep[slot, levels + 1 : levels + 2, :] = level_row
             keep[slot, levels + 2 : levels + 3, :] = bout_row
             lower[levels + 1 : levels + 2, :] = level_row
@@ -369,7 +473,9 @@
     lon_a = send.at[4 * height : 4 * height + rows, :]
     lon_b = send.at[4 * height + rows : 4 * height + 2 * rows, :]
     write_lat_edges(adjoint, levels, rows, lat_a, lat_b, lat_odd)
-    write_lon_edges(adjoint, levels, rows, pad, lon_a, lon_b, lon_odd)
+    low, high = lon_edges([(k, adjoint[at_level(k), :]) for k in range(levels)], levels)
+    lon_a[...] = jnp.where(lon_odd, low, high)
+    lon_b[...] = jnp.where(lon_odd, high, low)
 
 
 def final_kernel(
@@ -393,14 +499,14 @@
 
 
 def gather_kernel(levels, height, mine, other, grad_in, grad_bin, grad_out, grad_bout):
-    lon_odd = lax.axis_index("core") == 1
+    keeps_out = half_odd()
     quarter = lax.axis_index("lat") % 4
     block = mine.shape[1]
     for step in range(4):
         at = pl.ds(pl.multiple_of((step ^ quarter) * block, block), block)
         rows = slice(step * height, (step + 1) * height)
-        inner = jnp.where(lon_odd, other[rows, :], mine[rows, :])
-        outer = jnp.where(lon_odd, mine[rows, :], other[rows, :])
+        inner = jnp.where(keeps_out, other[rows, :], mine[rows, :])
+        outer = jnp.where(keeps_out, mine[rows, :], other[rows, :])
         grad_in[:, at] = inner[0:levels, :]
         grad_bin[:, at] = inner[levels : levels + 1, :]
         grad_out[:, at] = outer[0:levels, :]
@@ -409,6 +515,12 @@
 
 def flip(count, by):
     return [(i, i ^ by) for i in range(count)]
+
+
+def cross_flip(count, by):
+    return [
+        (2 * i + core, 2 * (i ^ by) + (core ^ turn_of(by))) for i in range(count) for core in range(2)
+    ]
 
 
 def far_pairs(count, ring):
@@ -469,7 +581,6 @@
         ],
         in_specs=[vmem] * 4,
         out_specs=[vmem] * 4,
-        scratch_shapes=[pad],
         compiler_params=params,
     )(zero, tracer, land_mask, bottom)
     energy = pl.pallas_call(
@@ -491,7 +602,7 @@
 
     flat_scratch = pltpu.VMEM(flat, f32)
     wide = sds((pad_levels, span), f32)
-    wet_tracer, wi_t, wi_b, wo_t, wo_b, bias, up = pl.pallas_call(
+    wet_tracer, wi_t, wi_b, wo_t, wo_b, bias, kappa_col = pl.pallas_call(
         lambda *refs: prepare_kernel(levels, *refs),
         out_shape=[
             wide,
@@ -500,7 +611,7 @@
             sds((pad_levels, hid), bf16),
             sds((hid, pad_levels), bf16),
             sds((pad_levels, cols), f32),
-            sds(flat, f32),
+            sds((pad_levels, cols), f32),
         ],
         in_specs=[vmem] * 7,
         out_specs=[vmem] * 7,
@@ -509,7 +620,7 @@
         cost_estimate=ahead,
     )(tracer, depth, w_in, b_in, w_out_t, b_out, kappa)
 
-    radius_row, x_b, hidden, slope, gate, down = pl.pallas_call(
+    radius_row, x_b, hidden, slope, gate, sinking = pl.pallas_call(
         lambda *refs: network_kernel(levels, rows, column_count, *refs),
         out_shape=[
             sds((1, pad_levels), f32),
@@ -519,10 +630,11 @@
             wide,
             sds(flat, f32),
         ],
-        in_specs=[vmem] * 6,
+        in_specs=[vmem] * 5,
         out_specs=[vmem] * 6,
+        scratch_shapes=[pltpu.VMEM((pad_levels, span), f32)],
         compiler_params=params,
-    )(energy, wet_tracer, wi_t, wo_t, bias, up)
+    )(energy, wet_tracer, wi_t, wo_t, bias)
 
     keep, send, adjoint, lat_a, lat_b, d_inputs = pl.pallas_call(
         lambda *refs: solve_kernel(levels, 1.0 / math.sqrt(column_count), *refs),
@@ -542,11 +654,11 @@
             pltpu.VMEM((pad_levels, span), f32),
             pltpu.VMEM((pad_levels, span), bf16),
             pltpu.VMEM((hid, span), bf16),
-            *[flat_scratch] * 6,
+            *[flat_scratch] * 5,
         ],
         compiler_params=params,
     )(
-        tracer, t_north, t_south, t_west, t_east, wet_tracer, cotangent, depth, up, down,
+        tracer, t_north, t_south, t_west, t_east, wet_tracer, cotangent, depth, kappa_col, sinking,
         wo_b, wi_b, x_b, hidden, slope, gate,
     )
 
@@ -555,8 +667,8 @@
     lon_near = got[4 * height : 4 * height + rows]
     lon_pass = got[4 * height + rows :]
     part = chip[0]
-    for step in (1, 2, 3):
-        part = part + lax.ppermute(chip[step], "lat", flip(lats, step))
+    for step in (3, 1, 2):
+        part = part + lax.ppermute(chip[step], ("lat", "core"), cross_flip(lats, step))
     step = 4
     while step < lats:
         part = part + lax.ppermute(part, "lat", flip(lats, step))
@@ -589,7 +701,7 @@
         north, south, west, east, t_north, t_south, t_west, t_east,
     )
 
-    came = {step: lax.ppermute(part, "lat", flip(lats, step)) for step in (1, 2, 3)}
+    came = {step: lax.ppermute(part, ("lat", "core"), cross_flip(lats, step)) for step in (1, 2, 3)}
     mine = [part] + [came[step] for step in range(1, 4)]
     mine, tracer_adjoint = lax.optimization_barrier((mine, tracer_adjoint))
     mine = jnp.concatenate(mine, 0)

time: 46.9 us -> 46.7 us (level)
    ppermute x1, starting transfers between devices: 0.07 us -> 0.78 us  [shards(): other = lax.ppermute(mine, 'core', flip(2, 1))]
    ppermute x6, starting transfers between devices: 7.11 us -> 6.55 us  [the longest x3 3.27 us: shards(): lax.ppermute(part, ('lat', 'core'), cross_flip(lats, step))]
  transfers between devices with their start and end apart: 18 -> 18, of which waited for: 10 -> 9; matrix products, arithmetic and copies ran while one was open for 0% -> 0% of each run, Pallas kernels for 9% -> 9%
where the time goes in v7:
time: 46.7 us; the launch traced here: 46.5 us
  starting transfers between devices  25.3 us (54%)
  waiting for transfers between devices  11.7 us (25%)
  Pallas kernels  7.42 us (16%)
  local copies, waits for them, and re-layouts  1.04 us (2%)
  between operations  0.91 us (2%)
    ppermute x1, starting transfers between devices, shards(): lax.ppermute(small[rows:], ('z', 'core'), far_pairs(lons, True))  4.55 us
    ppermute x3, starting transfers between devices, shards(): lax.ppermute(packed, 'z', flip(chips, step))  4.45 us
    ppermute x3, waiting for transfers between devices, shards(): lax.ppermute(packed, 'z', flip(chips, step))  3.78 us
    all_to_all x1, starting transfers between devices, shards(): energy = lax.all_to_all(energy, ('lat', 'z', 'core'), 0, 0, tiled=True)  3.48 us
    all_to_all x1, waiting for transfers between devices, shards(): energy = lax.all_to_all(energy, ('lat', 'z', 'core'), 0, 0, tiled=True)  3.33 us
    ppermute x3, starting transfers between devices, shards(): lax.ppermute(part, ('lat', 'core'), cross_flip(lats, step))  3.27 us
    ppermute x3, starting transfers between devices, shards(): lax.ppermute(chip[step], ('lat', 'core'), cross_flip(lats, step))  3.27 us
    ppermute x2, starting transfers between devices, swap_lat(): lax.ppermute(lat_b, 'lat', far_pairs(lats, True))  2.94 us
  transfers between devices with their start and end apart: 18, of which 9 were waited for; matrix products, arithmetic and copies ran while one was open for 0% of the time, Pallas kernels for 9%

profile of v7, /device:TPU:0, one launch (start us, length us, event | category | flops | bytes accessed | tf_op | source)
XLA Modules:
  0.0 46.5 jit_solution(11912471012774776913)
XLA Ops:
  2.0 4.6 %collective-permute-start.3 = (f32[8,128]{1,0:T(8,128)S(1)}, f32[8,128]{1,0:T(8,128)S(1)}, u32[]{:S(2)}, u32[]{:S(2)}) collective-permute-start(f32[8,128]{1,0:T(8,128)S(1)} %get-tuple-element.80), channel_id=1, source_target_pairs={{1,2},{3,4},{5,6},{7,0},{2,1},{4,3},{6,5},{0,7},{9,10},{11,12},{13... | collective-permute-start | bytes 12296 | tf_op jit(solution)/shard_map/ppermute | solution.py:599
  6.5 0.8 %shard_map.131 = f32[32,1,128]{2,1,0:T(1,128)} custom-call(f32[800,128]{1,0:T(8,128)S(1)} %bitcast.26, f32[8,128]{1,0:T(8,128)S(1)} %get-tuple-element.40.refs_1_.refs_7_.refs_5_), custom_call_target="tpu_custom_call" | custom-call | flops 1000000000 | bytes 100000000 | tf_op jit(solution)/shard_map/pallas_call | solution.py:586
  7.3 3.5 %all-to-all-start = ((f32[32,1,128]{2,1,0:T(1,128)}), f32[32,1,128]{2,1,0:T(1,128)S(1)}, u32[]{:S(2)}, u32[]{:S(2)}) async-start(f32[32,1,128]{2,1,0:T(1,128)} %shard_map.131), calls=%async_computation | async-start | bytes 32768 | tf_op jit(solution)/shard_map/all_to_all | solution.py:595
  10.8 1.8 %collective-permute-start = (f32[104,128]{1,0:T(8,128)S(1)}, f32[104,128]{1,0:T(8,128)S(1)}, u32[]{:S(2)}, u32[]{:S(2)}) collective-permute-start(f32[104,128]{1,0:T(8,128)S(1)} %get-tuple-element.37), channel_id=1, source_target_pairs={{0,8},{8,0},{16,24},{24,16},{1,9},{9,1},{17,25},{25,17},{2,10},{10... | collective-permute-start | bytes 159752 | tf_op jit(solution)/shard_map/ppermute | solution.py:540
  12.6 1.5 %collective-permute-start.1 = (f32[104,128]{1,0:T(8,128)S(1)}, f32[104,128]{1,0:T(8,128)S(1)}, u32[]{:S(2)}, u32[]{:S(2)}) collective-permute-start(f32[104,128]{1,0:T(8,128)S(1)} %get-tuple-element.38), channel_id=1, source_target_pairs={{8,16},{24,0},{16,8},{0,24},{9,17},{25,1},{17,9},{1,25},{10,18},{2... | collective-permute-start | bytes 159752 | tf_op jit(solution)/shard_map/ppermute | solution.py:541
  14.5 3.3 %all-to-all-done.refs_0_ = f32[32,1,128]{2,1,0:T(1,128)S(1)} async-done(((f32[32,1,128]{2,1,0:T(1,128)}), f32[32,1,128]{2,1,0:T(1,128)S(1)}, u32[]{:S(2)}, u32[]{:S(2)}) %all-to-all-start) | async-done | bytes 16416 | tf_op jit(solution)/shard_map/all_to_all | solution.py:595
  17.9 1.4 %shard_map.132 = (f32[1,128]{1,0:T(1,128)S(1)}, bf16[128,1024]{1,0:T(8,128)(2,1)S(1)}, bf16[512,1024]{1,0:T(8,128)(2,1)S(1)}, f32[512,1024]{1,0:T(8,128)S(1)}, f...) custom-call(f32[32,1,128]{2,1,0:T(1,128)S(1)} %all-to-all-done.refs_0_, ...), custom_call_target="tpu_custom_call" | custom-call | tf_op jit(solution)/shard_map/pallas_call | solution.py:623
  19.4 2.3 %shard_map.133 = (f32[4,104,128]{2,1,0:T(8,128)S(1)}, f32[432,128]{1,0:T(8,128)S(1)}, f32[800,128]{1,0:T(8,128)S(1)}, f32[104,128]{1,0:T(8,128)S(1)}, f32[104,12...) custom-call(f32[800,128]{1,0:T(8,128)S(1)} %bitcast.28, f32[104,128]{1,0:T(8,128)S(1)} %get-tuple-element.77.refs_1_.refs_10_, ...), custom_call_target="tpu_custom_call" | custom-call | tf_op jit(solution)/shard_map/pallas_call | solution.py:639
  21.7 1.5 %collective-permute-done.4 = f32[432,128]{1,0:T(8,128)S(1)} collective-permute-done((f32[432,128]{1,0:T(8,128)S(1)}, f32[432,128]{1,0:T(8,128)S(1)}, u32[]{:S(2)}, u32[]{:S(2)}) %collective-permute-start.4) | collective-permute-done | bytes 221216 | tf_op jit(solution)/shard_map/ppermute | solution.py:665
  23.2 0.7 %collective-permute-start.5 = (f32[104,128]{1,0:T(8,128)S(1)}, f32[104,128]{1,0:T(8,128)S(1)}, u32[]{:S(2)}, u32[]{:S(2)}) collective-permute-start(f32[104,128]{1,0:T(8,128)S(1)} %get-tuple-element.71), channel_id=1, source_target_pairs={{0,24},{1,25},{8,16},{9,17},{16,8},{17,9},{24,0},{25,1},{2,26},{3,... | collective-permute-start | bytes 159752 | tf_op jit(solution)/shard_map/ppermute | solution.py:671
  23.9 0.9 %collective-permute-start.7 = (f32[104,128]{1,0:T(8,128)S(1)}, f32[104,128]{1,0:T(8,128)S(1)}, u32[]{:S(2)}, u32[]{:S(2)}) collective-permute-start(f32[104,128]{1,0:T(8,128)S(1)} %get-tuple-element.72), channel_id=1, source_target_pairs={{0,17},{1,16},{8,25},{9,24},{16,1},{17,0},{24,9},{25,8},{2,19},{3,... | collective-permute-start | bytes 159752 | tf_op jit(solution)/shard_map/ppermute | solution.py:671
  24.8 1.7 %collective-permute-start.6 = (f32[104,128]{1,0:T(8,128)S(1)}, f32[104,128]{1,0:T(8,128)S(1)}, u32[]{:S(2)}, u32[]{:S(2)}) collective-permute-start(f32[104,128]{1,0:T(8,128)S(1)} %get-tuple-element.73), channel_id=1, source_target_pairs={{0,9},{1,8},{8,1},{9,0},{16,25},{17,24},{24,17},{25,16},{2,11},{3,... | collective-permute-start | bytes 159752 | tf_op jit(solution)/shard_map/ppermute | solution.py:671
  27.1 1.5 %collective-permute-start.15 = (f32[104,128]{1,0:T(8,128)S(1)}, f32[104,128]{1,0:T(8,128)S(1)}, u32[]{:S(2)}, u32[]{:S(2)}) collective-permute-start(f32[104,128]{1,0:T(8,128)S(1)} %get-tuple-element.59), channel_id=1, source_target_pairs={{8,16},{24,0},{16,8},{0,24},{9,17},{25,1},{17,9},{1,25},{10,18},{2... | collective-permute-start | bytes 159752 | tf_op jit(solution)/shard_map/ppermute | solution.py:541
  29.2 2.1 %collective-permute-start.10 = (f32[112,128]{1,0:T(8,128)S(1)}, f32[112,128]{1,0:T(8,128)S(1)}, u32[]{:S(2)}, u32[]{:S(2)}) collective-permute-start(f32[112,128]{1,0:T(8,128)S(1)} %pad_maximum_fusion), channel_id=1, source_target_pairs={{0,6},{2,4},{4,2},{6,0},{1,7},{3,5},{5,3},{7,1},{8,14},{10,12},{12... | collective-permute-start | bytes 172040 | tf_op jit(solution)/shard_map/ppermute | solution.py:679
  31.3 2.3 %collective-permute-start.8 = (f32[112,128]{1,0:T(8,128)S(1)}, f32[112,128]{1,0:T(8,128)S(1)}, u32[]{:S(2)}, u32[]{:S(2)}) collective-permute-start(f32[112,128]{1,0:T(8,128)S(1)} %pad_maximum_fusion), channel_id=1, source_target_pairs={{0,2},{2,0},{4,6},{6,4},{1,3},{3,1},{5,7},{7,5},{8,10},{10,8},{12,... | collective-permute-start | bytes 172040 | tf_op jit(solution)/shard_map/ppermute | solution.py:679
  33.7 2.0 %collective-permute-done.10 = f32[112,128]{1,0:T(8,128)S(1)} collective-permute-done((f32[112,128]{1,0:T(8,128)S(1)}, f32[112,128]{1,0:T(8,128)S(1)}, u32[]{:S(2)}, u32[]{:S(2)}) %collective-permute-start.10) | collective-permute-done | bytes 57376 | tf_op jit(solution)/shard_map/ppermute | solution.py:679
  35.7 1.7 %collective-permute-done.9 = f32[112,128]{1,0:T(8,128)S(1)} collective-permute-done((f32[112,128]{1,0:T(8,128)S(1)}, f32[112,128]{1,0:T(8,128)S(1)}, u32[]{:S(2)}, u32[]{:S(2)}) %collective-permute-start.9) | collective-permute-done | bytes 57376 | tf_op jit(solution)/shard_map/ppermute | solution.py:679
  37.5 1.6 %collective-permute-start.13 = (f32[104,128]{1,0:T(8,128)S(1)}, f32[104,128]{1,0:T(8,128)S(1)}, u32[]{:S(2)}, u32[]{:S(2)}) collective-permute-start(f32[104,128]{1,0:T(8,128)S(1)} %slice_add_fusion.refs_1_), channel_id=1, source_target_pairs={{0,24},{1,25},{8,16},{9,17},{16,8},{17,9},{24,0},{25,1},{2,26},{3,... | collective-permute-start | bytes 159752 | tf_op jit(solution)/shard_map/ppermute | solution.py:704
  39.1 1.0 %collective-permute-start.12 = (f32[104,128]{1,0:T(8,128)S(1)}, f32[104,128]{1,0:T(8,128)S(1)}, u32[]{:S(2)}, u32[]{:S(2)}) collective-permute-start(f32[104,128]{1,0:T(8,128)S(1)} %slice_add_fusion.refs_1_), channel_id=1, source_target_pairs={{0,17},{1,16},{8,25},{9,24},{16,1},{17,0},{24,9},{25,8},{2,19},{3,... | collective-permute-start | bytes 159752 | tf_op jit(solution)/shard_map/ppermute | solution.py:704
  40.8 1.5 %shard_map.134 = f32[800,128]{1,0:T(8,128)} custom-call(f32[1,128]{1,0:T(1,128)S(1)} %get-tuple-element.55.refs_0_, f32[104,128]{1,0:T(8,128)S(1)} %slice_add_fusion.refs_1_, f32[800,128]{1,0:T(8,128)S(1)} %get-tuple-element.56.refs_2_, f32[128,1024]{1,0:T(8,128)S(1)} %get-tuple-element.41.refs_1_.refs_5_.refs_3_, ...), custom_call_target="tpu_custom_call" | custom-call | tf_op jit(solution)/shard_map/pallas_call | solution.py:693
  42.6 1.1 %collective-permute-done.12 = f32[104,128]{1,0:T(8,128)S(1)} collective-permute-done((f32[104,128]{1,0:T(8,128)S(1)}, f32[104,128]{1,0:T(8,128)S(1)}, u32[]{:S(2)}, u32[]{:S(2)}) %collective-permute-start.12) | collective-permute-done | bytes 53280 | tf_op jit(solution)/shard_map/ppermute | solution.py:704
  43.8 0.8 %collective-permute-start.16 = (f32[416,128]{1,0:T(8,128)S(1)}, f32[416,128]{1,0:T(8,128)S(1)}, u32[]{:S(2)}, u32[]{:S(2)}) collective-permute-start(f32[416,128]{1,0:T(8,128)S(1)} %constant_dynamic-update-slice_fusion.refs_0_), channel_id=1, source_target_pairs={{0,1},{1,0},{2,3},{3,2},{4,5},{5,4},{6,7},{7,6},{8,9},{9,8},{10,11... | collective-permute-start | bytes 638984 | tf_op jit(solution)/shard_map/ppermute | solution.py:708
  44.5 1.1 %collective-permute-done.16.refs_1_ = f32[416,128]{1,0:T(8,128)S(1)} collective-permute-done((f32[416,128]{1,0:T(8,128)S(1)}, f32[416,128]{1,0:T(8,128)S(1)}, u32[]{:S(2)}, u32[]{:S(2)}) %collective-permute-start.16) | collective-permute-done | bytes 213024 | tf_op jit(solution)/shard_map/ppermute | solution.py:708
  45.6 0.8 %shard_map.135 = (f32[100,512]{1,0:T(8,128)}, f32[1,512]{1,0:T(1,128)}, f32[100,512]{1,0:T(8,128)}, f32[1,100]{1,0:T(1,128)}) custom-call(f32[416,128]{1,0:T(8,128)S(1)} %constant_dynamic-update-slice_fusion.refs_0_, f32[416,128]{1,0:T(8,128)S(1)} %collective-permute-done.16.refs_1_), custom_call_target="tpu_custom_call" | custom-call | tf_op jit(solution)/shard_map/pallas_call | solution.py:709
  (54 shorter events, 4.1 us)
Async XLA Ops:
  0.7 13.4 %copy-start.4 = (bf16[100,512]{1,0:T(8,128)(2,1)S(1)}, bf16[100,512]{1,0:T(8,128)(2,1)}, u32[]{:S(2)}) copy-start(bf16[100,512]{1,0:T(8,128)(2,1)} %refs_2_.3) | copy-start | bytes 307204
  0.7 13.4 %copy-start.5 = (bf16[512,100]{0,1:T(8,128)(2,1)S(1)}, bf16[512,100]{0,1:T(8,128)(2,1)}, u32[]{:S(2)}) copy-start(bf16[512,100]{0,1:T(8,128)(2,1)} %param.16) | copy-start | bytes 307204
  0.7 13.4 %copy-start.6 = (f32[512]{0:T(512)S(1)}, f32[512]{0:T(512)}, u32[]{:S(2)}) copy-start(f32[512]{0:T(512)} %param.15) | copy-start | bytes 6148
  0.7 13.4 %copy-start.7 = (f32[100]{0:T(128)S(1)}, f32[100]{0:T(128)}, u32[]{:S(2)}) copy-start(f32[100]{0:T(128)} %param.17) | copy-start | bytes 1204
  0.7 13.4 %copy-start.8 = (f32[100]{0:T(128)S(1)}, f32[100]{0:T(128)}, u32[]{:S(2)}) copy-start(f32[100]{0:T(128)} %param.13) | copy-start | bytes 1204
  2.0 12.6 %collective-permute-start.3 = (f32[8,128]{1,0:T(8,128)S(1)}, f32[8,128]{1,0:T(8,128)S(1)}, u32[]{:S(2)}, u32[]{:S(2)}) collective-permute-start(f32[8,128]{1,0:T(8,128)S(1)} %get-tuple-element.80), channel_id=1, source_target_pairs={{1,2},{3,4},{5,6},{7,0},{2,1},{4,3},{6,5},{0,7},{9,10},{11,12},{13... | collective-permute-start | bytes 12296 | tf_op jit(solution)/shard_map/ppermute | solution.py:599
  6.5 8.0 %collective-permute-start.2 = (f32[8,128]{1,0:T(8,128)S(1)}, f32[8,128]{1,0:T(8,128)S(1)}, u32[]{:S(2)}, u32[]{:S(2)}) collective-permute-start(f32[8,128]{1,0:T(8,128)S(1)} %get-tuple-element.81), channel_id=1, source_target_pairs={{0,1},{1,0},{2,3},{3,2},{4,5},{5,4},{6,7},{7,6},{8,9},{9,8},{10,11... | collective-permute-start | bytes 12296 | tf_op jit(solution)/shard_map/ppermute | solution.py:598
  7.3 10.6 %all-to-all-start = ((f32[32,1,128]{2,1,0:T(1,128)}), f32[32,1,128]{2,1,0:T(1,128)S(1)}, u32[]{:S(2)}, u32[]{:S(2)}) async-start(f32[32,1,128]{2,1,0:T(1,128)} %shard_map.131), calls=%async_computation | async-start | bytes 32768 | tf_op jit(solution)/shard_map/all_to_all | solution.py:595
  10.8 8.5 %collective-permute-start = (f32[104,128]{1,0:T(8,128)S(1)}, f32[104,128]{1,0:T(8,128)S(1)}, u32[]{:S(2)}, u32[]{:S(2)}) collective-permute-start(f32[104,128]{1,0:T(8,128)S(1)} %get-tuple-element.37), channel_id=1, source_target_pairs={{0,8},{8,0},{16,24},{24,16},{1,9},{9,1},{17,25},{25,17},{2,10},{10... | collective-permute-start | bytes 159752 | tf_op jit(solution)/shard_map/ppermute | solution.py:540
  12.6 6.7 %collective-permute-start.1 = (f32[104,128]{1,0:T(8,128)S(1)}, f32[104,128]{1,0:T(8,128)S(1)}, u32[]{:S(2)}, u32[]{:S(2)}) collective-permute-start(f32[104,128]{1,0:T(8,128)S(1)} %get-tuple-element.38), channel_id=1, source_target_pairs={{8,16},{24,0},{16,8},{0,24},{9,17},{25,1},{17,9},{1,25},{10,18},{2... | collective-permute-start | bytes 159752 | tf_op jit(solution)/shard_map/ppermute | solution.py:541
  14.1 5.2 %copy-start.1 = (f32[100,8,128]{2,1,0:T(8,128)S(1)}, f32[100,8,128]{2,1,0:T(8,128)}, u32[]{:S(2)}) copy-start(f32[100,8,128]{2,1,0:T(8,128)} %param.10) | copy-start | bytes 1228804
  21.6 1.5 %collective-permute-start.4 = (f32[432,128]{1,0:T(8,128)S(1)}, f32[432,128]{1,0:T(8,128)S(1)}, u32[]{:S(2)}, u32[]{:S(2)}) collective-permute-start(f32[432,128]{1,0:T(8,128)S(1)} %get-tuple-element.54), channel_id=1, source_target_pairs={{0,1},{1,0},{2,3},{3,2},{4,5},{5,4},{6,7},{7,6},{8,9},{9,8},{10,11... | collective-permute-start | bytes 663560 | tf_op jit(solution)/shard_map/ppermute | solution.py:665
  23.2 5.6 %collective-permute-start.5 = (f32[104,128]{1,0:T(8,128)S(1)}, f32[104,128]{1,0:T(8,128)S(1)}, u32[]{:S(2)}, u32[]{:S(2)}) collective-permute-start(f32[104,128]{1,0:T(8,128)S(1)} %get-tuple-element.71), channel_id=1, source_target_pairs={{0,24},{1,25},{8,16},{9,17},{16,8},{17,9},{24,0},{25,1},{2,26},{3,... | collective-permute-start | bytes 159752 | tf_op jit(solution)/shard_map/ppermute | solution.py:671
  23.9 5.2 %collective-permute-start.7 = (f32[104,128]{1,0:T(8,128)S(1)}, f32[104,128]{1,0:T(8,128)S(1)}, u32[]{:S(2)}, u32[]{:S(2)}) collective-permute-start(f32[104,128]{1,0:T(8,128)S(1)} %get-tuple-element.72), channel_id=1, source_target_pairs={{0,17},{1,16},{8,25},{9,24},{16,1},{17,0},{24,9},{25,8},{2,19},{3,... | collective-permute-start | bytes 159752 | tf_op jit(solution)/shard_map/ppermute | solution.py:671
  24.8 4.4 %collective-permute-start.6 = (f32[104,128]{1,0:T(8,128)S(1)}, f32[104,128]{1,0:T(8,128)S(1)}, u32[]{:S(2)}, u32[]{:S(2)}) collective-permute-start(f32[104,128]{1,0:T(8,128)S(1)} %get-tuple-element.73), channel_id=1, source_target_pairs={{0,9},{1,8},{8,1},{9,0},{16,25},{17,24},{24,17},{25,16},{2,11},{3,... | collective-permute-start | bytes 159752 | tf_op jit(solution)/shard_map/ppermute | solution.py:671
  26.5 7.1 %collective-permute-start.14 = (f32[104,128]{1,0:T(8,128)S(1)}, f32[104,128]{1,0:T(8,128)S(1)}, u32[]{:S(2)}, u32[]{:S(2)}) collective-permute-start(f32[104,128]{1,0:T(8,128)S(1)} %get-tuple-element.58), channel_id=1, source_target_pairs={{0,8},{8,0},{16,24},{24,16},{1,9},{9,1},{17,25},{25,17},{2,10},{10... | collective-permute-start | bytes 159752 | tf_op jit(solution)/shard_map/ppermute | solution.py:540
  27.1 6.6 %collective-permute-start.15 = (f32[104,128]{1,0:T(8,128)S(1)}, f32[104,128]{1,0:T(8,128)S(1)}, u32[]{:S(2)}, u32[]{:S(2)}) collective-permute-start(f32[104,128]{1,0:T(8,128)S(1)} %get-tuple-element.59), channel_id=1, source_target_pairs={{8,16},{24,0},{16,8},{0,24},{9,17},{25,1},{17,9},{1,25},{10,18},{2... | collective-permute-start | bytes 159752 | tf_op jit(solution)/shard_map/ppermute | solution.py:541
  29.2 6.5 %collective-permute-start.10 = (f32[112,128]{1,0:T(8,128)S(1)}, f32[112,128]{1,0:T(8,128)S(1)}, u32[]{:S(2)}, u32[]{:S(2)}) collective-permute-start(f32[112,128]{1,0:T(8,128)S(1)} %pad_maximum_fusion), channel_id=1, source_target_pairs={{0,6},{2,4},{4,2},{6,0},{1,7},{3,5},{5,3},{7,1},{8,14},{10,12},{12... | collective-permute-start | bytes 172040 | tf_op jit(solution)/shard_map/ppermute | solution.py:679
  31.3 6.2 %collective-permute-start.9 = (f32[112,128]{1,0:T(8,128)S(1)}, f32[112,128]{1,0:T(8,128)S(1)}, u32[]{:S(2)}, u32[]{:S(2)}) collective-permute-start(f32[112,128]{1,0:T(8,128)S(1)} %pad_maximum_fusion), channel_id=1, source_target_pairs={{0,4},{2,6},{4,0},{6,2},{1,5},{3,7},{5,1},{7,3},{8,12},{10,14},{12... | collective-permute-start | bytes 172040 | tf_op jit(solution)/shard_map/ppermute | solution.py:679
  31.3 6.1 %collective-permute-start.8 = (f32[112,128]{1,0:T(8,128)S(1)}, f32[112,128]{1,0:T(8,128)S(1)}, u32[]{:S(2)}, u32[]{:S(2)}) collective-permute-start(f32[112,128]{1,0:T(8,128)S(1)} %pad_maximum_fusion), channel_id=1, source_target_pairs={{0,2},{2,0},{4,6},{6,4},{1,3},{3,1},{5,7},{7,5},{8,10},{10,8},{12,... | collective-permute-start | bytes 172040 | tf_op jit(solution)/shard_map/ppermute | solution.py:679
  37.5 5.2 %collective-permute-start.13 = (f32[104,128]{1,0:T(8,128)S(1)}, f32[104,128]{1,0:T(8,128)S(1)}, u32[]{:S(2)}, u32[]{:S(2)}) collective-permute-start(f32[104,128]{1,0:T(8,128)S(1)} %slice_add_fusion.refs_1_), channel_id=1, source_target_pairs={{0,24},{1,25},{8,16},{9,17},{16,8},{17,9},{24,0},{25,1},{2,26},{3,... | collective-permute-start | bytes 159752 | tf_op jit(solution)/shard_map/ppermute | solution.py:704
  39.1 4.6 %collective-permute-start.12 = (f32[104,128]{1,0:T(8,128)S(1)}, f32[104,128]{1,0:T(8,128)S(1)}, u32[]{:S(2)}, u32[]{:S(2)}) collective-permute-start(f32[104,128]{1,0:T(8,128)S(1)} %slice_add_fusion.refs_1_), channel_id=1, source_target_pairs={{0,17},{1,16},{8,25},{9,24},{16,1},{17,0},{24,9},{25,8},{2,19},{3,... | collective-permute-start | bytes 159752 | tf_op jit(solution)/shard_map/ppermute | solution.py:704
  40.1 3.6 %collective-permute-start.11 = (f32[104,128]{1,0:T(8,128)S(1)}, f32[104,128]{1,0:T(8,128)S(1)}, u32[]{:S(2)}, u32[]{:S(2)}) collective-permute-start(f32[104,128]{1,0:T(8,128)S(1)} %slice_add_fusion.refs_1_), channel_id=1, source_target_pairs={{0,9},{1,8},{8,1},{9,0},{16,25},{17,24},{24,17},{25,16},{2,11},{3,... | collective-permute-start | bytes 159752 | tf_op jit(solution)/shard_map/ppermute | solution.py:704
  43.8 1.9 %collective-permute-start.16 = (f32[416,128]{1,0:T(8,128)S(1)}, f32[416,128]{1,0:T(8,128)S(1)}, u32[]{:S(2)}, u32[]{:S(2)}) collective-permute-start(f32[416,128]{1,0:T(8,128)S(1)} %constant_dynamic-update-slice_fusion.refs_0_), channel_id=1, source_target_pairs={{0,1},{1,0},{2,3},{3,2},{4,5},{5,4},{6,7},{7,6},{8,9},{9,8},{10,11... | collective-permute-start | bytes 638984 | tf_op jit(solution)/shard_map/ppermute | solution.py:708
  (3 other events, 2.4 us)

commit v8 on v7

--- a/solution.py
+++ b/solution.py
@@ -642,8 +642,8 @@
             sds((4, height, hid // 4), f32),
             sds((4 * height + 2 * rows, hid // 4), f32),
             sds(flat, f32),
-            lat_edge,
-            lat_edge,
+            sds((height + rows, cols), f32),
+            sds((height + rows, cols), f32),
             sds((rows, height, cols), f32),
         ],
         in_specs=[vmem] * 16,
@@ -673,6 +673,7 @@
     while step < lats:
         part = part + lax.ppermute(part, "lat", flip(lats, step))
         step *= 2
+    part, lat_a, lat_b = lax.optimization_barrier((part, lat_a, lat_b))
     north, south = swap_lat(lat_odd, lats, lat_a, lat_b)
     if chips == 4:
         packed = jnp.concatenate([part, lon_pass], 0)

time: 46.7 us -> 46.1 us (0.987)
  waiting for transfers between devices: 11.7 us -> 11.2 us
    ppermute x3, waiting for transfers between devices: 3.78 us -> 1.48 us  [shards(): lax.ppermute(packed, 'z', flip(chips, step))]
    ppermute x3, waiting for transfers between devices: 0.59 us -> 2.65 us  [shards(): lax.ppermute(chip[step], ('lat', 'core'), cross_flip(lats, step))]
  transfers between devices with their start and end apart: 18 -> 18, of which waited for: 9 -> 8; matrix products, arithmetic and copies ran while one was open for 0% -> 0% of each run, Pallas kernels for 9% -> 9%
where the time goes in v8:
time: 46.1 us; the launch traced here: 45.9 us
  starting transfers between devices  25.2 us (55%)
  waiting for transfers between devices  11.2 us (24%)
  Pallas kernels  7.43 us (16%)
  local copies, waits for them, and re-layouts  1.04 us (2%)
  between operations  0.92 us (2%)
    ppermute x1, starting transfers between devices, shards(): lax.ppermute(small[rows:], ('z', 'core'), far_pairs(lons, True))  4.55 us
    ppermute x3, starting transfers between devices, shards(): lax.ppermute(packed, 'z', flip(chips, step))  4.45 us
    all_to_all x1, starting transfers between devices, shards(): energy = lax.all_to_all(energy, ('lat', 'z', 'core'), 0, 0, tiled=True)  3.48 us
    all_to_all x1, waiting for transfers between devices, shards(): energy = lax.all_to_all(energy, ('lat', 'z', 'core'), 0, 0, tiled=True)  3.33 us
    ppermute x3, starting transfers between devices, shards(): lax.ppermute(chip[step], ('lat', 'core'), cross_flip(lats, step))  3.27 us
    ppermute x3, starting transfers between devices, shards(): lax.ppermute(part, ('lat', 'core'), cross_flip(lats, step))  3.27 us
    ppermute x2, starting transfers between devices, swap_lat(): lax.ppermute(lat_b, 'lat', far_pairs(lats, True))  2.92 us
    ppermute x2, starting transfers between devices, swap_lat(): lax.ppermute(lat_a, 'lat', flip(lats, 1))  2.7 us
  transfers between devices with their start and end apart: 18, of which 8 were waited for; matrix products, arithmetic and copies ran while one was open for 0% of the time, Pallas kernels for 9%

profile of v8, /device:TPU:0, one launch (start us, length us, event | category | flops | bytes accessed | tf_op | source)
XLA Modules:
  0.0 45.9 jit_solution(15632869457337283241)
XLA Ops:
  2.0 4.6 %collective-permute-start.3 = (f32[8,128]{1,0:T(8,128)S(1)}, f32[8,128]{1,0:T(8,128)S(1)}, u32[]{:S(2)}, u32[]{:S(2)}) collective-permute-start(f32[8,128]{1,0:T(8,128)S(1)} %get-tuple-element.86), channel_id=1, source_target_pairs={{1,2},{3,4},{5,6},{7,0},{2,1},{4,3},{6,5},{0,7},{9,10},{11,12},{13... | collective-permute-start | bytes 12296 | tf_op jit(solution)/shard_map/ppermute | solution.py:599
  6.5 0.8 %shard_map.131 = f32[32,1,128]{2,1,0:T(1,128)} custom-call(f32[800,128]{1,0:T(8,128)S(1)} %bitcast.26, f32[8,128]{1,0:T(8,128)S(1)} %get-tuple-element.43.refs_1_.refs_7_.refs_5_), custom_call_target="tpu_custom_call" | custom-call | flops 1000000000 | bytes 100000000 | tf_op jit(solution)/shard_map/pallas_call | solution.py:586
  7.3 3.5 %all-to-all-start = ((f32[32,1,128]{2,1,0:T(1,128)}), f32[32,1,128]{2,1,0:T(1,128)S(1)}, u32[]{:S(2)}, u32[]{:S(2)}) async-start(f32[32,1,128]{2,1,0:T(1,128)} %shard_map.131), calls=%async_computation | async-start | bytes 32768 | tf_op jit(solution)/shard_map/all_to_all | solution.py:595
  10.8 1.8 %collective-permute-start = (f32[104,128]{1,0:T(8,128)S(1)}, f32[104,128]{1,0:T(8,128)S(1)}, u32[]{:S(2)}, u32[]{:S(2)}) collective-permute-start(f32[104,128]{1,0:T(8,128)S(1)} %get-tuple-element.40), channel_id=1, source_target_pairs={{0,8},{8,0},{16,24},{24,16},{1,9},{9,1},{17,25},{25,17},{2,10},{10... | collective-permute-start | bytes 159752 | tf_op jit(solution)/shard_map/ppermute | solution.py:540
  12.6 1.5 %collective-permute-start.1 = (f32[104,128]{1,0:T(8,128)S(1)}, f32[104,128]{1,0:T(8,128)S(1)}, u32[]{:S(2)}, u32[]{:S(2)}) collective-permute-start(f32[104,128]{1,0:T(8,128)S(1)} %get-tuple-element.41), channel_id=1, source_target_pairs={{8,16},{24,0},{16,8},{0,24},{9,17},{25,1},{17,9},{1,25},{10,18},{2... | collective-permute-start | bytes 159752 | tf_op jit(solution)/shard_map/ppermute | solution.py:541
  14.5 3.3 %all-to-all-done.refs_0_ = f32[32,1,128]{2,1,0:T(1,128)S(1)} async-done(((f32[32,1,128]{2,1,0:T(1,128)}), f32[32,1,128]{2,1,0:T(1,128)S(1)}, u32[]{:S(2)}, u32[]{:S(2)}) %all-to-all-start) | async-done | bytes 16416 | tf_op jit(solution)/shard_map/all_to_all | solution.py:595
  17.9 1.4 %shard_map.132 = (f32[1,128]{1,0:T(1,128)S(1)}, bf16[128,1024]{1,0:T(8,128)(2,1)S(1)}, bf16[512,1024]{1,0:T(8,128)(2,1)S(1)}, f32[512,1024]{1,0:T(8,128)S(1)}, f...) custom-call(f32[32,1,128]{2,1,0:T(1,128)S(1)} %all-to-all-done.refs_0_, ...), custom_call_target="tpu_custom_call" | custom-call | tf_op jit(solution)/shard_map/pallas_call | solution.py:623
  19.4 2.3 %shard_map.133 = (f32[4,104,128]{2,1,0:T(8,128)S(1)}, f32[432,128]{1,0:T(8,128)S(1)}, f32[800,128]{1,0:T(8,128)S(1)}, f32[112,128]{1,0:T(8,128)S(1)}, f32[112,12...) custom-call(f32[800,128]{1,0:T(8,128)S(1)} %bitcast.28, f32[104,128]{1,0:T(8,128)S(1)} %get-tuple-element.83.refs_1_.refs_10_, ...), custom_call_target="tpu_custom_call" | custom-call | tf_op jit(solution)/shard_map/pallas_call | solution.py:639
  21.7 1.5 %collective-permute-done.4 = f32[432,128]{1,0:T(8,128)S(1)} collective-permute-done((f32[432,128]{1,0:T(8,128)S(1)}, f32[432,128]{1,0:T(8,128)S(1)}, u32[]{:S(2)}, u32[]{:S(2)}) %collective-permute-start.4) | collective-permute-done | bytes 221216 | tf_op jit(solution)/shard_map/ppermute | solution.py:665
  23.9 0.9 %collective-permute-start.7 = (f32[104,128]{1,0:T(8,128)S(1)}, f32[104,128]{1,0:T(8,128)S(1)}, u32[]{:S(2)}, u32[]{:S(2)}) collective-permute-start(f32[104,128]{1,0:T(8,128)S(1)} %get-tuple-element.78), channel_id=1, source_target_pairs={{0,17},{1,16},{8,25},{9,24},{16,1},{17,0},{24,9},{25,8},{2,19},{3,... | collective-permute-start | bytes 159752 | tf_op jit(solution)/shard_map/ppermute | solution.py:671
  24.8 1.7 %collective-permute-start.6 = (f32[104,128]{1,0:T(8,128)S(1)}, f32[104,128]{1,0:T(8,128)S(1)}, u32[]{:S(2)}, u32[]{:S(2)}) collective-permute-start(f32[104,128]{1,0:T(8,128)S(1)} %get-tuple-element.79), channel_id=1, source_target_pairs={{0,9},{1,8},{8,1},{9,0},{16,25},{17,24},{24,17},{25,16},{2,11},{3,... | collective-permute-start | bytes 159752 | tf_op jit(solution)/shard_map/ppermute | solution.py:671
  26.5 2.3 %collective-permute-done.5 = f32[104,128]{1,0:T(8,128)S(1)} collective-permute-done((f32[104,128]{1,0:T(8,128)S(1)}, f32[104,128]{1,0:T(8,128)S(1)}, u32[]{:S(2)}, u32[]{:S(2)}) %collective-permute-start.5) | collective-permute-done | bytes 53280 | tf_op jit(solution)/shard_map/ppermute | solution.py:671
  29.2 2.0 %collective-permute-start.10 = (f32[112,128]{1,0:T(8,128)S(1)}, f32[112,128]{1,0:T(8,128)S(1)}, u32[]{:S(2)}, u32[]{:S(2)}) collective-permute-start(f32[112,128]{1,0:T(8,128)S(1)} %pad_maximum_fusion), channel_id=1, source_target_pairs={{0,6},{2,4},{4,2},{6,0},{1,7},{3,5},{5,3},{7,1},{8,14},{10,12},{12... | collective-permute-start | bytes 172040 | tf_op jit(solution)/shard_map/ppermute | solution.py:680
  31.3 2.3 %collective-permute-start.8 = (f32[112,128]{1,0:T(8,128)S(1)}, f32[112,128]{1,0:T(8,128)S(1)}, u32[]{:S(2)}, u32[]{:S(2)}) collective-permute-start(f32[112,128]{1,0:T(8,128)S(1)} %pad_maximum_fusion), channel_id=1, source_target_pairs={{0,2},{2,0},{4,6},{6,4},{1,3},{3,1},{5,7},{7,5},{8,10},{10,8},{12,... | collective-permute-start | bytes 172040 | tf_op jit(solution)/shard_map/ppermute | solution.py:680
  33.7 0.9 %collective-permute-start.14 = (f32[112,128]{1,0:T(8,128)S(1)}, f32[112,128]{1,0:T(8,128)S(1)}, u32[]{:S(2)}, u32[]{:S(2)}) collective-permute-start(f32[112,128]{1,0:T(8,128)S(1)} %get-tuple-element.64), channel_id=1, source_target_pairs={{0,8},{8,0},{16,24},{24,16},{1,9},{9,1},{17,25},{25,17},{2,10},{10... | collective-permute-start | bytes 172040 | tf_op jit(solution)/shard_map/ppermute | solution.py:540
  34.5 1.5 %collective-permute-start.15 = (f32[112,128]{1,0:T(8,128)S(1)}, f32[112,128]{1,0:T(8,128)S(1)}, u32[]{:S(2)}, u32[]{:S(2)}) collective-permute-start(f32[112,128]{1,0:T(8,128)S(1)} %get-tuple-element.65), channel_id=1, source_target_pairs={{8,16},{24,0},{16,8},{0,24},{9,17},{25,1},{17,9},{1,25},{10,18},{2... | collective-permute-start | bytes 172040 | tf_op jit(solution)/shard_map/ppermute | solution.py:541
  36.0 1.5 %collective-permute-done.9 = f32[112,128]{1,0:T(8,128)S(1)} collective-permute-done((f32[112,128]{1,0:T(8,128)S(1)}, f32[112,128]{1,0:T(8,128)S(1)}, u32[]{:S(2)}, u32[]{:S(2)}) %collective-permute-start.9) | collective-permute-done | bytes 57376 | tf_op jit(solution)/shard_map/ppermute | solution.py:680
  37.5 1.3 %collective-permute-start.13 = (f32[104,128]{1,0:T(8,128)S(1)}, f32[104,128]{1,0:T(8,128)S(1)}, u32[]{:S(2)}, u32[]{:S(2)}) collective-permute-start(f32[104,128]{1,0:T(8,128)S(1)} %slice_add_fusion.refs_1_), channel_id=1, source_target_pairs={{0,24},{1,25},{8,16},{9,17},{16,8},{17,9},{24,0},{25,1},{2,26},{3,... | collective-permute-start | bytes 159752 | tf_op jit(solution)/shard_map/ppermute | solution.py:705
  38.8 0.8 %collective-permute-start.12 = (f32[104,128]{1,0:T(8,128)S(1)}, f32[104,128]{1,0:T(8,128)S(1)}, u32[]{:S(2)}, u32[]{:S(2)}) collective-permute-start(f32[104,128]{1,0:T(8,128)S(1)} %slice_add_fusion.refs_1_), channel_id=1, source_target_pairs={{0,17},{1,16},{8,25},{9,24},{16,1},{17,0},{24,9},{25,8},{2,19},{3,... | collective-permute-start | bytes 159752 | tf_op jit(solution)/shard_map/ppermute | solution.py:705
  39.6 1.2 %collective-permute-start.11 = (f32[104,128]{1,0:T(8,128)S(1)}, f32[104,128]{1,0:T(8,128)S(1)}, u32[]{:S(2)}, u32[]{:S(2)}) collective-permute-start(f32[104,128]{1,0:T(8,128)S(1)} %slice_add_fusion.refs_1_), channel_id=1, source_target_pairs={{0,9},{1,8},{8,1},{9,0},{16,25},{17,24},{24,17},{25,16},{2,11},{3,... | collective-permute-start | bytes 159752 | tf_op jit(solution)/shard_map/ppermute | solution.py:705
  40.8 1.5 %shard_map.134 = f32[800,128]{1,0:T(8,128)} custom-call(f32[1,128]{1,0:T(1,128)S(1)} %get-tuple-element.61.refs_0_, f32[104,128]{1,0:T(8,128)S(1)} %slice_add_fusion.refs_1_, f32[800,128]{1,0:T(8,128)S(1)} %get-tuple-element.62.refs_2_, f32[128,1024]{1,0:T(8,128)S(1)} %get-tuple-element.44.refs_1_.refs_5_.refs_3_, ...), custom_call_target="tpu_custom_call" | custom-call | tf_op jit(solution)/shard_map/pallas_call | solution.py:694
  42.7 0.8 %collective-permute-done.12 = f32[104,128]{1,0:T(8,128)S(1)} collective-permute-done((f32[104,128]{1,0:T(8,128)S(1)}, f32[104,128]{1,0:T(8,128)S(1)}, u32[]{:S(2)}, u32[]{:S(2)}) %collective-permute-start.12) | collective-permute-done | bytes 53280 | tf_op jit(solution)/shard_map/ppermute | solution.py:705
  44.0 1.1 %collective-permute-done.16.refs_1_ = f32[416,128]{1,0:T(8,128)S(1)} collective-permute-done((f32[416,128]{1,0:T(8,128)S(1)}, f32[416,128]{1,0:T(8,128)S(1)}, u32[]{:S(2)}, u32[]{:S(2)}) %collective-permute-start.16) | collective-permute-done | bytes 213024 | tf_op jit(solution)/shard_map/ppermute | solution.py:709
  45.1 0.8 %shard_map.135 = (f32[100,512]{1,0:T(8,128)}, f32[1,512]{1,0:T(1,128)}, f32[100,512]{1,0:T(8,128)}, f32[1,100]{1,0:T(1,128)}) custom-call(f32[416,128]{1,0:T(8,128)S(1)} %constant_dynamic-update-slice_fusion.refs_0_, f32[416,128]{1,0:T(8,128)S(1)} %collective-permute-done.16.refs_1_), custom_call_target="tpu_custom_call" | custom-call | tf_op jit(solution)/shard_map/pallas_call | solution.py:710
  (54 shorter events, 3.8 us)
Async XLA Ops:
  0.7 13.4 %copy-start.4 = (bf16[100,512]{1,0:T(8,128)(2,1)S(1)}, bf16[100,512]{1,0:T(8,128)(2,1)}, u32[]{:S(2)}) copy-start(bf16[100,512]{1,0:T(8,128)(2,1)} %refs_2_.3) | copy-start | bytes 307204
  0.7 13.4 %copy-start.5 = (bf16[512,100]{0,1:T(8,128)(2,1)S(1)}, bf16[512,100]{0,1:T(8,128)(2,1)}, u32[]{:S(2)}) copy-start(bf16[512,100]{0,1:T(8,128)(2,1)} %param.16) | copy-start | bytes 307204
  0.7 13.4 %copy-start.6 = (f32[512]{0:T(512)S(1)}, f32[512]{0:T(512)}, u32[]{:S(2)}) copy-start(f32[512]{0:T(512)} %param.15) | copy-start | bytes 6148
  0.7 13.4 %copy-start.7 = (f32[100]{0:T(128)S(1)}, f32[100]{0:T(128)}, u32[]{:S(2)}) copy-start(f32[100]{0:T(128)} %param.17) | copy-start | bytes 1204
  0.7 13.4 %copy-start.8 = (f32[100]{0:T(128)S(1)}, f32[100]{0:T(128)}, u32[]{:S(2)}) copy-start(f32[100]{0:T(128)} %param.13) | copy-start | bytes 1204
  2.0 12.6 %collective-permute-start.3 = (f32[8,128]{1,0:T(8,128)S(1)}, f32[8,128]{1,0:T(8,128)S(1)}, u32[]{:S(2)}, u32[]{:S(2)}) collective-permute-start(f32[8,128]{1,0:T(8,128)S(1)} %get-tuple-element.86), channel_id=1, source_target_pairs={{1,2},{3,4},{5,6},{7,0},{2,1},{4,3},{6,5},{0,7},{9,10},{11,12},{13... | collective-permute-start | bytes 12296 | tf_op jit(solution)/shard_map/ppermute | solution.py:599
  6.5 8.0 %collective-permute-start.2 = (f32[8,128]{1,0:T(8,128)S(1)}, f32[8,128]{1,0:T(8,128)S(1)}, u32[]{:S(2)}, u32[]{:S(2)}) collective-permute-start(f32[8,128]{1,0:T(8,128)S(1)} %get-tuple-element.87), channel_id=1, source_target_pairs={{0,1},{1,0},{2,3},{3,2},{4,5},{5,4},{6,7},{7,6},{8,9},{9,8},{10,11... | collective-permute-start | bytes 12296 | tf_op jit(solution)/shard_map/ppermute | solution.py:598
  7.3 10.6 %all-to-all-start = ((f32[32,1,128]{2,1,0:T(1,128)}), f32[32,1,128]{2,1,0:T(1,128)S(1)}, u32[]{:S(2)}, u32[]{:S(2)}) async-start(f32[32,1,128]{2,1,0:T(1,128)} %shard_map.131), calls=%async_computation | async-start | bytes 32768 | tf_op jit(solution)/shard_map/all_to_all | solution.py:595
  10.8 8.5 %collective-permute-start = (f32[104,128]{1,0:T(8,128)S(1)}, f32[104,128]{1,0:T(8,128)S(1)}, u32[]{:S(2)}, u32[]{:S(2)}) collective-permute-start(f32[104,128]{1,0:T(8,128)S(1)} %get-tuple-element.40), channel_id=1, source_target_pairs={{0,8},{8,0},{16,24},{24,16},{1,9},{9,1},{17,25},{25,17},{2,10},{10... | collective-permute-start | bytes 159752 | tf_op jit(solution)/shard_map/ppermute | solution.py:540
  12.6 6.7 %collective-permute-start.1 = (f32[104,128]{1,0:T(8,128)S(1)}, f32[104,128]{1,0:T(8,128)S(1)}, u32[]{:S(2)}, u32[]{:S(2)}) collective-permute-start(f32[104,128]{1,0:T(8,128)S(1)} %get-tuple-element.41), channel_id=1, source_target_pairs={{8,16},{24,0},{16,8},{0,24},{9,17},{25,1},{17,9},{1,25},{10,18},{2... | collective-permute-start | bytes 159752 | tf_op jit(solution)/shard_map/ppermute | solution.py:541
  14.1 5.2 %copy-start.1 = (f32[100,8,128]{2,1,0:T(8,128)S(1)}, f32[100,8,128]{2,1,0:T(8,128)}, u32[]{:S(2)}) copy-start(f32[100,8,128]{2,1,0:T(8,128)} %param.10) | copy-start | bytes 1228804
  21.6 1.5 %collective-permute-start.4 = (f32[432,128]{1,0:T(8,128)S(1)}, f32[432,128]{1,0:T(8,128)S(1)}, u32[]{:S(2)}, u32[]{:S(2)}) collective-permute-start(f32[432,128]{1,0:T(8,128)S(1)} %get-tuple-element.57), channel_id=1, source_target_pairs={{0,1},{1,0},{2,3},{3,2},{4,5},{5,4},{6,7},{7,6},{8,9},{9,8},{10,11... | collective-permute-start | bytes 663560 | tf_op jit(solution)/shard_map/ppermute | solution.py:665
  23.3 5.6 %collective-permute-start.5 = (f32[104,128]{1,0:T(8,128)S(1)}, f32[104,128]{1,0:T(8,128)S(1)}, u32[]{:S(2)}, u32[]{:S(2)}) collective-permute-start(f32[104,128]{1,0:T(8,128)S(1)} %get-tuple-element.77), channel_id=1, source_target_pairs={{0,24},{1,25},{8,16},{9,17},{16,8},{17,9},{24,0},{25,1},{2,26},{3,... | collective-permute-start | bytes 159752 | tf_op jit(solution)/shard_map/ppermute | solution.py:671
  23.9 5.2 %collective-permute-start.7 = (f32[104,128]{1,0:T(8,128)S(1)}, f32[104,128]{1,0:T(8,128)S(1)}, u32[]{:S(2)}, u32[]{:S(2)}) collective-permute-start(f32[104,128]{1,0:T(8,128)S(1)} %get-tuple-element.78), channel_id=1, source_target_pairs={{0,17},{1,16},{8,25},{9,24},{16,1},{17,0},{24,9},{25,8},{2,19},{3,... | collective-permute-start | bytes 159752 | tf_op jit(solution)/shard_map/ppermute | solution.py:671
  24.8 4.4 %collective-permute-start.6 = (f32[104,128]{1,0:T(8,128)S(1)}, f32[104,128]{1,0:T(8,128)S(1)}, u32[]{:S(2)}, u32[]{:S(2)}) collective-permute-start(f32[104,128]{1,0:T(8,128)S(1)} %get-tuple-element.79), channel_id=1, source_target_pairs={{0,9},{1,8},{8,1},{9,0},{16,25},{17,24},{24,17},{25,16},{2,11},{3,... | collective-permute-start | bytes 159752 | tf_op jit(solution)/shard_map/ppermute | solution.py:671
  29.2 6.8 %collective-permute-start.10 = (f32[112,128]{1,0:T(8,128)S(1)}, f32[112,128]{1,0:T(8,128)S(1)}, u32[]{:S(2)}, u32[]{:S(2)}) collective-permute-start(f32[112,128]{1,0:T(8,128)S(1)} %pad_maximum_fusion), channel_id=1, source_target_pairs={{0,6},{2,4},{4,2},{6,0},{1,7},{3,5},{5,3},{7,1},{8,14},{10,12},{12... | collective-permute-start | bytes 172040 | tf_op jit(solution)/shard_map/ppermute | solution.py:680
  31.3 6.2 %collective-permute-start.9 = (f32[112,128]{1,0:T(8,128)S(1)}, f32[112,128]{1,0:T(8,128)S(1)}, u32[]{:S(2)}, u32[]{:S(2)}) collective-permute-start(f32[112,128]{1,0:T(8,128)S(1)} %pad_maximum_fusion), channel_id=1, source_target_pairs={{0,4},{2,6},{4,0},{6,2},{1,5},{3,7},{5,1},{7,3},{8,12},{10,14},{12... | collective-permute-start | bytes 172040 | tf_op jit(solution)/shard_map/ppermute | solution.py:680
  31.3 6.1 %collective-permute-start.8 = (f32[112,128]{1,0:T(8,128)S(1)}, f32[112,128]{1,0:T(8,128)S(1)}, u32[]{:S(2)}, u32[]{:S(2)}) collective-permute-start(f32[112,128]{1,0:T(8,128)S(1)} %pad_maximum_fusion), channel_id=1, source_target_pairs={{0,2},{2,0},{4,6},{6,4},{1,3},{3,1},{5,7},{7,5},{8,10},{10,8},{12,... | collective-permute-start | bytes 172040 | tf_op jit(solution)/shard_map/ppermute | solution.py:680
  33.7 7.1 %collective-permute-start.14 = (f32[112,128]{1,0:T(8,128)S(1)}, f32[112,128]{1,0:T(8,128)S(1)}, u32[]{:S(2)}, u32[]{:S(2)}) collective-permute-start(f32[112,128]{1,0:T(8,128)S(1)} %get-tuple-element.64), channel_id=1, source_target_pairs={{0,8},{8,0},{16,24},{24,16},{1,9},{9,1},{17,25},{25,17},{2,10},{10... | collective-permute-start | bytes 172040 | tf_op jit(solution)/shard_map/ppermute | solution.py:540
  34.5 6.2 %collective-permute-start.15 = (f32[112,128]{1,0:T(8,128)S(1)}, f32[112,128]{1,0:T(8,128)S(1)}, u32[]{:S(2)}, u32[]{:S(2)}) collective-permute-start(f32[112,128]{1,0:T(8,128)S(1)} %get-tuple-element.65), channel_id=1, source_target_pairs={{8,16},{24,0},{16,8},{0,24},{9,17},{25,1},{17,9},{1,25},{10,18},{2... | collective-permute-start | bytes 172040 | tf_op jit(solution)/shard_map/ppermute | solution.py:541
  37.5 5.2 %collective-permute-start.13 = (f32[104,128]{1,0:T(8,128)S(1)}, f32[104,128]{1,0:T(8,128)S(1)}, u32[]{:S(2)}, u32[]{:S(2)}) collective-permute-start(f32[104,128]{1,0:T(8,128)S(1)} %slice_add_fusion.refs_1_), channel_id=1, source_target_pairs={{0,24},{1,25},{8,16},{9,17},{16,8},{17,9},{24,0},{25,1},{2,26},{3,... | collective-permute-start | bytes 159752 | tf_op jit(solution)/shard_map/ppermute | solution.py:705
  38.8 4.7 %collective-permute-start.12 = (f32[104,128]{1,0:T(8,128)S(1)}, f32[104,128]{1,0:T(8,128)S(1)}, u32[]{:S(2)}, u32[]{:S(2)}) collective-permute-start(f32[104,128]{1,0:T(8,128)S(1)} %slice_add_fusion.refs_1_), channel_id=1, source_target_pairs={{0,17},{1,16},{8,25},{9,24},{16,1},{17,0},{24,9},{25,8},{2,19},{3,... | collective-permute-start | bytes 159752 | tf_op jit(solution)/shard_map/ppermute | solution.py:705
  39.6 3.9 %collective-permute-start.11 = (f32[104,128]{1,0:T(8,128)S(1)}, f32[104,128]{1,0:T(8,128)S(1)}, u32[]{:S(2)}, u32[]{:S(2)}) collective-permute-start(f32[104,128]{1,0:T(8,128)S(1)} %slice_add_fusion.refs_1_), channel_id=1, source_target_pairs={{0,9},{1,8},{8,1},{9,0},{16,25},{17,24},{24,17},{25,16},{2,11},{3,... | collective-permute-start | bytes 159752 | tf_op jit(solution)/shard_map/ppermute | solution.py:705
  43.5 1.6 %collective-permute-start.16 = (f32[416,128]{1,0:T(8,128)S(1)}, f32[416,128]{1,0:T(8,128)S(1)}, u32[]{:S(2)}, u32[]{:S(2)}) collective-permute-start(f32[416,128]{1,0:T(8,128)S(1)} %constant_dynamic-update-slice_fusion.refs_0_), channel_id=1, source_target_pairs={{0,1},{1,0},{2,3},{3,2},{4,5},{5,4},{6,7},{7,6},{8,9},{9,8},{10,11... | collective-permute-start | bytes 638984 | tf_op jit(solution)/shard_map/ppermute | solution.py:709
  (3 other events, 2.4 us)

commit v9 on v8

--- a/solution.py
+++ b/solution.py
@@ -667,7 +667,7 @@
     lon_near = got[4 * height : 4 * height + rows]
     lon_pass = got[4 * height + rows :]
     part = chip[0]
-    for step in (3, 1, 2):
+    for step in (3, 2, 1):
         part = part + lax.ppermute(chip[step], ("lat", "core"), cross_flip(lats, step))
     step = 4
     while step < lats:

time: 46.1 us -> 46 us (level)
  no operation moved by 1% of the time
where the time goes in v9:
time: 46 us; the launch traced here: 45.8 us
  starting transfers between devices  24.9 us (54%)
  waiting for transfers between devices  11.5 us (25%)
  Pallas kernels  7.43 us (16%)
  local copies, waits for them, and re-layouts  1.04 us (2%)
  between operations  0.92 us (2%)
    ppermute x1, starting transfers between devices, shards(): lax.ppermute(small[rows:], ('z', 'core'), far_pairs(lons, True))  4.55 us
    ppermute x3, starting transfers between devices, shards(): lax.ppermute(packed, 'z', flip(chips, step))  4.45 us
    all_to_all x1, starting transfers between devices, shards(): energy = lax.all_to_all(energy, ('lat', 'z', 'core'), 0, 0, tiled=True)  3.48 us
    all_to_all x1, waiting for transfers between devices, shards(): energy = lax.all_to_all(energy, ('lat', 'z', 'core'), 0, 0, tiled=True)  3.33 us
    ppermute x3, starting transfers between devices, shards(): lax.ppermute(chip[step], ('lat', 'core'), cross_flip(lats, step))  3.27 us
    ppermute x3, starting transfers between devices, shards(): lax.ppermute(part, ('lat', 'core'), cross_flip(lats, step))  3.27 us
    ppermute x2, starting transfers between devices, swap_lat(): lax.ppermute(lat_b, 'lat', far_pairs(lats, True))  3.1 us
    ppermute x3, waiting for transfers between devices, shards(): lax.ppermute(chip[step], ('lat', 'core'), cross_flip(lats, step))  2.59 us
  transfers between devices with their start and end apart: 18, of which 8 were waited for; matrix products, arithmetic and copies ran while one was open for 0% of the time, Pallas kernels for 9%

profile of v9, /device:TPU:0, one launch (start us, length us, event | category | flops | bytes accessed | tf_op | source)
XLA Modules:
  0.0 45.8 jit_solution(8025892825079457866)
XLA Ops:
  2.0 4.6 %collective-permute-start.3 = (f32[8,128]{1,0:T(8,128)S(1)}, f32[8,128]{1,0:T(8,128)S(1)}, u32[]{:S(2)}, u32[]{:S(2)}) collective-permute-start(f32[8,128]{1,0:T(8,128)S(1)} %get-tuple-element.86), channel_id=1, source_target_pairs={{1,2},{3,4},{5,6},{7,0},{2,1},{4,3},{6,5},{0,7},{9,10},{11,12},{13... | collective-permute-start | bytes 12296 | tf_op jit(solution)/shard_map/ppermute | solution.py:599
  6.5 0.8 %shard_map.131 = f32[32,1,128]{2,1,0:T(1,128)} custom-call(f32[800,128]{1,0:T(8,128)S(1)} %bitcast.26, f32[8,128]{1,0:T(8,128)S(1)} %get-tuple-element.43.refs_1_.refs_7_.refs_5_), custom_call_target="tpu_custom_call" | custom-call | flops 1000000000 | bytes 100000000 | tf_op jit(solution)/shard_map/pallas_call | solution.py:586
  7.3 3.5 %all-to-all-start = ((f32[32,1,128]{2,1,0:T(1,128)}), f32[32,1,128]{2,1,0:T(1,128)S(1)}, u32[]{:S(2)}, u32[]{:S(2)}) async-start(f32[32,1,128]{2,1,0:T(1,128)} %shard_map.131), calls=%async_computation | async-start | bytes 32768 | tf_op jit(solution)/shard_map/all_to_all | solution.py:595
  10.8 1.8 %collective-permute-start = (f32[104,128]{1,0:T(8,128)S(1)}, f32[104,128]{1,0:T(8,128)S(1)}, u32[]{:S(2)}, u32[]{:S(2)}) collective-permute-start(f32[104,128]{1,0:T(8,128)S(1)} %get-tuple-element.40), channel_id=1, source_target_pairs={{0,8},{8,0},{16,24},{24,16},{1,9},{9,1},{17,25},{25,17},{2,10},{10... | collective-permute-start | bytes 159752 | tf_op jit(solution)/shard_map/ppermute | solution.py:540
  12.6 1.5 %collective-permute-start.1 = (f32[104,128]{1,0:T(8,128)S(1)}, f32[104,128]{1,0:T(8,128)S(1)}, u32[]{:S(2)}, u32[]{:S(2)}) collective-permute-start(f32[104,128]{1,0:T(8,128)S(1)} %get-tuple-element.41), channel_id=1, source_target_pairs={{8,16},{24,0},{16,8},{0,24},{9,17},{25,1},{17,9},{1,25},{10,18},{2... | collective-permute-start | bytes 159752 | tf_op jit(solution)/shard_map/ppermute | solution.py:541
  14.5 3.3 %all-to-all-done.refs_0_ = f32[32,1,128]{2,1,0:T(1,128)S(1)} async-done(((f32[32,1,128]{2,1,0:T(1,128)}), f32[32,1,128]{2,1,0:T(1,128)S(1)}, u32[]{:S(2)}, u32[]{:S(2)}) %all-to-all-start) | async-done | bytes 16416 | tf_op jit(solution)/shard_map/all_to_all | solution.py:595
  17.9 1.4 %shard_map.132 = (f32[1,128]{1,0:T(1,128)S(1)}, bf16[128,1024]{1,0:T(8,128)(2,1)S(1)}, bf16[512,1024]{1,0:T(8,128)(2,1)S(1)}, f32[512,1024]{1,0:T(8,128)S(1)}, f...) custom-call(f32[32,1,128]{2,1,0:T(1,128)S(1)} %all-to-all-done.refs_0_, ...), custom_call_target="tpu_custom_call" | custom-call | tf_op jit(solution)/shard_map/pallas_call | solution.py:623
  19.4 2.3 %shard_map.133 = (f32[4,104,128]{2,1,0:T(8,128)S(1)}, f32[432,128]{1,0:T(8,128)S(1)}, f32[800,128]{1,0:T(8,128)S(1)}, f32[112,128]{1,0:T(8,128)S(1)}, f32[112,12...) custom-call(f32[800,128]{1,0:T(8,128)S(1)} %bitcast.28, f32[104,128]{1,0:T(8,128)S(1)} %get-tuple-element.83.refs_1_.refs_10_, ...), custom_call_target="tpu_custom_call" | custom-call | tf_op jit(solution)/shard_map/pallas_call | solution.py:639
  21.7 1.5 %collective-permute-done.4 = f32[432,128]{1,0:T(8,128)S(1)} collective-permute-done((f32[432,128]{1,0:T(8,128)S(1)}, f32[432,128]{1,0:T(8,128)S(1)}, u32[]{:S(2)}, u32[]{:S(2)}) %collective-permute-start.4) | collective-permute-done | bytes 221216 | tf_op jit(solution)/shard_map/ppermute | solution.py:665
  23.3 0.7 %collective-permute-start.5 = (f32[104,128]{1,0:T(8,128)S(1)}, f32[104,128]{1,0:T(8,128)S(1)}, u32[]{:S(2)}, u32[]{:S(2)}) collective-permute-start(f32[104,128]{1,0:T(8,128)S(1)} %get-tuple-element.77), channel_id=1, source_target_pairs={{0,24},{1,25},{8,16},{9,17},{16,8},{17,9},{24,0},{25,1},{2,26},{3,... | collective-permute-start | bytes 159752 | tf_op jit(solution)/shard_map/ppermute | solution.py:671
  23.9 0.9 %collective-permute-start.7 = (f32[104,128]{1,0:T(8,128)S(1)}, f32[104,128]{1,0:T(8,128)S(1)}, u32[]{:S(2)}, u32[]{:S(2)}) collective-permute-start(f32[104,128]{1,0:T(8,128)S(1)} %get-tuple-element.78), channel_id=1, source_target_pairs={{0,9},{1,8},{8,1},{9,0},{16,25},{17,24},{24,17},{25,16},{2,11},{3,... | collective-permute-start | bytes 159752 | tf_op jit(solution)/shard_map/ppermute | solution.py:671
  24.8 1.7 %collective-permute-start.6 = (f32[104,128]{1,0:T(8,128)S(1)}, f32[104,128]{1,0:T(8,128)S(1)}, u32[]{:S(2)}, u32[]{:S(2)}) collective-permute-start(f32[104,128]{1,0:T(8,128)S(1)} %get-tuple-element.79), channel_id=1, source_target_pairs={{0,17},{1,16},{8,25},{9,24},{16,1},{17,0},{24,9},{25,8},{2,19},{3,... | collective-permute-start | bytes 159752 | tf_op jit(solution)/shard_map/ppermute | solution.py:671
  26.5 2.4 %collective-permute-done.5 = f32[104,128]{1,0:T(8,128)S(1)} collective-permute-done((f32[104,128]{1,0:T(8,128)S(1)}, f32[104,128]{1,0:T(8,128)S(1)}, u32[]{:S(2)}, u32[]{:S(2)}) %collective-permute-start.5) | collective-permute-done | bytes 53280 | tf_op jit(solution)/shard_map/ppermute | solution.py:671
  29.2 1.9 %collective-permute-start.10 = (f32[112,128]{1,0:T(8,128)S(1)}, f32[112,128]{1,0:T(8,128)S(1)}, u32[]{:S(2)}, u32[]{:S(2)}) collective-permute-start(f32[112,128]{1,0:T(8,128)S(1)} %pad_maximum_fusion), channel_id=1, source_target_pairs={{0,6},{2,4},{4,2},{6,0},{1,7},{3,5},{5,3},{7,1},{8,14},{10,12},{12... | collective-permute-start | bytes 172040 | tf_op jit(solution)/shard_map/ppermute | solution.py:680
  31.3 2.3 %collective-permute-start.8 = (f32[112,128]{1,0:T(8,128)S(1)}, f32[112,128]{1,0:T(8,128)S(1)}, u32[]{:S(2)}, u32[]{:S(2)}) collective-permute-start(f32[112,128]{1,0:T(8,128)S(1)} %pad_maximum_fusion), channel_id=1, source_target_pairs={{0,2},{2,0},{4,6},{6,4},{1,3},{3,1},{5,7},{7,5},{8,10},{10,8},{12,... | collective-permute-start | bytes 172040 | tf_op jit(solution)/shard_map/ppermute | solution.py:680
  33.6 0.7 %collective-permute-start.14 = (f32[112,128]{1,0:T(8,128)S(1)}, f32[112,128]{1,0:T(8,128)S(1)}, u32[]{:S(2)}, u32[]{:S(2)}) collective-permute-start(f32[112,128]{1,0:T(8,128)S(1)} %get-tuple-element.64), channel_id=1, source_target_pairs={{0,8},{8,0},{16,24},{24,16},{1,9},{9,1},{17,25},{25,17},{2,10},{10... | collective-permute-start | bytes 172040 | tf_op jit(solution)/shard_map/ppermute | solution.py:540
  34.3 1.6 %collective-permute-start.15 = (f32[112,128]{1,0:T(8,128)S(1)}, f32[112,128]{1,0:T(8,128)S(1)}, u32[]{:S(2)}, u32[]{:S(2)}) collective-permute-start(f32[112,128]{1,0:T(8,128)S(1)} %get-tuple-element.65), channel_id=1, source_target_pairs={{8,16},{24,0},{16,8},{0,24},{9,17},{25,1},{17,9},{1,25},{10,18},{2... | collective-permute-start | bytes 172040 | tf_op jit(solution)/shard_map/ppermute | solution.py:541
  35.9 1.6 %collective-permute-done.9 = f32[112,128]{1,0:T(8,128)S(1)} collective-permute-done((f32[112,128]{1,0:T(8,128)S(1)}, f32[112,128]{1,0:T(8,128)S(1)}, u32[]{:S(2)}, u32[]{:S(2)}) %collective-permute-start.9) | collective-permute-done | bytes 57376 | tf_op jit(solution)/shard_map/ppermute | solution.py:680
  37.5 1.2 %collective-permute-start.13 = (f32[104,128]{1,0:T(8,128)S(1)}, f32[104,128]{1,0:T(8,128)S(1)}, u32[]{:S(2)}, u32[]{:S(2)}) collective-permute-start(f32[104,128]{1,0:T(8,128)S(1)} %slice_add_fusion.refs_1_), channel_id=1, source_target_pairs={{0,24},{1,25},{8,16},{9,17},{16,8},{17,9},{24,0},{25,1},{2,26},{3,... | collective-permute-start | bytes 159752 | tf_op jit(solution)/shard_map/ppermute | solution.py:705
  39.0 1.8 %collective-permute-start.11 = (f32[104,128]{1,0:T(8,128)S(1)}, f32[104,128]{1,0:T(8,128)S(1)}, u32[]{:S(2)}, u32[]{:S(2)}) collective-permute-start(f32[104,128]{1,0:T(8,128)S(1)} %slice_add_fusion.refs_1_), channel_id=1, source_target_pairs={{0,9},{1,8},{8,1},{9,0},{16,25},{17,24},{24,17},{25,16},{2,11},{3,... | collective-permute-start | bytes 159752 | tf_op jit(solution)/shard_map/ppermute | solution.py:705
  40.8 1.5 %shard_map.134 = f32[800,128]{1,0:T(8,128)} custom-call(f32[1,128]{1,0:T(1,128)S(1)} %get-tuple-element.61.refs_0_, f32[104,128]{1,0:T(8,128)S(1)} %slice_add_fusion.refs_1_, f32[800,128]{1,0:T(8,128)S(1)} %get-tuple-element.62.refs_2_, f32[128,1024]{1,0:T(8,128)S(1)} %get-tuple-element.44.refs_1_.refs_5_.refs_3_, ...), custom_call_target="tpu_custom_call" | custom-call | tf_op jit(solution)/shard_map/pallas_call | solution.py:694
  42.7 0.7 %collective-permute-done.12 = f32[104,128]{1,0:T(8,128)S(1)} collective-permute-done((f32[104,128]{1,0:T(8,128)S(1)}, f32[104,128]{1,0:T(8,128)S(1)}, u32[]{:S(2)}, u32[]{:S(2)}) %collective-permute-start.12) | collective-permute-done | bytes 53280 | tf_op jit(solution)/shard_map/ppermute | solution.py:705
  43.6 1.4 %collective-permute-done.16.refs_1_ = f32[416,128]{1,0:T(8,128)S(1)} collective-permute-done((f32[416,128]{1,0:T(8,128)S(1)}, f32[416,128]{1,0:T(8,128)S(1)}, u32[]{:S(2)}, u32[]{:S(2)}) %collective-permute-start.16) | collective-permute-done | bytes 213024 | tf_op jit(solution)/shard_map/ppermute | solution.py:709
  45.0 0.8 %shard_map.135 = (f32[100,512]{1,0:T(8,128)}, f32[1,512]{1,0:T(1,128)}, f32[100,512]{1,0:T(8,128)}, f32[1,100]{1,0:T(1,128)}) custom-call(f32[416,128]{1,0:T(8,128)S(1)} %constant_dynamic-update-slice_fusion.refs_0_, f32[416,128]{1,0:T(8,128)S(1)} %collective-permute-done.16.refs_1_), custom_call_target="tpu_custom_call" | custom-call | tf_op jit(solution)/shard_map/pallas_call | solution.py:710
  (54 shorter events, 3.0 us)
Async XLA Ops:
  0.7 13.4 %copy-start.4 = (bf16[100,512]{1,0:T(8,128)(2,1)S(1)}, bf16[100,512]{1,0:T(8,128)(2,1)}, u32[]{:S(2)}) copy-start(bf16[100,512]{1,0:T(8,128)(2,1)} %refs_2_.3) | copy-start | bytes 307204
  0.7 13.4 %copy-start.5 = (bf16[512,100]{0,1:T(8,128)(2,1)S(1)}, bf16[512,100]{0,1:T(8,128)(2,1)}, u32[]{:S(2)}) copy-start(bf16[512,100]{0,1:T(8,128)(2,1)} %param.16) | copy-start | bytes 307204
  0.7 13.4 %copy-start.6 = (f32[512]{0:T(512)S(1)}, f32[512]{0:T(512)}, u32[]{:S(2)}) copy-start(f32[512]{0:T(512)} %param.15) | copy-start | bytes 6148
  0.7 13.4 %copy-start.7 = (f32[100]{0:T(128)S(1)}, f32[100]{0:T(128)}, u32[]{:S(2)}) copy-start(f32[100]{0:T(128)} %param.17) | copy-start | bytes 1204
  0.7 13.4 %copy-start.8 = (f32[100]{0:T(128)S(1)}, f32[100]{0:T(128)}, u32[]{:S(2)}) copy-start(f32[100]{0:T(128)} %param.13) | copy-start | bytes 1204
  2.0 12.6 %collective-permute-start.3 = (f32[8,128]{1,0:T(8,128)S(1)}, f32[8,128]{1,0:T(8,128)S(1)}, u32[]{:S(2)}, u32[]{:S(2)}) collective-permute-start(f32[8,128]{1,0:T(8,128)S(1)} %get-tuple-element.86), channel_id=1, source_target_pairs={{1,2},{3,4},{5,6},{7,0},{2,1},{4,3},{6,5},{0,7},{9,10},{11,12},{13... | collective-permute-start | bytes 12296 | tf_op jit(solution)/shard_map/ppermute | solution.py:599
  6.5 8.0 %collective-permute-start.2 = (f32[8,128]{1,0:T(8,128)S(1)}, f32[8,128]{1,0:T(8,128)S(1)}, u32[]{:S(2)}, u32[]{:S(2)}) collective-permute-start(f32[8,128]{1,0:T(8,128)S(1)} %get-tuple-element.87), channel_id=1, source_target_pairs={{0,1},{1,0},{2,3},{3,2},{4,5},{5,4},{6,7},{7,6},{8,9},{9,8},{10,11... | collective-permute-start | bytes 12296 | tf_op jit(solution)/shard_map/ppermute | solution.py:598
  7.3 10.6 %all-to-all-start = ((f32[32,1,128]{2,1,0:T(1,128)}), f32[32,1,128]{2,1,0:T(1,128)S(1)}, u32[]{:S(2)}, u32[]{:S(2)}) async-start(f32[32,1,128]{2,1,0:T(1,128)} %shard_map.131), calls=%async_computation | async-start | bytes 32768 | tf_op jit(solution)/shard_map/all_to_all | solution.py:595
  10.8 8.5 %collective-permute-start = (f32[104,128]{1,0:T(8,128)S(1)}, f32[104,128]{1,0:T(8,128)S(1)}, u32[]{:S(2)}, u32[]{:S(2)}) collective-permute-start(f32[104,128]{1,0:T(8,128)S(1)} %get-tuple-element.40), channel_id=1, source_target_pairs={{0,8},{8,0},{16,24},{24,16},{1,9},{9,1},{17,25},{25,17},{2,10},{10... | collective-permute-start | bytes 159752 | tf_op jit(solution)/shard_map/ppermute | solution.py:540
  12.6 6.7 %collective-permute-start.1 = (f32[104,128]{1,0:T(8,128)S(1)}, f32[104,128]{1,0:T(8,128)S(1)}, u32[]{:S(2)}, u32[]{:S(2)}) collective-permute-start(f32[104,128]{1,0:T(8,128)S(1)} %get-tuple-element.41), channel_id=1, source_target_pairs={{8,16},{24,0},{16,8},{0,24},{9,17},{25,1},{17,9},{1,25},{10,18},{2... | collective-permute-start | bytes 159752 | tf_op jit(solution)/shard_map/ppermute | solution.py:541
  14.1 5.2 %copy-start.1 = (f32[100,8,128]{2,1,0:T(8,128)S(1)}, f32[100,8,128]{2,1,0:T(8,128)}, u32[]{:S(2)}) copy-start(f32[100,8,128]{2,1,0:T(8,128)} %param.10) | copy-start | bytes 1228804
  21.6 1.5 %collective-permute-start.4 = (f32[432,128]{1,0:T(8,128)S(1)}, f32[432,128]{1,0:T(8,128)S(1)}, u32[]{:S(2)}, u32[]{:S(2)}) collective-permute-start(f32[432,128]{1,0:T(8,128)S(1)} %get-tuple-element.57), channel_id=1, source_target_pairs={{0,1},{1,0},{2,3},{3,2},{4,5},{5,4},{6,7},{7,6},{8,9},{9,8},{10,11... | collective-permute-start | bytes 663560 | tf_op jit(solution)/shard_map/ppermute | solution.py:665
  23.3 5.7 %collective-permute-start.5 = (f32[104,128]{1,0:T(8,128)S(1)}, f32[104,128]{1,0:T(8,128)S(1)}, u32[]{:S(2)}, u32[]{:S(2)}) collective-permute-start(f32[104,128]{1,0:T(8,128)S(1)} %get-tuple-element.77), channel_id=1, source_target_pairs={{0,24},{1,25},{8,16},{9,17},{16,8},{17,9},{24,0},{25,1},{2,26},{3,... | collective-permute-start | bytes 159752 | tf_op jit(solution)/shard_map/ppermute | solution.py:671
  23.9 5.0 %collective-permute-start.7 = (f32[104,128]{1,0:T(8,128)S(1)}, f32[104,128]{1,0:T(8,128)S(1)}, u32[]{:S(2)}, u32[]{:S(2)}) collective-permute-start(f32[104,128]{1,0:T(8,128)S(1)} %get-tuple-element.78), channel_id=1, source_target_pairs={{0,9},{1,8},{8,1},{9,0},{16,25},{17,24},{24,17},{25,16},{2,11},{3,... | collective-permute-start | bytes 159752 | tf_op jit(solution)/shard_map/ppermute | solution.py:671
  24.8 4.3 %collective-permute-start.6 = (f32[104,128]{1,0:T(8,128)S(1)}, f32[104,128]{1,0:T(8,128)S(1)}, u32[]{:S(2)}, u32[]{:S(2)}) collective-permute-start(f32[104,128]{1,0:T(8,128)S(1)} %get-tuple-element.79), channel_id=1, source_target_pairs={{0,17},{1,16},{8,25},{9,24},{16,1},{17,0},{24,9},{25,8},{2,19},{3,... | collective-permute-start | bytes 159752 | tf_op jit(solution)/shard_map/ppermute | solution.py:671
  29.2 6.8 %collective-permute-start.10 = (f32[112,128]{1,0:T(8,128)S(1)}, f32[112,128]{1,0:T(8,128)S(1)}, u32[]{:S(2)}, u32[]{:S(2)}) collective-permute-start(f32[112,128]{1,0:T(8,128)S(1)} %pad_maximum_fusion), channel_id=1, source_target_pairs={{0,6},{2,4},{4,2},{6,0},{1,7},{3,5},{5,3},{7,1},{8,14},{10,12},{12... | collective-permute-start | bytes 172040 | tf_op jit(solution)/shard_map/ppermute | solution.py:680
  31.1 6.4 %collective-permute-start.9 = (f32[112,128]{1,0:T(8,128)S(1)}, f32[112,128]{1,0:T(8,128)S(1)}, u32[]{:S(2)}, u32[]{:S(2)}) collective-permute-start(f32[112,128]{1,0:T(8,128)S(1)} %pad_maximum_fusion), channel_id=1, source_target_pairs={{0,4},{2,6},{4,0},{6,2},{1,5},{3,7},{5,1},{7,3},{8,12},{10,14},{12... | collective-permute-start | bytes 172040 | tf_op jit(solution)/shard_map/ppermute | solution.py:680
  31.3 6.2 %collective-permute-start.8 = (f32[112,128]{1,0:T(8,128)S(1)}, f32[112,128]{1,0:T(8,128)S(1)}, u32[]{:S(2)}, u32[]{:S(2)}) collective-permute-start(f32[112,128]{1,0:T(8,128)S(1)} %pad_maximum_fusion), channel_id=1, source_target_pairs={{0,2},{2,0},{4,6},{6,4},{1,3},{3,1},{5,7},{7,5},{8,10},{10,8},{12,... | collective-permute-start | bytes 172040 | tf_op jit(solution)/shard_map/ppermute | solution.py:680
  33.6 7.2 %collective-permute-start.14 = (f32[112,128]{1,0:T(8,128)S(1)}, f32[112,128]{1,0:T(8,128)S(1)}, u32[]{:S(2)}, u32[]{:S(2)}) collective-permute-start(f32[112,128]{1,0:T(8,128)S(1)} %get-tuple-element.64), channel_id=1, source_target_pairs={{0,8},{8,0},{16,24},{24,16},{1,9},{9,1},{17,25},{25,17},{2,10},{10... | collective-permute-start | bytes 172040 | tf_op jit(solution)/shard_map/ppermute | solution.py:540
  34.3 6.5 %collective-permute-start.15 = (f32[112,128]{1,0:T(8,128)S(1)}, f32[112,128]{1,0:T(8,128)S(1)}, u32[]{:S(2)}, u32[]{:S(2)}) collective-permute-start(f32[112,128]{1,0:T(8,128)S(1)} %get-tuple-element.65), channel_id=1, source_target_pairs={{8,16},{24,0},{16,8},{0,24},{9,17},{25,1},{17,9},{1,25},{10,18},{2... | collective-permute-start | bytes 172040 | tf_op jit(solution)/shard_map/ppermute | solution.py:541
  37.5 5.2 %collective-permute-start.13 = (f32[104,128]{1,0:T(8,128)S(1)}, f32[104,128]{1,0:T(8,128)S(1)}, u32[]{:S(2)}, u32[]{:S(2)}) collective-permute-start(f32[104,128]{1,0:T(8,128)S(1)} %slice_add_fusion.refs_1_), channel_id=1, source_target_pairs={{0,24},{1,25},{8,16},{9,17},{16,8},{17,9},{24,0},{25,1},{2,26},{3,... | collective-permute-start | bytes 159752 | tf_op jit(solution)/shard_map/ppermute | solution.py:705
  38.8 4.7 %collective-permute-start.12 = (f32[104,128]{1,0:T(8,128)S(1)}, f32[104,128]{1,0:T(8,128)S(1)}, u32[]{:S(2)}, u32[]{:S(2)}) collective-permute-start(f32[104,128]{1,0:T(8,128)S(1)} %slice_add_fusion.refs_1_), channel_id=1, source_target_pairs={{0,17},{1,16},{8,25},{9,24},{16,1},{17,0},{24,9},{25,8},{2,19},{3,... | collective-permute-start | bytes 159752 | tf_op jit(solution)/shard_map/ppermute | solution.py:705
  39.0 4.5 %collective-permute-start.11 = (f32[104,128]{1,0:T(8,128)S(1)}, f32[104,128]{1,0:T(8,128)S(1)}, u32[]{:S(2)}, u32[]{:S(2)}) collective-permute-start(f32[104,128]{1,0:T(8,128)S(1)} %slice_add_fusion.refs_1_), channel_id=1, source_target_pairs={{0,9},{1,8},{8,1},{9,0},{16,25},{17,24},{24,17},{25,16},{2,11},{3,... | collective-permute-start | bytes 159752 | tf_op jit(solution)/shard_map/ppermute | solution.py:705
  43.5 1.5 %collective-permute-start.16 = (f32[416,128]{1,0:T(8,128)S(1)}, f32[416,128]{1,0:T(8,128)S(1)}, u32[]{:S(2)}, u32[]{:S(2)}) collective-permute-start(f32[416,128]{1,0:T(8,128)S(1)} %constant_dynamic-update-slice_fusion.refs_0_), channel_id=1, source_target_pairs={{0,1},{1,0},{2,3},{3,2},{4,5},{5,4},{6,7},{7,6},{8,9},{9,8},{10,11... | collective-permute-start | bytes 638984 | tf_op jit(solution)/shard_map/ppermute | solution.py:709
  (3 other events, 2.4 us)

commit v10 on v9

--- a/solution.py
+++ b/solution.py
@@ -46,15 +46,15 @@
     cols = field_ref.shape[1]
     first = row_of(field_ref, 0, levels, rows)
     last = row_of(field_ref, rows - 1, levels, rows)
-    tail = (lat_a.shape[0] - levels, cols)
-    first_tail = last_tail = jnp.zeros(tail, f32)
-    if depth is not None:
-        first_tail = jnp.broadcast_to(depth[0:1, :], tail)
-        last_tail = jnp.broadcast_to(depth[rows - 1 : rows, :], tail)
     lat_a[0:levels, :] = jnp.where(lat_odd, first, last)
     lat_b[0:levels, :] = jnp.where(lat_odd, last, first)
-    lat_a[levels:, :] = jnp.where(lat_odd, first_tail, last_tail)
-    lat_b[levels:, :] = jnp.where(lat_odd, last_tail, first_tail)
+    for out, odd in ((lat_a, lat_odd), (lat_b, jnp.logical_not(lat_odd))):
+        tail = (out.shape[0] - levels, cols)
+        if depth is None:
+            out[levels:, :] = jnp.zeros(tail, f32)
+        else:
+            first_tail = jnp.broadcast_to(depth[0:1, :], tail)
+            out[levels:, :] = jnp.where(odd, first_tail, jnp.broadcast_to(depth[depth.shape[0] - 1 :, :], tail))
 
 
 def lon_edges(values, levels):
@@ -435,10 +435,27 @@
     bout_row = lane_sums(pad, bout) * scale
 
     block = hid // 4
+    contract = (((1,), (1,)), ((), ()))
+    used = round_up(levels + 3, 16)
+    lat_odd, lon_odd = odd_places()
+    keeps_out = half_odd()
+    quarter = lax.axis_index("lat") % 4
+    height = keep.shape[1]
+    wides = [slice(2 * half * block, (2 * half + 2) * block) for half in range(2)]
+    outs = []
     for part in range(4):
         at = slice(part * block, (part + 1) * block)
         d_hidden = jnp.dot(wo_b[at, :], dl_b[...], preferred_element_type=f32)
         dp_b[at, :] = (d_hidden * slope[at, :]).astype(bf16)
+        if part % 2:
+            outs.append(
+                lax.dot_general(
+                    dl_b[0:used, :], hidden[wides[part // 2], :], contract, preferred_element_type=f32
+                )
+            )
+    ins = [
+        lax.dot_general(x_b[0:used, :], dp_b[wide, :], contract, preferred_element_type=f32) for wide in wides
+    ]
     d_in = jnp.dot(wi_b[0 : round_up(levels, 16), :], dp_b[...], preferred_element_type=f32)
     level = jnp.zeros((levels, cols), f32)
     for row in range(rows):
@@ -448,16 +465,8 @@
         level = level + part * wet_tracer[0:levels, at]
     level_row = lane_sums(pad, level)
 
-    contract = (((1,), (1,)), ((), ()))
-    used = round_up(levels + 3, 16)
-    lat_odd, lon_odd = odd_places()
-    keeps_out = half_odd()
-    quarter = lax.axis_index("lat") % 4
-    height = keep.shape[1]
     for half in range(2):
-        wide = slice(2 * half * block, (2 * half + 2) * block)
-        both_in = lax.dot_general(x_b[0:used, :], dp_b[wide, :], contract, preferred_element_type=f32)
-        both_out = lax.dot_general(dl_b[0:used, :], hidden[wide, :], contract, preferred_element_type=f32)
+        both_in, both_out = ins[half], outs[half]
         for part in range(2):
             at = slice(part * block, (part + 1) * block)
             slot = (2 * half + part) ^ quarter
@@ -535,11 +544,9 @@
 
 
 def swap_lat(lat_odd, lats, lat_a, lat_b):
-    return in_order(
-        lat_odd,
-        lax.ppermute(lat_a, "lat", flip(lats, 1)),
-        lax.ppermute(lat_b, "lat", far_pairs(lats, True)),
-    )
+    near = lax.ppermute(lat_a, "lat", flip(lats, 1))
+    far = lax.ppermute(lat_b, "lat", far_pairs(lats, True))
+    return in_order(lat_odd, near[: far.shape[0]], far)
 
 
 def shards(tracer, cotangent, land_mask, bottom, kappa, w_in, b_in, w_out, b_out):
@@ -575,7 +582,7 @@
         lambda zero, *refs: edge_kernel(levels, *refs),
         out_shape=[
             sds((2 * rows, pad_levels), f32),
-            lat_edge,
+            sds((height + rows, cols), f32),
             lat_edge,
             sds((rows, cols), f32),
         ],

time: 46 us -> 46 us (level)
  no operation moved by 1% of the time
where the time goes in v10:
time: 46 us; the launch traced here: 45.8 us
  starting transfers between devices  24.9 us (54%)
  waiting for transfers between devices  11.5 us (25%)
  Pallas kernels  7.4 us (16%)
  local copies, waits for them, and re-layouts  1.04 us (2%)
  between operations  0.92 us (2%)
    ppermute x1, starting transfers between devices, shards(): lax.ppermute(small[rows:], ('z', 'core'), far_pairs(lons, True))  4.55 us
    ppermute x3, starting transfers between devices, shards(): lax.ppermute(packed, 'z', flip(chips, step))  4.45 us
    ppermute x2, starting transfers between devices, swap_lat(): far = lax.ppermute(lat_b, 'lat', far_pairs(lats, True))  4.38 us
    all_to_all x1, starting transfers between devices, shards(): energy = lax.all_to_all(energy, ('lat', 'z', 'core'), 0, 0, tiled=True)  3.48 us
    all_to_all x1, waiting for transfers between devices, shards(): energy = lax.all_to_all(energy, ('lat', 'z', 'core'), 0, 0, tiled=True)  3.33 us
    ppermute x3, starting transfers between devices, shards(): lax.ppermute(chip[step], ('lat', 'core'), cross_flip(lats, step))  3.27 us
    ppermute x3, starting transfers between devices, shards(): lax.ppermute(part, ('lat', 'core'), cross_flip(lats, step))  3.27 us
    ppermute x3, waiting for transfers between devices, shards(): lax.ppermute(chip[step], ('lat', 'core'), cross_flip(lats, step))  2.59 us
  transfers between devices with their start and end apart: 18, of which 8 were waited for; matrix products, arithmetic and copies ran while one was open for 0% of the time, Pallas kernels for 9%

profile of v10, /device:TPU:0, one launch (start us, length us, event | category | flops | bytes accessed | tf_op | source)
XLA Modules:
  0.0 45.8 jit_solution(3389891625746260898)
XLA Ops:
  0.7 0.6 %copy-done.3 = s32[8,128]{1,0:T(8,128)S(1)} copy-done((s32[8,128]{1,0:T(8,128)S(1)}, s32[8,128]{1,0:T(8,128)}, u32[]{:S(2)}) %copy-start.3) | copy-done | bytes 4120
  2.0 4.6 %collective-permute-start.3 = (f32[8,128]{1,0:T(8,128)S(1)}, f32[8,128]{1,0:T(8,128)S(1)}, u32[]{:S(2)}, u32[]{:S(2)}) collective-permute-start(f32[8,128]{1,0:T(8,128)S(1)} %get-tuple-element.86), channel_id=1, source_target_pairs={{1,2},{3,4},{5,6},{7,0},{2,1},{4,3},{6,5},{0,7},{9,10},{11,12},{13... | collective-permute-start | bytes 12296 | tf_op jit(solution)/shard_map/ppermute | solution.py:606
  6.5 0.8 %shard_map.131 = f32[32,1,128]{2,1,0:T(1,128)} custom-call(f32[800,128]{1,0:T(8,128)S(1)} %bitcast.26, f32[8,128]{1,0:T(8,128)S(1)} %get-tuple-element.43.refs_1_.refs_7_.refs_5_), custom_call_target="tpu_custom_call" | custom-call | flops 1000000000 | bytes 100000000 | tf_op jit(solution)/shard_map/pallas_call | solution.py:593
  7.3 3.5 %all-to-all-start = ((f32[32,1,128]{2,1,0:T(1,128)}), f32[32,1,128]{2,1,0:T(1,128)S(1)}, u32[]{:S(2)}, u32[]{:S(2)}) async-start(f32[32,1,128]{2,1,0:T(1,128)} %shard_map.131), calls=%async_computation | async-start | bytes 32768 | tf_op jit(solution)/shard_map/all_to_all | solution.py:602
  10.8 2.7 %collective-permute-start.1 = (f32[104,128]{1,0:T(8,128)S(1)}, f32[104,128]{1,0:T(8,128)S(1)}, u32[]{:S(2)}, u32[]{:S(2)}) collective-permute-start(f32[104,128]{1,0:T(8,128)S(1)} %get-tuple-element.41), channel_id=1, source_target_pairs={{8,16},{24,0},{16,8},{0,24},{9,17},{25,1},{17,9},{1,25},{10,18},{2... | collective-permute-start | bytes 159752 | tf_op jit(solution)/shard_map/ppermute | solution.py:548
  14.5 3.3 %all-to-all-done.refs_0_ = f32[32,1,128]{2,1,0:T(1,128)S(1)} async-done(((f32[32,1,128]{2,1,0:T(1,128)}), f32[32,1,128]{2,1,0:T(1,128)S(1)}, u32[]{:S(2)}, u32[]{:S(2)}) %all-to-all-start) | async-done | bytes 16416 | tf_op jit(solution)/shard_map/all_to_all | solution.py:602
  17.9 1.4 %shard_map.132 = (f32[1,128]{1,0:T(1,128)S(1)}, bf16[128,1024]{1,0:T(8,128)(2,1)S(1)}, bf16[512,1024]{1,0:T(8,128)(2,1)S(1)}, f32[512,1024]{1,0:T(8,128)S(1)}, f...) custom-call(f32[32,1,128]{2,1,0:T(1,128)S(1)} %all-to-all-done.refs_0_, ...), custom_call_target="tpu_custom_call" | custom-call | tf_op jit(solution)/shard_map/pallas_call | solution.py:630
  19.4 2.2 %shard_map.133 = (f32[4,104,128]{2,1,0:T(8,128)S(1)}, f32[432,128]{1,0:T(8,128)S(1)}, f32[800,128]{1,0:T(8,128)S(1)}, f32[112,128]{1,0:T(8,128)S(1)}, f32[112,12...) custom-call(f32[800,128]{1,0:T(8,128)S(1)} %bitcast.28, f32[104,128]{1,0:T(8,128)S(1)} %get-tuple-element.83.refs_1_.refs_10_, ...), custom_call_target="tpu_custom_call" | custom-call | tf_op jit(solution)/shard_map/pallas_call | solution.py:646
  21.7 1.5 %collective-permute-done.4 = f32[432,128]{1,0:T(8,128)S(1)} collective-permute-done((f32[432,128]{1,0:T(8,128)S(1)}, f32[432,128]{1,0:T(8,128)S(1)}, u32[]{:S(2)}, u32[]{:S(2)}) %collective-permute-start.4) | collective-permute-done | bytes 221216 | tf_op jit(solution)/shard_map/ppermute | solution.py:672
  23.2 0.7 %collective-permute-start.5 = (f32[104,128]{1,0:T(8,128)S(1)}, f32[104,128]{1,0:T(8,128)S(1)}, u32[]{:S(2)}, u32[]{:S(2)}) collective-permute-start(f32[104,128]{1,0:T(8,128)S(1)} %get-tuple-element.77), channel_id=1, source_target_pairs={{0,24},{1,25},{8,16},{9,17},{16,8},{17,9},{24,0},{25,1},{2,26},{3,... | collective-permute-start | bytes 159752 | tf_op jit(solution)/shard_map/ppermute | solution.py:678
  23.9 0.9 %collective-permute-start.7 = (f32[104,128]{1,0:T(8,128)S(1)}, f32[104,128]{1,0:T(8,128)S(1)}, u32[]{:S(2)}, u32[]{:S(2)}) collective-permute-start(f32[104,128]{1,0:T(8,128)S(1)} %get-tuple-element.78), channel_id=1, source_target_pairs={{0,9},{1,8},{8,1},{9,0},{16,25},{17,24},{24,17},{25,16},{2,11},{3,... | collective-permute-start | bytes 159752 | tf_op jit(solution)/shard_map/ppermute | solution.py:678
  24.8 1.7 %collective-permute-start.6 = (f32[104,128]{1,0:T(8,128)S(1)}, f32[104,128]{1,0:T(8,128)S(1)}, u32[]{:S(2)}, u32[]{:S(2)}) collective-permute-start(f32[104,128]{1,0:T(8,128)S(1)} %get-tuple-element.79), channel_id=1, source_target_pairs={{0,17},{1,16},{8,25},{9,24},{16,1},{17,0},{24,9},{25,8},{2,19},{3,... | collective-permute-start | bytes 159752 | tf_op jit(solution)/shard_map/ppermute | solution.py:678
  26.5 2.4 %collective-permute-done.5 = f32[104,128]{1,0:T(8,128)S(1)} collective-permute-done((f32[104,128]{1,0:T(8,128)S(1)}, f32[104,128]{1,0:T(8,128)S(1)}, u32[]{:S(2)}, u32[]{:S(2)}) %collective-permute-start.5) | collective-permute-done | bytes 53280 | tf_op jit(solution)/shard_map/ppermute | solution.py:678
  29.1 1.9 %collective-permute-start.10 = (f32[112,128]{1,0:T(8,128)S(1)}, f32[112,128]{1,0:T(8,128)S(1)}, u32[]{:S(2)}, u32[]{:S(2)}) collective-permute-start(f32[112,128]{1,0:T(8,128)S(1)} %pad_maximum_fusion), channel_id=1, source_target_pairs={{0,6},{2,4},{4,2},{6,0},{1,7},{3,5},{5,3},{7,1},{8,14},{10,12},{12... | collective-permute-start | bytes 172040 | tf_op jit(solution)/shard_map/ppermute | solution.py:687
  31.2 2.4 %collective-permute-start.8 = (f32[112,128]{1,0:T(8,128)S(1)}, f32[112,128]{1,0:T(8,128)S(1)}, u32[]{:S(2)}, u32[]{:S(2)}) collective-permute-start(f32[112,128]{1,0:T(8,128)S(1)} %pad_maximum_fusion), channel_id=1, source_target_pairs={{0,2},{2,0},{4,6},{6,4},{1,3},{3,1},{5,7},{7,5},{8,10},{10,8},{12,... | collective-permute-start | bytes 172040 | tf_op jit(solution)/shard_map/ppermute | solution.py:687
  33.6 0.7 %collective-permute-start.14 = (f32[112,128]{1,0:T(8,128)S(1)}, f32[112,128]{1,0:T(8,128)S(1)}, u32[]{:S(2)}, u32[]{:S(2)}) collective-permute-start(f32[112,128]{1,0:T(8,128)S(1)} %get-tuple-element.64), channel_id=1, source_target_pairs={{0,8},{8,0},{16,24},{24,16},{1,9},{9,1},{17,25},{25,17},{2,10},{10... | collective-permute-start | bytes 172040 | tf_op jit(solution)/shard_map/ppermute | solution.py:547
  34.2 1.6 %collective-permute-start.15 = (f32[112,128]{1,0:T(8,128)S(1)}, f32[112,128]{1,0:T(8,128)S(1)}, u32[]{:S(2)}, u32[]{:S(2)}) collective-permute-start(f32[112,128]{1,0:T(8,128)S(1)} %get-tuple-element.65), channel_id=1, source_target_pairs={{8,16},{24,0},{16,8},{0,24},{9,17},{25,1},{17,9},{1,25},{10,18},{2... | collective-permute-start | bytes 172040 | tf_op jit(solution)/shard_map/ppermute | solution.py:548
  35.9 1.6 %collective-permute-done.9 = f32[112,128]{1,0:T(8,128)S(1)} collective-permute-done((f32[112,128]{1,0:T(8,128)S(1)}, f32[112,128]{1,0:T(8,128)S(1)}, u32[]{:S(2)}, u32[]{:S(2)}) %collective-permute-start.9) | collective-permute-done | bytes 57376 | tf_op jit(solution)/shard_map/ppermute | solution.py:687
  37.5 1.2 %collective-permute-start.13 = (f32[104,128]{1,0:T(8,128)S(1)}, f32[104,128]{1,0:T(8,128)S(1)}, u32[]{:S(2)}, u32[]{:S(2)}) collective-permute-start(f32[104,128]{1,0:T(8,128)S(1)} %slice_add_fusion.refs_1_), channel_id=1, source_target_pairs={{0,24},{1,25},{8,16},{9,17},{16,8},{17,9},{24,0},{25,1},{2,26},{3,... | collective-permute-start | bytes 159752 | tf_op jit(solution)/shard_map/ppermute | solution.py:712
  38.9 1.8 %collective-permute-start.11 = (f32[104,128]{1,0:T(8,128)S(1)}, f32[104,128]{1,0:T(8,128)S(1)}, u32[]{:S(2)}, u32[]{:S(2)}) collective-permute-start(f32[104,128]{1,0:T(8,128)S(1)} %slice_add_fusion.refs_1_), channel_id=1, source_target_pairs={{0,9},{1,8},{8,1},{9,0},{16,25},{17,24},{24,17},{25,16},{2,11},{3,... | collective-permute-start | bytes 159752 | tf_op jit(solution)/shard_map/ppermute | solution.py:712
  40.8 1.5 %shard_map.134 = f32[800,128]{1,0:T(8,128)} custom-call(f32[1,128]{1,0:T(1,128)S(1)} %get-tuple-element.61.refs_0_, f32[104,128]{1,0:T(8,128)S(1)} %slice_add_fusion.refs_1_, f32[800,128]{1,0:T(8,128)S(1)} %get-tuple-element.62.refs_2_, f32[128,1024]{1,0:T(8,128)S(1)} %get-tuple-element.44.refs_1_.refs_5_.refs_3_, ...), custom_call_target="tpu_custom_call" | custom-call | tf_op jit(solution)/shard_map/pallas_call | solution.py:701
  42.7 0.7 %collective-permute-done.12 = f32[104,128]{1,0:T(8,128)S(1)} collective-permute-done((f32[104,128]{1,0:T(8,128)S(1)}, f32[104,128]{1,0:T(8,128)S(1)}, u32[]{:S(2)}, u32[]{:S(2)}) %collective-permute-start.12) | collective-permute-done | bytes 53280 | tf_op jit(solution)/shard_map/ppermute | solution.py:712
  43.6 1.4 %collective-permute-done.16.refs_1_ = f32[416,128]{1,0:T(8,128)S(1)} collective-permute-done((f32[416,128]{1,0:T(8,128)S(1)}, f32[416,128]{1,0:T(8,128)S(1)}, u32[]{:S(2)}, u32[]{:S(2)}) %collective-permute-start.16) | collective-permute-done | bytes 213024 | tf_op jit(solution)/shard_map/ppermute | solution.py:716
  45.0 0.8 %shard_map.135 = (f32[100,512]{1,0:T(8,128)}, f32[1,512]{1,0:T(1,128)}, f32[100,512]{1,0:T(8,128)}, f32[1,100]{1,0:T(1,128)}) custom-call(f32[416,128]{1,0:T(8,128)S(1)} %constant_dynamic-update-slice_fusion.refs_0_, f32[416,128]{1,0:T(8,128)S(1)} %collective-permute-done.16.refs_1_), custom_call_target="tpu_custom_call" | custom-call | tf_op jit(solution)/shard_map/pallas_call | solution.py:717
  (54 shorter events, 3.0 us)
Async XLA Ops:
  0.7 13.4 %copy-start.4 = (bf16[100,512]{1,0:T(8,128)(2,1)S(1)}, bf16[100,512]{1,0:T(8,128)(2,1)}, u32[]{:S(2)}) copy-start(bf16[100,512]{1,0:T(8,128)(2,1)} %refs_2_.3) | copy-start | bytes 307204
  0.7 13.4 %copy-start.5 = (bf16[512,100]{0,1:T(8,128)(2,1)S(1)}, bf16[512,100]{0,1:T(8,128)(2,1)}, u32[]{:S(2)}) copy-start(bf16[512,100]{0,1:T(8,128)(2,1)} %param.16) | copy-start | bytes 307204
  0.7 13.4 %copy-start.6 = (f32[512]{0:T(512)S(1)}, f32[512]{0:T(512)}, u32[]{:S(2)}) copy-start(f32[512]{0:T(512)} %param.15) | copy-start | bytes 6148
  0.7 13.4 %copy-start.7 = (f32[100]{0:T(128)S(1)}, f32[100]{0:T(128)}, u32[]{:S(2)}) copy-start(f32[100]{0:T(128)} %param.17) | copy-start | bytes 1204
  0.7 13.4 %copy-start.8 = (f32[100]{0:T(128)S(1)}, f32[100]{0:T(128)}, u32[]{:S(2)}) copy-start(f32[100]{0:T(128)} %param.13) | copy-start | bytes 1204
  2.0 12.6 %collective-permute-start.3 = (f32[8,128]{1,0:T(8,128)S(1)}, f32[8,128]{1,0:T(8,128)S(1)}, u32[]{:S(2)}, u32[]{:S(2)}) collective-permute-start(f32[8,128]{1,0:T(8,128)S(1)} %get-tuple-element.86), channel_id=1, source_target_pairs={{1,2},{3,4},{5,6},{7,0},{2,1},{4,3},{6,5},{0,7},{9,10},{11,12},{13... | collective-permute-start | bytes 12296 | tf_op jit(solution)/shard_map/ppermute | solution.py:606
  6.5 8.0 %collective-permute-start.2 = (f32[8,128]{1,0:T(8,128)S(1)}, f32[8,128]{1,0:T(8,128)S(1)}, u32[]{:S(2)}, u32[]{:S(2)}) collective-permute-start(f32[8,128]{1,0:T(8,128)S(1)} %get-tuple-element.87), channel_id=1, source_target_pairs={{0,1},{1,0},{2,3},{3,2},{4,5},{5,4},{6,7},{7,6},{8,9},{9,8},{10,11... | collective-permute-start | bytes 12296 | tf_op jit(solution)/shard_map/ppermute | solution.py:605
  7.3 10.6 %all-to-all-start = ((f32[32,1,128]{2,1,0:T(1,128)}), f32[32,1,128]{2,1,0:T(1,128)S(1)}, u32[]{:S(2)}, u32[]{:S(2)}) async-start(f32[32,1,128]{2,1,0:T(1,128)} %shard_map.131), calls=%async_computation | async-start | bytes 32768 | tf_op jit(solution)/shard_map/all_to_all | solution.py:602
  10.8 8.5 %collective-permute-start.1 = (f32[104,128]{1,0:T(8,128)S(1)}, f32[104,128]{1,0:T(8,128)S(1)}, u32[]{:S(2)}, u32[]{:S(2)}) collective-permute-start(f32[104,128]{1,0:T(8,128)S(1)} %get-tuple-element.41), channel_id=1, source_target_pairs={{8,16},{24,0},{16,8},{0,24},{9,17},{25,1},{17,9},{1,25},{10,18},{2... | collective-permute-start | bytes 159752 | tf_op jit(solution)/shard_map/ppermute | solution.py:548
  13.5 5.8 %collective-permute-start = (f32[112,128]{1,0:T(8,128)S(1)}, f32[112,128]{1,0:T(8,128)S(1)}, u32[]{:S(2)}, u32[]{:S(2)}) collective-permute-start(f32[112,128]{1,0:T(8,128)S(1)} %get-tuple-element.40), channel_id=1, source_target_pairs={{0,8},{8,0},{16,24},{24,16},{1,9},{9,1},{17,25},{25,17},{2,10},{10... | collective-permute-start | bytes 172040 | tf_op jit(solution)/shard_map/ppermute | solution.py:547
  14.1 5.2 %copy-start.1 = (f32[100,8,128]{2,1,0:T(8,128)S(1)}, f32[100,8,128]{2,1,0:T(8,128)}, u32[]{:S(2)}) copy-start(f32[100,8,128]{2,1,0:T(8,128)} %param.10) | copy-start | bytes 1228804
  21.6 1.5 %collective-permute-start.4 = (f32[432,128]{1,0:T(8,128)S(1)}, f32[432,128]{1,0:T(8,128)S(1)}, u32[]{:S(2)}, u32[]{:S(2)}) collective-permute-start(f32[432,128]{1,0:T(8,128)S(1)} %get-tuple-element.57), channel_id=1, source_target_pairs={{0,1},{1,0},{2,3},{3,2},{4,5},{5,4},{6,7},{7,6},{8,9},{9,8},{10,11... | collective-permute-start | bytes 663560 | tf_op jit(solution)/shard_map/ppermute | solution.py:672
  23.2 5.7 %collective-permute-start.5 = (f32[104,128]{1,0:T(8,128)S(1)}, f32[104,128]{1,0:T(8,128)S(1)}, u32[]{:S(2)}, u32[]{:S(2)}) collective-permute-start(f32[104,128]{1,0:T(8,128)S(1)} %get-tuple-element.77), channel_id=1, source_target_pairs={{0,24},{1,25},{8,16},{9,17},{16,8},{17,9},{24,0},{25,1},{2,26},{3,... | collective-permute-start | bytes 159752 | tf_op jit(solution)/shard_map/ppermute | solution.py:678
  23.9 5.0 %collective-permute-start.7 = (f32[104,128]{1,0:T(8,128)S(1)}, f32[104,128]{1,0:T(8,128)S(1)}, u32[]{:S(2)}, u32[]{:S(2)}) collective-permute-start(f32[104,128]{1,0:T(8,128)S(1)} %get-tuple-element.78), channel_id=1, source_target_pairs={{0,9},{1,8},{8,1},{9,0},{16,25},{17,24},{24,17},{25,16},{2,11},{3,... | collective-permute-start | bytes 159752 | tf_op jit(solution)/shard_map/ppermute | solution.py:678
  24.8 4.3 %collective-permute-start.6 = (f32[104,128]{1,0:T(8,128)S(1)}, f32[104,128]{1,0:T(8,128)S(1)}, u32[]{:S(2)}, u32[]{:S(2)}) collective-permute-start(f32[104,128]{1,0:T(8,128)S(1)} %get-tuple-element.79), channel_id=1, source_target_pairs={{0,17},{1,16},{8,25},{9,24},{16,1},{17,0},{24,9},{25,8},{2,19},{3,... | collective-permute-start | bytes 159752 | tf_op jit(solution)/shard_map/ppermute | solution.py:678
  29.1 6.8 %collective-permute-start.10 = (f32[112,128]{1,0:T(8,128)S(1)}, f32[112,128]{1,0:T(8,128)S(1)}, u32[]{:S(2)}, u32[]{:S(2)}) collective-permute-start(f32[112,128]{1,0:T(8,128)S(1)} %pad_maximum_fusion), channel_id=1, source_target_pairs={{0,6},{2,4},{4,2},{6,0},{1,7},{3,5},{5,3},{7,1},{8,14},{10,12},{12... | collective-permute-start | bytes 172040 | tf_op jit(solution)/shard_map/ppermute | solution.py:687
  31.0 6.5 %collective-permute-start.9 = (f32[112,128]{1,0:T(8,128)S(1)}, f32[112,128]{1,0:T(8,128)S(1)}, u32[]{:S(2)}, u32[]{:S(2)}) collective-permute-start(f32[112,128]{1,0:T(8,128)S(1)} %pad_maximum_fusion), channel_id=1, source_target_pairs={{0,4},{2,6},{4,0},{6,2},{1,5},{3,7},{5,1},{7,3},{8,12},{10,14},{12... | collective-permute-start | bytes 172040 | tf_op jit(solution)/shard_map/ppermute | solution.py:687
  31.2 6.3 %collective-permute-start.8 = (f32[112,128]{1,0:T(8,128)S(1)}, f32[112,128]{1,0:T(8,128)S(1)}, u32[]{:S(2)}, u32[]{:S(2)}) collective-permute-start(f32[112,128]{1,0:T(8,128)S(1)} %pad_maximum_fusion), channel_id=1, source_target_pairs={{0,2},{2,0},{4,6},{6,4},{1,3},{3,1},{5,7},{7,5},{8,10},{10,8},{12,... | collective-permute-start | bytes 172040 | tf_op jit(solution)/shard_map/ppermute | solution.py:687
  33.6 7.2 %collective-permute-start.14 = (f32[112,128]{1,0:T(8,128)S(1)}, f32[112,128]{1,0:T(8,128)S(1)}, u32[]{:S(2)}, u32[]{:S(2)}) collective-permute-start(f32[112,128]{1,0:T(8,128)S(1)} %get-tuple-element.64), channel_id=1, source_target_pairs={{0,8},{8,0},{16,24},{24,16},{1,9},{9,1},{17,25},{25,17},{2,10},{10... | collective-permute-start | bytes 172040 | tf_op jit(solution)/shard_map/ppermute | solution.py:547
  34.2 6.5 %collective-permute-start.15 = (f32[112,128]{1,0:T(8,128)S(1)}, f32[112,128]{1,0:T(8,128)S(1)}, u32[]{:S(2)}, u32[]{:S(2)}) collective-permute-start(f32[112,128]{1,0:T(8,128)S(1)} %get-tuple-element.65), channel_id=1, source_target_pairs={{8,16},{24,0},{16,8},{0,24},{9,17},{25,1},{17,9},{1,25},{10,18},{2... | collective-permute-start | bytes 172040 | tf_op jit(solution)/shard_map/ppermute | solution.py:548
  37.5 5.2 %collective-permute-start.13 = (f32[104,128]{1,0:T(8,128)S(1)}, f32[104,128]{1,0:T(8,128)S(1)}, u32[]{:S(2)}, u32[]{:S(2)}) collective-permute-start(f32[104,128]{1,0:T(8,128)S(1)} %slice_add_fusion.refs_1_), channel_id=1, source_target_pairs={{0,24},{1,25},{8,16},{9,17},{16,8},{17,9},{24,0},{25,1},{2,26},{3,... | collective-permute-start | bytes 159752 | tf_op jit(solution)/shard_map/ppermute | solution.py:712
  38.7 4.6 %collective-permute-start.12 = (f32[104,128]{1,0:T(8,128)S(1)}, f32[104,128]{1,0:T(8,128)S(1)}, u32[]{:S(2)}, u32[]{:S(2)}) collective-permute-start(f32[104,128]{1,0:T(8,128)S(1)} %slice_add_fusion.refs_1_), channel_id=1, source_target_pairs={{0,17},{1,16},{8,25},{9,24},{16,1},{17,0},{24,9},{25,8},{2,19},{3,... | collective-permute-start | bytes 159752 | tf_op jit(solution)/shard_map/ppermute | solution.py:712
  38.9 4.4 %collective-permute-start.11 = (f32[104,128]{1,0:T(8,128)S(1)}, f32[104,128]{1,0:T(8,128)S(1)}, u32[]{:S(2)}, u32[]{:S(2)}) collective-permute-start(f32[104,128]{1,0:T(8,128)S(1)} %slice_add_fusion.refs_1_), channel_id=1, source_target_pairs={{0,9},{1,8},{8,1},{9,0},{16,25},{17,24},{24,17},{25,16},{2,11},{3,... | collective-permute-start | bytes 159752 | tf_op jit(solution)/shard_map/ppermute | solution.py:712
  43.4 1.5 %collective-permute-start.16 = (f32[416,128]{1,0:T(8,128)S(1)}, f32[416,128]{1,0:T(8,128)S(1)}, u32[]{:S(2)}, u32[]{:S(2)}) collective-permute-start(f32[416,128]{1,0:T(8,128)S(1)} %constant_dynamic-update-slice_fusion.refs_0_), channel_id=1, source_target_pairs={{0,1},{1,0},{2,3},{3,2},{4,5},{5,4},{6,7},{7,6},{8,9},{9,8},{10,11... | collective-permute-start | bytes 638984 | tf_op jit(solution)/shard_map/ppermute | solution.py:716
  (3 other events, 2.4 us)

commit v11 on v10

--- a/solution.py
+++ b/solution.py
@@ -340,6 +340,9 @@
 
     mid = levels // 2
     ones = jnp.ones((rows, cols), f32)
+    z, z_end = spread(0), spread(levels - 1)
+    u = cotangent[at_level(0), :]
+    u_end = cotangent[at_level(levels - 1), :]
     num, den = ones, ones
     num_end, den_end = ones, ones
     for step in range(mid):
@@ -348,9 +351,13 @@
         pivot = num + down * den
         over = 1.0 / pivot
         inv = den * over
-        inv_p[at_level(k), :] = inv
-        rate_a[at_level(k), :] = down * inv
-        rate_b[at_level(k), :] = up * inv
+        a, b = down * inv, up * inv
+        rate_a[at_level(k), :] = a
+        rate_b[at_level(k), :] = b
+        fwd_z[at_level(k), :] = z * inv
+        fwd_u[at_level(k), :] = u * inv
+        z = spread(k + 1) + a * z
+        u = cotangent[at_level(k + 1), :] + b * u
         num, den = pivot + up * num, pivot
         if step % 4 == 3:
             num, den = num * over, ones
@@ -360,41 +367,23 @@
             pivot = num_end + up * den_end
             over = 1.0 / pivot
             inv = den_end * over
-            inv_p[at_level(k), :] = inv
-            rate_a[at_level(k), :] = down * inv
-            rate_b[at_level(k), :] = up * inv
+            a, b = down * inv, up * inv
+            rate_a[at_level(k), :] = a
+            rate_b[at_level(k), :] = b
+            fwd_z[at_level(k), :] = z_end * inv
+            fwd_u[at_level(k), :] = u_end * inv
+            z_end = b * z_end
+            u_end = a * u_end
+            if k - 1 > mid:
+                z_end = spread(k - 1) + z_end
+                u_end = cotangent[at_level(k - 1), :] + u_end
             num_end, den_end = down * num_end, pivot
             if k - 1 > mid:
                 num_end = pivot + num_end
             if step % 4 == 3:
                 num_end, den_end = num_end * over, ones
-        mixed[at_level(step), :] = spread(step)
-        mixed[at_level(levels - 1 - step), :] = spread(levels - 1 - step)
-    if levels % 2:
-        mixed[at_level(mid), :] = spread(mid)
     middle = 1.0 / (num / den + num_end / den_end)
 
-    z = mixed[at_level(0), :]
-    u = cotangent[at_level(0), :]
-    z_end = mixed[at_level(levels - 1), :]
-    u_end = cotangent[at_level(levels - 1), :]
-    for step in range(mid):
-        k = step
-        inv, a, b = inv_p[at_level(k), :], rate_a[at_level(k), :], rate_b[at_level(k), :]
-        fwd_z[at_level(k), :] = z * inv
-        fwd_u[at_level(k), :] = u * inv
-        z = mixed[at_level(k + 1), :] + a * z
-        u = cotangent[at_level(k + 1), :] + b * u
-        k = levels - 1 - step
-        if k > mid:
-            inv, a, b = inv_p[at_level(k), :], rate_a[at_level(k), :], rate_b[at_level(k), :]
-            fwd_z[at_level(k), :] = z_end * inv
-            fwd_u[at_level(k), :] = u_end * inv
-            z_end = b * z_end
-            u_end = a * u_end
-            if k - 1 > mid:
-                z_end = mixed[at_level(k - 1), :] + z_end
-                u_end = cotangent[at_level(k - 1), :] + u_end
     x_up = x_down = (z + z_end) * middle
     y_up = y_down = (u + u_end) * middle
     adjoint[at_level(mid), :] = y_up

time: 46 us -> 46 us (level)
  no operation moved by 1% of the time
where the time goes in v11:
time: 46 us; the launch traced here: 45.8 us
  starting transfers between devices  24.9 us (54%)
  waiting for transfers between devices  11.5 us (25%)
  Pallas kernels  7.41 us (16%)
  local copies, waits for them, and re-layouts  1.04 us (2%)
  between operations  0.92 us (2%)
    ppermute x1, starting transfers between devices, shards(): lax.ppermute(small[rows:], ('z', 'core'), far_pairs(lons, True))  4.55 us
    ppermute x3, starting transfers between devices, shards(): lax.ppermute(packed, 'z', flip(chips, step))  4.45 us
    ppermute x2, starting transfers between devices, swap_lat(): far = lax.ppermute(lat_b, 'lat', far_pairs(lats, True))  4.39 us
    all_to_all x1, starting transfers between devices, shards(): energy = lax.all_to_all(energy, ('lat', 'z', 'core'), 0, 0, tiled=True)  3.48 us
    all_to_all x1, waiting for transfers between devices, shards(): energy = lax.all_to_all(energy, ('lat', 'z', 'core'), 0, 0, tiled=True)  3.33 us
    ppermute x3, starting transfers between devices, shards(): lax.ppermute(chip[step], ('lat', 'core'), cross_flip(lats, step))  3.27 us
    ppermute x3, starting transfers between devices, shards(): lax.ppermute(part, ('lat', 'core'), cross_flip(lats, step))  3.27 us
    ppermute x3, waiting for transfers between devices, shards(): lax.ppermute(chip[step], ('lat', 'core'), cross_flip(lats, step))  2.59 us
  transfers between devices with their start and end apart: 18, of which 8 were waited for; matrix products, arithmetic and copies ran while one was open for 0% of the time, Pallas kernels for 9%

profile of v11, /device:TPU:0, one launch (start us, length us, event | category | flops | bytes accessed | tf_op | source)
XLA Modules:
  0.0 45.8 jit_solution(5548339143744333177)
XLA Ops:
  0.7 0.6 %copy-done.3 = s32[8,128]{1,0:T(8,128)S(1)} copy-done((s32[8,128]{1,0:T(8,128)S(1)}, s32[8,128]{1,0:T(8,128)}, u32[]{:S(2)}) %copy-start.3) | copy-done | bytes 4120
  2.0 4.6 %collective-permute-start.3 = (f32[8,128]{1,0:T(8,128)S(1)}, f32[8,128]{1,0:T(8,128)S(1)}, u32[]{:S(2)}, u32[]{:S(2)}) collective-permute-start(f32[8,128]{1,0:T(8,128)S(1)} %get-tuple-element.86), channel_id=1, source_target_pairs={{1,2},{3,4},{5,6},{7,0},{2,1},{4,3},{6,5},{0,7},{9,10},{11,12},{13... | collective-permute-start | bytes 12296 | tf_op jit(solution)/shard_map/ppermute | solution.py:595
  6.5 0.8 %shard_map.131 = f32[32,1,128]{2,1,0:T(1,128)} custom-call(f32[800,128]{1,0:T(8,128)S(1)} %bitcast.26, f32[8,128]{1,0:T(8,128)S(1)} %get-tuple-element.43.refs_1_.refs_7_.refs_5_), custom_call_target="tpu_custom_call" | custom-call | flops 1000000000 | bytes 100000000 | tf_op jit(solution)/shard_map/pallas_call | solution.py:582
  7.3 3.5 %all-to-all-start = ((f32[32,1,128]{2,1,0:T(1,128)}), f32[32,1,128]{2,1,0:T(1,128)S(1)}, u32[]{:S(2)}, u32[]{:S(2)}) async-start(f32[32,1,128]{2,1,0:T(1,128)} %shard_map.131), calls=%async_computation | async-start | bytes 32768 | tf_op jit(solution)/shard_map/all_to_all | solution.py:591
  10.8 2.7 %collective-permute-start.1 = (f32[104,128]{1,0:T(8,128)S(1)}, f32[104,128]{1,0:T(8,128)S(1)}, u32[]{:S(2)}, u32[]{:S(2)}) collective-permute-start(f32[104,128]{1,0:T(8,128)S(1)} %get-tuple-element.41), channel_id=1, source_target_pairs={{8,16},{24,0},{16,8},{0,24},{9,17},{25,1},{17,9},{1,25},{10,18},{2... | collective-permute-start | bytes 159752 | tf_op jit(solution)/shard_map/ppermute | solution.py:537
  14.5 3.3 %all-to-all-done.refs_0_ = f32[32,1,128]{2,1,0:T(1,128)S(1)} async-done(((f32[32,1,128]{2,1,0:T(1,128)}), f32[32,1,128]{2,1,0:T(1,128)S(1)}, u32[]{:S(2)}, u32[]{:S(2)}) %all-to-all-start) | async-done | bytes 16416 | tf_op jit(solution)/shard_map/all_to_all | solution.py:591
  17.9 1.4 %shard_map.132 = (f32[1,128]{1,0:T(1,128)S(1)}, bf16[128,1024]{1,0:T(8,128)(2,1)S(1)}, bf16[512,1024]{1,0:T(8,128)(2,1)S(1)}, f32[512,1024]{1,0:T(8,128)S(1)}, f...) custom-call(f32[32,1,128]{2,1,0:T(1,128)S(1)} %all-to-all-done.refs_0_, ...), custom_call_target="tpu_custom_call" | custom-call | tf_op jit(solution)/shard_map/pallas_call | solution.py:619
  19.4 2.3 %shard_map.133 = (f32[4,104,128]{2,1,0:T(8,128)S(1)}, f32[432,128]{1,0:T(8,128)S(1)}, f32[800,128]{1,0:T(8,128)S(1)}, f32[112,128]{1,0:T(8,128)S(1)}, f32[112,12...) custom-call(f32[800,128]{1,0:T(8,128)S(1)} %bitcast.28, f32[104,128]{1,0:T(8,128)S(1)} %get-tuple-element.83.refs_1_.refs_10_, ...), custom_call_target="tpu_custom_call" | custom-call | tf_op jit(solution)/shard_map/pallas_call | solution.py:635
  21.7 1.5 %collective-permute-done.4 = f32[432,128]{1,0:T(8,128)S(1)} collective-permute-done((f32[432,128]{1,0:T(8,128)S(1)}, f32[432,128]{1,0:T(8,128)S(1)}, u32[]{:S(2)}, u32[]{:S(2)}) %collective-permute-start.4) | collective-permute-done | bytes 221216 | tf_op jit(solution)/shard_map/ppermute | solution.py:661
  23.2 0.7 %collective-permute-start.5 = (f32[104,128]{1,0:T(8,128)S(1)}, f32[104,128]{1,0:T(8,128)S(1)}, u32[]{:S(2)}, u32[]{:S(2)}) collective-permute-start(f32[104,128]{1,0:T(8,128)S(1)} %get-tuple-element.77), channel_id=1, source_target_pairs={{0,24},{1,25},{8,16},{9,17},{16,8},{17,9},{24,0},{25,1},{2,26},{3,... | collective-permute-start | bytes 159752 | tf_op jit(solution)/shard_map/ppermute | solution.py:667
  23.9 0.9 %collective-permute-start.7 = (f32[104,128]{1,0:T(8,128)S(1)}, f32[104,128]{1,0:T(8,128)S(1)}, u32[]{:S(2)}, u32[]{:S(2)}) collective-permute-start(f32[104,128]{1,0:T(8,128)S(1)} %get-tuple-element.78), channel_id=1, source_target_pairs={{0,9},{1,8},{8,1},{9,0},{16,25},{17,24},{24,17},{25,16},{2,11},{3,... | collective-permute-start | bytes 159752 | tf_op jit(solution)/shard_map/ppermute | solution.py:667
  24.8 1.7 %collective-permute-start.6 = (f32[104,128]{1,0:T(8,128)S(1)}, f32[104,128]{1,0:T(8,128)S(1)}, u32[]{:S(2)}, u32[]{:S(2)}) collective-permute-start(f32[104,128]{1,0:T(8,128)S(1)} %get-tuple-element.79), channel_id=1, source_target_pairs={{0,17},{1,16},{8,25},{9,24},{16,1},{17,0},{24,9},{25,8},{2,19},{3,... | collective-permute-start | bytes 159752 | tf_op jit(solution)/shard_map/ppermute | solution.py:667
  26.5 2.4 %collective-permute-done.5 = f32[104,128]{1,0:T(8,128)S(1)} collective-permute-done((f32[104,128]{1,0:T(8,128)S(1)}, f32[104,128]{1,0:T(8,128)S(1)}, u32[]{:S(2)}, u32[]{:S(2)}) %collective-permute-start.5) | collective-permute-done | bytes 53280 | tf_op jit(solution)/shard_map/ppermute | solution.py:667
  29.1 1.9 %collective-permute-start.10 = (f32[112,128]{1,0:T(8,128)S(1)}, f32[112,128]{1,0:T(8,128)S(1)}, u32[]{:S(2)}, u32[]{:S(2)}) collective-permute-start(f32[112,128]{1,0:T(8,128)S(1)} %pad_maximum_fusion), channel_id=1, source_target_pairs={{0,6},{2,4},{4,2},{6,0},{1,7},{3,5},{5,3},{7,1},{8,14},{10,12},{12... | collective-permute-start | bytes 172040 | tf_op jit(solution)/shard_map/ppermute | solution.py:676
  31.2 2.4 %collective-permute-start.8 = (f32[112,128]{1,0:T(8,128)S(1)}, f32[112,128]{1,0:T(8,128)S(1)}, u32[]{:S(2)}, u32[]{:S(2)}) collective-permute-start(f32[112,128]{1,0:T(8,128)S(1)} %pad_maximum_fusion), channel_id=1, source_target_pairs={{0,2},{2,0},{4,6},{6,4},{1,3},{3,1},{5,7},{7,5},{8,10},{10,8},{12,... | collective-permute-start | bytes 172040 | tf_op jit(solution)/shard_map/ppermute | solution.py:676
  33.6 0.6 %collective-permute-start.14 = (f32[112,128]{1,0:T(8,128)S(1)}, f32[112,128]{1,0:T(8,128)S(1)}, u32[]{:S(2)}, u32[]{:S(2)}) collective-permute-start(f32[112,128]{1,0:T(8,128)S(1)} %get-tuple-element.64), channel_id=1, source_target_pairs={{0,8},{8,0},{16,24},{24,16},{1,9},{9,1},{17,25},{25,17},{2,10},{10... | collective-permute-start | bytes 172040 | tf_op jit(solution)/shard_map/ppermute | solution.py:536
  34.2 1.7 %collective-permute-start.15 = (f32[112,128]{1,0:T(8,128)S(1)}, f32[112,128]{1,0:T(8,128)S(1)}, u32[]{:S(2)}, u32[]{:S(2)}) collective-permute-start(f32[112,128]{1,0:T(8,128)S(1)} %get-tuple-element.65), channel_id=1, source_target_pairs={{8,16},{24,0},{16,8},{0,24},{9,17},{25,1},{17,9},{1,25},{10,18},{2... | collective-permute-start | bytes 172040 | tf_op jit(solution)/shard_map/ppermute | solution.py:537
  35.9 1.6 %collective-permute-done.9 = f32[112,128]{1,0:T(8,128)S(1)} collective-permute-done((f32[112,128]{1,0:T(8,128)S(1)}, f32[112,128]{1,0:T(8,128)S(1)}, u32[]{:S(2)}, u32[]{:S(2)}) %collective-permute-start.9) | collective-permute-done | bytes 57376 | tf_op jit(solution)/shard_map/ppermute | solution.py:676
  37.5 1.2 %collective-permute-start.13 = (f32[104,128]{1,0:T(8,128)S(1)}, f32[104,128]{1,0:T(8,128)S(1)}, u32[]{:S(2)}, u32[]{:S(2)}) collective-permute-start(f32[104,128]{1,0:T(8,128)S(1)} %slice_add_fusion.refs_1_), channel_id=1, source_target_pairs={{0,24},{1,25},{8,16},{9,17},{16,8},{17,9},{24,0},{25,1},{2,26},{3,... | collective-permute-start | bytes 159752 | tf_op jit(solution)/shard_map/ppermute | solution.py:701
  39.0 1.8 %collective-permute-start.11 = (f32[104,128]{1,0:T(8,128)S(1)}, f32[104,128]{1,0:T(8,128)S(1)}, u32[]{:S(2)}, u32[]{:S(2)}) collective-permute-start(f32[104,128]{1,0:T(8,128)S(1)} %slice_add_fusion.refs_1_), channel_id=1, source_target_pairs={{0,9},{1,8},{8,1},{9,0},{16,25},{17,24},{24,17},{25,16},{2,11},{3,... | collective-permute-start | bytes 159752 | tf_op jit(solution)/shard_map/ppermute | solution.py:701
  40.8 1.5 %shard_map.134 = f32[800,128]{1,0:T(8,128)} custom-call(f32[1,128]{1,0:T(1,128)S(1)} %get-tuple-element.61.refs_0_, f32[104,128]{1,0:T(8,128)S(1)} %slice_add_fusion.refs_1_, f32[800,128]{1,0:T(8,128)S(1)} %get-tuple-element.62.refs_2_, f32[128,1024]{1,0:T(8,128)S(1)} %get-tuple-element.44.refs_1_.refs_5_.refs_3_, ...), custom_call_target="tpu_custom_call" | custom-call | tf_op jit(solution)/shard_map/pallas_call | solution.py:690
  42.7 0.7 %collective-permute-done.12 = f32[104,128]{1,0:T(8,128)S(1)} collective-permute-done((f32[104,128]{1,0:T(8,128)S(1)}, f32[104,128]{1,0:T(8,128)S(1)}, u32[]{:S(2)}, u32[]{:S(2)}) %collective-permute-start.12) | collective-permute-done | bytes 53280 | tf_op jit(solution)/shard_map/ppermute | solution.py:701
  43.6 1.4 %collective-permute-done.16.refs_1_ = f32[416,128]{1,0:T(8,128)S(1)} collective-permute-done((f32[416,128]{1,0:T(8,128)S(1)}, f32[416,128]{1,0:T(8,128)S(1)}, u32[]{:S(2)}, u32[]{:S(2)}) %collective-permute-start.16) | collective-permute-done | bytes 213024 | tf_op jit(solution)/shard_map/ppermute | solution.py:705
  45.0 0.8 %shard_map.135 = (f32[100,512]{1,0:T(8,128)}, f32[1,512]{1,0:T(1,128)}, f32[100,512]{1,0:T(8,128)}, f32[1,100]{1,0:T(1,128)}) custom-call(f32[416,128]{1,0:T(8,128)S(1)} %constant_dynamic-update-slice_fusion.refs_0_, f32[416,128]{1,0:T(8,128)S(1)} %collective-permute-done.16.refs_1_), custom_call_target="tpu_custom_call" | custom-call | tf_op jit(solution)/shard_map/pallas_call | solution.py:706
  (54 shorter events, 3.0 us)
Async XLA Ops:
  0.7 13.4 %copy-start.4 = (bf16[100,512]{1,0:T(8,128)(2,1)S(1)}, bf16[100,512]{1,0:T(8,128)(2,1)}, u32[]{:S(2)}) copy-start(bf16[100,512]{1,0:T(8,128)(2,1)} %refs_2_.3) | copy-start | bytes 307204
  0.7 13.4 %copy-start.5 = (bf16[512,100]{0,1:T(8,128)(2,1)S(1)}, bf16[512,100]{0,1:T(8,128)(2,1)}, u32[]{:S(2)}) copy-start(bf16[512,100]{0,1:T(8,128)(2,1)} %param.16) | copy-start | bytes 307204
  0.7 13.4 %copy-start.6 = (f32[512]{0:T(512)S(1)}, f32[512]{0:T(512)}, u32[]{:S(2)}) copy-start(f32[512]{0:T(512)} %param.15) | copy-start | bytes 6148
  0.7 13.4 %copy-start.7 = (f32[100]{0:T(128)S(1)}, f32[100]{0:T(128)}, u32[]{:S(2)}) copy-start(f32[100]{0:T(128)} %param.17) | copy-start | bytes 1204
  0.7 13.4 %copy-start.8 = (f32[100]{0:T(128)S(1)}, f32[100]{0:T(128)}, u32[]{:S(2)}) copy-start(f32[100]{0:T(128)} %param.13) | copy-start | bytes 1204
  2.0 12.6 %collective-permute-start.3 = (f32[8,128]{1,0:T(8,128)S(1)}, f32[8,128]{1,0:T(8,128)S(1)}, u32[]{:S(2)}, u32[]{:S(2)}) collective-permute-start(f32[8,128]{1,0:T(8,128)S(1)} %get-tuple-element.86), channel_id=1, source_target_pairs={{1,2},{3,4},{5,6},{7,0},{2,1},{4,3},{6,5},{0,7},{9,10},{11,12},{13... | collective-permute-start | bytes 12296 | tf_op jit(solution)/shard_map/ppermute | solution.py:595
  6.5 8.0 %collective-permute-start.2 = (f32[8,128]{1,0:T(8,128)S(1)}, f32[8,128]{1,0:T(8,128)S(1)}, u32[]{:S(2)}, u32[]{:S(2)}) collective-permute-start(f32[8,128]{1,0:T(8,128)S(1)} %get-tuple-element.87), channel_id=1, source_target_pairs={{0,1},{1,0},{2,3},{3,2},{4,5},{5,4},{6,7},{7,6},{8,9},{9,8},{10,11... | collective-permute-start | bytes 12296 | tf_op jit(solution)/shard_map/ppermute | solution.py:594
  7.3 10.6 %all-to-all-start = ((f32[32,1,128]{2,1,0:T(1,128)}), f32[32,1,128]{2,1,0:T(1,128)S(1)}, u32[]{:S(2)}, u32[]{:S(2)}) async-start(f32[32,1,128]{2,1,0:T(1,128)} %shard_map.131), calls=%async_computation | async-start | bytes 32768 | tf_op jit(solution)/shard_map/all_to_all | solution.py:591
  10.8 8.5 %collective-permute-start.1 = (f32[104,128]{1,0:T(8,128)S(1)}, f32[104,128]{1,0:T(8,128)S(1)}, u32[]{:S(2)}, u32[]{:S(2)}) collective-permute-start(f32[104,128]{1,0:T(8,128)S(1)} %get-tuple-element.41), channel_id=1, source_target_pairs={{8,16},{24,0},{16,8},{0,24},{9,17},{25,1},{17,9},{1,25},{10,18},{2... | collective-permute-start | bytes 159752 | tf_op jit(solution)/shard_map/ppermute | solution.py:537
  13.5 5.8 %collective-permute-start = (f32[112,128]{1,0:T(8,128)S(1)}, f32[112,128]{1,0:T(8,128)S(1)}, u32[]{:S(2)}, u32[]{:S(2)}) collective-permute-start(f32[112,128]{1,0:T(8,128)S(1)} %get-tuple-element.40), channel_id=1, source_target_pairs={{0,8},{8,0},{16,24},{24,16},{1,9},{9,1},{17,25},{25,17},{2,10},{10... | collective-permute-start | bytes 172040 | tf_op jit(solution)/shard_map/ppermute | solution.py:536
  14.1 5.2 %copy-start.1 = (f32[100,8,128]{2,1,0:T(8,128)S(1)}, f32[100,8,128]{2,1,0:T(8,128)}, u32[]{:S(2)}) copy-start(f32[100,8,128]{2,1,0:T(8,128)} %param.10) | copy-start | bytes 1228804
  21.6 1.5 %collective-permute-start.4 = (f32[432,128]{1,0:T(8,128)S(1)}, f32[432,128]{1,0:T(8,128)S(1)}, u32[]{:S(2)}, u32[]{:S(2)}) collective-permute-start(f32[432,128]{1,0:T(8,128)S(1)} %get-tuple-element.57), channel_id=1, source_target_pairs={{0,1},{1,0},{2,3},{3,2},{4,5},{5,4},{6,7},{7,6},{8,9},{9,8},{10,11... | collective-permute-start | bytes 663560 | tf_op jit(solution)/shard_map/ppermute | solution.py:661
  23.2 5.7 %collective-permute-start.5 = (f32[104,128]{1,0:T(8,128)S(1)}, f32[104,128]{1,0:T(8,128)S(1)}, u32[]{:S(2)}, u32[]{:S(2)}) collective-permute-start(f32[104,128]{1,0:T(8,128)S(1)} %get-tuple-element.77), channel_id=1, source_target_pairs={{0,24},{1,25},{8,16},{9,17},{16,8},{17,9},{24,0},{25,1},{2,26},{3,... | collective-permute-start | bytes 159752 | tf_op jit(solution)/shard_map/ppermute | solution.py:667
  23.9 5.0 %collective-permute-start.7 = (f32[104,128]{1,0:T(8,128)S(1)}, f32[104,128]{1,0:T(8,128)S(1)}, u32[]{:S(2)}, u32[]{:S(2)}) collective-permute-start(f32[104,128]{1,0:T(8,128)S(1)} %get-tuple-element.78), channel_id=1, source_target_pairs={{0,9},{1,8},{8,1},{9,0},{16,25},{17,24},{24,17},{25,16},{2,11},{3,... | collective-permute-start | bytes 159752 | tf_op jit(solution)/shard_map/ppermute | solution.py:667
  24.8 4.3 %collective-permute-start.6 = (f32[104,128]{1,0:T(8,128)S(1)}, f32[104,128]{1,0:T(8,128)S(1)}, u32[]{:S(2)}, u32[]{:S(2)}) collective-permute-start(f32[104,128]{1,0:T(8,128)S(1)} %get-tuple-element.79), channel_id=1, source_target_pairs={{0,17},{1,16},{8,25},{9,24},{16,1},{17,0},{24,9},{25,8},{2,19},{3,... | collective-permute-start | bytes 159752 | tf_op jit(solution)/shard_map/ppermute | solution.py:667
  29.1 6.8 %collective-permute-start.10 = (f32[112,128]{1,0:T(8,128)S(1)}, f32[112,128]{1,0:T(8,128)S(1)}, u32[]{:S(2)}, u32[]{:S(2)}) collective-permute-start(f32[112,128]{1,0:T(8,128)S(1)} %pad_maximum_fusion), channel_id=1, source_target_pairs={{0,6},{2,4},{4,2},{6,0},{1,7},{3,5},{5,3},{7,1},{8,14},{10,12},{12... | collective-permute-start | bytes 172040 | tf_op jit(solution)/shard_map/ppermute | solution.py:676
  31.0 6.5 %collective-permute-start.9 = (f32[112,128]{1,0:T(8,128)S(1)}, f32[112,128]{1,0:T(8,128)S(1)}, u32[]{:S(2)}, u32[]{:S(2)}) collective-permute-start(f32[112,128]{1,0:T(8,128)S(1)} %pad_maximum_fusion), channel_id=1, source_target_pairs={{0,4},{2,6},{4,0},{6,2},{1,5},{3,7},{5,1},{7,3},{8,12},{10,14},{12... | collective-permute-start | bytes 172040 | tf_op jit(solution)/shard_map/ppermute | solution.py:676
  31.2 6.3 %collective-permute-start.8 = (f32[112,128]{1,0:T(8,128)S(1)}, f32[112,128]{1,0:T(8,128)S(1)}, u32[]{:S(2)}, u32[]{:S(2)}) collective-permute-start(f32[112,128]{1,0:T(8,128)S(1)} %pad_maximum_fusion), channel_id=1, source_target_pairs={{0,2},{2,0},{4,6},{6,4},{1,3},{3,1},{5,7},{7,5},{8,10},{10,8},{12,... | collective-permute-start | bytes 172040 | tf_op jit(solution)/shard_map/ppermute | solution.py:676
  33.6 7.2 %collective-permute-start.14 = (f32[112,128]{1,0:T(8,128)S(1)}, f32[112,128]{1,0:T(8,128)S(1)}, u32[]{:S(2)}, u32[]{:S(2)}) collective-permute-start(f32[112,128]{1,0:T(8,128)S(1)} %get-tuple-element.64), channel_id=1, source_target_pairs={{0,8},{8,0},{16,24},{24,16},{1,9},{9,1},{17,25},{25,17},{2,10},{10... | collective-permute-start | bytes 172040 | tf_op jit(solution)/shard_map/ppermute | solution.py:536
  34.2 6.6 %collective-permute-start.15 = (f32[112,128]{1,0:T(8,128)S(1)}, f32[112,128]{1,0:T(8,128)S(1)}, u32[]{:S(2)}, u32[]{:S(2)}) collective-permute-start(f32[112,128]{1,0:T(8,128)S(1)} %get-tuple-element.65), channel_id=1, source_target_pairs={{8,16},{24,0},{16,8},{0,24},{9,17},{25,1},{17,9},{1,25},{10,18},{2... | collective-permute-start | bytes 172040 | tf_op jit(solution)/shard_map/ppermute | solution.py:537
  37.5 5.2 %collective-permute-start.13 = (f32[104,128]{1,0:T(8,128)S(1)}, f32[104,128]{1,0:T(8,128)S(1)}, u32[]{:S(2)}, u32[]{:S(2)}) collective-permute-start(f32[104,128]{1,0:T(8,128)S(1)} %slice_add_fusion.refs_1_), channel_id=1, source_target_pairs={{0,24},{1,25},{8,16},{9,17},{16,8},{17,9},{24,0},{25,1},{2,26},{3,... | collective-permute-start | bytes 159752 | tf_op jit(solution)/shard_map/ppermute | solution.py:701
  38.7 4.6 %collective-permute-start.12 = (f32[104,128]{1,0:T(8,128)S(1)}, f32[104,128]{1,0:T(8,128)S(1)}, u32[]{:S(2)}, u32[]{:S(2)}) collective-permute-start(f32[104,128]{1,0:T(8,128)S(1)} %slice_add_fusion.refs_1_), channel_id=1, source_target_pairs={{0,17},{1,16},{8,25},{9,24},{16,1},{17,0},{24,9},{25,8},{2,19},{3,... | collective-permute-start | bytes 159752 | tf_op jit(solution)/shard_map/ppermute | solution.py:701
  39.0 4.4 %collective-permute-start.11 = (f32[104,128]{1,0:T(8,128)S(1)}, f32[104,128]{1,0:T(8,128)S(1)}, u32[]{:S(2)}, u32[]{:S(2)}) collective-permute-start(f32[104,128]{1,0:T(8,128)S(1)} %slice_add_fusion.refs_1_), channel_id=1, source_target_pairs={{0,9},{1,8},{8,1},{9,0},{16,25},{17,24},{24,17},{25,16},{2,11},{3,... | collective-permute-start | bytes 159752 | tf_op jit(solution)/shard_map/ppermute | solution.py:701
  43.4 1.5 %collective-permute-start.16 = (f32[416,128]{1,0:T(8,128)S(1)}, f32[416,128]{1,0:T(8,128)S(1)}, u32[]{:S(2)}, u32[]{:S(2)}) collective-permute-start(f32[416,128]{1,0:T(8,128)S(1)} %constant_dynamic-update-slice_fusion.refs_0_), channel_id=1, source_target_pairs={{0,1},{1,0},{2,3},{3,2},{4,5},{5,4},{6,7},{7,6},{8,9},{9,8},{10,11... | collective-permute-start | bytes 638984 | tf_op jit(solution)/shard_map/ppermute | solution.py:705
  (3 other events, 2.4 us)

commit v12 on v10

--- a/solution.py
+++ b/solution.py
@@ -507,19 +507,21 @@
         out[pl.ds(row, levels, stride=rows), :] = value + wet * d_wet
 
 
-def gather_kernel(levels, height, mine, other, grad_in, grad_bin, grad_out, grad_bout):
+def gather_kernel(levels, height, part, partner, mine_ref, other_ref, grad_in, grad_bin, grad_out, grad_bout):
     keeps_out = half_odd()
     quarter = lax.axis_index("lat") % 4
-    block = mine.shape[1]
+    block = part.shape[1]
     for step in range(4):
+        mine, other = (mine_ref, other_ref) if step else (part, partner)
         at = pl.ds(pl.multiple_of((step ^ quarter) * block, block), block)
-        rows = slice(step * height, (step + 1) * height)
+        first = max(step - 1, 0) * height
+        rows = slice(first, first + height)
         inner = jnp.where(keeps_out, other[rows, :], mine[rows, :])
         outer = jnp.where(keeps_out, mine[rows, :], other[rows, :])
         grad_in[:, at] = inner[0:levels, :]
         grad_bin[:, at] = inner[levels : levels + 1, :]
         grad_out[:, at] = outer[0:levels, :]
-    grad_bout[...] = mine[levels + 2 : levels + 3, 0:levels]
+    grad_bout[...] = part[levels + 2 : levels + 3, 0:levels]
 
 
 def flip(count, by):
@@ -710,7 +712,8 @@
     )
 
     came = {step: lax.ppermute(part, ("lat", "core"), cross_flip(lats, step)) for step in (1, 2, 3)}
-    mine = [part] + [came[step] for step in range(1, 4)]
+    partner = lax.ppermute(part, "core", flip(2, 1))
+    mine = [came[step] for step in range(1, 4)]
     mine, tracer_adjoint = lax.optimization_barrier((mine, tracer_adjoint))
     mine = jnp.concatenate(mine, 0)
     other = lax.ppermute(mine, "core", flip(2, 1))
@@ -722,10 +725,10 @@
             sds((levels, hid), f32),
             sds((1, levels), f32),
         ],
-        in_specs=[vmem] * 2,
+        in_specs=[vmem] * 4,
         out_specs=[vmem] * 4,
         compiler_params=params,
-    )(mine, other)
+    )(part, partner, mine, other)
     return (
         tracer_adjoint.reshape(levels, rows, cols),
         grad_w_in,

time: 46 us -> 46 us (level)
    ppermute x1, waiting for transfers between devices: 1.36 us -> 0.01 us  [shards(): other = lax.ppermute(mine, 'core', flip(2, 1))]
    ppermute x0 -> x1, waiting for transfers between devices: none -> 0.95 us  [shards(): partner = lax.ppermute(part, 'core', flip(2, 1))]
    unnamed x21 -> x20, local copies, waits for them, and re-layouts: 0.99 us -> 0.99 us
  transfers between devices with their start and end apart: 18 -> 19, of which waited for: 8 -> 8; matrix products, arithmetic and copies ran while one was open for 0% -> 0% of each run, Pallas kernels for 9% -> 9%
where the time goes in v12:
time: 46 us; the launch traced here: 45.8 us
  starting transfers between devices  25.3 us (55%)
  waiting for transfers between devices  11.1 us (24%)
  Pallas kernels  7.4 us (16%)
  local copies, waits for them, and re-layouts  1.03 us (2%)
  between operations  0.91 us (2%)
    ppermute x1, starting transfers between devices, shards(): lax.ppermute(small[rows:], ('z', 'core'), far_pairs(lons, True))  4.55 us
    ppermute x3, starting transfers between devices, shards(): lax.ppermute(packed, 'z', flip(chips, step))  4.45 us
    ppermute x2, starting transfers between devices, swap_lat(): far = lax.ppermute(lat_b, 'lat', far_pairs(lats, True))  4.38 us
    all_to_all x1, starting transfers between devices, shards(): energy = lax.all_to_all(energy, ('lat', 'z', 'core'), 0, 0, tiled=True)  3.48 us
    all_to_all x1, waiting for transfers between devices, shards(): energy = lax.all_to_all(energy, ('lat', 'z', 'core'), 0, 0, tiled=True)  3.33 us
    ppermute x3, starting transfers between devices, shards(): lax.ppermute(chip[step], ('lat', 'core'), cross_flip(lats, step))  3.27 us
    ppermute x3, starting transfers between devices, shards(): lax.ppermute(part, ('lat', 'core'), cross_flip(lats, step))  3.27 us
    ppermute x3, waiting for transfers between devices, shards(): lax.ppermute(chip[step], ('lat', 'core'), cross_flip(lats, step))  2.59 us
  transfers between devices with their start and end apart: 19, of which 8 were waited for; matrix products, arithmetic and copies ran while one was open for 0% of the time, Pallas kernels for 9%

profile of v12, /device:TPU:0, one launch (start us, length us, event | category | flops | bytes accessed | tf_op | source)
XLA Modules:
  0.0 45.8 jit_solution(16800834251683548)
XLA Ops:
  0.7 0.6 %copy-done.3 = s32[8,128]{1,0:T(8,128)S(1)} copy-done((s32[8,128]{1,0:T(8,128)S(1)}, s32[8,128]{1,0:T(8,128)}, u32[]{:S(2)}) %copy-start.3) | copy-done | bytes 4120
  2.0 4.6 %collective-permute-start.3 = (f32[8,128]{1,0:T(8,128)S(1)}, f32[8,128]{1,0:T(8,128)S(1)}, u32[]{:S(2)}, u32[]{:S(2)}) collective-permute-start(f32[8,128]{1,0:T(8,128)S(1)} %get-tuple-element.84), channel_id=1, source_target_pairs={{1,2},{3,4},{5,6},{7,0},{2,1},{4,3},{6,5},{0,7},{9,10},{11,12},{13... | collective-permute-start | bytes 12296 | tf_op jit(solution)/shard_map/ppermute | solution.py:608
  6.5 0.8 %shard_map.131 = f32[32,1,128]{2,1,0:T(1,128)} custom-call(f32[800,128]{1,0:T(8,128)S(1)} %bitcast.26, f32[8,128]{1,0:T(8,128)S(1)} %get-tuple-element.42.refs_1_.refs_7_.refs_5_), custom_call_target="tpu_custom_call" | custom-call | flops 1000000000 | bytes 100000000 | tf_op jit(solution)/shard_map/pallas_call | solution.py:595
  7.3 3.5 %all-to-all-start = ((f32[32,1,128]{2,1,0:T(1,128)}), f32[32,1,128]{2,1,0:T(1,128)S(1)}, u32[]{:S(2)}, u32[]{:S(2)}) async-start(f32[32,1,128]{2,1,0:T(1,128)} %shard_map.131), calls=%async_computation | async-start | bytes 32768 | tf_op jit(solution)/shard_map/all_to_all | solution.py:604
  10.8 2.7 %collective-permute-start.1 = (f32[104,128]{1,0:T(8,128)S(1)}, f32[104,128]{1,0:T(8,128)S(1)}, u32[]{:S(2)}, u32[]{:S(2)}) collective-permute-start(f32[104,128]{1,0:T(8,128)S(1)} %get-tuple-element.40), channel_id=1, source_target_pairs={{8,16},{24,0},{16,8},{0,24},{9,17},{25,1},{17,9},{1,25},{10,18},{2... | collective-permute-start | bytes 159752 | tf_op jit(solution)/shard_map/ppermute | solution.py:550
  14.5 3.3 %all-to-all-done.refs_0_ = f32[32,1,128]{2,1,0:T(1,128)S(1)} async-done(((f32[32,1,128]{2,1,0:T(1,128)}), f32[32,1,128]{2,1,0:T(1,128)S(1)}, u32[]{:S(2)}, u32[]{:S(2)}) %all-to-all-start) | async-done | bytes 16416 | tf_op jit(solution)/shard_map/all_to_all | solution.py:604
  17.9 1.4 %shard_map.132 = (f32[1,128]{1,0:T(1,128)S(1)}, bf16[128,1024]{1,0:T(8,128)(2,1)S(1)}, bf16[512,1024]{1,0:T(8,128)(2,1)S(1)}, f32[512,1024]{1,0:T(8,128)S(1)}, f...) custom-call(f32[32,1,128]{2,1,0:T(1,128)S(1)} %all-to-all-done.refs_0_, ...), custom_call_target="tpu_custom_call" | custom-call | tf_op jit(solution)/shard_map/pallas_call | solution.py:632
  19.4 2.2 %shard_map.133 = (f32[4,104,128]{2,1,0:T(8,128)S(1)}, f32[432,128]{1,0:T(8,128)S(1)}, f32[800,128]{1,0:T(8,128)S(1)}, f32[112,128]{1,0:T(8,128)S(1)}, f32[112,12...) custom-call(f32[800,128]{1,0:T(8,128)S(1)} %bitcast.28, f32[104,128]{1,0:T(8,128)S(1)} %get-tuple-element.81.refs_1_.refs_10_, ...), custom_call_target="tpu_custom_call" | custom-call | tf_op jit(solution)/shard_map/pallas_call | solution.py:648
  21.7 1.5 %collective-permute-done.4 = f32[432,128]{1,0:T(8,128)S(1)} collective-permute-done((f32[432,128]{1,0:T(8,128)S(1)}, f32[432,128]{1,0:T(8,128)S(1)}, u32[]{:S(2)}, u32[]{:S(2)}) %collective-permute-start.4) | collective-permute-done | bytes 221216 | tf_op jit(solution)/shard_map/ppermute | solution.py:674
  23.2 0.7 %collective-permute-start.5 = (f32[104,128]{1,0:T(8,128)S(1)}, f32[104,128]{1,0:T(8,128)S(1)}, u32[]{:S(2)}, u32[]{:S(2)}) collective-permute-start(f32[104,128]{1,0:T(8,128)S(1)} %get-tuple-element.75), channel_id=1, source_target_pairs={{0,24},{1,25},{8,16},{9,17},{16,8},{17,9},{24,0},{25,1},{2,26},{3,... | collective-permute-start | bytes 159752 | tf_op jit(solution)/shard_map/ppermute | solution.py:680
  23.9 0.9 %collective-permute-start.7 = (f32[104,128]{1,0:T(8,128)S(1)}, f32[104,128]{1,0:T(8,128)S(1)}, u32[]{:S(2)}, u32[]{:S(2)}) collective-permute-start(f32[104,128]{1,0:T(8,128)S(1)} %get-tuple-element.76), channel_id=1, source_target_pairs={{0,9},{1,8},{8,1},{9,0},{16,25},{17,24},{24,17},{25,16},{2,11},{3,... | collective-permute-start | bytes 159752 | tf_op jit(solution)/shard_map/ppermute | solution.py:680
  24.8 1.7 %collective-permute-start.6 = (f32[104,128]{1,0:T(8,128)S(1)}, f32[104,128]{1,0:T(8,128)S(1)}, u32[]{:S(2)}, u32[]{:S(2)}) collective-permute-start(f32[104,128]{1,0:T(8,128)S(1)} %get-tuple-element.77), channel_id=1, source_target_pairs={{0,17},{1,16},{8,25},{9,24},{16,1},{17,0},{24,9},{25,8},{2,19},{3,... | collective-permute-start | bytes 159752 | tf_op jit(solution)/shard_map/ppermute | solution.py:680
  26.5 2.4 %collective-permute-done.5 = f32[104,128]{1,0:T(8,128)S(1)} collective-permute-done((f32[104,128]{1,0:T(8,128)S(1)}, f32[104,128]{1,0:T(8,128)S(1)}, u32[]{:S(2)}, u32[]{:S(2)}) %collective-permute-start.5) | collective-permute-done | bytes 53280 | tf_op jit(solution)/shard_map/ppermute | solution.py:680
  29.1 1.9 %collective-permute-start.10 = (f32[112,128]{1,0:T(8,128)S(1)}, f32[112,128]{1,0:T(8,128)S(1)}, u32[]{:S(2)}, u32[]{:S(2)}) collective-permute-start(f32[112,128]{1,0:T(8,128)S(1)} %pad_maximum_fusion), channel_id=1, source_target_pairs={{0,6},{2,4},{4,2},{6,0},{1,7},{3,5},{5,3},{7,1},{8,14},{10,12},{12... | collective-permute-start | bytes 172040 | tf_op jit(solution)/shard_map/ppermute | solution.py:689
  31.2 2.4 %collective-permute-start.8 = (f32[112,128]{1,0:T(8,128)S(1)}, f32[112,128]{1,0:T(8,128)S(1)}, u32[]{:S(2)}, u32[]{:S(2)}) collective-permute-start(f32[112,128]{1,0:T(8,128)S(1)} %pad_maximum_fusion), channel_id=1, source_target_pairs={{0,2},{2,0},{4,6},{6,4},{1,3},{3,1},{5,7},{7,5},{8,10},{10,8},{12,... | collective-permute-start | bytes 172040 | tf_op jit(solution)/shard_map/ppermute | solution.py:689
  33.6 0.7 %collective-permute-start.14 = (f32[112,128]{1,0:T(8,128)S(1)}, f32[112,128]{1,0:T(8,128)S(1)}, u32[]{:S(2)}, u32[]{:S(2)}) collective-permute-start(f32[112,128]{1,0:T(8,128)S(1)} %get-tuple-element.63), channel_id=1, source_target_pairs={{0,8},{8,0},{16,24},{24,16},{1,9},{9,1},{17,25},{25,17},{2,10},{10... | collective-permute-start | bytes 172040 | tf_op jit(solution)/shard_map/ppermute | solution.py:549
  34.2 1.6 %collective-permute-start.15 = (f32[112,128]{1,0:T(8,128)S(1)}, f32[112,128]{1,0:T(8,128)S(1)}, u32[]{:S(2)}, u32[]{:S(2)}) collective-permute-start(f32[112,128]{1,0:T(8,128)S(1)} %get-tuple-element.64), channel_id=1, source_target_pairs={{8,16},{24,0},{16,8},{0,24},{9,17},{25,1},{17,9},{1,25},{10,18},{2... | collective-permute-start | bytes 172040 | tf_op jit(solution)/shard_map/ppermute | solution.py:550
  35.9 1.6 %collective-permute-done.9 = f32[112,128]{1,0:T(8,128)S(1)} collective-permute-done((f32[112,128]{1,0:T(8,128)S(1)}, f32[112,128]{1,0:T(8,128)S(1)}, u32[]{:S(2)}, u32[]{:S(2)}) %collective-permute-start.9) | collective-permute-done | bytes 57376 | tf_op jit(solution)/shard_map/ppermute | solution.py:689
  37.5 1.2 %collective-permute-start.13 = (f32[104,128]{1,0:T(8,128)S(1)}, f32[104,128]{1,0:T(8,128)S(1)}, u32[]{:S(2)}, u32[]{:S(2)}) collective-permute-start(f32[104,128]{1,0:T(8,128)S(1)} %slice_add_fusion.refs_1_.refs_0_), channel_id=1, source_target_pairs={{0,24},{1,25},{8,16},{9,17},{16,8},{17,9},{24,0},{25,1},{2,26},{3,... | collective-permute-start | bytes 159752 | tf_op jit(solution)/shard_map/ppermute | solution.py:714
  38.9 1.8 %collective-permute-start.11 = (f32[104,128]{1,0:T(8,128)S(1)}, f32[104,128]{1,0:T(8,128)S(1)}, u32[]{:S(2)}, u32[]{:S(2)}) collective-permute-start(f32[104,128]{1,0:T(8,128)S(1)} %slice_add_fusion.refs_1_.refs_0_), channel_id=1, source_target_pairs={{0,9},{1,8},{8,1},{9,0},{16,25},{17,24},{24,17},{25,16},{2,11},{3,... | collective-permute-start | bytes 159752 | tf_op jit(solution)/shard_map/ppermute | solution.py:714
  40.8 1.5 %shard_map.134 = f32[800,128]{1,0:T(8,128)} custom-call(f32[1,128]{1,0:T(1,128)S(1)} %get-tuple-element.60.refs_0_, f32[104,128]{1,0:T(8,128)S(1)} %slice_add_fusion.refs_1_.refs_0_, f32[800,128]{1,0:T(8,128)S(1)} %get-tuple-element.61.refs_2_, f32[128,1024]{1,0:T(8,128)S(1)} %get-tuple-element.43.refs_1_.refs_5_.refs_3_, ...), custom_call_target="tpu_custom_call" | custom-call | tf_op jit(solution)/shard_map/pallas_call | solution.py:703
  42.7 0.7 %collective-permute-done.12 = f32[104,128]{1,0:T(8,128)S(1)} collective-permute-done((f32[104,128]{1,0:T(8,128)S(1)}, f32[104,128]{1,0:T(8,128)S(1)}, u32[]{:S(2)}, u32[]{:S(2)}) %collective-permute-start.12) | collective-permute-done | bytes 53280 | tf_op jit(solution)/shard_map/ppermute | solution.py:714
  44.0 1.0 %collective-permute-done.16.refs_1_ = f32[104,128]{1,0:T(8,128)S(1)} collective-permute-done((f32[104,128]{1,0:T(8,128)S(1)}, f32[104,128]{1,0:T(8,128)S(1)}, u32[]{:S(2)}, u32[]{:S(2)}) %collective-permute-start.16) | collective-permute-done | bytes 53280 | tf_op jit(solution)/shard_map/ppermute | solution.py:715
  45.0 0.8 %shard_map.135 = (f32[100,512]{1,0:T(8,128)}, f32[1,512]{1,0:T(1,128)}, f32[100,512]{1,0:T(8,128)}, f32[1,100]{1,0:T(1,128)}) custom-call(f32[104,128]{1,0:T(8,128)S(1)} %slice_add_fusion.refs_1_.refs_0_, f32[104,128]{1,0:T(8,128)S(1)} %collective-permute-done.16.refs_1_, f32[312,128]{1,0:T(8,128)S(1)} %constant_dynamic-update-slice_fusion.refs_2_, ...), custom_call_target="tpu_custom_call" | custom-call | tf_op jit(solution)/shard_map/pallas_call | solution.py:720
  (55 shorter events, 3.4 us)
Async XLA Ops:
  0.7 13.4 %copy-start.4 = (bf16[100,512]{1,0:T(8,128)(2,1)S(1)}, bf16[100,512]{1,0:T(8,128)(2,1)}, u32[]{:S(2)}) copy-start(bf16[100,512]{1,0:T(8,128)(2,1)} %refs_2_.3) | copy-start | bytes 307204
  0.7 13.4 %copy-start.5 = (bf16[512,100]{0,1:T(8,128)(2,1)S(1)}, bf16[512,100]{0,1:T(8,128)(2,1)}, u32[]{:S(2)}) copy-start(bf16[512,100]{0,1:T(8,128)(2,1)} %param.16) | copy-start | bytes 307204
  0.7 13.4 %copy-start.6 = (f32[512]{0:T(512)S(1)}, f32[512]{0:T(512)}, u32[]{:S(2)}) copy-start(f32[512]{0:T(512)} %param.15) | copy-start | bytes 6148
  0.7 13.4 %copy-start.7 = (f32[100]{0:T(128)S(1)}, f32[100]{0:T(128)}, u32[]{:S(2)}) copy-start(f32[100]{0:T(128)} %param.17) | copy-start | bytes 1204
  0.7 13.4 %copy-start.8 = (f32[100]{0:T(128)S(1)}, f32[100]{0:T(128)}, u32[]{:S(2)}) copy-start(f32[100]{0:T(128)} %param.13) | copy-start | bytes 1204
  2.0 12.6 %collective-permute-start.3 = (f32[8,128]{1,0:T(8,128)S(1)}, f32[8,128]{1,0:T(8,128)S(1)}, u32[]{:S(2)}, u32[]{:S(2)}) collective-permute-start(f32[8,128]{1,0:T(8,128)S(1)} %get-tuple-element.84), channel_id=1, source_target_pairs={{1,2},{3,4},{5,6},{7,0},{2,1},{4,3},{6,5},{0,7},{9,10},{11,12},{13... | collective-permute-start | bytes 12296 | tf_op jit(solution)/shard_map/ppermute | solution.py:608
  6.5 8.0 %collective-permute-start.2 = (f32[8,128]{1,0:T(8,128)S(1)}, f32[8,128]{1,0:T(8,128)S(1)}, u32[]{:S(2)}, u32[]{:S(2)}) collective-permute-start(f32[8,128]{1,0:T(8,128)S(1)} %get-tuple-element.85), channel_id=1, source_target_pairs={{0,1},{1,0},{2,3},{3,2},{4,5},{5,4},{6,7},{7,6},{8,9},{9,8},{10,11... | collective-permute-start | bytes 12296 | tf_op jit(solution)/shard_map/ppermute | solution.py:607
  7.3 10.6 %all-to-all-start = ((f32[32,1,128]{2,1,0:T(1,128)}), f32[32,1,128]{2,1,0:T(1,128)S(1)}, u32[]{:S(2)}, u32[]{:S(2)}) async-start(f32[32,1,128]{2,1,0:T(1,128)} %shard_map.131), calls=%async_computation | async-start | bytes 32768 | tf_op jit(solution)/shard_map/all_to_all | solution.py:604
  10.8 8.5 %collective-permute-start.1 = (f32[104,128]{1,0:T(8,128)S(1)}, f32[104,128]{1,0:T(8,128)S(1)}, u32[]{:S(2)}, u32[]{:S(2)}) collective-permute-start(f32[104,128]{1,0:T(8,128)S(1)} %get-tuple-element.40), channel_id=1, source_target_pairs={{8,16},{24,0},{16,8},{0,24},{9,17},{25,1},{17,9},{1,25},{10,18},{2... | collective-permute-start | bytes 159752 | tf_op jit(solution)/shard_map/ppermute | solution.py:550
  13.5 5.8 %collective-permute-start = (f32[112,128]{1,0:T(8,128)S(1)}, f32[112,128]{1,0:T(8,128)S(1)}, u32[]{:S(2)}, u32[]{:S(2)}) collective-permute-start(f32[112,128]{1,0:T(8,128)S(1)} %get-tuple-element.39), channel_id=1, source_target_pairs={{0,8},{8,0},{16,24},{24,16},{1,9},{9,1},{17,25},{25,17},{2,10},{10... | collective-permute-start | bytes 172040 | tf_op jit(solution)/shard_map/ppermute | solution.py:549
  21.6 1.5 %collective-permute-start.4 = (f32[432,128]{1,0:T(8,128)S(1)}, f32[432,128]{1,0:T(8,128)S(1)}, u32[]{:S(2)}, u32[]{:S(2)}) collective-permute-start(f32[432,128]{1,0:T(8,128)S(1)} %get-tuple-element.56), channel_id=1, source_target_pairs={{0,1},{1,0},{2,3},{3,2},{4,5},{5,4},{6,7},{7,6},{8,9},{9,8},{10,11... | collective-permute-start | bytes 663560 | tf_op jit(solution)/shard_map/ppermute | solution.py:674
  23.2 5.7 %collective-permute-start.5 = (f32[104,128]{1,0:T(8,128)S(1)}, f32[104,128]{1,0:T(8,128)S(1)}, u32[]{:S(2)}, u32[]{:S(2)}) collective-permute-start(f32[104,128]{1,0:T(8,128)S(1)} %get-tuple-element.75), channel_id=1, source_target_pairs={{0,24},{1,25},{8,16},{9,17},{16,8},{17,9},{24,0},{25,1},{2,26},{3,... | collective-permute-start | bytes 159752 | tf_op jit(solution)/shard_map/ppermute | solution.py:680
  23.9 5.0 %collective-permute-start.7 = (f32[104,128]{1,0:T(8,128)S(1)}, f32[104,128]{1,0:T(8,128)S(1)}, u32[]{:S(2)}, u32[]{:S(2)}) collective-permute-start(f32[104,128]{1,0:T(8,128)S(1)} %get-tuple-element.76), channel_id=1, source_target_pairs={{0,9},{1,8},{8,1},{9,0},{16,25},{17,24},{24,17},{25,16},{2,11},{3,... | collective-permute-start | bytes 159752 | tf_op jit(solution)/shard_map/ppermute | solution.py:680
  24.8 4.3 %collective-permute-start.6 = (f32[104,128]{1,0:T(8,128)S(1)}, f32[104,128]{1,0:T(8,128)S(1)}, u32[]{:S(2)}, u32[]{:S(2)}) collective-permute-start(f32[104,128]{1,0:T(8,128)S(1)} %get-tuple-element.77), channel_id=1, source_target_pairs={{0,17},{1,16},{8,25},{9,24},{16,1},{17,0},{24,9},{25,8},{2,19},{3,... | collective-permute-start | bytes 159752 | tf_op jit(solution)/shard_map/ppermute | solution.py:680
  29.1 6.8 %collective-permute-start.10 = (f32[112,128]{1,0:T(8,128)S(1)}, f32[112,128]{1,0:T(8,128)S(1)}, u32[]{:S(2)}, u32[]{:S(2)}) collective-permute-start(f32[112,128]{1,0:T(8,128)S(1)} %pad_maximum_fusion), channel_id=1, source_target_pairs={{0,6},{2,4},{4,2},{6,0},{1,7},{3,5},{5,3},{7,1},{8,14},{10,12},{12... | collective-permute-start | bytes 172040 | tf_op jit(solution)/shard_map/ppermute | solution.py:689
  31.0 6.5 %collective-permute-start.9 = (f32[112,128]{1,0:T(8,128)S(1)}, f32[112,128]{1,0:T(8,128)S(1)}, u32[]{:S(2)}, u32[]{:S(2)}) collective-permute-start(f32[112,128]{1,0:T(8,128)S(1)} %pad_maximum_fusion), channel_id=1, source_target_pairs={{0,4},{2,6},{4,0},{6,2},{1,5},{3,7},{5,1},{7,3},{8,12},{10,14},{12... | collective-permute-start | bytes 172040 | tf_op jit(solution)/shard_map/ppermute | solution.py:689
  31.2 6.3 %collective-permute-start.8 = (f32[112,128]{1,0:T(8,128)S(1)}, f32[112,128]{1,0:T(8,128)S(1)}, u32[]{:S(2)}, u32[]{:S(2)}) collective-permute-start(f32[112,128]{1,0:T(8,128)S(1)} %pad_maximum_fusion), channel_id=1, source_target_pairs={{0,2},{2,0},{4,6},{6,4},{1,3},{3,1},{5,7},{7,5},{8,10},{10,8},{12,... | collective-permute-start | bytes 172040 | tf_op jit(solution)/shard_map/ppermute | solution.py:689
  33.6 7.2 %collective-permute-start.14 = (f32[112,128]{1,0:T(8,128)S(1)}, f32[112,128]{1,0:T(8,128)S(1)}, u32[]{:S(2)}, u32[]{:S(2)}) collective-permute-start(f32[112,128]{1,0:T(8,128)S(1)} %get-tuple-element.63), channel_id=1, source_target_pairs={{0,8},{8,0},{16,24},{24,16},{1,9},{9,1},{17,25},{25,17},{2,10},{10... | collective-permute-start | bytes 172040 | tf_op jit(solution)/shard_map/ppermute | solution.py:549
  34.2 6.5 %collective-permute-start.15 = (f32[112,128]{1,0:T(8,128)S(1)}, f32[112,128]{1,0:T(8,128)S(1)}, u32[]{:S(2)}, u32[]{:S(2)}) collective-permute-start(f32[112,128]{1,0:T(8,128)S(1)} %get-tuple-element.64), channel_id=1, source_target_pairs={{8,16},{24,0},{16,8},{0,24},{9,17},{25,1},{17,9},{1,25},{10,18},{2... | collective-permute-start | bytes 172040 | tf_op jit(solution)/shard_map/ppermute | solution.py:550
  37.5 5.2 %collective-permute-start.13 = (f32[104,128]{1,0:T(8,128)S(1)}, f32[104,128]{1,0:T(8,128)S(1)}, u32[]{:S(2)}, u32[]{:S(2)}) collective-permute-start(f32[104,128]{1,0:T(8,128)S(1)} %slice_add_fusion.refs_1_.refs_0_), channel_id=1, source_target_pairs={{0,24},{1,25},{8,16},{9,17},{16,8},{17,9},{24,0},{25,1},{2,26},{3,... | collective-permute-start | bytes 159752 | tf_op jit(solution)/shard_map/ppermute | solution.py:714
  38.7 4.6 %collective-permute-start.12 = (f32[104,128]{1,0:T(8,128)S(1)}, f32[104,128]{1,0:T(8,128)S(1)}, u32[]{:S(2)}, u32[]{:S(2)}) collective-permute-start(f32[104,128]{1,0:T(8,128)S(1)} %slice_add_fusion.refs_1_.refs_0_), channel_id=1, source_target_pairs={{0,17},{1,16},{8,25},{9,24},{16,1},{17,0},{24,9},{25,8},{2,19},{3,... | collective-permute-start | bytes 159752 | tf_op jit(solution)/shard_map/ppermute | solution.py:714
  38.9 4.4 %collective-permute-start.11 = (f32[104,128]{1,0:T(8,128)S(1)}, f32[104,128]{1,0:T(8,128)S(1)}, u32[]{:S(2)}, u32[]{:S(2)}) collective-permute-start(f32[104,128]{1,0:T(8,128)S(1)} %slice_add_fusion.refs_1_.refs_0_), channel_id=1, source_target_pairs={{0,9},{1,8},{8,1},{9,0},{16,25},{17,24},{24,17},{25,16},{2,11},{3,... | collective-permute-start | bytes 159752 | tf_op jit(solution)/shard_map/ppermute | solution.py:714
  43.4 1.5 %collective-permute-start.17 = (f32[312,128]{1,0:T(8,128)S(1)}, f32[312,128]{1,0:T(8,128)S(1)}, u32[]{:S(2)}, u32[]{:S(2)}) collective-permute-start(f32[312,128]{1,0:T(8,128)S(1)} %constant_dynamic-update-slice_fusion.refs_2_), channel_id=1, source_target_pairs={{0,1},{1,0},{2,3},{3,2},{4,5},{5,4},{6,7},{7,6},{8,9},{9,8},{10,11... | collective-permute-start | bytes 479240 | tf_op jit(solution)/shard_map/ppermute | solution.py:719
  43.6 1.4 %collective-permute-start.16 = (f32[104,128]{1,0:T(8,128)S(1)}, f32[104,128]{1,0:T(8,128)S(1)}, u32[]{:S(2)}, u32[]{:S(2)}) collective-permute-start(f32[104,128]{1,0:T(8,128)S(1)} %slice_add_fusion.refs_1_.refs_0_), channel_id=1, source_target_pairs={{0,1},{1,0},{2,3},{3,2},{4,5},{5,4},{6,7},{7,6},{8,9},{9,8},{10,11... | collective-permute-start | bytes 159752 | tf_op jit(solution)/shard_map/ppermute | solution.py:715
  (4 other events, 7.6 us)
